TPU v7x, 32 devices: a whole 2x2x4 slice. The times are simulated.
32 devices in a mesh: grp: 2 (over y), wide: 16 (over z, x, core).
Axes of the slice: x: 2, y: 2, z: 4, core: 2. Of those that a mesh axis runs over, the one named last changes fastest.
Arguments:
- source_points: bfloat16 [64, 12288], P(None, ('grp', 'wide')), parts along dimension 1, may hold values from -25 to 25
- target_points: bfloat16 [64, 4096], P(None, ('grp', 'wide')), parts along dimension 1, may hold values from -25 to 25
- source_logw: bfloat16 [12288], P(('grp', 'wide')), parts along dimension 0, may hold values from -1 to 1
- target_logw: bfloat16 [4096], P(('grp', 'wide')), parts along dimension 0, may hold values from -1 to 1
- inverse_eps: float32 [1], replicated, may hold values from 0.08 to 0.12
Outputs:
- mapped: float32 [64, 12288], P(None, ('grp', 'wide')), parts along dimension 1
- target_potential: float32 [4096], P(('grp', 'wide')), parts along dimension 0
There are 2 independent parts, one for each index of `grp`. A program takes and returns all parts, laid end to end along the dimension named above; an argument that names none is the same for every part. Nothing has to cross between parts.
All inputs are finite; a program needn't handle non-finite values.
Results may differ from a plain program's by a relative error of at most 0.0024.
Values may be sent and summed in bfloat16 or wider, within the bound.
No kernel may reach another device: no remote copies, remote signals or barrier semaphores. Data moves between devices by JAX's collectives and lax.ppermute only.
A program may use at most 64 MiB of HBM per device.

v0:
```python
import math

import jax
import jax.numpy as jnp
from jax import lax
from jax.sharding import PartitionSpec as P

ITERS = 2


def sq_norms(points):
    return jnp.sum(jnp.square(points.astype(jnp.float32)), axis=0)


def tile_scores(left, sq_left, right, sq_right, term, inverse):
    cross = lax.dot_general(
        left, right, (((0,), (0,)), ((), ())), preferred_element_type=jnp.float32
    )
    return term[None, :] - inverse * (sq_left[:, None] + sq_right[None, :] - 2.0 * cross)


def online_lse(left, sq_left, right, sq_right, term, inverse):
    total = right.shape[1]
    width = math.gcd(total, 2048)

    def online_advance(block_id, carry):
        running, totals = carry
        begin = block_id * width
        piece = lax.dynamic_slice_in_dim(right, begin, width, 1)
        sq_piece = lax.dynamic_slice_in_dim(sq_right, begin, width, 0)
        term_piece = lax.dynamic_slice_in_dim(term, begin, width, 0)
        scores = tile_scores(left, sq_left, piece, sq_piece, term_piece, inverse)
        updated = jnp.maximum(running, jnp.max(scores, axis=1))
        totals = totals * jnp.exp(running - updated) + jnp.sum(
            jnp.exp(scores - updated[:, None]), axis=1
        )
        return (updated, totals)

    rows = left.shape[1]
    start_state = (jnp.full((rows,), -jnp.inf, jnp.float32), jnp.zeros((rows,), jnp.float32))
    running, totals = lax.fori_loop(0, total // width, online_advance, start_state)
    return running + jnp.log(totals)


def barycentre(left, sq_left, right, sq_right, term, inverse, final_lse):
    total = right.shape[1]
    width = math.gcd(total, 2048)

    def barycentre_advance(block_id, accum):
        begin = block_id * width
        piece = lax.dynamic_slice_in_dim(right, begin, width, 1)
        sq_piece = lax.dynamic_slice_in_dim(sq_right, begin, width, 0)
        term_piece = lax.dynamic_slice_in_dim(term, begin, width, 0)
        scores = tile_scores(left, sq_left, piece, sq_piece, term_piece, inverse)
        weights = jnp.exp(scores - final_lse[:, None]).astype(jnp.bfloat16)
        return accum + lax.dot_general(
            weights, piece, (((1,), (1,)), ((), ())), preferred_element_type=jnp.float32
        )

    start_accum = jnp.zeros((left.shape[1], right.shape[0]), jnp.float32)
    return lax.fori_loop(0, total // width, barycentre_advance, start_accum).T


def on_device(source_points, target_points, source_logw, target_logw, inverse_eps):
    inverse = inverse_eps[0]
    all_targets, all_logb = (
        lax.all_gather(target_points, "wide", axis=1, tiled=True),
        lax.all_gather(target_logw, "wide", axis=0, tiled=True),
    )
    sq_targets = sq_norms(all_targets)
    sq_sources = sq_norms(source_points)
    sq_own_targets = sq_norms(target_points)
    weight_b = all_logb.astype(jnp.float32)
    tgt_rows = target_points.shape[1]
    all_sources, all_loga = (
        lax.all_gather(source_points, "wide", axis=1, tiled=True),
        lax.all_gather(source_logw, "wide", axis=0, tiled=True),
    )
    sq_all_sources = sq_norms(all_sources)
    weight_all_a = all_loga.astype(jnp.float32)
    target_pot = jnp.zeros((all_targets.shape[1],), jnp.float32)
    own_pot = jnp.zeros((tgt_rows,), jnp.float32)
    for iteration in range(ITERS):
        source_pot = -online_lse(
            source_points, sq_sources, all_targets, sq_targets, target_pot + weight_b, inverse
        )
        all_source_pot = lax.all_gather(source_pot, "wide", axis=0, tiled=True)
        own_pot = -online_lse(
            target_points,
            sq_own_targets,
            all_sources,
            sq_all_sources,
            all_source_pot + weight_all_a,
            inverse,
        )
        target_pot = lax.all_gather(own_pot, "wide", axis=0, tiled=True)
    final_term = target_pot + weight_b
    final_lse = online_lse(source_points, sq_sources, all_targets, sq_targets, final_term, inverse)
    mapped = barycentre(
        source_points, sq_sources, all_targets, sq_targets, final_term, inverse, final_lse
    )
    return (mapped, own_pot)


def solution(mesh):
    placed = (
        P(None, ("grp", "wide")),
        P(None, ("grp", "wide")),
        P(("grp", "wide")),
        P(("grp", "wide")),
        P(),
    )
    return jax.shard_map(
        on_device,
        mesh=mesh,
        in_specs=placed,
        out_specs=(P(None, ("grp", "wide")), P(("grp", "wide"))),
        check_vma=False,
    )
```

profile of v0, /device:TPU:0, one launch (start us, length us, event | category | flops | bytes accessed | tf_op | source)
XLA Modules:
  0.0 191.3 jit_solution(6549057550252474907)
XLA Ops:
  0.6 23.1 %all-gather = bf16[16,1,128]{2,1,0:T(2,128)(2,1)S(1)} all-gather(bf16[1,1,128]{2,1,0:T(2,128)(2,1)} %bitcast.46), channel_id=1, replica_groups=mesh['grp'=2,'wide'=16] {'wide'}, dimensions={0}, use_global_device_ids=true | all-gather | bytes 4352 | tf_op jit(solution)/shard_map/all_gather | solution.py:68
  23.8 18.4 %all_gather.25 = bf16[64,2048]{1,0:T(8,128)(2,1)S(1)} all-gather(bf16[64,128]{1,0:T(8,128)(2,1)} %param.10), channel_id=1, replica_groups=mesh['grp'=2,'wide'=16] {'wide'}, dimensions={1}, use_global_device_ids=true | all-gather | bytes 278528 | tf_op jit(solution)/shard_map/all_gather | solution.py:67
  42.1 0.1 multiply_reduce_fusion.1
  42.2 0.8 multiply_reduce_fusion.2
  43.7 0.0 copy-start.3
  43.7 0.0 copy-start.1
  43.7 1.8 subtract_reduce_fusion.1
  45.5 0.0 copy-start.2
  45.5 0.7 exponential_reduce_fusion.4
  46.2 18.8 %all-gather.1 = f32[16,1,384]{2,1,0:T(1,128)S(1)} all-gather(f32[1,1,384]{2,1,0:T(1,128)S(1)} %reshape.32), channel_id=1, replica_groups=mesh['grp'=2,'wide'=16] {'wide'}, dimensions={0}, use_global_device_ids=true | all-gather | bytes 26112 | tf_op jit(solution)/shard_map/all_gather | solution.py:87
  65.0 0.0 copy-done.3
  65.0 17.5 %all-gather.2 = bf16[16,1,384]{2,1,0:T(2,128)(2,1)S(1)} all-gather(bf16[1,1,384]{2,1,0:T(2,128)(2,1)S(1)} %reshape.34), channel_id=1, replica_groups=mesh['grp'=2,'wide'=16] {'wide'}, dimensions={0}, use_global_device_ids=true | all-gather | bytes 13056 | tf_op jit(solution)/shard_map/all_gather | solution.py:77
  82.5 0.0 copy-done.1
  82.6 20.9 %all_gather.28 = bf16[64,6144]{1,0:T(8,128)(2,1)S(1)} all-gather(bf16[64,384]{1,0:T(8,128)(2,1)S(1)} %copy-done.1), channel_id=1, replica_groups=mesh['grp'=2,'wide'=16] {'wide'}, dimensions={1}, use_global_device_ids=true | all-gather | bytes 835584 | tf_op jit(solution)/shard_map/all_gather | solution.py:76
  103.5 0.0 copy-start
  103.5 0.9 copy-done
  104.4 0.2 multiply_reduce_fusion
  104.6 0.0 copy-done.2
  104.7 14.8 %while.20 = (s32[]{:T(128)}, f32[128]{0:T(128)S(1)}, f32[128]{0:T(128)S(1)}, f32[6144]{0:T(1024)S(1)}, f32[]{:T(128)}, /*index=5*/f32[128]{0:T(128)S(1)}, f32[61...) while((s32[]{:T(128)}, f32[128]{0:T(128)S(1)}, ...), condition=%wide.region_9.10_spmd.clone, body=%wide.region_6.9_spmd.clone.sunk | while | flops 35652228 | bytes 2432706 | solution.py:41
  104.7 3.3 %fusion.36 = (f32[128]{0:T(128)S(1)}, f32[128,2048]{0,1:T(8,128)}) fusion(bf16[64,128]{1,0:T(8,128)(2,1)S(1)} %get-tuple-element.690, bf16[64,6144]{1,0:T(8,128)(2,1)} %get-tuple-element.689, s32[]{:T(128)S(6)} %select_n.38, f32[2048]{0:T(1024)S(1)} %dynamic_slice.87, f32[128]{0:T(128)S(1)} %get-tuple-element.687, f32[]{:T(128)} %get-tuple-element.686, ...), kind=kOutput, calls=%fused_computation.47.clone.1 | convolution fusion | flops 35127168 | bytes 1345028 | tf_op jit(solution)/shard_map/while/body/eval_jaxpr/dot_general | solution.py:16
  108.1 1.5 exponential_reduce_fusion.7
  109.7 3.3 %fusion.36 = (f32[128]{0:T(128)S(1)}, f32[128,2048]{0,1:T(8,128)}) fusion(bf16[64,128]{1,0:T(8,128)(2,1)S(1)} %get-tuple-element.690, bf16[64,6144]{1,0:T(8,128)(2,1)} %get-tuple-element.689, s32[]{:T(128)S(6)} %select_n.38, f32[2048]{0:T(1024)S(1)} %dynamic_slice.87, f32[128]{0:T(128)S(1)} %get-tuple-element.687, f32[]{:T(128)} %get-tuple-element.686, ...), kind=kOutput, calls=%fused_computation.47.clone.1 | convolution fusion | flops 35127168 | bytes 1345028 | tf_op jit(solution)/shard_map/while/body/eval_jaxpr/dot_general | solution.py:16
  113.0 1.5 exponential_reduce_fusion.7
  114.6 3.3 %fusion.36 = (f32[128]{0:T(128)S(1)}, f32[128,2048]{0,1:T(8,128)}) fusion(bf16[64,128]{1,0:T(8,128)(2,1)S(1)} %get-tuple-element.690, bf16[64,6144]{1,0:T(8,128)(2,1)} %get-tuple-element.689, s32[]{:T(128)S(6)} %select_n.38, f32[2048]{0:T(1024)S(1)} %dynamic_slice.87, f32[128]{0:T(128)S(1)} %get-tuple-element.687, f32[]{:T(128)} %get-tuple-element.686, ...), kind=kOutput, calls=%fused_computation.47.clone.1 | convolution fusion | flops 35127168 | bytes 1345028 | tf_op jit(solution)/shard_map/while/body/eval_jaxpr/dot_general | solution.py:16
  118.0 1.5 exponential_reduce_fusion.7
  119.5 17.3 %all-gather.3 = f32[16,1,128]{2,1,0:T(1,128)S(1)} all-gather(f32[1,1,128]{2,1,0:T(1,128)S(1)} %negate_bitcast_fusion), channel_id=1, replica_groups=mesh['grp'=2,'wide'=16] {'wide'}, dimensions={0}, use_global_device_ids=true | all-gather | bytes 8704 | tf_op jit(solution)/shard_map/all_gather | solution.py:96
  136.9 0.3 subtract_reduce_fusion
  137.2 0.7 exponential_reduce_fusion.3
  137.9 18.8 %all-gather.4 = f32[16,1,384]{2,1,0:T(1,128)S(1)} all-gather(f32[1,1,384]{2,1,0:T(1,128)S(1)} %reshape.38), channel_id=1, replica_groups=mesh['grp'=2,'wide'=16] {'wide'}, dimensions={0}, use_global_device_ids=true | all-gather | bytes 26112 | tf_op jit(solution)/shard_map/all_gather | solution.py:87
  156.7 14.8 %while.21 = (s32[]{:T(128)}, f32[128]{0:T(128)S(1)}, f32[128]{0:T(128)S(1)}, f32[6144]{0:T(1024)S(1)}, f32[]{:T(128)}, /*index=5*/f32[128]{0:T(128)S(1)}, f32[61...) while((s32[]{:T(128)}, f32[128]{0:T(128)S(1)}, ...), condition=%wide.region_15.0_spmd.clone, body=%wide.region_12.0_spmd.clone.sunk | while | flops 35652228 | bytes 2432706 | solution.py:41
  156.8 3.3 %fusion.40 = (f32[128]{0:T(128)S(1)}, f32[128,2048]{0,1:T(8,128)}) fusion(bf16[64,128]{1,0:T(8,128)(2,1)S(1)} %get-tuple-element.729, bf16[64,6144]{1,0:T(8,128)(2,1)} %get-tuple-element.728, s32[]{:T(128)S(6)} %select_n.39, f32[2048]{0:T(1024)S(1)} %dynamic_slice.90, f32[128]{0:T(128)S(1)} %get-tuple-element.726, f32[]{:T(128)} %get-tuple-element.725, ...), kind=kOutput, calls=%fused_computation.48.clone.1 | convolution fusion | flops 35127168 | bytes 1345028 | tf_op jit(solution)/shard_map/while/body/eval_jaxpr/dot_general | solution.py:16
  160.1 1.5 exponential_reduce_fusion.8
  161.7 3.3 %fusion.40 = (f32[128]{0:T(128)S(1)}, f32[128,2048]{0,1:T(8,128)}) fusion(bf16[64,128]{1,0:T(8,128)(2,1)S(1)} %get-tuple-element.729, bf16[64,6144]{1,0:T(8,128)(2,1)} %get-tuple-element.728, s32[]{:T(128)S(6)} %select_n.39, f32[2048]{0:T(1024)S(1)} %dynamic_slice.90, f32[128]{0:T(128)S(1)} %get-tuple-element.726, f32[]{:T(128)} %get-tuple-element.725, ...), kind=kOutput, calls=%fused_computation.48.clone.1 | convolution fusion | flops 35127168 | bytes 1345028 | tf_op jit(solution)/shard_map/while/body/eval_jaxpr/dot_general | solution.py:16
  165.1 1.5 exponential_reduce_fusion.8
  166.7 3.3 %fusion.40 = (f32[128]{0:T(128)S(1)}, f32[128,2048]{0,1:T(8,128)}) fusion(bf16[64,128]{1,0:T(8,128)(2,1)S(1)} %get-tuple-element.729, bf16[64,6144]{1,0:T(8,128)(2,1)} %get-tuple-element.728, s32[]{:T(128)S(6)} %select_n.39, f32[2048]{0:T(1024)S(1)} %dynamic_slice.90, f32[128]{0:T(128)S(1)} %get-tuple-element.726, f32[]{:T(128)} %get-tuple-element.725, ...), kind=kOutput, calls=%fused_computation.48.clone.1 | convolution fusion | flops 35127168 | bytes 1345028 | tf_op jit(solution)/shard_map/while/body/eval_jaxpr/dot_general | solution.py:16
  170.0 1.5 exponential_reduce_fusion.8
  171.6 0.0 copy-start.4
  171.6 17.3 %all-gather.5 = f32[16,1,128]{2,1,0:T(1,128)S(1)} all-gather(f32[1,1,128]{2,1,0:T(1,128)S(1)} %bitcast.47), channel_id=1, replica_groups=mesh['grp'=2,'wide'=16] {'wide'}, dimensions={0}, use_global_device_ids=true | all-gather | bytes 8704 | tf_op jit(solution)/shard_map/all_gather | solution.py:96
  189.0 0.3 subtract_reduce_fusion.2
  189.3 0.7 exponential_reduce_fusion.2
  189.9 0.0 copy-done.4
  189.9 1.4 fusion.19
  (48 shorter events, 0.5 us)
Async XLA Ops:
  43.7 21.3 %copy-start.3 = (bf16[384]{0:T(512)(128)(2,1)S(1)}, bf16[384]{0:T(512)(128)(2,1)}, u32[]{:S(2)}) copy-start(bf16[384]{0:T(512)(128)(2,1)} %param.11) | copy-start | bytes 2308
  43.7 38.9 %copy-start.1 = (bf16[64,384]{1,0:T(8,128)(2,1)S(1)}, bf16[64,384]{1,0:T(8,128)(2,1)}, u32[]{:S(2)}) copy-start(bf16[64,384]{1,0:T(8,128)(2,1)} %param.9) | copy-start | bytes 147460
  45.5 59.1 %copy-start.2 = (bf16[64,128]{1,0:T(8,128)(2,1)S(1)}, bf16[64,128]{1,0:T(8,128)(2,1)}, u32[]{:S(2)}) copy-start(bf16[64,128]{1,0:T(8,128)(2,1)} %param.10) | copy-start | bytes 49156
  103.5 0.9 copy-start
  171.6 18.3 %copy-start.4 = (f32[128]{0:T(128)}, f32[128]{0:T(128)S(1)}, u32[]{:S(2)}) copy-start(f32[128]{0:T(128)S(1)} %add_negate_fusion.2) | copy-start | bytes 1540
where the time goes:
time: 192 us; the launch traced here: 191 us
  blocking collectives  152 us (79%)
  matrix products  23.2 us (12%)
  other arithmetic  13.1 us (7%)
    all_gather x2, blocking collectives, on_device(): all_source_pot = lax.all_gather(source_pot, 'wide', axis=0, tiled=True)  37.7 us
    all_gather x2, blocking collectives, on_device(): target_pot = lax.all_gather(own_pot, 'wide', axis=0, tiled=True)  34.7 us
    all_gather x1, blocking collectives, on_device(): lax.all_gather(target_logw, 'wide', axis=0, tiled=True)  23.1 us
    dot_general x7, matrix products, tile_scores(): lax.dot_general(left, right, (((0,), (0,)), ((), ())), preferred_element_...  21.9 us
    all_gather x1, blocking collectives, on_device(): lax.all_gather(source_points, 'wide', axis=1, tiled=True)  20.9 us
    all_gather x1, blocking collectives, on_device(): lax.all_gather(target_points, 'wide', axis=1, tiled=True)  18.4 us
    all_gather x1, blocking collectives, on_device(): lax.all_gather(source_logw, 'wide', axis=0, tiled=True)  17.5 us
    reduce_sum x9, other arithmetic, online_advance(): jnp.sum(jnp.exp(scores - updated[:, None]), axis=1)  11.1 us

commit v1 on v0

v1 whole, which is shorter than its diff:
```python
import jax
import jax.numpy as jnp
from jax import lax
from jax.sharding import PartitionSpec as P

ITERS = 2
AXIS = "wide"


def sq_norms(points):
    return jnp.sum(jnp.square(points.astype(jnp.float32)), axis=0)


def digit_groups(count, widest):
    bits = count.bit_length() - 1
    groups, low = [], 0
    while low < bits:
        width = min(widest, bits - low)
        groups.append((low, width))
        low += width
    return groups


def lse_across(partial, count, widest):
    for low, width in digit_groups(count, widest):
        held = [partial]
        for digit in range(1, 1 << width):
            pairs = [(source, source ^ (digit << low)) for source in range(count)]
            held.append(lax.ppermute(partial, AXIS, pairs))
        stacked = jnp.stack(held)
        peak = jnp.max(stacked, axis=0)
        partial = peak + jnp.log(jnp.sum(jnp.exp(stacked - peak[None]), axis=0))
    return partial


def gather_targets(points, logw, count):
    feat, own = points.shape
    pad = -(feat + 1) % 16
    packed = jnp.concatenate(
        [points, logw[None, :], jnp.zeros((pad, own), points.dtype)], axis=0
    )
    spread = jnp.broadcast_to(packed[None], (count,) + packed.shape)
    every = lax.all_to_all(spread, AXIS, 0, 0, tiled=True)
    joined = every.transpose(1, 0, 2).reshape(packed.shape[0], count * own)
    return joined[:feat], joined[feat]


def on_device(source_points, target_points, source_logw, target_logw, inverse_eps, count):
    inverse = inverse_eps[0]
    own = target_points.shape[1]
    targets, logb = gather_targets(target_points, target_logw, count)
    weight_a = source_logw.astype(jnp.float32)
    weight_b = logb.astype(jnp.float32)
    cross = lax.dot_general(
        source_points, targets, (((0,), (0,)), ((), ())), preferred_element_type=jnp.float32
    )
    cost = inverse * (
        sq_norms(source_points)[:, None] + sq_norms(targets)[None, :] - 2.0 * cross
    )

    def row_lse(term):
        scores = term[None, :] - cost
        peak = jnp.max(scores, axis=1)
        return scores, peak + jnp.log(jnp.sum(jnp.exp(scores - peak[:, None]), axis=1))

    target_pot = jnp.zeros((targets.shape[1],), jnp.float32)
    for iteration in range(ITERS):
        source_pot = -row_lse(target_pot + weight_b)[1]
        scores = (source_pot + weight_a)[:, None] - cost
        peak = jnp.max(scores, axis=0)
        partial = peak + jnp.log(jnp.sum(jnp.exp(scores - peak[None, :]), axis=0))
        target_pot = -lse_across(partial, count, 4 if iteration == 0 else 1)
    scores, final_lse = row_lse(target_pot + weight_b)
    plan = jnp.exp(scores - final_lse[:, None]).astype(jnp.bfloat16)
    mapped = lax.dot_general(
        targets, plan, (((1,), (1,)), ((), ())), preferred_element_type=jnp.float32
    )
    own_pot = lax.dynamic_slice_in_dim(target_pot, lax.axis_index(AXIS) * own, own)
    return (mapped, own_pot)


def solution(mesh):
    count = mesh.shape[AXIS]
    placed = (
        P(None, ("grp", "wide")),
        P(None, ("grp", "wide")),
        P(("grp", "wide")),
        P(("grp", "wide")),
        P(),
    )

    def body(*blocks):
        return on_device(*blocks, count)

    return jax.shard_map(
        body,
        mesh=mesh,
        in_specs=placed,
        out_specs=(P(None, ("grp", "wide")), P(("grp", "wide"))),
        check_vma=False,
    )
```

time: 192 us -> 71.7 us (0.37)
  blocking collectives: 152 us -> 0 us
  starting transfers between devices: 0 us -> 30 us
  waiting for transfers between devices: 0 us -> 22.9 us
  matrix products: 23.2 us -> 3.12 us
  other arithmetic: 13.1 us -> 8.81 us
  local copies, waits for them, and re-layouts: 1.09 us -> 4.91 us
    all_gather x8 -> x0, blocking collectives: 152 us -> none  [the longest x2 37.7 us: on_device(): all_source_pot = lax.all_gather(source_pot, 'wide', axis=0, tiled=True)]
    ppermute x0 -> x19, starting transfers between devices: none -> 22.6 us  [lse_across(): held.append(lax.ppermute(partial, AXIS, pairs))]
    dot_general x8 -> x2, matrix products: 23.2 us -> 3.12 us  [the longest x1 1.75 us: on_device(): lax.dot_general(source_points, targets, (((0,), (0,)), ((), ())), preferr...]
    ppermute x0 -> x19, waiting for transfers between devices: none -> 13.3 us  [lse_across(): held.append(lax.ppermute(partial, AXIS, pairs))]
    all_to_all x0 -> x1, waiting for transfers between devices: none -> 9.62 us  [gather_targets(): every = lax.all_to_all(spread, AXIS, 0, 0, tiled=True)]
    all_to_all x0 -> x1, starting transfers between devices: none -> 7.36 us  [gather_targets(): every = lax.all_to_all(spread, AXIS, 0, 0, tiled=True)]
    reduce_sum x9 -> x10, other arithmetic: 11.1 us -> 4.79 us  [the longest x2 1.88 us: on_device(): partial = peak + jnp.log(jnp.sum(jnp.exp(scores - peak[None, :]), axis=0))]
    another operation x0 -> x1, local copies, waits for them, and re-layouts: none -> 2.89 us  [lse_across(): stacked = jnp.stack(held)]
  transfers between devices with their start and end apart: 0 -> 20, of which waited for: 0 -> 8; matrix products, arithmetic and copies ran while one was open for 0% -> 1% of each run, Pallas kernels for 0% -> 0%
where the time goes in v1:
time: 71.7 us; the launch traced here: 71.2 us
  starting transfers between devices  30 us (42%)
  waiting for transfers between devices  22.9 us (32%)
  other arithmetic  8.81 us (12%)
  local copies, waits for them, and re-layouts  4.91 us (7%)
  matrix products  3.12 us (4%)
  between operations  1.5 us (2%)
    ppermute x19, starting transfers between devices, lse_across(): held.append(lax.ppermute(partial, AXIS, pairs))  22.6 us
    ppermute x19, waiting for transfers between devices, lse_across(): held.append(lax.ppermute(partial, AXIS, pairs))  13.3 us
    all_to_all x1, waiting for transfers between devices, gather_targets(): every = lax.all_to_all(spread, AXIS, 0, 0, tiled=True)  9.62 us
    all_to_all x1, starting transfers between devices, gather_targets(): every = lax.all_to_all(spread, AXIS, 0, 0, tiled=True)  7.36 us
    another operation x1, local copies, waits for them, and re-layouts, lse_across(): stacked = jnp.stack(held)  2.89 us
    reduce_sum x2, other arithmetic, on_device(): partial = peak + jnp.log(jnp.sum(jnp.exp(scores - peak[None, :]), axis=0))  1.88 us
    reduce_sum x3, other arithmetic, row_lse(): jnp.sum(jnp.exp(scores - peak[:, None]), axis=1)  1.79 us
    dot_general x1, matrix products, on_device(): lax.dot_general(source_points, targets, (((0,), (0,)), ((), ())), preferr...  1.75 us
  transfers between devices with their start and end apart: 20, of which 8 were waited for; matrix products, arithmetic and copies ran while one was open for 1% of the time, Pallas kernels for 0%

profile of v1, /device:TPU:0, one launch (start us, length us, event | category | flops | bytes accessed | tf_op | source)
XLA Modules:
  0.0 71.2 jit_solution(16046307773233356883)
XLA Ops:
  0.6 0.1 pad.10.clone
  0.7 0.8 %maximum_maximum_fusion = bf16[80,128]{1,0:T(8,128)(2,1)S(1)} fusion(bf16[1,128]{1,0:T(2,128)(2,1)} %bitcast.81, bf16[64,128]{1,0:T(8,128)(2,1)} %param.6, bf16[80]{0:T(256)(128)(2,1)S(1)} %pad.10.clone), kind=kLoop, calls=%fused_computation.22 | loop fusion | flops 61440 | bytes 37280 | tf_op jit(solution)/shard_map/concatenate | solution.py:39
  1.5 0.8 %broadcast_in_dim.8 = bf16[16,80,128]{2,1,0:T(8,128)(2,1)} broadcast(bf16[80,128]{1,0:T(8,128)(2,1)S(1)} %maximum_maximum_fusion), dimensions={1,2} | broadcast | bytes 348160 | tf_op jit(solution)/shard_map/broadcast_in_dim | solution.py:42
  2.3 7.4 %all-to-all-start = ((bf16[16,80,128]{2,1,0:T(8,128)(2,1)}), bf16[16,80,128]{2,1,0:T(8,128)(2,1)S(1)}, u32[]{:S(2)}, u32[]{:S(2)}) async-start(bf16[16,80,128]{2,1,0:T(8,128)(2,1)} %broadcast_in_dim.8), calls=%async_computation | async-start | bytes 655360 | tf_op jit(solution)/shard_map/all_to_all | solution.py:43
  10.3 0.8 %multiply_reduce_fusion.1 = f32[384]{0:T(512)S(1)} fusion(bf16[64,384]{1,0:T(8,128)(2,1)} %param.5), kind=kLoop, calls=%fused_computation.21 | loop fusion | flops 73344 | bytes 50688 | tf_op jit(solution)/shard_map/reduce_sum | solution.py:11
  11.1 9.6 %all-to-all-done = bf16[16,80,128]{2,1,0:T(8,128)(2,1)S(1)} async-done(((bf16[16,80,128]{2,1,0:T(8,128)(2,1)}), bf16[16,80,128]{2,1,0:T(8,128)(2,1)S(1)}, u32[]{:S(2)}, u32[]{:S(2)}) %all-to-all-start) | async-done | bytes 327712 | tf_op jit(solution)/shard_map/all_to_all | solution.py:43
  20.8 0.1 multiply_reduce_fusion
  20.8 0.0 copy-start.7
  20.8 1.8 %subtract_reduce_fusion.3 = (f32[384]{0:T(512)S(1)}, f32[384,2048]{0,1:T(8,128)S(1)}) fusion(f32[2048]{0:T(1024)S(1)} %bitcast.52, bf16[64,384]{1,0:T(8,128)(2,1)} %param.5, f32[2048]{0:T(1024)S(1)} %bitcast.80, f32[384]{0:T(512)S(1)} %multiply_reduce_fusion.1, f32[]{:T(128)} %bitcast.47, bf16[80,16,128]{2,0,1:T(8,128)(2,1)S(1)} %bitcast.50), kind=kOutput, calls=%fused_computation.11 | convolution fusion | flops 105381504 | bytes 3476996 | tf_op jit(solution)/shard_map/dot_general | solution.py:54
  22.6 0.6 exponential_reduce_fusion.4
  23.2 0.3 subtract_reduce_fusion.2
  23.6 0.9 %exponential_reduce_fusion.3 = f32[2048]{0:T(1024)S(1)} fusion(f32[384,2048]{0,1:T(8,128)S(1)} %get-tuple-element.5, f32[2048]{0:T(1024)S(1)} %subtract_reduce_fusion.2, f32[384]{0:T(512)S(1)} %convert_add_fusion.1), kind=kLoop, calls=%fused_computation.6 | loop fusion | flops 2357248 | bytes 3163648 | tf_op jit(solution)/shard_map/reduce_sum | solution.py:71
  24.5 0.3 collective-permute-start.3
  24.9 1.2 %collective-permute-start.4 = (f32[2048]{0:T(1024)S(1)}, f32[2048]{0:T(1024)S(1)}, u32[]{:S(2)}, u32[]{:S(2)}) collective-permute-start(f32[2048]{0:T(1024)S(1)} %log_add_fusion.4), channel_id=1, source_target_pairs={{0,5},{1,4},{2,7},{3,6},{4,1},{5,0},{6,3},{7,2},{8,13},{9,12},{10,... | collective-permute-start | bytes 24584 | tf_op jit(solution)/shard_map/ppermute | solution.py:29
  26.1 1.1 %collective-permute-start.5 = (f32[2048]{0:T(1024)S(1)}, f32[2048]{0:T(1024)S(1)}, u32[]{:S(2)}, u32[]{:S(2)}) collective-permute-start(f32[2048]{0:T(1024)S(1)} %log_add_fusion.4), channel_id=1, source_target_pairs={{0,6},{1,7},{2,4},{3,5},{4,2},{5,3},{6,0},{7,1},{8,14},{9,15},{10,... | collective-permute-start | bytes 24584 | tf_op jit(solution)/shard_map/ppermute | solution.py:29
  27.2 1.8 %collective-permute-start.6 = (f32[2048]{0:T(1024)S(1)}, f32[2048]{0:T(1024)S(1)}, u32[]{:S(2)}, u32[]{:S(2)}) collective-permute-start(f32[2048]{0:T(1024)S(1)} %log_add_fusion.4), channel_id=1, source_target_pairs={{0,7},{1,6},{2,5},{3,4},{4,3},{5,2},{6,1},{7,0},{8,15},{9,14},{10,... | collective-permute-start | bytes 24584 | tf_op jit(solution)/shard_map/ppermute | solution.py:29
  29.0 1.4 %collective-permute-start.7 = (f32[2048]{0:T(1024)S(1)}, f32[2048]{0:T(1024)S(1)}, u32[]{:S(2)}, u32[]{:S(2)}) collective-permute-start(f32[2048]{0:T(1024)S(1)} %log_add_fusion.4), channel_id=1, source_target_pairs={{0,8},{1,9},{2,10},{3,11},{4,12},{5,13},{6,14},{7,15},{8,0},{9,1},... | collective-permute-start | bytes 24584 | tf_op jit(solution)/shard_map/ppermute | solution.py:29
  30.4 0.0 collective-permute-done.3
  30.4 0.9 %collective-permute-start.8 = (f32[2048]{0:T(1024)S(1)}, f32[2048]{0:T(1024)S(1)}, u32[]{:S(2)}, u32[]{:S(2)}) collective-permute-start(f32[2048]{0:T(1024)S(1)} %log_add_fusion.4), channel_id=1, source_target_pairs={{0,9},{1,8},{2,11},{3,10},{4,13},{5,12},{6,15},{7,14},{8,1},{9,0},... | collective-permute-start | bytes 24584 | tf_op jit(solution)/shard_map/ppermute | solution.py:29
  31.3 0.0 collective-permute-done.4
  31.4 1.0 %collective-permute-start.9 = (f32[2048]{0:T(1024)S(1)}, f32[2048]{0:T(1024)S(1)}, u32[]{:S(2)}, u32[]{:S(2)}) collective-permute-start(f32[2048]{0:T(1024)S(1)} %log_add_fusion.4), channel_id=1, source_target_pairs={{0,10},{1,11},{2,8},{3,9},{4,14},{5,15},{6,12},{7,13},{8,2},{9,3},... | collective-permute-start | bytes 24584 | tf_op jit(solution)/shard_map/ppermute | solution.py:29
  32.3 0.0 collective-permute-done.5
  32.3 2.9 %collective-permute-start.10 = (f32[2048]{0:T(1024)S(1)}, f32[2048]{0:T(1024)S(1)}, u32[]{:S(2)}, u32[]{:S(2)}) collective-permute-start(f32[2048]{0:T(1024)S(1)} %log_add_fusion.4), channel_id=1, source_target_pairs={{0,11},{1,10},{2,9},{3,8},{4,15},{5,14},{6,13},{7,12},{8,3},{9,2},... | collective-permute-start | bytes 24584 | tf_op jit(solution)/shard_map/ppermute | solution.py:29
  35.2 0.0 collective-permute-done.6
  35.2 1.1 %collective-permute-start.11 = (f32[2048]{0:T(1024)S(1)}, f32[2048]{0:T(1024)S(1)}, u32[]{:S(2)}, u32[]{:S(2)}) collective-permute-start(f32[2048]{0:T(1024)S(1)} %log_add_fusion.4), channel_id=1, source_target_pairs={{0,12},{1,13},{2,14},{3,15},{4,8},{5,9},{6,10},{7,11},{8,4},{9,5},... | collective-permute-start | bytes 24584 | tf_op jit(solution)/shard_map/ppermute | solution.py:29
  36.3 0.0 collective-permute-done.7
  36.3 2.1 %collective-permute-start.12 = (f32[2048]{0:T(1024)S(1)}, f32[2048]{0:T(1024)S(1)}, u32[]{:S(2)}, u32[]{:S(2)}) collective-permute-start(f32[2048]{0:T(1024)S(1)} %log_add_fusion.4), channel_id=1, source_target_pairs={{0,13},{1,12},{2,15},{3,14},{4,9},{5,8},{6,11},{7,10},{8,5},{9,4},... | collective-permute-start | bytes 24584 | tf_op jit(solution)/shard_map/ppermute | solution.py:29
  38.5 0.0 collective-permute-done.8
  38.5 2.0 %collective-permute-start.13 = (f32[2048]{0:T(1024)S(1)}, f32[2048]{0:T(1024)S(1)}, u32[]{:S(2)}, u32[]{:S(2)}) collective-permute-start(f32[2048]{0:T(1024)S(1)} %log_add_fusion.4), channel_id=1, source_target_pairs={{0,14},{1,15},{2,12},{3,13},{4,10},{5,11},{6,8},{7,9},{8,6},{9,7},... | collective-permute-start | bytes 24584 | tf_op jit(solution)/shard_map/ppermute | solution.py:29
  40.5 0.0 collective-permute-done.9
  40.5 2.8 %collective-permute-start.14 = (f32[2048]{0:T(1024)S(1)}, f32[2048]{0:T(1024)S(1)}, u32[]{:S(2)}, u32[]{:S(2)}) collective-permute-start(f32[2048]{0:T(1024)S(1)} %log_add_fusion.4), channel_id=1, source_target_pairs={{0,15},{1,14},{2,13},{3,12},{4,11},{5,10},{6,9},{7,8},{8,7},{9,6},... | collective-permute-start | bytes 24584 | tf_op jit(solution)/shard_map/ppermute | solution.py:29
  43.2 0.0 collective-permute-done.10
  43.2 0.1 collective-permute-start
  43.3 0.0 collective-permute-done.11
  43.3 0.7 collective-permute-start.1
  44.0 0.0 collective-permute-done.12
  44.0 1.1 %collective-permute-start.2 = (f32[2048]{0:T(1024)S(1)}, f32[2048]{0:T(1024)S(1)}, u32[]{:S(2)}, u32[]{:S(2)}) collective-permute-start(f32[2048]{0:T(1024)S(1)} %log_add_fusion.4), channel_id=1, source_target_pairs={{0,3},{1,2},{2,1},{3,0},{4,7},{5,6},{6,5},{7,4},{8,11},{9,10},{10,... | collective-permute-start | bytes 24584 | tf_op jit(solution)/shard_map/ppermute | solution.py:29
  45.1 0.0 collective-permute-done.13
  45.1 1.1 %collective-permute-done.14 = f32[2048]{0:T(1024)S(1)} collective-permute-done((f32[2048]{0:T(1024)S(1)}, f32[2048]{0:T(1024)S(1)}, u32[]{:S(2)}, u32[]{:S(2)}) %collective-permute-start.14) | collective-permute-done | bytes 8224 | tf_op jit(solution)/shard_map/ppermute | solution.py:29
  46.3 0.0 collective-permute-done
  46.3 0.7 collective-permute-done.1
  47.0 0.2 collective-permute-done.2
  47.2 0.4 copy-done.5
  47.6 0.2 copy-done.6
  47.7 2.9 %stack.94 = f32[16,2048]{1,0:T(8,128)} concatenate(f32[1,2048]{1,0:T(1,128)S(1)} %bitcast.56, f32[1,2048]{1,0:T(1,128)} %bitcast.73, f32[1,2048]{1,0:T(1,128)} %bitcast.74, f32[1,2048]{1,0:T(1,128)} %bitcast.75, f32[1,2048]{1,0:T(1,128)S(1)} %bitcast.61, f32[1,2048]{1,0:T(1,128)S(1)} %bitcast.62, f32[1,2048]{1,0:T(1,128)S(1)} %bitcast.63, f32[1,2048]{1,0:T(1,128)S(1)} %bitcast.64, ...), dimensions={0} | concatenate | bytes 262144 | tf_op jit(solution)/shard_map/stack | solution.py:30
  50.6 0.8 %maximum_maximum_fusion.1 = f32[2048]{0:T(1024)S(1)} fusion(f32[2048]{0:T(1024)} %copy-done.3, f32[2048]{0:T(1024)} %copy-done.2, f32[2048]{0:T(1024)} %copy-done.1, f32[2048]{0:T(1024)} %copy-done, f32[2048]{0:T(1024)S(1)} %collective-permute-done.10, f32[2048]{0:T(1024)S(1)} %collective-permute-done.9, f32[2048]{0:T(1024)S(1)} %collective-permute-done.8, ...), kind=kLoop, calls=%fused_computation.42 | loop fusion | flops 30720 | bytes 139264 | tf_op jit(solution)/shard_map/reduce_max | solution.py:31
  51.4 0.9 %exponential_reduce_fusion.5 = f32[2048]{0:T(1024)S(1)} fusion(f32[16,2048]{1,0:T(8,128)} %stack.94, f32[2048]{0:T(1024)S(1)} %maximum_maximum_fusion.1), kind=kLoop, calls=%fused_computation.20 | loop fusion | flops 63488 | bytes 147456 | tf_op jit(solution)/shard_map/reduce_sum | solution.py:32
  52.4 0.0 copy-start.8
  52.4 0.4 subtract_reduce_fusion.1
  52.8 0.6 exponential_reduce_fusion.2
  53.4 0.3 subtract_reduce_fusion
  53.8 0.9 %exponential_reduce_fusion.1 = f32[2048]{0:T(1024)S(1)} fusion(f32[384,2048]{0,1:T(8,128)S(1)} %get-tuple-element.5, f32[2048]{0:T(1024)S(1)} %subtract_reduce_fusion, f32[384]{0:T(512)S(1)} %convert_add_fusion), kind=kLoop, calls=%fused_computation.4 | loop fusion | flops 2357248 | bytes 3163648 | tf_op jit(solution)/shard_map/reduce_sum | solution.py:71
  54.7 0.2 collective-permute-start.15
  54.9 1.1 %collective-permute-done.15 = f32[2048]{0:T(1024)S(1)} collective-permute-done((f32[2048]{0:T(1024)S(1)}, f32[2048]{0:T(1024)S(1)}, u32[]{:S(2)}, u32[]{:S(2)}) %collective-permute-start.15) | collective-permute-done | bytes 8224 | tf_op jit(solution)/shard_map/ppermute | solution.py:29
  56.0 1.3 %collective-permute-start.16 = (f32[2048]{0:T(1024)S(1)}, f32[2048]{0:T(1024)S(1)}, u32[]{:S(2)}, u32[]{:S(2)}) collective-permute-start(f32[2048]{0:T(1024)S(1)} %log_add_fusion.2), channel_id=1, source_target_pairs={{0,2},{1,3},{2,0},{3,1},{4,6},{5,7},{6,4},{7,5},{8,10},{9,11},{10,... | collective-permute-start | bytes 24584 | tf_op jit(solution)/shard_map/ppermute | solution.py:29
  57.4 2.4 %collective-permute-done.16 = f32[2048]{0:T(1024)S(1)} collective-permute-done((f32[2048]{0:T(1024)S(1)}, f32[2048]{0:T(1024)S(1)}, u32[]{:S(2)}, u32[]{:S(2)}) %collective-permute-start.16) | collective-permute-done | bytes 8224 | tf_op jit(solution)/shard_map/ppermute | solution.py:29
  59.8 0.1 collective-permute-start.17
  59.9 3.6 %collective-permute-done.17 = f32[2048]{0:T(1024)S(1)} collective-permute-done((f32[2048]{0:T(1024)S(1)}, f32[2048]{0:T(1024)S(1)}, u32[]{:S(2)}, u32[]{:S(2)}) %collective-permute-start.17) | collective-permute-done | bytes 8224 | tf_op jit(solution)/shard_map/ppermute | solution.py:29
  63.6 0.4 collective-permute-start.18
  64.0 4.2 %collective-permute-done.18 = f32[2048]{0:T(1024)S(1)} collective-permute-done((f32[2048]{0:T(1024)S(1)}, f32[2048]{0:T(1024)S(1)}, u32[]{:S(2)}, u32[]{:S(2)}) %collective-permute-start.18) | collective-permute-done | bytes 8224 | tf_op jit(solution)/shard_map/ppermute | solution.py:29
  68.3 0.4 subtract_reduce_fusion.4
  68.6 0.6 exponential_reduce_fusion
  69.2 1.4 %fusion.1 = f32[64,384]{1,0:T(8,128)} fusion(f32[384,2048]{0,1:T(8,128)S(1)} %get-tuple-element.5, f32[384]{0:T(512)S(1)} %log_add_fusion.5, f32[2048]{0:T(1024)S(1)} %get-tuple-element.2, bf16[80,16,128]{2,0,1:T(8,128)(2,1)S(1)} %bitcast.51), kind=kOutput, calls=%fused_computation.13 | convolution fusion | flops 103022592 | bytes 3516416 | tf_op jit(solution)/shard_map/dot_general | solution.py:75
  70.6 0.6 dynamic_slice.3
  (34 shorter events, 0.3 us)
Async XLA Ops:
  2.3 18.5 %all-to-all-start = ((bf16[16,80,128]{2,1,0:T(8,128)(2,1)}), bf16[16,80,128]{2,1,0:T(8,128)(2,1)S(1)}, u32[]{:S(2)}, u32[]{:S(2)}) async-start(bf16[16,80,128]{2,1,0:T(8,128)(2,1)} %broadcast_in_dim.8), calls=%async_computation | async-start | bytes 655360 | tf_op jit(solution)/shard_map/all_to_all | solution.py:43
  20.8 2.4 %copy-start.7 = (bf16[384]{0:T(512)(128)(2,1)S(1)}, bf16[384]{0:T(512)(128)(2,1)}, u32[]{:S(2)}) copy-start(bf16[384]{0:T(512)(128)(2,1)} %param.7) | copy-start | bytes 2308
  24.5 5.9 %collective-permute-start.3 = (f32[2048]{0:T(1024)S(1)}, f32[2048]{0:T(1024)S(1)}, u32[]{:S(2)}, u32[]{:S(2)}) collective-permute-start(f32[2048]{0:T(1024)S(1)} %log_add_fusion.4), channel_id=1, source_target_pairs={{0,4},{1,5},{2,6},{3,7},{4,0},{5,1},{6,2},{7,3},{8,12},{9,13},{10,... | collective-permute-start | bytes 24584 | tf_op jit(solution)/shard_map/ppermute | solution.py:29
  24.9 6.5 %collective-permute-start.4 = (f32[2048]{0:T(1024)S(1)}, f32[2048]{0:T(1024)S(1)}, u32[]{:S(2)}, u32[]{:S(2)}) collective-permute-start(f32[2048]{0:T(1024)S(1)} %log_add_fusion.4), channel_id=1, source_target_pairs={{0,5},{1,4},{2,7},{3,6},{4,1},{5,0},{6,3},{7,2},{8,13},{9,12},{10,... | collective-permute-start | bytes 24584 | tf_op jit(solution)/shard_map/ppermute | solution.py:29
  26.1 6.3 %collective-permute-start.5 = (f32[2048]{0:T(1024)S(1)}, f32[2048]{0:T(1024)S(1)}, u32[]{:S(2)}, u32[]{:S(2)}) collective-permute-start(f32[2048]{0:T(1024)S(1)} %log_add_fusion.4), channel_id=1, source_target_pairs={{0,6},{1,7},{2,4},{3,5},{4,2},{5,3},{6,0},{7,1},{8,14},{9,15},{10,... | collective-permute-start | bytes 24584 | tf_op jit(solution)/shard_map/ppermute | solution.py:29
  27.2 8.1 %collective-permute-start.6 = (f32[2048]{0:T(1024)S(1)}, f32[2048]{0:T(1024)S(1)}, u32[]{:S(2)}, u32[]{:S(2)}) collective-permute-start(f32[2048]{0:T(1024)S(1)} %log_add_fusion.4), channel_id=1, source_target_pairs={{0,7},{1,6},{2,5},{3,4},{4,3},{5,2},{6,1},{7,0},{8,15},{9,14},{10,... | collective-permute-start | bytes 24584 | tf_op jit(solution)/shard_map/ppermute | solution.py:29
  29.0 7.3 %collective-permute-start.7 = (f32[2048]{0:T(1024)S(1)}, f32[2048]{0:T(1024)S(1)}, u32[]{:S(2)}, u32[]{:S(2)}) collective-permute-start(f32[2048]{0:T(1024)S(1)} %log_add_fusion.4), channel_id=1, source_target_pairs={{0,8},{1,9},{2,10},{3,11},{4,12},{5,13},{6,14},{7,15},{8,0},{9,1},... | collective-permute-start | bytes 24584 | tf_op jit(solution)/shard_map/ppermute | solution.py:29
  30.4 8.1 %collective-permute-start.8 = (f32[2048]{0:T(1024)S(1)}, f32[2048]{0:T(1024)S(1)}, u32[]{:S(2)}, u32[]{:S(2)}) collective-permute-start(f32[2048]{0:T(1024)S(1)} %log_add_fusion.4), channel_id=1, source_target_pairs={{0,9},{1,8},{2,11},{3,10},{4,13},{5,12},{6,15},{7,14},{8,1},{9,0},... | collective-permute-start | bytes 24584 | tf_op jit(solution)/shard_map/ppermute | solution.py:29
  31.4 9.1 %collective-permute-start.9 = (f32[2048]{0:T(1024)S(1)}, f32[2048]{0:T(1024)S(1)}, u32[]{:S(2)}, u32[]{:S(2)}) collective-permute-start(f32[2048]{0:T(1024)S(1)} %log_add_fusion.4), channel_id=1, source_target_pairs={{0,10},{1,11},{2,8},{3,9},{4,14},{5,15},{6,12},{7,13},{8,2},{9,3},... | collective-permute-start | bytes 24584 | tf_op jit(solution)/shard_map/ppermute | solution.py:29
  32.3 10.9 %collective-permute-start.10 = (f32[2048]{0:T(1024)S(1)}, f32[2048]{0:T(1024)S(1)}, u32[]{:S(2)}, u32[]{:S(2)}) collective-permute-start(f32[2048]{0:T(1024)S(1)} %log_add_fusion.4), channel_id=1, source_target_pairs={{0,11},{1,10},{2,9},{3,8},{4,15},{5,14},{6,13},{7,12},{8,3},{9,2},... | collective-permute-start | bytes 24584 | tf_op jit(solution)/shard_map/ppermute | solution.py:29
  35.2 8.1 %collective-permute-start.11 = (f32[2048]{0:T(1024)S(1)}, f32[2048]{0:T(1024)S(1)}, u32[]{:S(2)}, u32[]{:S(2)}) collective-permute-start(f32[2048]{0:T(1024)S(1)} %log_add_fusion.4), channel_id=1, source_target_pairs={{0,12},{1,13},{2,14},{3,15},{4,8},{5,9},{6,10},{7,11},{8,4},{9,5},... | collective-permute-start | bytes 24584 | tf_op jit(solution)/shard_map/ppermute | solution.py:29
  36.3 7.7 %collective-permute-start.12 = (f32[2048]{0:T(1024)S(1)}, f32[2048]{0:T(1024)S(1)}, u32[]{:S(2)}, u32[]{:S(2)}) collective-permute-start(f32[2048]{0:T(1024)S(1)} %log_add_fusion.4), channel_id=1, source_target_pairs={{0,13},{1,12},{2,15},{3,14},{4,9},{5,8},{6,11},{7,10},{8,5},{9,4},... | collective-permute-start | bytes 24584 | tf_op jit(solution)/shard_map/ppermute | solution.py:29
  38.5 6.7 %collective-permute-start.13 = (f32[2048]{0:T(1024)S(1)}, f32[2048]{0:T(1024)S(1)}, u32[]{:S(2)}, u32[]{:S(2)}) collective-permute-start(f32[2048]{0:T(1024)S(1)} %log_add_fusion.4), channel_id=1, source_target_pairs={{0,14},{1,15},{2,12},{3,13},{4,10},{5,11},{6,8},{7,9},{8,6},{9,7},... | collective-permute-start | bytes 24584 | tf_op jit(solution)/shard_map/ppermute | solution.py:29
  40.5 5.8 %collective-permute-start.14 = (f32[2048]{0:T(1024)S(1)}, f32[2048]{0:T(1024)S(1)}, u32[]{:S(2)}, u32[]{:S(2)}) collective-permute-start(f32[2048]{0:T(1024)S(1)} %log_add_fusion.4), channel_id=1, source_target_pairs={{0,15},{1,14},{2,13},{3,12},{4,11},{5,10},{6,9},{7,8},{8,7},{9,6},... | collective-permute-start | bytes 24584 | tf_op jit(solution)/shard_map/ppermute | solution.py:29
  43.2 3.0 %collective-permute-start = (f32[2048]{0:T(1024)S(1)}, f32[2048]{0:T(1024)S(1)}, u32[]{:S(2)}, u32[]{:S(2)}) collective-permute-start(f32[2048]{0:T(1024)S(1)} %log_add_fusion.4), channel_id=1, source_target_pairs={{0,1},{1,0},{2,3},{3,2},{4,5},{5,4},{6,7},{7,6},{8,9},{9,8},{10,11... | collective-permute-start | bytes 24584 | tf_op jit(solution)/shard_map/ppermute | solution.py:29
  43.3 3.8 %copy-start = (f32[2048]{0:T(1024)}, f32[2048]{0:T(1024)S(1)}, u32[]{:S(2)}) copy-start(f32[2048]{0:T(1024)S(1)} %collective-permute-done.11) | copy-start | bytes 24580
  43.3 3.7 %collective-permute-start.1 = (f32[2048]{0:T(1024)S(1)}, f32[2048]{0:T(1024)S(1)}, u32[]{:S(2)}, u32[]{:S(2)}) collective-permute-start(f32[2048]{0:T(1024)S(1)} %log_add_fusion.4), channel_id=1, source_target_pairs={{0,2},{1,3},{2,0},{3,1},{4,6},{5,7},{6,4},{7,5},{8,10},{9,11},{10,... | collective-permute-start | bytes 24584 | tf_op jit(solution)/shard_map/ppermute | solution.py:29
  44.0 3.2 %copy-start.1 = (f32[2048]{0:T(1024)}, f32[2048]{0:T(1024)S(1)}, u32[]{:S(2)}) copy-start(f32[2048]{0:T(1024)S(1)} %collective-permute-done.12) | copy-start | bytes 24580
  44.0 3.1 %collective-permute-start.2 = (f32[2048]{0:T(1024)S(1)}, f32[2048]{0:T(1024)S(1)}, u32[]{:S(2)}, u32[]{:S(2)}) collective-permute-start(f32[2048]{0:T(1024)S(1)} %log_add_fusion.4), channel_id=1, source_target_pairs={{0,3},{1,2},{2,1},{3,0},{4,7},{5,6},{6,5},{7,4},{8,11},{9,10},{10,... | collective-permute-start | bytes 24584 | tf_op jit(solution)/shard_map/ppermute | solution.py:29
  45.1 2.0 %copy-start.2 = (f32[2048]{0:T(1024)}, f32[2048]{0:T(1024)S(1)}, u32[]{:S(2)}) copy-start(f32[2048]{0:T(1024)S(1)} %collective-permute-done.13) | copy-start | bytes 24580
  46.3 0.9 %copy-start.3 = (f32[2048]{0:T(1024)}, f32[2048]{0:T(1024)S(1)}, u32[]{:S(2)}) copy-start(f32[2048]{0:T(1024)S(1)} %collective-permute-done.14) | copy-start | bytes 24580
  46.3 0.9 %copy-start.4 = (f32[2048]{0:T(1024)}, f32[2048]{0:T(1024)S(1)}, u32[]{:S(2)}) copy-start(f32[2048]{0:T(1024)S(1)} %collective-permute-done) | copy-start | bytes 24580
  47.0 0.6 copy-start.5
  47.1 0.6 copy-start.6
  52.4 1.0 %copy-start.8 = (bf16[384]{0:T(512)(128)(2,1)S(1)}, bf16[384]{0:T(512)(128)(2,1)}, u32[]{:S(2)}) copy-start(bf16[384]{0:T(512)(128)(2,1)} %param.7) | copy-start | bytes 2308
  54.7 1.2 %collective-permute-start.15 = (f32[2048]{0:T(1024)S(1)}, f32[2048]{0:T(1024)S(1)}, u32[]{:S(2)}, u32[]{:S(2)}) collective-permute-start(f32[2048]{0:T(1024)S(1)} %log_add_fusion.3), channel_id=1, source_target_pairs={{0,1},{1,0},{2,3},{3,2},{4,5},{5,4},{6,7},{7,6},{8,9},{9,8},{10,11... | collective-permute-start | bytes 24584 | tf_op jit(solution)/shard_map/ppermute | solution.py:29
  56.0 3.7 %collective-permute-start.16 = (f32[2048]{0:T(1024)S(1)}, f32[2048]{0:T(1024)S(1)}, u32[]{:S(2)}, u32[]{:S(2)}) collective-permute-start(f32[2048]{0:T(1024)S(1)} %log_add_fusion.2), channel_id=1, source_target_pairs={{0,2},{1,3},{2,0},{3,1},{4,6},{5,7},{6,4},{7,5},{8,10},{9,11},{10,... | collective-permute-start | bytes 24584 | tf_op jit(solution)/shard_map/ppermute | solution.py:29
  59.8 3.7 %collective-permute-start.17 = (f32[2048]{0:T(1024)S(1)}, f32[2048]{0:T(1024)S(1)}, u32[]{:S(2)}, u32[]{:S(2)}) collective-permute-start(f32[2048]{0:T(1024)S(1)} %log_add_fusion.1), channel_id=1, source_target_pairs={{0,4},{1,5},{2,6},{3,7},{4,0},{5,1},{6,2},{7,3},{8,12},{9,13},{10,... | collective-permute-start | bytes 24584 | tf_op jit(solution)/shard_map/ppermute | solution.py:29
  63.6 4.6 %collective-permute-start.18 = (f32[2048]{0:T(1024)S(1)}, f32[2048]{0:T(1024)S(1)}, u32[]{:S(2)}, u32[]{:S(2)}) collective-permute-start(f32[2048]{0:T(1024)S(1)} %log_add_fusion), channel_id=1, source_target_pairs={{0,8},{1,9},{2,10},{3,11},{4,12},{5,13},{6,14},{7,15},{8,0},{9,1},... | collective-permute-start | bytes 24584 | tf_op jit(solution)/shard_map/ppermute | solution.py:29

commit v2 on v1

--- a/solution.py
+++ b/solution.py
@@ -11,26 +11,35 @@
     return jnp.sum(jnp.square(points.astype(jnp.float32)), axis=0)
 
 
-def digit_groups(count, widest):
+def digit_stages(count):
     bits = count.bit_length() - 1
-    groups, low = [], 0
+    stages, low = [], 0
     while low < bits:
-        width = min(widest, bits - low)
-        groups.append((low, width))
+        width = min(1 if low < 2 else 2, bits - low)
+        stages.append((low, width))
         low += width
-    return groups
+    return stages
 
 
-def lse_across(partial, count, widest):
-    for low, width in digit_groups(count, widest):
-        held = [partial]
-        for digit in range(1, 1 << width):
-            pairs = [(source, source ^ (digit << low)) for source in range(count)]
-            held.append(lax.ppermute(partial, AXIS, pairs))
-        stacked = jnp.stack(held)
+def line_groups(count, low, width):
+    span, mask = 1 << width, ((1 << width) - 1) << low
+    bases = [index for index in range(count) if index & mask == 0]
+    return [[base | (digit << low) for digit in range(span)] for base in bases]
+
+
+def lse_staged(partial, count):
+    for low, width in reversed(digit_stages(count)):
+        stacked = lax.all_gather(
+            partial, AXIS, axis_index_groups=line_groups(count, low, width)
+        )
         peak = jnp.max(stacked, axis=0)
         partial = peak + jnp.log(jnp.sum(jnp.exp(stacked - peak[None]), axis=0))
     return partial
+
+
+def lse_reduced(peak, total):
+    highest = lax.pmax(peak, AXIS)
+    return highest + jnp.log(lax.psum(total * jnp.exp(peak - highest), AXIS))
 
 
 def gather_targets(points, logw, count):
@@ -39,8 +48,11 @@
     packed = jnp.concatenate(
         [points, logw[None, :], jnp.zeros((pad, own), points.dtype)], axis=0
     )
-    spread = jnp.broadcast_to(packed[None], (count,) + packed.shape)
-    every = lax.all_to_all(spread, AXIS, 0, 0, tiled=True)
+    every = packed[None]
+    for low, width in digit_stages(count):
+        every = lax.all_gather(
+            every, AXIS, axis_index_groups=line_groups(count, low, width), tiled=True
+        )
     joined = every.transpose(1, 0, 2).reshape(packed.shape[0], count * own)
     return joined[:feat], joined[feat]
 
@@ -68,8 +80,11 @@
         source_pot = -row_lse(target_pot + weight_b)[1]
         scores = (source_pot + weight_a)[:, None] - cost
         peak = jnp.max(scores, axis=0)
-        partial = peak + jnp.log(jnp.sum(jnp.exp(scores - peak[None, :]), axis=0))
-        target_pot = -lse_across(partial, count, 4 if iteration == 0 else 1)
+        total = jnp.sum(jnp.exp(scores - peak[None, :]), axis=0)
+        if iteration == 0:
+            target_pot = -lse_staged(peak + jnp.log(total), count)
+        else:
+            target_pot = -lse_reduced(peak, total)
     scores, final_lse = row_lse(target_pot + weight_b)
     plan = jnp.exp(scores - final_lse[:, None]).astype(jnp.bfloat16)
     mapped = lax.dot_general(

time: 71.7 us -> 119 us (1.66)
  blocking collectives: 0 us -> 106 us
  starting transfers between devices: 30 us -> 0 us
  waiting for transfers between devices: 22.9 us -> 0 us
  local copies, waits for them, and re-layouts: 4.91 us -> 0.72 us
  other arithmetic: 8.81 us -> 7.05 us
    all_gather x0 -> x6, blocking collectives: none -> 41.6 us  [the longest x3 22.3 us: gather_targets(): lax.all_gather(every, AXIS, axis_index_groups=line_groups(count, low, wid...]
    pmax x0 -> x1, blocking collectives: none -> 34.4 us  [lse_reduced(): highest = lax.pmax(peak, AXIS)]
    psum x0 -> x1, blocking collectives: none -> 30 us  [lse_reduced(): return highest + jnp.log(lax.psum(total * jnp.exp(peak - highest), AXIS))]
    ppermute x19 -> x0, starting transfers between devices: 22.6 us -> none  [lse_across(): held.append(lax.ppermute(partial, AXIS, pairs))]
    ppermute x19 -> x0, waiting for transfers between devices: 13.3 us -> none  [lse_across(): held.append(lax.ppermute(partial, AXIS, pairs))]
    all_to_all x1 -> x0, waiting for transfers between devices: 9.62 us -> none  [gather_targets(): every = lax.all_to_all(spread, AXIS, 0, 0, tiled=True)]
    all_to_all x1 -> x0, starting transfers between devices: 7.36 us -> none  [gather_targets(): every = lax.all_to_all(spread, AXIS, 0, 0, tiled=True)]
    another operation x1 -> x0, local copies, waits for them, and re-layouts: 2.89 us -> none  [lse_across(): stacked = jnp.stack(held)]
  transfers between devices with their start and end apart: 20 -> 0, of which waited for: 8 -> 0; matrix products, arithmetic and copies ran while one was open for 1% -> 0% of each run, Pallas kernels for 0% -> 0%
where the time goes in v2:
time: 119 us; the launch traced here: 118 us
  blocking collectives  106 us (89%)
  other arithmetic  7.05 us (6%)
  matrix products  3.11 us (3%)
  between operations  1.47 us (1%)
    pmax x1, blocking collectives, lse_reduced(): highest = lax.pmax(peak, AXIS)  34.4 us
    psum x1, blocking collectives, lse_reduced(): return highest + jnp.log(lax.psum(total * jnp.exp(peak - highest), AXIS))  30 us
    all_gather x3, blocking collectives, gather_targets(): lax.all_gather(every, AXIS, axis_index_groups=line_groups(count, low, wid...  22.3 us
    all_gather x3, blocking collectives, lse_staged(): lax.all_gather(partial, AXIS, axis_index_groups=line_groups(count, low, w...  19.3 us

profile of v2, /device:TPU:0, one launch (start us, length us, event | category | flops | bytes accessed | tf_op | source)
XLA Modules:
  0.0 118.4 jit_solution(10600611384736445255)
XLA Ops:
  1.3 0.1 pad.2.clone
  1.4 0.8 multiply_reduce_fusion.1
  2.2 0.8 maximum_maximum_fusion
  3.0 1.9 %all-gather = bf16[160,128]{1,0:T(8,128)(2,1)S(1)} all-gather(bf16[80,128]{1,0:T(8,128)(2,1)S(1)} %maximum_maximum_fusion), channel_id=2, replica_groups={{0,1},{2,3},{4,5},{6,7},{8,9},{10,11},{12,13},{14,15},{16,17},{18,19},{..., dimensions={0}, use_global_device_ids=true | all-gather | bytes 61440 | tf_op jit(solution)/shard_map/all_gather | solution.py:53
  4.9 5.4 %all_gather.22 = bf16[4,80,128]{2,1,0:T(8,128)(2,1)S(1)} all-gather(bf16[2,80,128]{2,1,0:T(8,128)(2,1)S(1)} %bitcast.29), channel_id=1, replica_groups={{0,2},{1,3},{4,6},{5,7},{8,10},{9,11},{12,14},{13,15},{16,18},{17,19},{..., dimensions={0}, use_global_device_ids=true | all-gather | bytes 122880 | tf_op jit(solution)/shard_map/all_gather | solution.py:53
  10.4 14.9 %all_gather.23 = bf16[16,80,128]{2,1,0:T(8,128)(2,1)S(1)} all-gather(bf16[4,80,128]{2,1,0:T(8,128)(2,1)S(1)} %all_gather.22), channel_id=1, replica_groups={{0,4,8,12},{1,5,9,13},{2,6,10,14},{3,7,11,15},{16,20,24,28},{17,21,25,2..., dimensions={0}, use_global_device_ids=true | all-gather | bytes 409600 | tf_op jit(solution)/shard_map/all_gather | solution.py:53
  25.3 0.1 multiply_reduce_fusion
  25.4 0.0 copy-start
  25.4 1.7 %subtract_reduce_fusion.3 = (f32[384]{0:T(512)S(1)}, f32[384,2048]{0,1:T(8,128)S(1)}) fusion(f32[2048]{0:T(1024)S(1)} %bitcast.30, bf16[64,384]{1,0:T(8,128)(2,1)} %param.5, f32[2048]{0:T(1024)S(1)} %bitcast.34, f32[384]{0:T(512)S(1)} %multiply_reduce_fusion.1, f32[]{:T(128)} %bitcast.24, bf16[80,16,128]{2,0,1:T(8,128)(2,1)S(1)} %bitcast.27), kind=kOutput, calls=%fused_computation.11 | convolution fusion | flops 105381504 | bytes 3476996 | tf_op jit(solution)/shard_map/dot_general | solution.py:66
  27.2 0.6 exponential_reduce_fusion.4
  27.8 0.0 copy-done
  27.8 0.4 subtract_reduce_fusion.2
  28.2 0.9 exponential_reduce_fusion.3
  29.1 13.1 %all-gather.1 = f32[8192]{0:T(1024)S(1)} all-gather(f32[2048]{0:T(1024)S(1)} %log_add_fusion.2), channel_id=3, replica_groups={{0,4,8,12},{1,5,9,13},{2,6,10,14},{3,7,11,15},{16,20,24,28},{17,21,25,2..., dimensions={0}, use_global_device_ids=true | all-gather | bytes 40960 | tf_op jit(solution)/shard_map/all_gather | solution.py:32
  42.4 4.4 %all-gather.2 = f32[4096]{0:T(1024)S(1)} all-gather(f32[2048]{0:T(1024)S(1)} %log_add_fusion.1), channel_id=4, replica_groups={{0,2},{1,3},{4,6},{5,7},{8,10},{9,11},{12,14},{13,15},{16,18},{17,19},{..., dimensions={0}, use_global_device_ids=true | all-gather | bytes 24576 | tf_op jit(solution)/shard_map/all_gather | solution.py:32
  46.8 1.8 %all-gather.3 = f32[4096]{0:T(1024)S(1)} all-gather(f32[2048]{0:T(1024)S(1)} %log_add_fusion), channel_id=5, replica_groups={{0,1},{2,3},{4,5},{6,7},{8,9},{10,11},{12,13},{14,15},{16,17},{18,19},{..., dimensions={0}, use_global_device_ids=true | all-gather | bytes 24576 | tf_op jit(solution)/shard_map/all_gather | solution.py:32
  48.7 0.4 subtract_reduce_fusion.1
  49.1 0.6 exponential_reduce_fusion.2
  49.7 0.4 subtract_reduce_fusion
  50.1 0.9 exponential_reduce_fusion.1
  51.0 34.4 %pmax.7 = f32[2048]{0:T(1024)S(1)} all-reduce(f32[2048]{0:T(1024)S(1)} %subtract_reduce_fusion), channel_id=1, replica_groups=mesh['grp'=2,'wide'=16] {'wide'}, use_global_device_ids=true, to_apply=%region_15.0 | all-reduce | flops 2048 | bytes 16384 | tf_op jit(solution)/shard_map/pmax | solution.py:41
  85.4 30.0 %psum.7 = f32[2048]{0:T(1024)S(1)} all-reduce(f32[2048]{0:T(1024)S(1)} %exponential_multiply_fusion), channel_id=1, replica_groups=mesh['grp'=2,'wide'=16] {'wide'}, use_global_device_ids=true, to_apply=%region_17.0 | all-reduce | flops 2048 | bytes 16384 | tf_op jit(solution)/shard_map/psum | solution.py:42
  115.4 0.6 dynamic_slice.3
  116.0 0.3 subtract_reduce_fusion.4
  116.4 0.6 exponential_reduce_fusion
  117.0 1.4 %fusion.1 = f32[64,384]{1,0:T(8,128)} fusion(f32[384,2048]{0,1:T(8,128)S(1)} %get-tuple-element.5, f32[384]{0:T(512)S(1)} %log_add_fusion.3, f32[2048]{0:T(1024)S(1)} %get-tuple-element.2, bf16[80,16,128]{2,0,1:T(8,128)(2,1)S(1)} %bitcast.28), kind=kOutput, calls=%fused_computation.13 | convolution fusion | flops 103022592 | bytes 3516416 | tf_op jit(solution)/shard_map/dot_general | solution.py:90
  (20 shorter events, 0.3 us)
Async XLA Ops:
  25.4 2.4 %copy-start = (bf16[384]{0:T(512)(128)(2,1)S(1)}, bf16[384]{0:T(512)(128)(2,1)}, u32[]{:S(2)}) copy-start(bf16[384]{0:T(512)(128)(2,1)} %param.7) | copy-start | bytes 2308

commit v3 on v1

--- a/solution.py
+++ b/solution.py
@@ -11,25 +11,40 @@
     return jnp.sum(jnp.square(points.astype(jnp.float32)), axis=0)
 
 
-def digit_groups(count, widest):
-    bits = count.bit_length() - 1
-    groups, low = [], 0
-    while low < bits:
-        width = min(widest, bits - low)
-        groups.append((low, width))
-        low += width
-    return groups
+def same_core(count):
+    return [list(range(core, count, 2)) for core in range(2)]
 
 
-def lse_across(partial, count, widest):
-    for low, width in digit_groups(count, widest):
-        held = [partial]
-        for digit in range(1, 1 << width):
-            pairs = [(source, source ^ (digit << low)) for source in range(count)]
-            held.append(lax.ppermute(partial, AXIS, pairs))
-        stacked = jnp.stack(held)
-        peak = jnp.max(stacked, axis=0)
-        partial = peak + jnp.log(jnp.sum(jnp.exp(stacked - peak[None]), axis=0))
+def swap(value, count, step):
+    return lax.ppermute(value, AXIS, [(source, source ^ step) for source in range(count)])
+
+
+def join_lse(held):
+    stacked = jnp.stack(held) if isinstance(held, list) else held
+    peak = jnp.max(stacked, axis=0)
+    return peak + jnp.log(jnp.sum(jnp.exp(stacked - peak[None]), axis=0))
+
+
+def lse_spread(partial, count):
+    partial = join_lse([partial, swap(partial, count, 1)])
+    chips = count // 2
+    spread = jnp.broadcast_to(partial[None], (chips,) + partial.shape)
+    every = lax.all_to_all(
+        spread, AXIS, 0, 0, axis_index_groups=same_core(count), tiled=True
+    )
+    return join_lse(every)
+
+
+def lse_swapped(partial, count):
+    bits = count.bit_length() - 1
+    for low in range(min(2, bits)):
+        partial = join_lse([partial, swap(partial, count, 1 << low)])
+    low = 2
+    while low < bits:
+        width = min(2, bits - low)
+        digits = range((1 << width) - 1, 0, -1)
+        partial = join_lse([partial] + [swap(partial, count, digit << low) for digit in digits])
+        low += width
     return partial
 
 
@@ -39,9 +54,16 @@
     packed = jnp.concatenate(
         [points, logw[None, :], jnp.zeros((pad, own), points.dtype)], axis=0
     )
-    spread = jnp.broadcast_to(packed[None], (count,) + packed.shape)
-    every = lax.all_to_all(spread, AXIS, 0, 0, tiled=True)
-    joined = every.transpose(1, 0, 2).reshape(packed.shape[0], count * own)
+    chips = count // 2
+    spread = jnp.broadcast_to(packed[None], (chips,) + packed.shape)
+    every = lax.all_to_all(
+        spread, AXIS, 0, 0, axis_index_groups=same_core(count), tiled=True
+    )
+    other = swap(every, count, 1)
+    first = lax.axis_index(AXIS) % 2 == 0
+    pair = jnp.stack([jnp.where(first, every, other), jnp.where(first, other, every)], axis=1)
+    joined = pair.reshape((count,) + packed.shape).transpose(1, 0, 2)
+    joined = joined.reshape(packed.shape[0], count * own)
     return joined[:feat], joined[feat]
 
 
@@ -69,7 +91,8 @@
         scores = (source_pot + weight_a)[:, None] - cost
         peak = jnp.max(scores, axis=0)
         partial = peak + jnp.log(jnp.sum(jnp.exp(scores - peak[None, :]), axis=0))
-        target_pot = -lse_across(partial, count, 4 if iteration == 0 else 1)
+        combine = lse_spread if iteration == 0 else lse_swapped
+        target_pot = -combine(partial, count)
     scores, final_lse = row_lse(target_pot + weight_b)
     plan = jnp.exp(scores - final_lse[:, None]).astype(jnp.bfloat16)
     mapped = lax.dot_general(

time: 71.7 us -> 50.1 us (0.70)
  starting transfers between devices: 30 us -> 5.55 us
  blocking collectives: 0 us -> 24.2 us
  waiting for transfers between devices: 22.9 us -> 7.44 us
  local copies, waits for them, and re-layouts: 4.91 us -> 0.73 us
  other arithmetic: 8.81 us -> 7.26 us
    all_to_all x0 -> x2, blocking collectives: none -> 24.2 us  [the longest x1 14.6 us: gather_targets(): lax.all_to_all(spread, AXIS, 0, 0, axis_index_groups=same_core(count), ti...]
    ppermute x19 -> x7, starting transfers between devices: 22.6 us -> 5.55 us  [swap(): lax.ppermute(value, AXIS, [(source, source ^ step) for source in range(co...]
    all_to_all x1 -> x0, waiting for transfers between devices: 9.62 us -> none  [gather_targets(): every = lax.all_to_all(spread, AXIS, 0, 0, tiled=True)]
    all_to_all x1 -> x0, starting transfers between devices: 7.36 us -> none  [gather_targets(): every = lax.all_to_all(spread, AXIS, 0, 0, tiled=True)]
    ppermute x19 -> x7, waiting for transfers between devices: 13.3 us -> 7.44 us  [swap(): lax.ppermute(value, AXIS, [(source, source ^ step) for source in range(co...]
    another operation x1 -> x0, local copies, waits for them, and re-layouts: 2.89 us -> none  [lse_across(): stacked = jnp.stack(held)]
    reduce_sum x5, other arithmetic: 1.11 us -> 0.23 us  [join_lse(): return peak + jnp.log(jnp.sum(jnp.exp(stacked - peak[None]), axis=0))]
    reduce_max x5, other arithmetic: 0.83 us -> 0.07 us  [join_lse(): peak = jnp.max(stacked, axis=0)]
  transfers between devices with their start and end apart: 20 -> 7, of which waited for: 8 -> 5; matrix products, arithmetic and copies ran while one was open for 1% -> 2% of each run, Pallas kernels for 0% -> 0%
where the time goes in v3:
time: 50.1 us; the launch traced here: 49.7 us
  blocking collectives  24.2 us (48%)
  waiting for transfers between devices  7.44 us (15%)
  other arithmetic  7.26 us (14%)
  starting transfers between devices  5.55 us (11%)
  matrix products  3.11 us (6%)
  between operations  1.51 us (3%)
  local copies, waits for them, and re-layouts  0.73 us (1%)
    all_to_all x1, blocking collectives, gather_targets(): lax.all_to_all(spread, AXIS, 0, 0, axis_index_groups=same_core(count), ti...  14.6 us
    all_to_all x1, blocking collectives, lse_spread(): lax.all_to_all(spread, AXIS, 0, 0, axis_index_groups=same_core(count), ti...  9.54 us
    ppermute x7, waiting for transfers between devices, swap(): lax.ppermute(value, AXIS, [(source, source ^ step) for source in range(co...  7.44 us
    ppermute x7, starting transfers between devices, swap(): lax.ppermute(value, AXIS, [(source, source ^ step) for source in range(co...  5.55 us
    reduce_sum x2, other arithmetic, on_device(): partial = peak + jnp.log(jnp.sum(jnp.exp(scores - peak[None, :]), axis=0))  1.89 us
    reduce_sum x3, other arithmetic, row_lse(): jnp.sum(jnp.exp(scores - peak[:, None]), axis=1)  1.8 us
    dot_general x1, matrix products, on_device(): lax.dot_general(source_points, targets, (((0,), (0,)), ((), ())), preferr...  1.75 us
    dot_general x1, matrix products, on_device(): lax.dot_general(targets, plan, (((1,), (1,)), ((), ())), preferred_elemen...  1.36 us
  transfers between devices with their start and end apart: 7, of which 5 were waited for; matrix products, arithmetic and copies ran while one was open for 2% of the time, Pallas kernels for 0%

profile of v3, /device:TPU:0, one launch (start us, length us, event | category | flops | bytes accessed | tf_op | source)
XLA Modules:
  0.0 49.7 jit_solution(14339384197160219484)
XLA Ops:
  0.6 0.1 pad.14.clone
  0.7 0.8 %maximum_maximum_fusion = bf16[80,128]{1,0:T(8,128)(2,1)S(1)} fusion(bf16[1,128]{1,0:T(2,128)(2,1)} %bitcast.67, bf16[64,128]{1,0:T(8,128)(2,1)} %param.6, bf16[80]{0:T(256)(128)(2,1)S(1)} %pad.14.clone), kind=kLoop, calls=%fused_computation.30 | loop fusion | flops 61440 | bytes 37280 | tf_op jit(solution)/shard_map/concatenate | solution.py:54
  1.6 14.6 %all_to_all.14 = bf16[8,80,128]{2,1,0:T(8,128)(2,1)S(1)} all-to-all(bf16[8,80,128]{2,1,0:T(8,128)(2,1)S(1)} %broadcast_in_dim.10), channel_id=1, replica_groups={{0,2,4,6,8,10,12,14},{1,3,5,7,9,11,13,15},{16,18,20,22,24,26,28,30},{17..., dimensions={0} | all-to-all | bytes 327680 | tf_op jit(solution)/shard_map/all_to_all | solution.py:59
  16.2 0.0 collective-permute-start
  16.8 0.8 %multiply_reduce_fusion.1 = f32[384]{0:T(512)S(1)} fusion(bf16[64,384]{1,0:T(8,128)(2,1)} %param.5), kind=kLoop, calls=%fused_computation.23 | loop fusion | flops 73344 | bytes 50688 | tf_op jit(solution)/shard_map/reduce_sum | solution.py:11
  17.7 0.0 collective-permute-done
  17.7 0.1 multiply_reduce_fusion
  17.8 0.0 copy-start
  17.8 1.7 %subtract_reduce_fusion.3 = (f32[384]{0:T(512)S(1)}, f32[384,2048]{0,1:T(8,128)S(1)}) fusion(f32[2048]{0:T(1024)S(1)} %bitcast.52, bf16[64,384]{1,0:T(8,128)(2,1)} %param.5, f32[2048]{0:T(1024)S(1)} %bitcast.66, f32[384]{0:T(512)S(1)} %multiply_reduce_fusion.1, f32[]{:T(128)} %bitcast.47, bf16[80,16,128]{2,0,1:T(8,128)(2,1)S(1)} %bitcast.50), kind=kOutput, calls=%fused_computation.11 | convolution fusion | flops 105381504 | bytes 3476996 | tf_op jit(solution)/shard_map/dot_general | solution.py:76
  19.6 0.6 %exponential_reduce_fusion.4 = f32[384]{0:T(512)S(1)} fusion(f32[384,2048]{0,1:T(8,128)S(1)} %get-tuple-element.7, f32[384]{0:T(512)S(1)} %get-tuple-element.6, f32[2048]{0:T(1024)S(1)} %bitcast.53), kind=kLoop, calls=%fused_computation.7 | loop fusion | flops 2358912 | bytes 3156992 | tf_op jit(solution)/shard_map/reduce_sum | solution.py:86
  20.2 0.0 copy-done
  20.2 0.4 subtract_reduce_fusion.2
  20.6 0.9 %exponential_reduce_fusion.3 = f32[2048]{0:T(1024)S(1)} fusion(f32[384,2048]{0,1:T(8,128)S(1)} %get-tuple-element.7, f32[2048]{0:T(1024)S(1)} %subtract_reduce_fusion.2, f32[384]{0:T(512)S(1)} %convert_add_fusion.1), kind=kLoop, calls=%fused_computation.6 | loop fusion | flops 2357248 | bytes 3163648 | tf_op jit(solution)/shard_map/reduce_sum | solution.py:93
  21.5 0.6 %collective-permute-start.1 = (f32[2048]{0:T(1024)S(1)}, f32[2048]{0:T(1024)S(1)}, u32[]{:S(2)}, u32[]{:S(2)}) collective-permute-start(f32[2048]{0:T(1024)S(1)} %log_add_fusion.4), channel_id=1, source_target_pairs={{0,1},{1,0},{2,3},{3,2},{4,5},{5,4},{6,7},{7,6},{8,9},{9,8},{10,11... | collective-permute-start | bytes 24584 | tf_op jit(solution)/shard_map/ppermute | solution.py:19
  22.1 0.8 %collective-permute-done.1 = f32[2048]{0:T(1024)S(1)} collective-permute-done((f32[2048]{0:T(1024)S(1)}, f32[2048]{0:T(1024)S(1)}, u32[]{:S(2)}, u32[]{:S(2)}) %collective-permute-start.1) | collective-permute-done | bytes 8224 | tf_op jit(solution)/shard_map/ppermute | solution.py:19
  23.0 9.5 %all_to_all.15 = f32[8,1,2048]{2,1,0:T(1,128)S(1)} all-to-all(f32[8,1,2048]{2,1,0:T(1,128)S(1)} %broadcast_in_dim.11), channel_id=1, replica_groups={{0,2,4,6,8,10,12,14},{1,3,5,7,9,11,13,15},{16,18,20,22,24,26,28,30},{17..., dimensions={0} | all-to-all | bytes 131072 | tf_op jit(solution)/shard_map/all_to_all | solution.py:32
  32.6 0.1 reduce_max.107
  32.7 0.0 copy-start.1
  32.7 0.4 subtract_reduce_fusion.1
  33.1 0.6 %exponential_reduce_fusion.2 = f32[384]{0:T(512)S(1)} fusion(f32[384,2048]{0,1:T(8,128)S(1)} %get-tuple-element.7, f32[384]{0:T(512)S(1)} %subtract_reduce_fusion.1, f32[2048]{0:T(1024)S(1)} %negate_add_fusion), kind=kLoop, calls=%fused_computation.5 | loop fusion | flops 2358912 | bytes 3156992 | tf_op jit(solution)/shard_map/reduce_sum | solution.py:86
  33.7 0.0 copy-done.1
  33.7 0.4 subtract_reduce_fusion
  34.0 0.9 %exponential_reduce_fusion.1 = f32[2048]{0:T(1024)S(1)} fusion(f32[384,2048]{0,1:T(8,128)S(1)} %get-tuple-element.7, f32[2048]{0:T(1024)S(1)} %subtract_reduce_fusion, f32[384]{0:T(512)S(1)} %convert_add_fusion), kind=kLoop, calls=%fused_computation.4 | loop fusion | flops 2357248 | bytes 3163648 | tf_op jit(solution)/shard_map/reduce_sum | solution.py:93
  35.0 0.1 collective-permute-start.2
  35.1 1.2 %collective-permute-done.2 = f32[2048]{0:T(1024)S(1)} collective-permute-done((f32[2048]{0:T(1024)S(1)}, f32[2048]{0:T(1024)S(1)}, u32[]{:S(2)}, u32[]{:S(2)}) %collective-permute-start.2) | collective-permute-done | bytes 8224 | tf_op jit(solution)/shard_map/ppermute | solution.py:19
  36.3 0.5 collective-permute-start.3
  36.8 3.3 %collective-permute-done.3 = f32[2048]{0:T(1024)S(1)} collective-permute-done((f32[2048]{0:T(1024)S(1)}, f32[2048]{0:T(1024)S(1)}, u32[]{:S(2)}, u32[]{:S(2)}) %collective-permute-start.3) | collective-permute-done | bytes 8224 | tf_op jit(solution)/shard_map/ppermute | solution.py:19
  40.1 0.3 collective-permute-start.6
  40.4 0.9 %collective-permute-start.5 = (f32[2048]{0:T(1024)S(1)}, f32[2048]{0:T(1024)S(1)}, u32[]{:S(2)}, u32[]{:S(2)}) collective-permute-start(f32[2048]{0:T(1024)S(1)} %log_add_fusion), channel_id=1, source_target_pairs={{0,8},{1,9},{2,10},{3,11},{4,12},{5,13},{6,14},{7,15},{8,0},{9,1},... | collective-permute-start | bytes 24584 | tf_op jit(solution)/shard_map/ppermute | solution.py:19
  41.3 3.3 %collective-permute-start.4 = (f32[2048]{0:T(1024)S(1)}, f32[2048]{0:T(1024)S(1)}, u32[]{:S(2)}, u32[]{:S(2)}) collective-permute-start(f32[2048]{0:T(1024)S(1)} %log_add_fusion), channel_id=1, source_target_pairs={{0,12},{1,13},{2,14},{3,15},{4,8},{5,9},{6,10},{7,11},{8,4},{9,5},... | collective-permute-start | bytes 24584 | tf_op jit(solution)/shard_map/ppermute | solution.py:19
  44.6 0.0 collective-permute-done.6
  44.6 0.4 collective-permute-done.5
  44.9 1.8 %collective-permute-done.4 = f32[2048]{0:T(1024)S(1)} collective-permute-done((f32[2048]{0:T(1024)S(1)}, f32[2048]{0:T(1024)S(1)}, u32[]{:S(2)}, u32[]{:S(2)}) %collective-permute-start.4) | collective-permute-done | bytes 8224 | tf_op jit(solution)/shard_map/ppermute | solution.py:19
  46.7 0.1 fusion.9
  46.8 0.4 subtract_reduce_fusion.4
  47.2 0.6 %exponential_reduce_fusion = f32[384]{0:T(512)S(1)} fusion(f32[384,2048]{0,1:T(8,128)S(1)} %get-tuple-element.7, f32[384]{0:T(512)S(1)} %subtract_reduce_fusion.4, f32[2048]{0:T(1024)S(1)} %get-tuple-element.2), kind=kLoop, calls=%fused_computation.3 | loop fusion | flops 2358912 | bytes 3156992 | tf_op jit(solution)/shard_map/reduce_sum | solution.py:86
  47.8 1.4 %fusion.1 = f32[64,384]{1,0:T(8,128)} fusion(f32[384,2048]{0,1:T(8,128)S(1)} %get-tuple-element.7, f32[384]{0:T(512)S(1)} %log_add_fusion.5, f32[2048]{0:T(1024)S(1)} %get-tuple-element.2, bf16[80,16,128]{2,0,1:T(8,128)(2,1)S(1)} %bitcast.51), kind=kOutput, calls=%fused_computation.13 | convolution fusion | flops 103022592 | bytes 3516416 | tf_op jit(solution)/shard_map/dot_general | solution.py:98
  49.2 0.6 %dynamic_slice.3 = f32[128]{0:T(128)} dynamic-slice(f32[2048]{0:T(1024)S(1)} %get-tuple-element.3, s32[]{:T(128)S(6)} %select_n.26), dynamic_slice_sizes={128} | dynamic-slice | bytes 1028 | tf_op jit(solution)/shard_map/dynamic_slice | solution.py:101
  (24 shorter events, 0.4 us)
Async XLA Ops:
  16.2 1.5 %collective-permute-start = (bf16[8,80,128]{2,1,0:T(8,128)(2,1)S(1)}, bf16[8,80,128]{2,1,0:T(8,128)(2,1)S(1)}, u32[]{:S(2)}, u32[]{:S(2)}) collective-permute-start(bf16[8,80,128]{2,1,0:T(8,128)(2,1)S(1)} %all_to_all.14), channel_id=1, source_target_pairs={{0,1},{1,0},{2,3},{3,2},{4,5},{5,4},{6,7},{7,6},{8,9},{9,8},{10,11... | collective-permute-start | bytes 491528 | tf_op jit(solution)/shard_map/ppermute | solution.py:19
  17.8 2.4 %copy-start = (bf16[384]{0:T(512)(128)(2,1)S(1)}, bf16[384]{0:T(512)(128)(2,1)}, u32[]{:S(2)}) copy-start(bf16[384]{0:T(512)(128)(2,1)} %param.7) | copy-start | bytes 2308
  21.5 1.4 %collective-permute-start.1 = (f32[2048]{0:T(1024)S(1)}, f32[2048]{0:T(1024)S(1)}, u32[]{:S(2)}, u32[]{:S(2)}) collective-permute-start(f32[2048]{0:T(1024)S(1)} %log_add_fusion.4), channel_id=1, source_target_pairs={{0,1},{1,0},{2,3},{3,2},{4,5},{5,4},{6,7},{7,6},{8,9},{9,8},{10,11... | collective-permute-start | bytes 24584 | tf_op jit(solution)/shard_map/ppermute | solution.py:19
  32.7 1.0 %copy-start.1 = (bf16[384]{0:T(512)(128)(2,1)S(1)}, bf16[384]{0:T(512)(128)(2,1)}, u32[]{:S(2)}) copy-start(bf16[384]{0:T(512)(128)(2,1)} %param.7) | copy-start | bytes 2308
  35.0 1.2 %collective-permute-start.2 = (f32[2048]{0:T(1024)S(1)}, f32[2048]{0:T(1024)S(1)}, u32[]{:S(2)}, u32[]{:S(2)}) collective-permute-start(f32[2048]{0:T(1024)S(1)} %log_add_fusion.2), channel_id=1, source_target_pairs={{0,1},{1,0},{2,3},{3,2},{4,5},{5,4},{6,7},{7,6},{8,9},{9,8},{10,11... | collective-permute-start | bytes 24584 | tf_op jit(solution)/shard_map/ppermute | solution.py:19
  36.3 3.7 %collective-permute-start.3 = (f32[2048]{0:T(1024)S(1)}, f32[2048]{0:T(1024)S(1)}, u32[]{:S(2)}, u32[]{:S(2)}) collective-permute-start(f32[2048]{0:T(1024)S(1)} %log_add_fusion.1), channel_id=1, source_target_pairs={{0,2},{1,3},{2,0},{3,1},{4,6},{5,7},{6,4},{7,5},{8,10},{9,11},{10,... | collective-permute-start | bytes 24584 | tf_op jit(solution)/shard_map/ppermute | solution.py:19
  40.1 4.5 %collective-permute-start.6 = (f32[2048]{0:T(1024)S(1)}, f32[2048]{0:T(1024)S(1)}, u32[]{:S(2)}, u32[]{:S(2)}) collective-permute-start(f32[2048]{0:T(1024)S(1)} %log_add_fusion), channel_id=1, source_target_pairs={{0,4},{1,5},{2,6},{3,7},{4,0},{5,1},{6,2},{7,3},{8,12},{9,13},{10,... | collective-permute-start | bytes 24584 | tf_op jit(solution)/shard_map/ppermute | solution.py:19
  40.4 4.5 %collective-permute-start.5 = (f32[2048]{0:T(1024)S(1)}, f32[2048]{0:T(1024)S(1)}, u32[]{:S(2)}, u32[]{:S(2)}) collective-permute-start(f32[2048]{0:T(1024)S(1)} %log_add_fusion), channel_id=1, source_target_pairs={{0,8},{1,9},{2,10},{3,11},{4,12},{5,13},{6,14},{7,15},{8,0},{9,1},... | collective-permute-start | bytes 24584 | tf_op jit(solution)/shard_map/ppermute | solution.py:19
  41.3 5.4 %collective-permute-start.4 = (f32[2048]{0:T(1024)S(1)}, f32[2048]{0:T(1024)S(1)}, u32[]{:S(2)}, u32[]{:S(2)}) collective-permute-start(f32[2048]{0:T(1024)S(1)} %log_add_fusion), channel_id=1, source_target_pairs={{0,12},{1,13},{2,14},{3,15},{4,8},{5,9},{6,10},{7,11},{8,4},{9,5},... | collective-permute-start | bytes 24584 | tf_op jit(solution)/shard_map/ppermute | solution.py:19

commit v4 on v1

v4 whole, which is shorter than its diff:
```python
import functools
import math

import jax
import jax.numpy as jnp
from jax import lax
from jax.experimental import pallas as pl
from jax.experimental.pallas import tpu as pltpu
from jax.sharding import PartitionSpec as P

ITERS = 2
AXIS = "wide"
LOG2E = math.log2(math.e)
LANES = 128
ROWS = 128
DEPTH = 256
SMALL_ROW = 2.0**-64
SMALL_COL = 2.0**-32
LARGE_COL = 2.0**100
FLOOR = -1e30

EXTRA = 64


def three_terms(value):
    high = value.astype(jnp.bfloat16)
    rest = value - high.astype(jnp.float32)
    middle = rest.astype(jnp.bfloat16)
    low = (rest - middle.astype(jnp.float32)).astype(jnp.bfloat16)
    return high, middle, low


def pick_rows(shape, rows, rest):
    index = lax.broadcasted_iota(jnp.int32, shape, 0)
    out = jnp.full(shape, rest, jnp.float32)
    for place, row in enumerate(rows):
        out = jnp.where(index == place, row, out)
    return out


def stage_source(points, logw, scale):
    feat, count = points.shape
    wide = points.astype(jnp.float32)
    shift = scale * jnp.sum(wide * wide, axis=0, keepdims=True)
    shift = shift.astype(jnp.bfloat16).astype(jnp.float32)
    extras = pick_rows((LANES - feat, count), [1.0, 1.0, 1.0, -shift, logw], 0.0)
    turned = jnp.concatenate([wide, extras], axis=0).T
    lane = lax.broadcasted_iota(jnp.int32, turned.shape, 1)
    high, middle, low = three_terms(jnp.where(lane < feat, 2.0 * scale, 1.0) * turned)
    low = pltpu.roll(low.astype(jnp.float32), feat, 1)
    tail = jnp.where(lane < feat, middle.astype(jnp.float32), low).astype(jnp.bfloat16)
    return high, tail


def stage_targets(parts, previous, scale, taug, g_ref, q_ref, feat):
    place = 0
    for part in parts:
        for block in range(part.shape[0]):
            at = pl.ds(place * LANES, LANES)
            coords = part[block, :feat, :]
            wide = coords.astype(jnp.float32)
            q_ref[:, at] = scale * jnp.sum(wide * wide, axis=0, keepdims=True)
            logw = part[block, feat : feat + 16, :].astype(jnp.float32)[0:1]
            g_ref[:, at] = logw * LOG2E
            taug[0:feat, at] = coords
            taug[2 * feat : 3 * feat, at] = coords
            taug[3 * feat : 4 * feat, at] = coords
            place += 1
    total = place * LANES
    potential = None
    if previous is not None:
        own, other, g_old = (ref[...] for ref in previous)
        other = jnp.concatenate([other[:, total // 2 :], other[:, : total // 2]], axis=1)
        peak = jnp.maximum(own, other)
        potential = g_old - (peak + jnp.log2(jnp.exp2(own - peak) + jnp.exp2(other - peak)))
        g_ref[...] = g_ref[...] + potential
    g = g_ref[...]
    high, middle, low = three_terms(g - jnp.max(g) - q_ref[...])
    extras = pick_rows(
        (EXTRA, total),
        [high.astype(jnp.float32), middle.astype(jnp.float32), low.astype(jnp.float32), 1.0],
        0.0,
    )
    taug[EXTRA : 2 * EXTRA, :] = extras.astype(jnp.bfloat16)
    return potential


def exponents(left, taug, begin, width):
    return jnp.dot(left, taug[:, begin : begin + width], preferred_element_type=jnp.float32)


def row_logw(left):
    return left[:, EXTRA + 4 : EXTRA + 5].astype(jnp.float32) * LOG2E


def fast_tile(left, taug, p_ref, col_ref):
    total = taug.shape[1]
    width = min(total, 256)
    sums = jnp.zeros((ROWS, LANES), jnp.float32)
    for begin in range(0, total, width):
        p = jnp.exp2(exponents(left, taug, begin, width))
        p_ref[:, begin : begin + width] = p
        for lane in range(0, width, LANES):
            sums = sums + p[:, lane : lane + LANES]
    s = jnp.sum(sums, axis=1, keepdims=True)
    weight = jnp.exp2(row_logw(left)) / s
    for begin in range(0, total, width):
        p = p_ref[:, begin : begin + width] * weight
        col_ref[:, begin : begin + width] += jnp.sum(p.reshape(ROWS // 8, 8, width), axis=0)
    return jnp.min(s.reshape(ROWS // 8, 8, 1), axis=0)


def column_sums(xaug, taug, p_ref, col_ref, top_ref, out_ref):
    total = taug.shape[1]
    tiles = xaug.shape[0] // ROWS
    side = p_ref.shape[0]
    col_ref[...] = jnp.zeros_like(col_ref)

    def advance(step, least):
        for slot in range(side):
            left = xaug[pl.ds(pl.multiple_of((step * side + slot) * ROWS, ROWS), ROWS), :]
            least = jnp.minimum(least, fast_tile(left, taug, p_ref.at[slot], col_ref))
        return least

    least = lax.fori_loop(0, tiles // side, advance, jnp.full((8, 1), 1e30, jnp.float32))
    cols = jnp.sum(col_ref[...], axis=0, keepdims=True)
    out_ref[...] = jnp.log2(cols)
    fine = jnp.logical_and(
        jnp.min(least) >= SMALL_ROW,
        jnp.logical_and(jnp.min(cols) >= SMALL_COL, jnp.max(cols) <= LARGE_COL),
    )

    @pl.when(jnp.logical_not(fine))
    def _():
        col_ref[...] = jnp.zeros_like(col_ref)
        top_ref[...] = jnp.full_like(top_ref, FLOOR)

        def careful(step, carry):
            left = xaug[pl.ds(pl.multiple_of(step * ROWS, ROWS), ROWS), :]
            e = exponents(left, taug, 0, total)
            peak = jnp.max(e, axis=1, keepdims=True)
            s = jnp.sum(jnp.exp2(e - peak), axis=1, keepdims=True)
            term = e + (row_logw(left) - peak - jnp.log2(s))
            old = top_ref[...]
            top = jnp.maximum(old, jnp.max(term, axis=0, keepdims=True))
            added = jnp.sum(jnp.exp2(term - top), axis=0, keepdims=True)
            col_ref[0:1, :] = col_ref[0:1, :] * jnp.exp2(old - top) + added
            top_ref[...] = top
            return carry

        lax.fori_loop(0, tiles, careful, 0)
        out_ref[...] = top_ref[...] + jnp.log2(col_ref[0:1, :])


def first_kernel(n_x, n_t, feat, inverse, *refs):
    xs, ts, logws = refs[:n_x], refs[n_x : n_x + n_t], refs[n_x + n_t]
    xaug, out_ref, g_ref, taug, q_ref, p_ref, col_ref, top_ref = refs[n_x + n_t + 1 :]
    scale = inverse[0] * LOG2E
    count = xs[0].shape[2]
    place = 0
    for part in xs:
        for block in range(part.shape[0]):
            high, tail = stage_source(part[block], logws[place : place + 1, :], scale)
            rows = pl.ds(place * count, count)
            xaug[rows, 0:LANES] = high
            xaug[rows, LANES:DEPTH] = tail
            place += 1
    stage_targets(ts, None, scale, taug, g_ref, q_ref, feat)
    column_sums(xaug, taug, p_ref, col_ref, top_ref, out_ref)


def next_kernel(n_t, feat, inverse, xaug, own, other, g_old, *refs):
    ts = refs[:n_t]
    out_ref, g_ref, taug, q_ref, p_ref, col_ref, top_ref = refs[n_t:]
    scale = inverse[0] * LOG2E
    stage_targets(ts, (own, other, g_old), scale, taug, g_ref, q_ref, feat)
    column_sums(xaug, taug, p_ref, col_ref, top_ref, out_ref)


def map_kernel(n_t, feat, inverse, xaug, own, other, g_old, *refs):
    ts = refs[:n_t]
    mapped_ref, pot_ref, g_ref, taug, q_ref, p_ref, plan_ref = refs[n_t:]
    scale = inverse[0] * LOG2E
    potential = stage_targets(ts, (own, other, g_old), scale, taug, g_ref, q_ref, feat)
    pot_ref[...] = potential[:, :LANES] * (1.0 / LOG2E)
    total = taug.shape[1]
    width = min(total, 256)

    for begin_row in range(0, xaug.shape[0], ROWS):
        rows = slice(begin_row, begin_row + ROWS)
        left = xaug[rows, :]
        sums = jnp.zeros((ROWS, LANES), jnp.float32)
        for begin in range(0, total, width):
            p = jnp.exp2(exponents(left, taug, begin, width))
            p_ref[:, begin : begin + width] = p
            for lane in range(0, width, LANES):
                sums = sums + p[:, lane : lane + LANES]
        s = jnp.sum(sums, axis=1, keepdims=True)
        inv_s = 1.0 / s
        for begin in range(0, total, width):
            piece = slice(begin, begin + width)
            plan_ref[rows, piece] = (p_ref[:, piece] * inv_s).astype(jnp.bfloat16)

        @pl.when(jnp.logical_not(jnp.min(s) >= SMALL_ROW))
        def _():
            e = exponents(left, taug, 0, total)
            e = e - jnp.max(e, axis=1, keepdims=True)
            e = e - jnp.log2(jnp.sum(jnp.exp2(e), axis=1, keepdims=True))
            plan_ref[rows, :] = jnp.exp2(e).astype(jnp.bfloat16)

    mapped_ref[...] = lax.dot_general(
        taug[0:feat, :],
        plan_ref[...],
        (((1,), (1,)), ((), ())),
        preferred_element_type=jnp.float32,
    )


def swap(value, count, step):
    return lax.ppermute(value, AXIS, [(source, source ^ step) for source in range(count)])


def chip_stages(count):
    high, stages = count.bit_length() - 1, []
    while high > 1:
        width = min(2, high - 1)
        stages.append((high - width, width))
        high -= width
    return stages


def gather_chips(block, count):
    parts = [block[None]]
    for low, width in chip_stages(count):
        held = parts[0] if len(parts) == 1 else jnp.concatenate(parts, axis=0)
        digits = range((1 << width) - 1, 0, -1)
        parts = [held] + [swap(held, count, digit << low) for digit in digits]
    return parts


def on_device(source_points, target_points, source_logw, target_logw, inverse_eps, count):
    feat, own_sources = source_points.shape
    own_targets = target_points.shape[1]
    extra_rows = own_sources // LANES
    pad = -(1 + extra_rows) % 16
    packed = jnp.concatenate(
        [
            target_points,
            target_logw[None, :],
            source_logw.reshape(extra_rows, LANES),
            jnp.zeros((pad, own_targets), target_points.dtype),
        ],
        axis=0,
    )
    mine = gather_chips(packed, count)
    theirs = [swap(part, count, 1) for part in mine]
    ts = mine + theirs
    xs = gather_chips(source_points, count)
    chips = count // 2
    logws = jnp.concatenate(
        [part[:, feat + 1 : feat + 1 + extra_rows] for part in mine], axis=0
    ).reshape(chips, own_sources).astype(jnp.float32)

    total, rows = count * own_targets, chips * own_sources
    side = 3 if total <= 4096 else 1
    f32, bf16 = jnp.float32, jnp.bfloat16
    vmem = pl.BlockSpec(memory_space=pltpu.VMEM)
    smem = pl.BlockSpec(memory_space=pltpu.SMEM)
    params = pltpu.CompilerParams(vmem_limit_bytes=(24 if total <= 4096 else 56) << 20)
    line = jax.ShapeDtypeStruct((1, total), f32)
    sums_scratch = [
        pltpu.VMEM((DEPTH, total), bf16),
        pltpu.VMEM((1, total), f32),
        pltpu.VMEM((side, ROWS, total), f32),
        pltpu.VMEM((8, total), f32),
        pltpu.VMEM((1, total), f32),
    ]

    xaug, sums, g = pl.pallas_call(
        functools.partial(first_kernel, len(xs), len(ts), feat),
        out_shape=[jax.ShapeDtypeStruct((rows, DEPTH), bf16), line, line],
        in_specs=[smem] + [vmem] * (len(xs) + len(ts) + 1),
        out_specs=[vmem] * 3,
        scratch_shapes=sums_scratch,
        compiler_params=params,
    )(inverse_eps, *xs, *ts, logws)
    for _ in range(ITERS - 1):
        sums, g = pl.pallas_call(
            functools.partial(next_kernel, len(ts), feat),
            out_shape=[line, line],
            in_specs=[smem] + [vmem] * (4 + len(ts)),
            out_specs=[vmem] * 2,
            scratch_shapes=sums_scratch,
            compiler_params=params,
        )(inverse_eps, xaug, sums, swap(sums, count, 1), g, *ts)
    mapped, potential = pl.pallas_call(
        functools.partial(map_kernel, len(ts), feat),
        out_shape=[
            jax.ShapeDtypeStruct((feat, own_sources), f32),
            jax.ShapeDtypeStruct((1, own_targets), f32),
        ],
        in_specs=[smem] + [vmem] * (4 + len(ts)),
        out_specs=[vmem] * 2,
        scratch_shapes=[
            pltpu.VMEM((1, total), f32),
            pltpu.VMEM((DEPTH, total), bf16),
            pltpu.VMEM((1, total), f32),
            pltpu.VMEM((ROWS, total), f32),
            pltpu.VMEM((own_sources, total), bf16),
        ],
        compiler_params=params,
    )(inverse_eps, xaug[:own_sources], sums, swap(sums, count, 1), g, *ts)
    return (mapped, potential.reshape(own_targets))


def solution(mesh):
    count = mesh.shape[AXIS]
    placed = (
        P(None, ("grp", "wide")),
        P(None, ("grp", "wide")),
        P(("grp", "wide")),
        P(("grp", "wide")),
        P(),
    )

    def body(*blocks):
        return on_device(*blocks, count)

    return jax.shard_map(
        body,
        mesh=mesh,
        in_specs=placed,
        out_specs=(P(None, ("grp", "wide")), P(("grp", "wide"))),
        check_vma=False,
    )
```

time: 71.7 us -> 90.8 us (1.27)
  Pallas kernels: 0 us -> 65 us
  starting transfers between devices: 30 us -> 13.8 us
  waiting for transfers between devices: 22.9 us -> 8.63 us
  other arithmetic: 8.81 us -> 1.68 us
  local copies, waits for them, and re-layouts: 4.91 us -> 0.11 us
  matrix products: 3.12 us -> 0 us
    pallas_call x0 -> x3, Pallas kernels: none -> 65 us  [the longest x1 30.4 us: on_device(): pl.pallas_call(functools.partial(first_kernel, len(xs), len(ts), feat), o...]
    all_to_all x1 -> x0, waiting for transfers between devices: 9.62 us -> none  [gather_targets(): every = lax.all_to_all(spread, AXIS, 0, 0, tiled=True)]
    ppermute x19 -> x12, starting transfers between devices: 22.6 us -> 13.8 us  [swap(): lax.ppermute(value, AXIS, [(source, source ^ step) for source in range(co...]
    all_to_all x1 -> x0, starting transfers between devices: 7.36 us -> none  [gather_targets(): every = lax.all_to_all(spread, AXIS, 0, 0, tiled=True)]
    reduce_sum x12 -> x0, other arithmetic: 5.68 us -> none  [the longest x2 1.88 us: on_device(): partial = peak + jnp.log(jnp.sum(jnp.exp(scores - peak[None, :]), axis=0))]
    ppermute x19 -> x12, waiting for transfers between devices: 13.3 us -> 8.63 us  [swap(): lax.ppermute(value, AXIS, [(source, source ^ step) for source in range(co...]
    dot_general x2 -> x0, matrix products: 3.12 us -> none  [the longest x1 1.75 us: on_device(): lax.dot_general(source_points, targets, (((0,), (0,)), ((), ())), preferr...]
    another operation x1 -> x0, local copies, waits for them, and re-layouts: 2.89 us -> none  [lse_across(): stacked = jnp.stack(held)]
  transfers between devices with their start and end apart: 20 -> 12, of which waited for: 8 -> 6; matrix products, arithmetic and copies ran while one was open for 1% -> 2% of each run, Pallas kernels for 0% -> 0%
where the time goes in v4:
time: 90.8 us; the launch traced here: 90.6 us
  Pallas kernels  65 us (72%)
  starting transfers between devices  13.8 us (15%)
  waiting for transfers between devices  8.63 us (10%)
  other arithmetic  1.68 us (2%)
  between operations  1.35 us (1%)
    pallas_call x1, Pallas kernels, on_device(): pl.pallas_call(functools.partial(first_kernel, len(xs), len(ts), feat), o...  30.4 us
    pallas_call x1, Pallas kernels, on_device(): pl.pallas_call(functools.partial(next_kernel, len(ts), feat), out_shape=[...  29.7 us
    ppermute x12, starting transfers between devices, swap(): lax.ppermute(value, AXIS, [(source, source ^ step) for source in range(co...  13.8 us
    ppermute x12, waiting for transfers between devices, swap(): lax.ppermute(value, AXIS, [(source, source ^ step) for source in range(co...  8.63 us
    pallas_call x1, Pallas kernels, on_device(): pl.pallas_call(functools.partial(map_kernel, len(ts), feat), out_shape=[j...  4.92 us
  transfers between devices with their start and end apart: 12, of which 6 were waited for; matrix products, arithmetic and copies ran while one was open for 2% of the time, Pallas kernels for 0%

profile of v4, /device:TPU:0, one launch (start us, length us, event | category | flops | bytes accessed | tf_op | source)
XLA Modules:
  0.0 90.6 jit_solution(10810989910155660232)
XLA Ops:
  0.6 3.1 %collective-permute-start.2 = (bf16[1,64,384]{2,1,0:T(8,128)(2,1)}, bf16[1,64,384]{2,1,0:T(8,128)(2,1)S(1)}, u32[]{:S(2)}, u32[]{:S(2)}) collective-permute-start(bf16[1,64,384]{2,1,0:T(8,128)(2,1)} %bitcast.12), channel_id=1, source_target_pairs={{0,4},{1,5},{2,6},{3,7},{4,0},{5,1},{6,2},{7,3},{8,12},{9,13},{10,... | collective-permute-start | bytes 147464 | tf_op jit(solution)/shard_map/ppermute | solution.py:220
  3.7 2.6 %collective-permute-start.1 = (bf16[1,64,384]{2,1,0:T(8,128)(2,1)}, bf16[1,64,384]{2,1,0:T(8,128)(2,1)S(1)}, u32[]{:S(2)}, u32[]{:S(2)}) collective-permute-start(bf16[1,64,384]{2,1,0:T(8,128)(2,1)} %bitcast.13), channel_id=1, source_target_pairs={{0,8},{1,9},{2,10},{3,11},{4,12},{5,13},{6,14},{7,15},{8,0},{9,1},... | collective-permute-start | bytes 147464 | tf_op jit(solution)/shard_map/ppermute | solution.py:220
  6.3 0.0 collective-permute-start
  6.3 0.1 pad.9.clone
  6.4 0.8 maximum_bitcast_fusion
  7.2 1.0 %collective-permute-start.6 = (bf16[1,80,128]{2,1,0:T(8,128)(2,1)S(1)}, bf16[1,80,128]{2,1,0:T(8,128)(2,1)S(1)}, u32[]{:S(2)}, u32[]{:S(2)}) collective-permute-start(bf16[1,80,128]{2,1,0:T(8,128)(2,1)S(1)} %maximum_bitcast_fusion), channel_id=1, source_target_pairs={{0,4},{1,5},{2,6},{3,7},{4,0},{5,1},{6,2},{7,3},{8,12},{9,13},{10,... | collective-permute-start | bytes 61448 | tf_op jit(solution)/shard_map/ppermute | solution.py:220
  8.2 3.5 %collective-permute-start.5 = (bf16[1,80,128]{2,1,0:T(8,128)(2,1)S(1)}, bf16[1,80,128]{2,1,0:T(8,128)(2,1)S(1)}, u32[]{:S(2)}, u32[]{:S(2)}) collective-permute-start(bf16[1,80,128]{2,1,0:T(8,128)(2,1)S(1)} %maximum_bitcast_fusion), channel_id=1, source_target_pairs={{0,8},{1,9},{2,10},{3,11},{4,12},{5,13},{6,14},{7,15},{8,0},{9,1},... | collective-permute-start | bytes 61448 | tf_op jit(solution)/shard_map/ppermute | solution.py:220
  11.7 0.0 collective-permute-done.2
  11.7 0.0 collective-permute-start.4
  11.7 0.0 collective-permute-done.1
  11.7 0.7 collective-permute-done
  12.4 0.8 pad_maximum_fusion.refs_0_
  13.2 1.6 %collective-permute-start.3 = (bf16[4,64,384]{2,1,0:T(8,128)(2,1)S(1)}, bf16[4,64,384]{2,1,0:T(8,128)(2,1)S(1)}, u32[]{:S(2)}, u32[]{:S(2)}) collective-permute-start(bf16[4,64,384]{2,1,0:T(8,128)(2,1)S(1)} %pad_maximum_fusion.refs_0_), channel_id=1, source_target_pairs={{0,2},{1,3},{2,0},{3,1},{4,6},{5,7},{6,4},{7,5},{8,10},{9,11},{10,... | collective-permute-start | bytes 589832 | tf_op jit(solution)/shard_map/ppermute | solution.py:220
  14.8 0.0 collective-permute-done.6
  14.8 0.0 collective-permute-done.5
  14.8 2.4 %collective-permute-done.4 = bf16[1,80,128]{2,1,0:T(8,128)(2,1)S(1)} collective-permute-done((bf16[1,80,128]{2,1,0:T(8,128)(2,1)S(1)}, bf16[1,80,128]{2,1,0:T(8,128)(2,1)S(1)}, u32[]{:S(2)}, u32[]{:S(2)}) %collective-permute-start.4) | collective-permute-done | bytes 20512 | tf_op jit(solution)/shard_map/ppermute | solution.py:220
  17.3 1.6 %collective-permute-start.7 = (bf16[4,80,128]{2,1,0:T(8,128)(2,1)S(1)}, bf16[4,80,128]{2,1,0:T(8,128)(2,1)S(1)}, u32[]{:S(2)}, u32[]{:S(2)}) collective-permute-start(bf16[4,80,128]{2,1,0:T(8,128)(2,1)S(1)} %pad_maximum_fusion.1.refs_2_.refs_0_), channel_id=1, source_target_pairs={{0,2},{1,3},{2,0},{3,1},{4,6},{5,7},{6,4},{7,5},{8,10},{9,11},{10,... | collective-permute-start | bytes 245768 | tf_op jit(solution)/shard_map/ppermute | solution.py:220
  19.5 0.1 collective-permute-start.8
  19.6 2.2 %collective-permute-done.7.refs_3_.refs_1_ = bf16[4,80,128]{2,1,0:T(8,128)(2,1)S(1)} collective-permute-done((bf16[4,80,128]{2,1,0:T(8,128)(2,1)S(1)}, bf16[4,80,128]{2,1,0:T(8,128)(2,1)S(1)}, u32[]{:S(2)}, u32[]{:S(2)}) %collective-permute-start.7) | collective-permute-done | bytes 81952 | tf_op jit(solution)/shard_map/ppermute | solution.py:220
  21.8 0.0 collective-permute-start.9
  21.8 0.0 collective-permute-done.8.refs_4_.refs_2_
  21.8 1.2 %collective-permute-done.9.refs_5_.refs_3_ = bf16[4,80,128]{2,1,0:T(8,128)(2,1)S(1)} collective-permute-done((bf16[4,80,128]{2,1,0:T(8,128)(2,1)S(1)}, bf16[4,80,128]{2,1,0:T(8,128)(2,1)S(1)}, u32[]{:S(2)}, u32[]{:S(2)}) %collective-permute-start.9) | collective-permute-done | bytes 81952 | tf_op jit(solution)/shard_map/ppermute | solution.py:220
  23.1 0.0 collective-permute-done.3.refs_1_
  23.1 30.4 %shard_map.68 = (bf16[3072,256]{1,0:T(8,128)(2,1)S(1)}, f32[1,2048]{1,0:T(1,128)S(1)}, f32[1,2048]{1,0:T(1,128)S(1)}) custom-call(f32[1]{0:T(128)S(6)} %copy.10.inverse, bf16[4,64,384]{2,1,0:T(8,128)(2,1)S(1)} %pad_maximum_fusion.refs_0_, bf16[4,64,384]{2,1,0:T(8,128)(2,1)S(1)} %collective-permute-done.3.refs_1_, ...), custom_call_target="tpu_custom_call" | custom-call | tf_op jit(solution)/shard_map/pallas_call | solution.py:279
  53.4 0.2 collective-permute-start.10
  53.7 1.0 %collective-permute-done.10.other = f32[1,2048]{1,0:T(1,128)S(1)} collective-permute-done((f32[1,2048]{1,0:T(1,128)S(1)}, f32[1,2048]{1,0:T(1,128)S(1)}, u32[]{:S(2)}, u32[]{:S(2)}) %collective-permute-start.10) | collective-permute-done | bytes 8224 | tf_op jit(solution)/shard_map/ppermute | solution.py:220
  54.7 29.7 %shard_map.69 = (f32[1,2048]{1,0:T(1,128)S(1)}, f32[1,2048]{1,0:T(1,128)S(1)}) custom-call(f32[1]{0:T(128)S(6)} %copy.10.inverse, bf16[3072,256]{1,0:T(8,128)(2,1)S(1)} %get-tuple-element.9.xaug, f32[1,2048]{1,0:T(1,128)S(1)} %get-tuple-element.10.own, f32[1,2048]{1,0:T(1,128)S(1)} %collective-permute-done.10.other, f32[1,2048]{1,0:T(1,128)S(1)} %get-tuple-element.11.g_old, ...), custom_call_target="tpu_custom_call" | custom-call | tf_op jit(solution)/shard_map/pallas_call | solution.py:288
  84.4 0.2 collective-permute-start.11
  84.7 1.0 %collective-permute-done.11.other = f32[1,2048]{1,0:T(1,128)S(1)} collective-permute-done((f32[1,2048]{1,0:T(1,128)S(1)}, f32[1,2048]{1,0:T(1,128)S(1)}, u32[]{:S(2)}, u32[]{:S(2)}) %collective-permute-start.11) | collective-permute-done | bytes 8224 | tf_op jit(solution)/shard_map/ppermute | solution.py:220
  85.7 4.9 %shard_map.70 = (f32[64,384]{1,0:T(8,128)}, f32[1,128]{1,0:T(1,128)}) custom-call(f32[1]{0:T(128)S(6)} %copy.10.inverse, bf16[384,256]{1,0:T(8,128)(2,1)S(1)} %slice.11.xaug, f32[1,2048]{1,0:T(1,128)S(1)} %get-tuple-element.12.own, f32[1,2048]{1,0:T(1,128)S(1)} %collective-permute-done.11.other, f32[1,2048]{1,0:T(1,128)S(1)} %get-tuple-element.13.g_old, ...), custom_call_target="tpu_custom_call" | custom-call | tf_op jit(solution)/shard_map/pallas_call | solution.py:296
  (7 shorter events, 0.1 us)
Async XLA Ops:
  0.6 11.0 %collective-permute-start.2 = (bf16[1,64,384]{2,1,0:T(8,128)(2,1)}, bf16[1,64,384]{2,1,0:T(8,128)(2,1)S(1)}, u32[]{:S(2)}, u32[]{:S(2)}) collective-permute-start(bf16[1,64,384]{2,1,0:T(8,128)(2,1)} %bitcast.12), channel_id=1, source_target_pairs={{0,4},{1,5},{2,6},{3,7},{4,0},{5,1},{6,2},{7,3},{8,12},{9,13},{10,... | collective-permute-start | bytes 147464 | tf_op jit(solution)/shard_map/ppermute | solution.py:220
  3.7 8.0 %collective-permute-start.1 = (bf16[1,64,384]{2,1,0:T(8,128)(2,1)}, bf16[1,64,384]{2,1,0:T(8,128)(2,1)S(1)}, u32[]{:S(2)}, u32[]{:S(2)}) collective-permute-start(bf16[1,64,384]{2,1,0:T(8,128)(2,1)} %bitcast.13), channel_id=1, source_target_pairs={{0,8},{1,9},{2,10},{3,11},{4,12},{5,13},{6,14},{7,15},{8,0},{9,1},... | collective-permute-start | bytes 147464 | tf_op jit(solution)/shard_map/ppermute | solution.py:220
  6.3 6.1 %collective-permute-start = (bf16[1,64,384]{2,1,0:T(8,128)(2,1)}, bf16[1,64,384]{2,1,0:T(8,128)(2,1)S(1)}, u32[]{:S(2)}, u32[]{:S(2)}) collective-permute-start(bf16[1,64,384]{2,1,0:T(8,128)(2,1)} %bitcast.14), channel_id=1, source_target_pairs={{0,12},{1,13},{2,14},{3,15},{4,8},{5,9},{6,10},{7,11},{8,4},{9,5},... | collective-permute-start | bytes 147464 | tf_op jit(solution)/shard_map/ppermute | solution.py:220
  7.2 7.6 %collective-permute-start.6 = (bf16[1,80,128]{2,1,0:T(8,128)(2,1)S(1)}, bf16[1,80,128]{2,1,0:T(8,128)(2,1)S(1)}, u32[]{:S(2)}, u32[]{:S(2)}) collective-permute-start(bf16[1,80,128]{2,1,0:T(8,128)(2,1)S(1)} %maximum_bitcast_fusion), channel_id=1, source_target_pairs={{0,4},{1,5},{2,6},{3,7},{4,0},{5,1},{6,2},{7,3},{8,12},{9,13},{10,... | collective-permute-start | bytes 61448 | tf_op jit(solution)/shard_map/ppermute | solution.py:220
  8.2 6.6 %collective-permute-start.5 = (bf16[1,80,128]{2,1,0:T(8,128)(2,1)S(1)}, bf16[1,80,128]{2,1,0:T(8,128)(2,1)S(1)}, u32[]{:S(2)}, u32[]{:S(2)}) collective-permute-start(bf16[1,80,128]{2,1,0:T(8,128)(2,1)S(1)} %maximum_bitcast_fusion), channel_id=1, source_target_pairs={{0,8},{1,9},{2,10},{3,11},{4,12},{5,13},{6,14},{7,15},{8,0},{9,1},... | collective-permute-start | bytes 61448 | tf_op jit(solution)/shard_map/ppermute | solution.py:220
  11.7 5.6 %collective-permute-start.4 = (bf16[1,80,128]{2,1,0:T(8,128)(2,1)S(1)}, bf16[1,80,128]{2,1,0:T(8,128)(2,1)S(1)}, u32[]{:S(2)}, u32[]{:S(2)}) collective-permute-start(bf16[1,80,128]{2,1,0:T(8,128)(2,1)S(1)} %maximum_bitcast_fusion), channel_id=1, source_target_pairs={{0,12},{1,13},{2,14},{3,15},{4,8},{5,9},{6,10},{7,11},{8,4},{9,5},... | collective-permute-start | bytes 61448 | tf_op jit(solution)/shard_map/ppermute | solution.py:220
  13.2 9.8 %collective-permute-start.3 = (bf16[4,64,384]{2,1,0:T(8,128)(2,1)S(1)}, bf16[4,64,384]{2,1,0:T(8,128)(2,1)S(1)}, u32[]{:S(2)}, u32[]{:S(2)}) collective-permute-start(bf16[4,64,384]{2,1,0:T(8,128)(2,1)S(1)} %pad_maximum_fusion.refs_0_), channel_id=1, source_target_pairs={{0,2},{1,3},{2,0},{3,1},{4,6},{5,7},{6,4},{7,5},{8,10},{9,11},{10,... | collective-permute-start | bytes 589832 | tf_op jit(solution)/shard_map/ppermute | solution.py:220
  17.3 4.5 %collective-permute-start.7 = (bf16[4,80,128]{2,1,0:T(8,128)(2,1)S(1)}, bf16[4,80,128]{2,1,0:T(8,128)(2,1)S(1)}, u32[]{:S(2)}, u32[]{:S(2)}) collective-permute-start(bf16[4,80,128]{2,1,0:T(8,128)(2,1)S(1)} %pad_maximum_fusion.1.refs_2_.refs_0_), channel_id=1, source_target_pairs={{0,2},{1,3},{2,0},{3,1},{4,6},{5,7},{6,4},{7,5},{8,10},{9,11},{10,... | collective-permute-start | bytes 245768 | tf_op jit(solution)/shard_map/ppermute | solution.py:220
  19.5 2.3 %collective-permute-start.8 = (bf16[4,80,128]{2,1,0:T(8,128)(2,1)S(1)}, bf16[4,80,128]{2,1,0:T(8,128)(2,1)S(1)}, u32[]{:S(2)}, u32[]{:S(2)}) collective-permute-start(bf16[4,80,128]{2,1,0:T(8,128)(2,1)S(1)} %pad_maximum_fusion.1.refs_2_.refs_0_), channel_id=1, source_target_pairs={{0,1},{1,0},{2,3},{3,2},{4,5},{5,4},{6,7},{7,6},{8,9},{9,8},{10,11... | collective-permute-start | bytes 245768 | tf_op jit(solution)/shard_map/ppermute | solution.py:220
  21.8 1.3 %collective-permute-start.9 = (bf16[4,80,128]{2,1,0:T(8,128)(2,1)S(1)}, bf16[4,80,128]{2,1,0:T(8,128)(2,1)S(1)}, u32[]{:S(2)}, u32[]{:S(2)}) collective-permute-start(bf16[4,80,128]{2,1,0:T(8,128)(2,1)S(1)} %collective-permute-done.7.refs_3_.refs_1_), channel_id=1, source_target_pairs={{0,1},{1,0},{2,3},{3,2},{4,5},{5,4},{6,7},{7,6},{8,9},{9,8},{10,11... | collective-permute-start | bytes 245768 | tf_op jit(solution)/shard_map/ppermute | solution.py:220
  53.4 1.2 %collective-permute-start.10 = (f32[1,2048]{1,0:T(1,128)S(1)}, f32[1,2048]{1,0:T(1,128)S(1)}, u32[]{:S(2)}, u32[]{:S(2)}) collective-permute-start(f32[1,2048]{1,0:T(1,128)S(1)} %get-tuple-element.10.own), channel_id=1, source_target_pairs={{0,1},{1,0},{2,3},{3,2},{4,5},{5,4},{6,7},{7,6},{8,9},{9,8},{10,11... | collective-permute-start | bytes 24584 | tf_op jit(solution)/shard_map/ppermute | solution.py:220
  84.4 1.2 %collective-permute-start.11 = (f32[1,2048]{1,0:T(1,128)S(1)}, f32[1,2048]{1,0:T(1,128)S(1)}, u32[]{:S(2)}, u32[]{:S(2)}) collective-permute-start(f32[1,2048]{1,0:T(1,128)S(1)} %get-tuple-element.12.own), channel_id=1, source_target_pairs={{0,1},{1,0},{2,3},{3,2},{4,5},{5,4},{6,7},{7,6},{8,9},{9,8},{10,11... | collective-permute-start | bytes 24584 | tf_op jit(solution)/shard_map/ppermute | solution.py:220

commit v5 on v4

v5 whole, which is shorter than its diff:
```python
import functools
import math

import jax
import jax.numpy as jnp
from jax import lax
from jax.experimental import pallas as pl
from jax.experimental.pallas import tpu as pltpu
from jax.sharding import PartitionSpec as P

ITERS = 2
AXIS = "wide"
LOG2E = math.log2(math.e)
LANES = 128
DEPTH = 256
SMALL_ROW = 2.0**-64
SMALL_COL = 2.0**-32
LARGE_COL = 2.0**100
FLOOR = -1e30


def three_terms(value):
    high = value.astype(jnp.bfloat16)
    rest = value - high.astype(jnp.float32)
    middle = rest.astype(jnp.bfloat16)
    low = (rest - middle.astype(jnp.float32)).astype(jnp.bfloat16)
    return high, middle, low


def pick_rows(shape, rows):
    index = lax.broadcasted_iota(jnp.int32, shape, 0)
    out = jnp.zeros(shape, jnp.float32)
    for place, row in enumerate(rows):
        out = jnp.where(index == place, row, out)
    return out


def stage_source(points, scale, xaug, at):
    feat, count = points.shape
    wide = points.astype(jnp.float32)
    shift = scale * jnp.sum(wide * wide, axis=0, keepdims=True)
    shift = shift.astype(jnp.bfloat16).astype(jnp.float32)
    xaug[0:feat, at] = pick_rows((feat, count), [1.0, 1.0, 1.0, -shift]).astype(jnp.bfloat16)
    for place, term in enumerate(three_terms(2.0 * scale * wide)):
        xaug[(place + 1) * feat : (place + 2) * feat, at] = term


def stage_targets(parts, previous, scale, taug, g_ref, q_ref, feat):
    blocks = [(part, block) for part in parts for block in range(part.shape[0])]
    total = len(blocks) * LANES
    for place, (part, block) in enumerate(blocks):
        at = slice(place * LANES, (place + 1) * LANES)
        wide = part[block, :feat, :].astype(jnp.float32)
        q_ref[:, at] = scale * jnp.sum(wide * wide, axis=0, keepdims=True)
        logw = part[block, feat : feat + 16, :].astype(jnp.float32)[0:1]
        g_ref[:, at] = logw * LOG2E
    potential = None
    if previous is not None:
        own, other, g_old = (ref[...] for ref in previous)
        other = jnp.concatenate([other[:, total // 2 :], other[:, : total // 2]], axis=1)
        peak = jnp.maximum(own, other)
        potential = g_old - (peak + jnp.log2(jnp.exp2(own - peak) + jnp.exp2(other - peak)))
        g_ref[...] = g_ref[...] + potential
    g = g_ref[...]
    terms = [term.astype(jnp.float32) for term in three_terms(g - jnp.max(g) - q_ref[...])]
    for place, (part, block) in enumerate(blocks):
        at = slice(place * LANES, (place + 1) * LANES)
        extras = pick_rows((feat, LANES), [term[:, at] for term in terms] + [1.0])
        wide = part[block, :feat, :].astype(jnp.float32)
        turned = jnp.concatenate([extras, wide], axis=0).T
        lane = lax.broadcasted_iota(jnp.int32, turned.shape, 1)
        twice = jnp.where(lane < feat, pltpu.roll(turned, feat, 1), turned)
        taug[at, 0:LANES] = turned.astype(jnp.bfloat16)
        taug[at, LANES:DEPTH] = twice.astype(jnp.bfloat16)
    return potential


def exponents(left, right):
    return jnp.dot(left, right, preferred_element_type=jnp.float32)


def spread_rows(taug, right, p_ref, beside):
    total, width = taug.shape[0], right.shape[1]
    reach = min(total, 2048)
    sums = jnp.zeros((8, width), jnp.float32)
    for begin in range(0, total, reach):
        e = exponents(taug[begin : begin + reach, :], right)
        for inner in range(0, reach, LANES):
            p = jnp.exp2(e[inner : inner + LANES])
            p_ref[begin + inner : begin + inner + LANES, :] = p
            sums = sums + jnp.sum(p.reshape(LANES // 8, 8, width), axis=0)
            beside(slice(begin + inner, begin + inner + LANES))
    return jnp.sum(sums, axis=0, keepdims=True)


def add_columns(p_ref, weight, col_ref, rows):
    width = weight.shape[1]
    added = p_ref[rows, 0:LANES] * weight[:, 0:LANES]
    for lane in range(LANES, width, LANES):
        added = added + p_ref[rows, lane : lane + LANES] * weight[:, lane : lane + LANES]
    col_ref[rows, :] += added


def column_sums(xaug, logws, taug, p_refs, col_ref, top_ref, out_ref):
    total = taug.shape[0]
    width = p_refs[0].shape[1]
    tiles = xaug.shape[1] // width
    col_ref[...] = jnp.zeros_like(col_ref)

    def columns(tile):
        if isinstance(tile, int):
            return pl.ds(tile * width, width)
        return pl.ds(pl.multiple_of(tile * width, width), width)

    def step(tile, slot, held):
        def beside(rows):
            if held is not None:
                add_columns(p_refs[1 - slot], held, col_ref, rows)

        at = columns(tile)
        s = spread_rows(taug, xaug[:, at], p_refs[slot], beside)
        return s, jnp.exp2(logws[:, at] * LOG2E) / s

    def two_steps(pair, carry):
        least, weight = carry
        s1, weight1 = step(2 * pair + 1, 1, weight)
        s0, weight0 = step(2 * pair + 2, 0, weight1)
        return jnp.minimum(least, jnp.minimum(s0, s1)), weight0

    s, weight = step(0, 0, None)
    least, weight = lax.fori_loop(0, tiles // 2 - 1, two_steps, (s, weight))
    s, weight = step(tiles - 1, 1, weight)
    least = jnp.minimum(least, s)
    for begin in range(0, total, LANES):
        rows = slice(begin, begin + LANES)
        add_columns(p_refs[1], weight, col_ref, rows)
        out_ref[:, rows] = jnp.sum(col_ref[rows, :].T, axis=0, keepdims=True)
    cols = out_ref[...]
    out_ref[...] = jnp.log2(cols)
    fine = jnp.logical_and(
        jnp.min(least) >= SMALL_ROW,
        jnp.logical_and(jnp.min(cols) >= SMALL_COL, jnp.max(cols) <= LARGE_COL),
    )

    @pl.when(jnp.logical_not(fine))
    def _():
        col_ref[...] = jnp.zeros_like(col_ref)
        top_ref[...] = jnp.full_like(top_ref, FLOOR)
        blocks = total // LANES

        def block_rows(block):
            return pl.ds(pl.multiple_of(block * LANES, LANES), LANES)

        def careful(tile, carry):
            at = columns(tile)
            right = xaug[:, at]

            def highest(block, peak):
                e = exponents(taug[block_rows(block), :], right)
                return jnp.maximum(peak, jnp.max(e, axis=0, keepdims=True))

            peak = lax.fori_loop(0, blocks, highest, jnp.full((1, width), FLOOR, jnp.float32))

            def summed(block, s):
                e = exponents(taug[block_rows(block), :], right)
                return s + jnp.sum(jnp.exp2(e - peak), axis=0, keepdims=True)

            s = lax.fori_loop(0, blocks, summed, jnp.zeros((1, width), jnp.float32))
            shift = logws[:, at] * LOG2E - peak - jnp.log2(s)

            def collected(block, carry):
                rows = block_rows(block)
                term = exponents(taug[rows, :], right) + shift
                for lane in range(0, width, LANES):
                    piece = term[:, lane : lane + LANES]
                    old = top_ref[rows, :]
                    top = jnp.maximum(old, piece)
                    col_ref[rows, :] = col_ref[rows, :] * jnp.exp2(old - top) + jnp.exp2(
                        piece - top
                    )
                    top_ref[rows, :] = top
                return carry

            return lax.fori_loop(0, blocks, collected, carry)

        lax.fori_loop(0, tiles, careful, 0)
        for begin in range(0, total, LANES):
            rows = slice(begin, begin + LANES)
            tops = top_ref[rows, :].T
            top = jnp.max(tops, axis=0, keepdims=True)
            added = jnp.sum(col_ref[rows, :].T * jnp.exp2(tops - top), axis=0, keepdims=True)
            out_ref[:, rows] = top + jnp.log2(added)


def first_kernel(n_x, n_t, feat, inverse, logws, *refs):
    xs, ts = refs[:n_x], refs[n_x : n_x + n_t]
    xaug, out_ref, g_ref, taug, q_ref, p0, p1, col_ref, top_ref = refs[n_x + n_t :]
    scale = inverse[0] * LOG2E
    count = xs[0].shape[2]
    place = 0
    for part in xs:
        for block in range(part.shape[0]):
            stage_source(part[block], scale, xaug, slice(place * count, (place + 1) * count))
            place += 1
    stage_targets(ts, None, scale, taug, g_ref, q_ref, feat)
    column_sums(xaug, logws, taug, (p0, p1), col_ref, top_ref, out_ref)


def next_kernel(n_t, feat, inverse, logws, xaug, own, other, g_old, *refs):
    ts = refs[:n_t]
    out_ref, g_ref, taug, q_ref, p0, p1, col_ref, top_ref = refs[n_t:]
    scale = inverse[0] * LOG2E
    stage_targets(ts, (own, other, g_old), scale, taug, g_ref, q_ref, feat)
    column_sums(xaug, logws, taug, (p0, p1), col_ref, top_ref, out_ref)


def map_kernel(n_t, feat, inverse, xaug, own, other, g_old, *refs):
    ts = refs[:n_t]
    mapped_ref, pot_ref, g_ref, taug, q_ref, p_ref, plan_ref, coords = refs[n_t:]
    scale = inverse[0] * LOG2E
    potential = stage_targets(ts, (own, other, g_old), scale, taug, g_ref, q_ref, feat)
    pot_ref[...] = potential[:, :LANES] * (1.0 / LOG2E)
    place = 0
    for part in ts:
        for block in range(part.shape[0]):
            coords[:, place * LANES : (place + 1) * LANES] = part[block, :feat, :]
            place += 1
    total = taug.shape[0]
    right = xaug[...]
    s = spread_rows(taug, right, p_ref, lambda rows: None)
    weight = 1.0 / s
    for begin in range(0, total, LANES):
        rows = slice(begin, begin + LANES)
        plan_ref[rows, :] = (p_ref[rows, :] * weight).astype(jnp.bfloat16)

    @pl.when(jnp.logical_not(jnp.min(s) >= SMALL_ROW))
    def _():
        reach = min(total, 2048)
        peak = jnp.full(s.shape, FLOOR, jnp.float32)
        for begin in range(0, total, reach):
            rows = slice(begin, begin + reach)
            p_ref[rows, :] = exponents(taug[rows, :], right)
            peak = jnp.maximum(peak, jnp.max(p_ref[rows, :], axis=0, keepdims=True))
        sums = jnp.zeros(s.shape, jnp.float32)
        for begin in range(0, total, reach):
            rows = slice(begin, begin + reach)
            sums += jnp.sum(jnp.exp2(p_ref[rows, :] - peak), axis=0, keepdims=True)
        shift = peak + jnp.log2(sums)
        for begin in range(0, total, reach):
            rows = slice(begin, begin + reach)
            plan_ref[rows, :] = jnp.exp2(p_ref[rows, :] - shift).astype(jnp.bfloat16)

    mapped_ref[...] = jnp.dot(coords[...], plan_ref[...], preferred_element_type=jnp.float32)


def swap(value, count, step):
    return lax.ppermute(value, AXIS, [(source, source ^ step) for source in range(count)])


def chip_stages(count):
    high, stages = count.bit_length() - 1, []
    while high > 1:
        width = min(2, high - 1)
        stages.append((high - width, width))
        high -= width
    return stages


def gather_chips(block, count):
    parts = [block[None]]
    for low, width in chip_stages(count):
        held = parts[0] if len(parts) == 1 else jnp.concatenate(parts, axis=0)
        digits = range((1 << width) - 1, 0, -1)
        parts = [held] + [swap(held, count, digit << low) for digit in digits]
    return parts


def on_device(source_points, target_points, source_logw, target_logw, inverse_eps, count):
    feat, own_sources = source_points.shape
    own_targets = target_points.shape[1]
    extra_rows = own_sources // LANES
    pad = -(1 + extra_rows) % 16
    packed = jnp.concatenate(
        [
            target_points,
            target_logw[None, :],
            source_logw.reshape(extra_rows, LANES),
            jnp.zeros((pad, own_targets), target_points.dtype),
        ],
        axis=0,
    )
    mine = gather_chips(packed, count)
    theirs = [swap(part, count, 1) for part in mine]
    ts = mine + theirs
    xs = gather_chips(source_points, count)
    chips = count // 2
    logws = jnp.concatenate(
        [part[:, feat + 1 : feat + 1 + extra_rows] for part in mine], axis=0
    ).reshape(1, chips * own_sources).astype(jnp.float32)

    total, rows = count * own_targets, chips * own_sources
    small = total <= 4096
    width = 2 * LANES if small else LANES
    f32, bf16 = jnp.float32, jnp.bfloat16
    vmem = pl.BlockSpec(memory_space=pltpu.VMEM)
    smem = pl.BlockSpec(memory_space=pltpu.SMEM)
    params = pltpu.CompilerParams(vmem_limit_bytes=(24 if small else 60) << 20)
    line = jax.ShapeDtypeStruct((1, total), f32)
    sums_scratch = [
        pltpu.VMEM((total, DEPTH), bf16),
        pltpu.VMEM((1, total), f32),
        pltpu.VMEM((total, width), f32),
        pltpu.VMEM((total, width), f32),
        pltpu.VMEM((total, LANES), f32),
        pltpu.VMEM((total, LANES), f32),
    ]

    xaug, sums, g = pl.pallas_call(
        functools.partial(first_kernel, len(xs), len(ts), feat),
        out_shape=[jax.ShapeDtypeStruct((DEPTH, rows), bf16), line, line],
        in_specs=[smem] + [vmem] * (len(xs) + len(ts) + 1),
        out_specs=[vmem] * 3,
        scratch_shapes=sums_scratch,
        compiler_params=params,
    )(inverse_eps, logws, *xs, *ts)
    for _ in range(ITERS - 1):
        sums, g = pl.pallas_call(
            functools.partial(next_kernel, len(ts), feat),
            out_shape=[line, line],
            in_specs=[smem] + [vmem] * (5 + len(ts)),
            out_specs=[vmem] * 2,
            scratch_shapes=sums_scratch,
            compiler_params=params,
        )(inverse_eps, logws, xaug, sums, swap(sums, count, 1), g, *ts)
    mapped, potential = pl.pallas_call(
        functools.partial(map_kernel, len(ts), feat),
        out_shape=[
            jax.ShapeDtypeStruct((feat, own_sources), f32),
            jax.ShapeDtypeStruct((1, own_targets), f32),
        ],
        in_specs=[smem] + [vmem] * (4 + len(ts)),
        out_specs=[vmem] * 2,
        scratch_shapes=[
            pltpu.VMEM((1, total), f32),
            pltpu.VMEM((total, DEPTH), bf16),
            pltpu.VMEM((1, total), f32),
            pltpu.VMEM((total, own_sources), f32),
            pltpu.VMEM((total, own_sources), bf16),
            pltpu.VMEM((feat, total), bf16),
        ],
        compiler_params=params,
    )(inverse_eps, xaug[:, :own_sources], sums, swap(sums, count, 1), g, *ts)
    return (mapped, potential.reshape(own_targets))


def solution(mesh):
    count = mesh.shape[AXIS]
    placed = (
        P(None, ("grp", "wide")),
        P(None, ("grp", "wide")),
        P(("grp", "wide")),
        P(("grp", "wide")),
        P(),
    )

    def body(*blocks):
        return on_device(*blocks, count)

    return jax.shard_map(
        body,
        mesh=mesh,
        in_specs=placed,
        out_specs=(P(None, ("grp", "wide")), P(("grp", "wide"))),
        check_vma=False,
    )
```

time: 90.8 us -> 263 us (2.90)
  Pallas kernels: 65 us -> 238 us
    pallas_call x1, Pallas kernels: 29.7 us -> 116 us  [on_device(): pl.pallas_call(functools.partial(next_kernel, len(ts), feat), out_shape=[...]
    pallas_call x1, Pallas kernels: 30.4 us -> 116 us  [on_device(): pl.pallas_call(functools.partial(first_kernel, len(xs), len(ts), feat), o...]
  transfers between devices with their start and end apart: 12 -> 12, of which waited for: 6 -> 6; matrix products, arithmetic and copies ran while one was open for 2% -> 1% of each run, Pallas kernels for 0% -> 0%
where the time goes in v5:
time: 263 us
  Pallas kernels  238 us (90%)
  starting transfers between devices  13.8 us (5%)
  waiting for transfers between devices  8.62 us (3%)
    pallas_call x1, Pallas kernels, on_device(): pl.pallas_call(functools.partial(first_kernel, len(xs), len(ts), feat), o...  116 us
    pallas_call x1, Pallas kernels, on_device(): pl.pallas_call(functools.partial(next_kernel, len(ts), feat), out_shape=[...  116 us
    ppermute x12, starting transfers between devices, swap(): lax.ppermute(value, AXIS, [(source, source ^ step) for source in range(co...  13.8 us
    ppermute x12, waiting for transfers between devices, swap(): lax.ppermute(value, AXIS, [(source, source ^ step) for source in range(co...  8.62 us
  transfers between devices with their start and end apart: 12, of which 6 were waited for; matrix products, arithmetic and copies ran while one was open for 1% of the time, Pallas kernels for 0%

profile of v5, /device:TPU:0, one launch (start us, length us, event | category | flops | bytes accessed | tf_op | source)
XLA Modules:
  0.0 263.2 jit_solution(12926085787757520181)
XLA Ops:
  0.6 3.1 %collective-permute-start.6 = (bf16[1,64,384]{2,1,0:T(8,128)(2,1)}, bf16[1,64,384]{2,1,0:T(8,128)(2,1)S(1)}, u32[]{:S(2)}, u32[]{:S(2)}) collective-permute-start(bf16[1,64,384]{2,1,0:T(8,128)(2,1)} %bitcast.6), channel_id=1, source_target_pairs={{0,4},{1,5},{2,6},{3,7},{4,0},{5,1},{6,2},{7,3},{8,12},{9,13},{10,... | collective-permute-start | bytes 147464 | tf_op jit(solution)/shard_map/ppermute | solution.py:257
  3.7 2.6 collective-permute-start.5
  6.3 0.0 collective-permute-start.4
  6.3 0.1 pad.13.clone
  6.4 0.8 maximum_bitcast_fusion
  7.2 1.0 collective-permute-start.2
  8.2 3.5 %collective-permute-start.1 = (bf16[1,80,128]{2,1,0:T(8,128)(2,1)S(1)}, bf16[1,80,128]{2,1,0:T(8,128)(2,1)S(1)}, u32[]{:S(2)}, u32[]{:S(2)}) collective-permute-start(bf16[1,80,128]{2,1,0:T(8,128)(2,1)S(1)} %maximum_bitcast_fusion), channel_id=1, source_target_pairs={{0,8},{1,9},{2,10},{3,11},{4,12},{5,13},{6,14},{7,15},{8,0},{9,1},... | collective-permute-start | bytes 61448 | tf_op jit(solution)/shard_map/ppermute | solution.py:257
  11.7 0.0 collective-permute-done.6
  11.7 0.0 collective-permute-start
  11.7 0.0 collective-permute-done.5
  11.7 0.7 collective-permute-done.4
  12.4 0.8 pad_maximum_fusion.refs_0_
  13.2 1.6 collective-permute-start.7
  14.8 0.0 collective-permute-done.2
  14.8 0.0 collective-permute-done.1
  14.8 2.4 collective-permute-done
  17.3 1.6 collective-permute-start.3
  19.5 0.1 collective-permute-start.8
  19.6 2.2 collective-permute-done.3.refs_3_.refs_1_
  21.8 0.0 collective-permute-start.9
  21.8 0.0 collective-permute-done.8.refs_4_.refs_2_
  21.8 1.2 collective-permute-done.9.refs_5_.refs_3_
  23.1 0.0 collective-permute-done.7.refs_1_
  23.1 116.4 %shard_map.68 = (bf16[256,3072]{1,0:T(8,128)(2,1)S(1)}, f32[1,2048]{1,0:T(1,128)S(1)}, f32[1,2048]{1,0:T(1,128)S(1)}) custom-call(f32[1]{0:T(128)S(6)} %copy.7.inverse, f32[1,3072]{1,0:T(1,128)S(1)} %reshape.27.logws, bf16[4,64,384]{2,1,0:T(8,128)(2,1)S(1)} %pad_maximum_fusion.refs_0_, bf16[4,64,384]{2,1,0:T(8,128)(2,1)S(1)} %collective-permute-done.7.refs_1_, ...), custom_call_target="tpu_custom_call" | custom-call | tf_op jit(solution)/shard_map/pallas_call | solution.py:318
  139.5 0.2 collective-permute-start.10
  139.7 1.0 collective-permute-done.10.other
  140.7 116.2 %shard_map.69 = (f32[1,2048]{1,0:T(1,128)S(1)}, f32[1,2048]{1,0:T(1,128)S(1)}) custom-call(f32[1]{0:T(128)S(6)} %copy.7.inverse, f32[1,3072]{1,0:T(1,128)S(1)} %reshape.27.logws, bf16[256,3072]{1,0:T(8,128)(2,1)S(1)} %get-tuple-element.9.xaug, f32[1,2048]{1,0:T(1,128)S(1)} %get-tuple-element.10.own, f32[1,2048]{1,0:T(1,128)S(1)} %collective-permute-done.10.other, ...), custom_call_target="tpu_custom_call" | custom-call | tf_op jit(solution)/shard_map/pallas_call | solution.py:327
  256.9 0.2 collective-permute-start.11
  257.2 1.0 collective-permute-done.11.other
  258.2 5.0 %shard_map.70 = (f32[64,384]{1,0:T(8,128)}, f32[1,128]{1,0:T(1,128)}) custom-call(f32[1]{0:T(128)S(6)} %copy.7.inverse, bf16[256,384]{1,0:T(8,128)(2,1)S(1)} %slice.11.xaug, f32[1,2048]{1,0:T(1,128)S(1)} %get-tuple-element.12.own, f32[1,2048]{1,0:T(1,128)S(1)} %collective-permute-done.11.other, f32[1,2048]{1,0:T(1,128)S(1)} %get-tuple-element.13.g_old, ...), custom_call_target="tpu_custom_call" | custom-call | tf_op jit(solution)/shard_map/pallas_call | solution.py:335
  (7 shorter events, 0.1 us)
Async XLA Ops:
  0.6 11.0 %collective-permute-start.6 = (bf16[1,64,384]{2,1,0:T(8,128)(2,1)}, bf16[1,64,384]{2,1,0:T(8,128)(2,1)S(1)}, u32[]{:S(2)}, u32[]{:S(2)}) collective-permute-start(bf16[1,64,384]{2,1,0:T(8,128)(2,1)} %bitcast.6), channel_id=1, source_target_pairs={{0,4},{1,5},{2,6},{3,7},{4,0},{5,1},{6,2},{7,3},{8,12},{9,13},{10,... | collective-permute-start | bytes 147464 | tf_op jit(solution)/shard_map/ppermute | solution.py:257
  3.7 8.0 %collective-permute-start.5 = (bf16[1,64,384]{2,1,0:T(8,128)(2,1)}, bf16[1,64,384]{2,1,0:T(8,128)(2,1)S(1)}, u32[]{:S(2)}, u32[]{:S(2)}) collective-permute-start(bf16[1,64,384]{2,1,0:T(8,128)(2,1)} %bitcast.7), channel_id=1, source_target_pairs={{0,8},{1,9},{2,10},{3,11},{4,12},{5,13},{6,14},{7,15},{8,0},{9,1},... | collective-permute-start | bytes 147464 | tf_op jit(solution)/shard_map/ppermute | solution.py:257
  6.3 6.1 %collective-permute-start.4 = (bf16[1,64,384]{2,1,0:T(8,128)(2,1)}, bf16[1,64,384]{2,1,0:T(8,128)(2,1)S(1)}, u32[]{:S(2)}, u32[]{:S(2)}) collective-permute-start(bf16[1,64,384]{2,1,0:T(8,128)(2,1)} %bitcast.8), channel_id=1, source_target_pairs={{0,12},{1,13},{2,14},{3,15},{4,8},{5,9},{6,10},{7,11},{8,4},{9,5},... | collective-permute-start | bytes 147464 | tf_op jit(solution)/shard_map/ppermute | solution.py:257
  7.2 7.6 %collective-permute-start.2 = (bf16[1,80,128]{2,1,0:T(8,128)(2,1)S(1)}, bf16[1,80,128]{2,1,0:T(8,128)(2,1)S(1)}, u32[]{:S(2)}, u32[]{:S(2)}) collective-permute-start(bf16[1,80,128]{2,1,0:T(8,128)(2,1)S(1)} %maximum_bitcast_fusion), channel_id=1, source_target_pairs={{0,4},{1,5},{2,6},{3,7},{4,0},{5,1},{6,2},{7,3},{8,12},{9,13},{10,... | collective-permute-start | bytes 61448 | tf_op jit(solution)/shard_map/ppermute | solution.py:257
  8.2 6.6 %collective-permute-start.1 = (bf16[1,80,128]{2,1,0:T(8,128)(2,1)S(1)}, bf16[1,80,128]{2,1,0:T(8,128)(2,1)S(1)}, u32[]{:S(2)}, u32[]{:S(2)}) collective-permute-start(bf16[1,80,128]{2,1,0:T(8,128)(2,1)S(1)} %maximum_bitcast_fusion), channel_id=1, source_target_pairs={{0,8},{1,9},{2,10},{3,11},{4,12},{5,13},{6,14},{7,15},{8,0},{9,1},... | collective-permute-start | bytes 61448 | tf_op jit(solution)/shard_map/ppermute | solution.py:257
  11.7 5.6 %collective-permute-start = (bf16[1,80,128]{2,1,0:T(8,128)(2,1)S(1)}, bf16[1,80,128]{2,1,0:T(8,128)(2,1)S(1)}, u32[]{:S(2)}, u32[]{:S(2)}) collective-permute-start(bf16[1,80,128]{2,1,0:T(8,128)(2,1)S(1)} %maximum_bitcast_fusion), channel_id=1, source_target_pairs={{0,12},{1,13},{2,14},{3,15},{4,8},{5,9},{6,10},{7,11},{8,4},{9,5},... | collective-permute-start | bytes 61448 | tf_op jit(solution)/shard_map/ppermute | solution.py:257
  13.2 9.8 %collective-permute-start.7 = (bf16[4,64,384]{2,1,0:T(8,128)(2,1)S(1)}, bf16[4,64,384]{2,1,0:T(8,128)(2,1)S(1)}, u32[]{:S(2)}, u32[]{:S(2)}) collective-permute-start(bf16[4,64,384]{2,1,0:T(8,128)(2,1)S(1)} %pad_maximum_fusion.refs_0_), channel_id=1, source_target_pairs={{0,2},{1,3},{2,0},{3,1},{4,6},{5,7},{6,4},{7,5},{8,10},{9,11},{10,... | collective-permute-start | bytes 589832 | tf_op jit(solution)/shard_map/ppermute | solution.py:257
  17.3 4.5 %collective-permute-start.3 = (bf16[4,80,128]{2,1,0:T(8,128)(2,1)S(1)}, bf16[4,80,128]{2,1,0:T(8,128)(2,1)S(1)}, u32[]{:S(2)}, u32[]{:S(2)}) collective-permute-start(bf16[4,80,128]{2,1,0:T(8,128)(2,1)S(1)} %pad_maximum_fusion.1.refs_2_.refs_0_), channel_id=1, source_target_pairs={{0,2},{1,3},{2,0},{3,1},{4,6},{5,7},{6,4},{7,5},{8,10},{9,11},{10,... | collective-permute-start | bytes 245768 | tf_op jit(solution)/shard_map/ppermute | solution.py:257
  19.5 2.3 collective-permute-start.8
  21.8 1.3 collective-permute-start.9
  139.5 1.2 collective-permute-start.10
  256.9 1.2 collective-permute-start.11

commit v6 on v5

v6 whole, which is shorter than its diff:
```python
import functools
import math

import jax
import jax.numpy as jnp
from jax import lax
from jax.experimental import pallas as pl
from jax.experimental.pallas import tpu as pltpu
from jax.sharding import PartitionSpec as P

ITERS = 2
AXIS = "wide"
LOG2E = math.log2(math.e)
LANES = 128
DEPTH = 256
SMALL_ROW = 2.0**-64
SMALL_COL = 2.0**-32
LARGE_COL = 2.0**100
FLOOR = -1e30


def three_terms(value):
    high = value.astype(jnp.bfloat16)
    rest = value - high.astype(jnp.float32)
    middle = rest.astype(jnp.bfloat16)
    low = (rest - middle.astype(jnp.float32)).astype(jnp.bfloat16)
    return high, middle, low


def pick_rows(shape, rows):
    index = lax.broadcasted_iota(jnp.int32, shape, 0)
    out = jnp.zeros(shape, jnp.float32)
    for place, row in enumerate(rows):
        out = jnp.where(index == place, row, out)
    return out


def stage_source(points, scale, xaug, at):
    feat, count = points.shape
    wide = points.astype(jnp.float32)
    shift = scale * jnp.sum(wide * wide, axis=0, keepdims=True)
    shift = shift.astype(jnp.bfloat16).astype(jnp.float32)
    xaug[0:feat, at] = pick_rows((feat, count), [1.0, 1.0, 1.0, -shift]).astype(jnp.bfloat16)
    for place, term in enumerate(three_terms(2.0 * scale * wide)):
        xaug[(place + 1) * feat : (place + 2) * feat, at] = term


def stage_sources(parts, scale, xaug):
    place = 0
    for part in parts:
        count = part.shape[2]
        for block in range(part.shape[0]):
            stage_source(part[block], scale, xaug, slice(place * count, (place + 1) * count))
            place += 1


def target_lines(part, block, scale, feat):
    wide = part[block, :feat, :].astype(jnp.float32)
    logw = part[block, feat : feat + 16, :].astype(jnp.float32)[0:1]
    return scale * jnp.sum(wide * wide, axis=0, keepdims=True), logw * LOG2E


def stage_targets(parts, scale, taug, begin, feat):
    for part in parts:
        for block in range(part.shape[0]):
            q, logw = target_lines(part, block, scale, feat)
            terms = [term.astype(jnp.float32) for term in three_terms(logw - q)]
            extras = pick_rows((feat, LANES), terms + [1.0])
            wide = part[block, :feat, :].astype(jnp.float32)
            turned = jnp.concatenate([extras, wide], axis=0).T
            lane = lax.broadcasted_iota(jnp.int32, turned.shape, 1)
            twice = jnp.where(lane < feat, pltpu.roll(turned, feat, 1), turned)
            taug[begin : begin + LANES, 0:LANES] = turned.astype(jnp.bfloat16)
            taug[begin : begin + LANES, LANES:DEPTH] = twice.astype(jnp.bfloat16)
            begin += LANES


def renew_targets(own, other, g, q, logw, taug):
    total = own.shape[1]
    other = jnp.concatenate([other[:, total // 2 :], other[:, : total // 2]], axis=1)
    peak = jnp.maximum(own, other)
    potential = g - (peak + jnp.log2(jnp.exp2(own - peak) + jnp.exp2(other - peak)))
    g = potential + logw
    terms = [term.astype(jnp.float32) for term in three_terms(g - jnp.max(g) - q)]
    for begin in range(0, total, LANES):
        rows = slice(begin, begin + LANES)
        extras = pick_rows((8, LANES), [term[:, rows] for term in terms] + [1.0])
        taug[rows, 0:8] = extras.T.astype(jnp.bfloat16)
    return potential, g


def exponents(left, right):
    return jnp.dot(left, right, preferred_element_type=jnp.float32)


def spread_rows(taug, right, p_ref, beside):
    total, width = taug.shape[0], right.shape[1]
    reach = min(total, 2048)
    sums = jnp.zeros((8, width), jnp.float32)
    for begin in range(0, total, reach):
        e = exponents(taug[begin : begin + reach, :], right)
        for inner in range(0, reach, LANES):
            rows = slice(begin + inner, begin + inner + LANES)
            beside(rows)
            p = jnp.exp2(e[inner : inner + LANES])
            p_ref[rows, :] = p
            sums = sums + jnp.sum(p.reshape(LANES // 8, 8, width), axis=0)
    return jnp.sum(sums, axis=0, keepdims=True)


def add_columns(p_ref, weight, col_ref, rows):
    width = weight.shape[1]
    added = p_ref[rows, 0:LANES] * weight[:, 0:LANES]
    for lane in range(LANES, width, LANES):
        added = added + p_ref[rows, lane : lane + LANES] * weight[:, lane : lane + LANES]
    col_ref[rows, :] += added


def tile_columns(tile, width):
    if isinstance(tile, int):
        return pl.ds(tile * width, width)
    return pl.ds(pl.multiple_of(tile * width, width), width)


def add_sources(xaug, logws, taug, p_refs, col_ref):
    total = taug.shape[0]
    width = p_refs[0].shape[1]
    tiles = xaug.shape[1] // width
    if p_refs[1].shape != p_refs[0].shape:
        p_refs = (p_refs[0], p_refs[0])

    def step(tile, slot, held):
        def beside(rows):
            if held is not None:
                add_columns(p_refs[1 - slot], held, col_ref, rows)

        at = tile_columns(tile, width)
        s = spread_rows(taug, xaug[:, at], p_refs[slot], beside)
        return s, jnp.exp2(logws[:, at] * LOG2E) / s

    def two_steps(pair, carry):
        least, weight = carry
        s1, weight1 = step(2 * pair + 1, 1, weight)
        s0, weight0 = step(2 * pair + 2, 0, weight1)
        return jnp.minimum(least, jnp.minimum(s0, s1)), weight0

    s, weight = step(0, 0, None)
    least, weight = lax.fori_loop(0, tiles // 2 - 1, two_steps, (s, weight))
    s, weight = step(tiles - 1, 1, weight)
    for begin in range(0, total, LANES):
        add_columns(p_refs[1], weight, col_ref, slice(begin, begin + LANES))
    return jnp.minimum(least, s)


def lane_totals(col_ref, out_ref):
    total = col_ref.shape[0]
    reach = min(total, 2048)
    ones = jnp.ones((16, 2 * LANES), jnp.bfloat16)
    for begin in range(0, total, reach):
        high, middle, _ = three_terms(col_ref[begin : begin + reach, :])
        both = jnp.concatenate([high, middle], axis=1)
        added = lax.dot_general(
            ones, both, (((1,), (1,)), ((), ())), preferred_element_type=jnp.float32
        )
        out_ref[:, begin : begin + reach] = added[0:1]


def finish_sums(pieces, taug, least, p_ref, col_ref, out_ref):
    total = taug.shape[0]
    lane_totals(col_ref, out_ref)
    cols = out_ref[...]
    out_ref[...] = jnp.log2(cols)
    fine = jnp.logical_and(
        jnp.min(least) >= SMALL_ROW,
        jnp.logical_and(jnp.min(cols) >= SMALL_COL, jnp.max(cols) <= LARGE_COL),
    )

    top_ref = p_ref.at[:, 0:LANES]

    @pl.when(jnp.logical_not(fine))
    def _():
        col_ref[...] = jnp.zeros_like(col_ref)
        top_ref[...] = jnp.full_like(top_ref, FLOOR)
        blocks = total // LANES

        def block_rows(block):
            return pl.ds(pl.multiple_of(block * LANES, LANES), LANES)

        def careful(xaug, logws, tile, carry):
            at = tile_columns(tile, LANES)
            right = xaug[:, at]

            def highest(block, peak):
                e = exponents(taug[block_rows(block), :], right)
                return jnp.maximum(peak, jnp.max(e, axis=0, keepdims=True))

            peak = lax.fori_loop(0, blocks, highest, jnp.full((1, LANES), FLOOR, jnp.float32))

            def summed(block, s):
                e = exponents(taug[block_rows(block), :], right)
                return s + jnp.sum(jnp.exp2(e - peak), axis=0, keepdims=True)

            s = lax.fori_loop(0, blocks, summed, jnp.zeros((1, LANES), jnp.float32))
            shift = logws[:, at] * LOG2E - peak - jnp.log2(s)

            def collected(block, carry):
                rows = block_rows(block)
                term = exponents(taug[rows, :], right) + shift
                old = top_ref[rows, :]
                top = jnp.maximum(old, term)
                col_ref[rows, :] = col_ref[rows, :] * jnp.exp2(old - top) + jnp.exp2(term - top)
                top_ref[rows, :] = top
                return carry

            return lax.fori_loop(0, blocks, collected, carry)

        for xaug, logws in pieces:
            tiles = xaug.shape[1] // LANES
            lax.fori_loop(0, tiles, functools.partial(careful, xaug, logws), 0)

        def turned(block, carry):
            rows = block_rows(block)
            tops = top_ref[rows, :].T
            top = jnp.max(tops, axis=0, keepdims=True)
            added = jnp.sum(col_ref[rows, :].T * jnp.exp2(tops - top), axis=0, keepdims=True)
            out_ref[:, rows] = top + jnp.log2(added)
            return carry

        lax.fori_loop(0, blocks, turned, 0)


def part_kernel(n_t, feat, inverse, points, *refs):
    ts, (taug, copy_ref) = refs[:n_t], refs[n_t:]
    copy_ref[0] = points[...]
    stage_targets(ts, inverse[0] * LOG2E, taug, 0, feat)


def more_kernel(n_t, feat, inverse, *refs):
    ts, (taug,) = refs[:n_t], refs[n_t:]
    stage_targets(ts, inverse[0] * LOG2E, taug, 0, feat)


def near_kernel(n_x, n_staged, n_t, n_late, feat, inverse, logws, *refs):
    xs, refs = refs[:n_x], refs[n_x:]
    staged, refs = refs[:n_staged], refs[n_staged:]
    ts, refs = refs[:n_t], refs[n_t:]
    late = ts[n_t - n_late :]
    xaug, taug, col_ref, least_ref, g_ref, q_ref, p0, p1 = refs
    scale = inverse[0] * LOG2E
    stage_sources(xs, scale, xaug)
    place = 0
    for part in ts:
        for block in range(part.shape[0]):
            at = slice(place * LANES, (place + 1) * LANES)
            q_ref[:, at], g_ref[:, at] = target_lines(part, block, scale, feat)
            place += 1
    begin = 0
    for part in staged:
        taug[begin : begin + part.shape[0], :] = part[...]
        begin += part.shape[0]
    stage_targets(late, scale, taug, begin, feat)
    col_ref[...] = jnp.zeros_like(col_ref)
    least_ref[...] = add_sources(xaug, logws, taug, (p0, p1), col_ref)


def far_kernel(n_x, inverse, near_logws, logws, near_xaug, taug, near_col, near_least, *refs):
    xs, refs = refs[:n_x], refs[n_x:]
    xaug, out_ref, p0, p1, col_ref = refs
    stage_sources(xs, inverse[0] * LOG2E, xaug)
    col_ref[...] = near_col[...]
    least = add_sources(xaug, logws, taug, (p0, p1), col_ref)
    least = jnp.minimum(least, near_least[...])
    pieces = [(near_xaug, near_logws), (xaug, logws)]
    finish_sums(pieces, taug, least, p0, col_ref, out_ref)


def next_kernel(near_logws, far_logws, near_xaug, far_xaug, old, own, other, g, q, logw, *refs):
    out_ref, g_ref, taug, p0, p1, col_ref = refs
    taug[...] = old[...]
    g_ref[...] = renew_targets(own[...], other[...], g[...], q[...], logw[...], taug)[1]
    col_ref[...] = jnp.zeros_like(col_ref)
    pieces = [(near_xaug, near_logws), (far_xaug, far_logws)]
    least = [add_sources(xaug, logws, taug, (p0, p1), col_ref) for xaug, logws in pieces]
    least = jnp.minimum(least[0], least[1])
    finish_sums(pieces, taug, least, p0, col_ref, out_ref)


def map_kernel(n_t, feat, xaug, old, own, other, g, q, logw, *refs):
    ts = refs[:n_t]
    mapped_ref, pot_ref, taug, p_ref, plan_ref, coords = refs[n_t:]
    taug[...] = old[...]
    potential = renew_targets(own[...], other[...], g[...], q[...], logw[...], taug)[0]
    pot_ref[...] = potential[:, :LANES] * (1.0 / LOG2E)
    place = 0
    for part in ts:
        for block in range(part.shape[0]):
            coords[:, place * LANES : (place + 1) * LANES] = part[block, :feat, :]
            place += 1
    total = taug.shape[0]
    right = xaug[:, : p_ref.shape[1]]
    s = spread_rows(taug, right, p_ref, lambda rows: None)
    weight = 1.0 / s
    for begin in range(0, total, LANES):
        rows = slice(begin, begin + LANES)
        plan_ref[rows, :] = (p_ref[rows, :] * weight).astype(jnp.bfloat16)

    @pl.when(jnp.logical_not(jnp.min(s) >= SMALL_ROW))
    def _():
        reach = min(total, 2048)
        peak = jnp.full(s.shape, FLOOR, jnp.float32)
        for begin in range(0, total, reach):
            rows = slice(begin, begin + reach)
            p_ref[rows, :] = exponents(taug[rows, :], right)
            peak = jnp.maximum(peak, jnp.max(p_ref[rows, :], axis=0, keepdims=True))
        sums = jnp.zeros(s.shape, jnp.float32)
        for begin in range(0, total, reach):
            rows = slice(begin, begin + reach)
            sums += jnp.sum(jnp.exp2(p_ref[rows, :] - peak), axis=0, keepdims=True)
        shift = peak + jnp.log2(sums)
        for begin in range(0, total, reach):
            rows = slice(begin, begin + reach)
            plan_ref[rows, :] = jnp.exp2(p_ref[rows, :] - shift).astype(jnp.bfloat16)

    mapped_ref[...] = jnp.dot(coords[...], plan_ref[...], preferred_element_type=jnp.float32)


def swap(value, count, step):
    return lax.ppermute(value, AXIS, [(source, source ^ step) for source in range(count)])


def chip_stages(count):
    high, stages = count.bit_length() - 1, []
    while high > 1:
        width = min(2, high - 1)
        stages.append((high - width, width))
        high -= width
    return stages


def gather_chips(block, count):
    parts = [block[None]]
    for low, width in chip_stages(count):
        held = parts[0] if len(parts) == 1 else jnp.concatenate(parts, axis=0)
        digits = range((1 << width) - 1, 0, -1)
        parts = [held] + [swap(held, count, digit << low) for digit in digits]
    return parts


def on_device(source_points, target_points, source_logw, target_logw, inverse_eps, count):
    feat, own_sources = source_points.shape
    own_targets = target_points.shape[1]
    extra_rows = own_sources // LANES
    pad = -(1 + extra_rows) % 16
    packed = jnp.concatenate(
        [
            target_points,
            target_logw[None, :],
            source_logw.reshape(extra_rows, LANES),
            jnp.zeros((pad, own_targets), target_points.dtype),
        ],
        axis=0,
    )
    f32, bf16 = jnp.float32, jnp.bfloat16
    total, chips = count * own_targets, count // 2
    small = total <= 4096
    width = 2 * LANES if small else LANES
    vmem = pl.BlockSpec(memory_space=pltpu.VMEM)
    smem = pl.BlockSpec(memory_space=pltpu.SMEM)
    params = pltpu.CompilerParams(vmem_limit_bytes=(24 if small else 63) << 20)
    line = jax.ShapeDtypeStruct((1, total), f32)

    def call(kernel, operands, outs, scratch=(), scalars=1):
        return pl.pallas_call(
            kernel,
            out_shape=outs,
            in_specs=[smem] * scalars + [vmem] * (len(operands) - scalars),
            out_specs=[vmem] * len(outs),
            scratch_shapes=list(scratch),
            compiler_params=params,
        )(*operands)

    def staged_shape(parts):
        rows = sum(part.shape[0] for part in parts) * own_targets
        return jax.ShapeDtypeStruct((rows, DEPTH), bf16)

    def logw_line(parts):
        rows = [part[:, feat + 1 : feat + 1 + extra_rows] for part in parts]
        return jnp.concatenate(rows, axis=0).reshape(1, -1).astype(f32)

    mine = gather_chips(packed, count)
    theirs = [swap(part, count, 1) for part in mine]
    first, second, late = [mine[0]], mine[1:] + theirs[:1], theirs[1:]
    ts = first + second + late
    taug_first, points = call(
        functools.partial(part_kernel, len(first), feat),
        [inverse_eps, source_points] + first,
        [staged_shape(first), jax.ShapeDtypeStruct((1, feat, own_sources), bf16)],
    )
    (taug_second,) = call(
        functools.partial(more_kernel, len(second), feat),
        [inverse_eps] + second,
        [staged_shape(second)],
    )
    xs = gather_chips(points[0], count)
    near, far = xs[:1], xs[1:]
    near_logws, far_logws = logw_line(mine[:1]), logw_line(mine[1:])
    near_rows, far_rows = near_logws.shape[1], far_logws.shape[1]

    p_scratch = pltpu.VMEM((total, width), f32)
    p_pair = [p_scratch, p_scratch if small else pltpu.VMEM((8, LANES), f32)]
    col_scratch = pltpu.VMEM((total, LANES), f32)
    near_xaug, taug, near_col, near_least, logw, q = call(
        functools.partial(near_kernel, len(near), 2, len(ts), len(late), feat),
        [inverse_eps, near_logws] + near + [taug_first, taug_second] + ts,
        [
            jax.ShapeDtypeStruct((DEPTH, near_rows), bf16),
            jax.ShapeDtypeStruct((total, DEPTH), bf16),
            jax.ShapeDtypeStruct((total, LANES), f32),
            jax.ShapeDtypeStruct((1, width), f32),
            line,
            line,
        ],
        p_pair,
    )
    far_xaug, sums = call(
        functools.partial(far_kernel, len(far)),
        [inverse_eps, near_logws, far_logws, near_xaug, taug, near_col, near_least] + far,
        [jax.ShapeDtypeStruct((DEPTH, far_rows), bf16), line],
        p_pair + [col_scratch],
    )
    g = logw
    for _ in range(ITERS - 1):
        lines = [sums, swap(sums, count, 1), g, q, logw]
        sums, g = call(
            next_kernel,
            [near_logws, far_logws, near_xaug, far_xaug, taug] + lines,
            [line, line],
            [pltpu.VMEM((total, DEPTH), bf16)] + p_pair + [col_scratch],
            scalars=0,
        )
    lines = [sums, swap(sums, count, 1), g, q, logw]
    mapped, potential = call(
        functools.partial(map_kernel, len(ts), feat),
        [near_xaug, taug] + lines + ts,
        [
            jax.ShapeDtypeStruct((feat, own_sources), f32),
            jax.ShapeDtypeStruct((1, own_targets), f32),
        ],
        [
            pltpu.VMEM((total, DEPTH), bf16),
            pltpu.VMEM((total, own_sources), f32),
            pltpu.VMEM((total, own_sources), bf16),
            pltpu.VMEM((feat, total), bf16),
        ],
        scalars=0,
    )
    return (mapped, potential.reshape(own_targets))


def solution(mesh):
    count = mesh.shape[AXIS]
    placed = (
        P(None, ("grp", "wide")),
        P(None, ("grp", "wide")),
        P(("grp", "wide")),
        P(("grp", "wide")),
        P(),
    )

    def body(*blocks):
        return on_device(*blocks, count)

    return jax.shard_map(
        body,
        mesh=mesh,
        in_specs=placed,
        out_specs=(P(None, ("grp", "wide")), P(("grp", "wide"))),
        check_vma=False,
    )
```

time: 263 us -> 436 us (1.66)
  Pallas kernels: 238 us -> 412 us
    pallas_call x3 -> x6, Pallas kernels: 238 us -> 412 us  [call(): pl.pallas_call(kernel, out_shape=outs, in_specs=[smem] * scalars + [vmem]...]
  transfers between devices with their start and end apart: 12 -> 12, of which waited for: 6 -> 8; matrix products, arithmetic and copies ran while one was open for 1% -> 0% of each run, Pallas kernels for 0% -> 1%
where the time goes in v6:
time: 436 us
  Pallas kernels  412 us (94%)
  starting transfers between devices  13.7 us (3%)
  waiting for transfers between devices  7.57 us (2%)
    pallas_call x6, Pallas kernels, call(): pl.pallas_call(kernel, out_shape=outs, in_specs=[smem] * scalars + [vmem]...  412 us
    ppermute x12, starting transfers between devices, swap(): lax.ppermute(value, AXIS, [(source, source ^ step) for source in range(co...  13.7 us
  transfers between devices with their start and end apart: 12, of which 8 were waited for; matrix products, arithmetic and copies ran while one was open for 0% of the time, Pallas kernels for 1%

profile of v6, /device:TPU:0, one launch (start us, length us, event | category | flops | bytes accessed | tf_op | source)
XLA Modules:
  0.0 436.1 jit_solution(11807152071519883608)
XLA Ops:
  0.6 0.1 pad.7.clone
  0.7 0.0 copy-start.1
  0.7 0.0 copy-start.2
  0.7 0.7 copy-done.1
  1.4 0.0 copy-done.2
  1.4 0.8 maximum_bitcast_fusion
  2.2 5.1 %collective-permute-start = (bf16[1,80,128]{2,1,0:T(8,128)(2,1)S(1)}, bf16[1,80,128]{2,1,0:T(8,128)(2,1)S(1)}, u32[]{:S(2)}, u32[]{:S(2)}) collective-permute-start(bf16[1,80,128]{2,1,0:T(8,128)(2,1)S(1)} %maximum_bitcast_fusion), channel_id=1, source_target_pairs={{0,12},{1,13},{2,14},{3,15},{4,8},{5,9},{6,10},{7,11},{8,4},{9,5},... | collective-permute-start | bytes 61448 | tf_op jit(solution)/shard_map/ppermute | solution.py:328
  7.3 0.0 collective-permute-start.1
  7.3 0.6 collective-permute-start.2
  8.6 0.0 copy-start
  8.6 0.5 collective-permute-done
  9.1 2.9 collective-permute-done.1
  12.0 0.0 collective-permute-done.2
  12.0 0.0 copy-done
  12.0 0.3 shard_map.68
  12.3 1.5 collective-permute-start.3
  13.8 0.6 collective-permute-start.4
  14.5 2.3 collective-permute-start.5
  16.7 1.5 collective-permute-start.6
  18.2 0.0 collective-permute-start.7
  18.3 0.0 collective-permute-done.3
  18.3 0.6 collective-permute-done.4
  18.9 0.5 collective-permute-done.5
  19.3 1.6 collective-permute-start.9
  20.9 0.3 collective-permute-done.6.refs_0_.refs_4_.refs_1_
  21.2 0.0 collective-permute-start.8
  21.2 0.0 collective-permute-done.7.refs_1_.refs_5_.refs_2_
  21.2 0.4 shard_map.69.refs_2_
  21.6 0.8 collective-permute-done.8.refs_6_.refs_3_
  22.5 3.6 shard_map.70
  26.0 0.0 collective-permute-done.9.refs_0_
  26.0 200.8 %shard_map.71 = (bf16[256,1536]{1,0:T(8,128)(2,1)S(1)}, f32[1,2048]{1,0:T(1,128)S(1)}) custom-call(f32[1]{0:T(128)S(6)} %copy.10.inverse, f32[1,1536]{1,0:T(1,128)S(1)} %reshape.42.logws.near_logws, f32[1,1536]{1,0:T(1,128)S(1)} %reshape.43.logws.far_logws, bf16[256,1536]{1,0:T(8,128)(2,1)S(1)} %get-tuple-element.18.near_xaug.xaug, ...), custom_call_target="tpu_custom_call" | custom-call | tf_op jit(solution)/shard_map/pallas_call | solution.py:373
  226.9 0.2 collective-permute-start.10
  227.1 1.0 collective-permute-done.10.other
  228.1 202.4 %shard_map.72 = (f32[1,2048]{1,0:T(1,128)S(1)}, f32[1,2048]{1,0:T(1,128)S(1)}) custom-call(f32[1,1536]{1,0:T(1,128)S(1)} %reshape.42.logws.near_logws, f32[1,1536]{1,0:T(1,128)S(1)} %reshape.43.logws.far_logws, bf16[256,1536]{1,0:T(8,128)(2,1)S(1)} %get-tuple-element.18.near_xaug.xaug, bf16[256,1536]{1,0:T(8,128)(2,1)S(1)} %get-tuple-element.22.far_xaug, ...), custom_call_target="tpu_custom_call" | custom-call | tf_op jit(solution)/shard_map/pallas_call | solution.py:373
  430.5 0.2 collective-permute-start.11
  430.8 1.0 collective-permute-done.11.other
  431.8 4.3 shard_map.73
  (10 shorter events, 0.1 us)
Async XLA Ops:
  0.7 0.7 copy-start.1
  0.7 0.7 copy-start.2
  2.2 6.9 %collective-permute-start = (bf16[1,80,128]{2,1,0:T(8,128)(2,1)S(1)}, bf16[1,80,128]{2,1,0:T(8,128)(2,1)S(1)}, u32[]{:S(2)}, u32[]{:S(2)}) collective-permute-start(bf16[1,80,128]{2,1,0:T(8,128)(2,1)S(1)} %maximum_bitcast_fusion), channel_id=1, source_target_pairs={{0,12},{1,13},{2,14},{3,15},{4,8},{5,9},{6,10},{7,11},{8,4},{9,5},... | collective-permute-start | bytes 61448 | tf_op jit(solution)/shard_map/ppermute | solution.py:328
  7.3 4.7 %collective-permute-start.1 = (bf16[1,80,128]{2,1,0:T(8,128)(2,1)S(1)}, bf16[1,80,128]{2,1,0:T(8,128)(2,1)S(1)}, u32[]{:S(2)}, u32[]{:S(2)}) collective-permute-start(bf16[1,80,128]{2,1,0:T(8,128)(2,1)S(1)} %maximum_bitcast_fusion), channel_id=1, source_target_pairs={{0,8},{1,9},{2,10},{3,11},{4,12},{5,13},{6,14},{7,15},{8,0},{9,1},... | collective-permute-start | bytes 61448 | tf_op jit(solution)/shard_map/ppermute | solution.py:328
  7.3 4.7 %collective-permute-start.2 = (bf16[1,80,128]{2,1,0:T(8,128)(2,1)S(1)}, bf16[1,80,128]{2,1,0:T(8,128)(2,1)S(1)}, u32[]{:S(2)}, u32[]{:S(2)}) collective-permute-start(bf16[1,80,128]{2,1,0:T(8,128)(2,1)S(1)} %maximum_bitcast_fusion), channel_id=1, source_target_pairs={{0,4},{1,5},{2,6},{3,7},{4,0},{5,1},{6,2},{7,3},{8,12},{9,13},{10,... | collective-permute-start | bytes 61448 | tf_op jit(solution)/shard_map/ppermute | solution.py:328
  8.6 3.4 copy-start
  12.3 6.0 %collective-permute-start.3 = (bf16[1,64,384]{2,1,0:T(8,128)(2,1)S(1)}, bf16[1,64,384]{2,1,0:T(8,128)(2,1)S(1)}, u32[]{:S(2)}, u32[]{:S(2)}) collective-permute-start(bf16[1,64,384]{2,1,0:T(8,128)(2,1)S(1)} %get-tuple-element.16), channel_id=1, source_target_pairs={{0,12},{1,13},{2,14},{3,15},{4,8},{5,9},{6,10},{7,11},{8,4},{9,5},... | collective-permute-start | bytes 147464 | tf_op jit(solution)/shard_map/ppermute | solution.py:328
  13.8 5.0 %collective-permute-start.4 = (bf16[1,64,384]{2,1,0:T(8,128)(2,1)S(1)}, bf16[1,64,384]{2,1,0:T(8,128)(2,1)S(1)}, u32[]{:S(2)}, u32[]{:S(2)}) collective-permute-start(bf16[1,64,384]{2,1,0:T(8,128)(2,1)S(1)} %get-tuple-element.16), channel_id=1, source_target_pairs={{0,8},{1,9},{2,10},{3,11},{4,12},{5,13},{6,14},{7,15},{8,0},{9,1},... | collective-permute-start | bytes 147464 | tf_op jit(solution)/shard_map/ppermute | solution.py:328
  14.5 4.9 %collective-permute-start.5 = (bf16[1,64,384]{2,1,0:T(8,128)(2,1)S(1)}, bf16[1,64,384]{2,1,0:T(8,128)(2,1)S(1)}, u32[]{:S(2)}, u32[]{:S(2)}) collective-permute-start(bf16[1,64,384]{2,1,0:T(8,128)(2,1)S(1)} %get-tuple-element.16), channel_id=1, source_target_pairs={{0,4},{1,5},{2,6},{3,7},{4,0},{5,1},{6,2},{7,3},{8,12},{9,13},{10,... | collective-permute-start | bytes 147464 | tf_op jit(solution)/shard_map/ppermute | solution.py:328
  16.7 4.4 %collective-permute-start.6 = (bf16[4,80,128]{2,1,0:T(8,128)(2,1)S(1)}, bf16[4,80,128]{2,1,0:T(8,128)(2,1)S(1)}, u32[]{:S(2)}, u32[]{:S(2)}) collective-permute-start(bf16[4,80,128]{2,1,0:T(8,128)(2,1)S(1)} %pad_maximum_fusion.refs_0_.refs_3_), channel_id=1, source_target_pairs={{0,2},{1,3},{2,0},{3,1},{4,6},{5,7},{6,4},{7,5},{8,10},{9,11},{10,... | collective-permute-start | bytes 245768 | tf_op jit(solution)/shard_map/ppermute | solution.py:328
  18.2 3.0 collective-permute-start.7
  19.3 6.7 %collective-permute-start.9 = (bf16[4,64,384]{2,1,0:T(8,128)(2,1)S(1)}, bf16[4,64,384]{2,1,0:T(8,128)(2,1)S(1)}, u32[]{:S(2)}, u32[]{:S(2)}) collective-permute-start(bf16[4,64,384]{2,1,0:T(8,128)(2,1)S(1)} %constant_dynamic-update-slice_fusion.refs_0_), channel_id=1, source_target_pairs={{0,2},{1,3},{2,0},{3,1},{4,6},{5,7},{6,4},{7,5},{8,10},{9,11},{10,... | collective-permute-start | bytes 589832 | tf_op jit(solution)/shard_map/ppermute | solution.py:328
  21.2 1.3 collective-permute-start.8
  226.9 1.2 collective-permute-start.10
  430.5 1.2 collective-permute-start.11

commit v7 on v6

--- a/solution.py
+++ b/solution.py
@@ -45,13 +45,12 @@
         xaug[(place + 1) * feat : (place + 2) * feat, at] = term
 
 
-def stage_sources(parts, scale, xaug):
-    place = 0
+def stage_sources(parts, scale, xaug, begin=0):
     for part in parts:
         count = part.shape[2]
         for block in range(part.shape[0]):
-            stage_source(part[block], scale, xaug, slice(place * count, (place + 1) * count))
-            place += 1
+            stage_source(part[block], scale, xaug, slice(begin, begin + count))
+            begin += count
 
 
 def target_lines(part, block, scale, feat):
@@ -75,11 +74,18 @@
             begin += LANES
 
 
-def renew_targets(own, other, g, q, logw, taug):
-    total = own.shape[1]
-    other = jnp.concatenate([other[:, total // 2 :], other[:, : total // 2]], axis=1)
-    peak = jnp.maximum(own, other)
-    potential = g - (peak + jnp.log2(jnp.exp2(own - peak) + jnp.exp2(other - peak)))
+def renew_targets(lines, flips, parts, g, q, logw, taug):
+    total = lines[0].shape[1]
+    size = total // (2 * parts)
+    held = []
+    for line, (core, digit) in zip(lines, flips):
+        value = line[...]
+        places = [(block ^ (core * parts)) ^ digit for block in range(2 * parts)]
+        pieces = [value[:, place * size : (place + 1) * size] for place in places]
+        held.append(jnp.concatenate(pieces, axis=1))
+    peak = functools.reduce(jnp.maximum, held)
+    added = functools.reduce(jnp.add, [jnp.exp2(value - peak) for value in held])
+    potential = g - (peak + jnp.log2(added))
     g = potential + logw
     terms = [term.astype(jnp.float32) for term in three_terms(g - jnp.max(g) - q)]
     for begin in range(0, total, LANES):
@@ -95,7 +101,7 @@
 
 def spread_rows(taug, right, p_ref, beside):
     total, width = taug.shape[0], right.shape[1]
-    reach = min(total, 2048)
+    reach = min(total, 512)
     sums = jnp.zeros((8, width), jnp.float32)
     for begin in range(0, total, reach):
         e = exponents(taug[begin : begin + reach, :], right)
@@ -165,7 +171,7 @@
         out_ref[:, begin : begin + reach] = added[0:1]
 
 
-def finish_sums(pieces, taug, least, p_ref, col_ref, out_ref):
+def finish_sums(xaug, logws, taug, least, p_ref, col_ref, out_ref):
     total = taug.shape[0]
     lane_totals(col_ref, out_ref)
     cols = out_ref[...]
@@ -186,7 +192,7 @@
         def block_rows(block):
             return pl.ds(pl.multiple_of(block * LANES, LANES), LANES)
 
-        def careful(xaug, logws, tile, carry):
+        def careful(tile, carry):
             at = tile_columns(tile, LANES)
             right = xaug[:, at]
 
@@ -214,9 +220,7 @@
 
             return lax.fori_loop(0, blocks, collected, carry)
 
-        for xaug, logws in pieces:
-            tiles = xaug.shape[1] // LANES
-            lax.fori_loop(0, tiles, functools.partial(careful, xaug, logws), 0)
+        lax.fori_loop(0, xaug.shape[1] // LANES, careful, 0)
 
         def turned(block, carry):
             rows = block_rows(block)
@@ -229,25 +233,21 @@
         lax.fori_loop(0, blocks, turned, 0)
 
 
-def part_kernel(n_t, feat, inverse, points, *refs):
-    ts, (taug, copy_ref) = refs[:n_t], refs[n_t:]
-    copy_ref[0] = points[...]
+def part_kernel(feat, inverse, *refs):
+    stage_targets(refs[:-1], inverse[0] * LOG2E, refs[-1], 0, feat)
+
+
+def part_copy_kernel(feat, inverse, points, *refs):
+    ts, (taug, copy_ref) = refs[:-2], refs[-2:]
+    copy_ref[...] = points[...]
     stage_targets(ts, inverse[0] * LOG2E, taug, 0, feat)
 
 
-def more_kernel(n_t, feat, inverse, *refs):
-    ts, (taug,) = refs[:n_t], refs[n_t:]
-    stage_targets(ts, inverse[0] * LOG2E, taug, 0, feat)
-
-
-def near_kernel(n_x, n_staged, n_t, n_late, feat, inverse, logws, *refs):
-    xs, refs = refs[:n_x], refs[n_x:]
-    staged, refs = refs[:n_staged], refs[n_staged:]
-    ts, refs = refs[:n_t], refs[n_t:]
-    late = ts[n_t - n_late :]
-    xaug, taug, col_ref, least_ref, g_ref, q_ref, p0, p1 = refs
+def near_kernel(parts, feat, inverse, logws, xs, mine, rest, theirs, *refs):
+    ts, refs = refs[: 2 * parts], refs[2 * parts :]
+    xaug, taug, out_ref, g_ref, q_ref, p0, p1, col_ref = refs
     scale = inverse[0] * LOG2E
-    stage_sources(xs, scale, xaug)
+    stage_sources([xs], scale, xaug)
     place = 0
     for part in ts:
         for block in range(part.shape[0]):
@@ -255,41 +255,38 @@
             q_ref[:, at], g_ref[:, at] = target_lines(part, block, scale, feat)
             place += 1
     begin = 0
-    for part in staged:
+    for part in (mine, rest, theirs):
         taug[begin : begin + part.shape[0], :] = part[...]
         begin += part.shape[0]
-    stage_targets(late, scale, taug, begin, feat)
+    stage_targets(ts[parts + 1 :], scale, taug, begin, feat)
     col_ref[...] = jnp.zeros_like(col_ref)
-    least_ref[...] = add_sources(xaug, logws, taug, (p0, p1), col_ref)
-
-
-def far_kernel(n_x, inverse, near_logws, logws, near_xaug, taug, near_col, near_least, *refs):
-    xs, refs = refs[:n_x], refs[n_x:]
-    xaug, out_ref, p0, p1, col_ref = refs
-    stage_sources(xs, inverse[0] * LOG2E, xaug)
-    col_ref[...] = near_col[...]
     least = add_sources(xaug, logws, taug, (p0, p1), col_ref)
-    least = jnp.minimum(least, near_least[...])
-    pieces = [(near_xaug, near_logws), (xaug, logws)]
-    finish_sums(pieces, taug, least, p0, col_ref, out_ref)
-
-
-def next_kernel(near_logws, far_logws, near_xaug, far_xaug, old, own, other, g, q, logw, *refs):
+    finish_sums(xaug, logws, taug, least, p0, col_ref, out_ref)
+
+
+def far_kernel(inverse, near_xaug, *refs):
+    xs, xaug = refs[:-1], refs[-1]
+    begin = near_xaug.shape[1]
+    xaug[:, 0:begin] = near_xaug[...]
+    stage_sources(xs, inverse[0] * LOG2E, xaug, begin)
+
+
+def next_kernel(flips, parts, logws, xaug, old, g, q, logw, *refs):
+    lines, refs = refs[: len(flips)], refs[len(flips) :]
     out_ref, g_ref, taug, p0, p1, col_ref = refs
     taug[...] = old[...]
-    g_ref[...] = renew_targets(own[...], other[...], g[...], q[...], logw[...], taug)[1]
+    g_ref[...] = renew_targets(lines, flips, parts, g[...], q[...], logw[...], taug)[1]
     col_ref[...] = jnp.zeros_like(col_ref)
-    pieces = [(near_xaug, near_logws), (far_xaug, far_logws)]
-    least = [add_sources(xaug, logws, taug, (p0, p1), col_ref) for xaug, logws in pieces]
-    least = jnp.minimum(least[0], least[1])
-    finish_sums(pieces, taug, least, p0, col_ref, out_ref)
-
-
-def map_kernel(n_t, feat, xaug, old, own, other, g, q, logw, *refs):
+    least = add_sources(xaug, logws, taug, (p0, p1), col_ref)
+    finish_sums(xaug, logws, taug, least, p0, col_ref, out_ref)
+
+
+def map_kernel(flips, parts, n_t, feat, xaug, old, g, q, logw, *refs):
+    lines, refs = refs[: len(flips)], refs[len(flips) :]
     ts = refs[:n_t]
     mapped_ref, pot_ref, taug, p_ref, plan_ref, coords = refs[n_t:]
     taug[...] = old[...]
-    potential = renew_targets(own[...], other[...], g[...], q[...], logw[...], taug)[0]
+    potential = renew_targets(lines, flips, parts, g[...], q[...], logw[...], taug)[0]
     pot_ref[...] = potential[:, :LANES] * (1.0 / LOG2E)
     place = 0
     for part in ts:
@@ -341,8 +338,7 @@
     parts = [block[None]]
     for low, width in chip_stages(count):
         held = parts[0] if len(parts) == 1 else jnp.concatenate(parts, axis=0)
-        digits = range((1 << width) - 1, 0, -1)
-        parts = [held] + [swap(held, count, digit << low) for digit in digits]
+        parts = [held] + [swap(held, count, digit << low) for digit in range(1, 1 << width)]
     return parts
 
 
@@ -389,59 +385,66 @@
 
     mine = gather_chips(packed, count)
     theirs = [swap(part, count, 1) for part in mine]
-    first, second, late = [mine[0]], mine[1:] + theirs[:1], theirs[1:]
-    ts = first + second + late
-    taug_first, points = call(
-        functools.partial(part_kernel, len(first), feat),
-        [inverse_eps, source_points] + first,
-        [staged_shape(first), jax.ShapeDtypeStruct((1, feat, own_sources), bf16)],
-    )
-    (taug_second,) = call(
-        functools.partial(more_kernel, len(second), feat),
-        [inverse_eps] + second,
-        [staged_shape(second)],
-    )
-    xs = gather_chips(points[0], count)
-    near, far = xs[:1], xs[1:]
-    near_logws, far_logws = logw_line(mine[:1]), logw_line(mine[1:])
-    near_rows, far_rows = near_logws.shape[1], far_logws.shape[1]
+    parts, low = len(mine), chip_stages(count)[-1][0]
+    ts = mine + theirs
+    (taug_mine,) = call(
+        functools.partial(part_kernel, feat),
+        [inverse_eps, mine[0]],
+        [staged_shape(mine[:1])],
+    )
+    taug_theirs, points = call(
+        functools.partial(part_copy_kernel, feat),
+        [inverse_eps, source_points, theirs[0]],
+        [staged_shape(theirs[:1]), jax.ShapeDtypeStruct((feat, own_sources), bf16)],
+    )
+    (taug_rest,) = call(
+        functools.partial(part_kernel, feat),
+        [inverse_eps] + mine[1:],
+        [staged_shape(mine[1:])],
+    )
+    xs = gather_chips(points, count)
+    logws = logw_line(mine)
+    near_rows, rows = xs[0].shape[0] * own_sources, chips * own_sources
 
     p_scratch = pltpu.VMEM((total, width), f32)
-    p_pair = [p_scratch, p_scratch if small else pltpu.VMEM((8, LANES), f32)]
-    col_scratch = pltpu.VMEM((total, LANES), f32)
-    near_xaug, taug, near_col, near_least, logw, q = call(
-        functools.partial(near_kernel, len(near), 2, len(ts), len(late), feat),
-        [inverse_eps, near_logws] + near + [taug_first, taug_second] + ts,
+    scratch = [
+        p_scratch,
+        p_scratch if small else pltpu.VMEM((8, LANES), f32),
+        pltpu.VMEM((total, LANES), f32),
+    ]
+    near_xaug, taug, sums, logw, q = call(
+        functools.partial(near_kernel, parts, feat),
+        [inverse_eps, logws, xs[0], taug_mine, taug_rest, taug_theirs] + ts,
         [
             jax.ShapeDtypeStruct((DEPTH, near_rows), bf16),
             jax.ShapeDtypeStruct((total, DEPTH), bf16),
-            jax.ShapeDtypeStruct((total, LANES), f32),
-            jax.ShapeDtypeStruct((1, width), f32),
+            line,
             line,
             line,
         ],
-        p_pair,
-    )
-    far_xaug, sums = call(
-        functools.partial(far_kernel, len(far)),
-        [inverse_eps, near_logws, far_logws, near_xaug, taug, near_col, near_least] + far,
-        [jax.ShapeDtypeStruct((DEPTH, far_rows), bf16), line],
-        p_pair + [col_scratch],
-    )
+        scratch,
+    )
+    (xaug,) = call(
+        far_kernel,
+        [inverse_eps, near_xaug] + xs[1:],
+        [jax.ShapeDtypeStruct((DEPTH, rows), bf16)],
+    )
+    lines = [sums] + [swap(sums, count, digit << low) for digit in range(1, parts)]
+    lines = lines + [swap(line_, count, 1) for line_ in lines]
+    flips = [(core, digit) for core in range(2) for digit in range(parts)]
     g = logw
     for _ in range(ITERS - 1):
-        lines = [sums, swap(sums, count, 1), g, q, logw]
         sums, g = call(
-            next_kernel,
-            [near_logws, far_logws, near_xaug, far_xaug, taug] + lines,
+            functools.partial(next_kernel, flips, parts),
+            [logws, xaug, taug, g, q, logw] + lines,
             [line, line],
-            [pltpu.VMEM((total, DEPTH), bf16)] + p_pair + [col_scratch],
+            [pltpu.VMEM((total, DEPTH), bf16)] + scratch,
             scalars=0,
         )
-    lines = [sums, swap(sums, count, 1), g, q, logw]
+        lines, flips = [sums, swap(sums, count, 1)], [(0, 0), (1, 0)]
     mapped, potential = call(
-        functools.partial(map_kernel, len(ts), feat),
-        [near_xaug, taug] + lines + ts,
+        functools.partial(map_kernel, flips, parts, len(ts), feat),
+        [near_xaug, taug, g, q, logw] + lines + ts,
         [
             jax.ShapeDtypeStruct((feat, own_sources), f32),
             jax.ShapeDtypeStruct((1, own_targets), f32),

time: 436 us -> 340 us (0.78)
  Pallas kernels: 412 us -> 309 us
  waiting for transfers between devices: 7.57 us -> 12.9 us
    pallas_call x6 -> x7, Pallas kernels: 412 us -> 309 us  [call(): pl.pallas_call(kernel, out_shape=outs, in_specs=[smem] * scalars + [vmem]...]
    ppermute x12 -> x14, waiting for transfers between devices: 7.57 us -> 12.9 us  [swap(): lax.ppermute(value, AXIS, [(source, source ^ step) for source in range(co...]
    ppermute x12 -> x14, starting transfers between devices: 13.7 us -> 14.9 us  [swap(): lax.ppermute(value, AXIS, [(source, source ^ step) for source in range(co...]
  transfers between devices with their start and end apart: 12 -> 14, of which waited for: 8 -> 8; matrix products, arithmetic and copies ran while one was open for 0% -> 0% of each run, Pallas kernels for 1% -> 31%
where the time goes in v7:
time: 340 us
  Pallas kernels  309 us (91%)
  starting transfers between devices  14.9 us (4%)
  waiting for transfers between devices  12.9 us (4%)
    pallas_call x7, Pallas kernels, call(): pl.pallas_call(kernel, out_shape=outs, in_specs=[smem] * scalars + [vmem]...  309 us
    ppermute x14, starting transfers between devices, swap(): lax.ppermute(value, AXIS, [(source, source ^ step) for source in range(co...  14.9 us
    ppermute x14, waiting for transfers between devices, swap(): lax.ppermute(value, AXIS, [(source, source ^ step) for source in range(co...  12.9 us
  transfers between devices with their start and end apart: 14, of which 8 were waited for; matrix products, arithmetic and copies ran while one was open for 0% of the time, Pallas kernels for 31%

profile of v7, /device:TPU:0, one launch (start us, length us, event | category | flops | bytes accessed | tf_op | source)
XLA Modules:
  0.0 340.0 jit_solution(3123461623596799584)
XLA Ops:
  0.6 0.1 pad.13.clone
  0.7 0.8 maximum_bitcast_fusion
  1.5 3.1 collective-permute-start
  4.6 2.6 collective-permute-start.1
  7.2 0.0 collective-permute-start.2
  7.2 0.0 collective-permute-done
  7.2 2.3 collective-permute-done.1
  9.5 3.3 collective-permute-done.2
  12.8 0.1 collective-permute-start.4
  13.5 0.6 collective-permute-done.4.refs_0_.refs_2_.refs_4_
  14.2 0.0 copy-start
  14.2 0.8 copy-done
  15.0 0.3 shard_map.68
  15.2 0.1 collective-permute-start.5
  15.3 0.8 collective-permute-start.6
  16.1 3.6 %collective-permute-start.7 = (bf16[1,64,384]{2,1,0:T(8,128)(2,1)S(1)}, bf16[1,64,384]{2,1,0:T(8,128)(2,1)S(1)}, u32[]{:S(2)}, u32[]{:S(2)}) collective-permute-start(bf16[1,64,384]{2,1,0:T(8,128)(2,1)S(1)} %bitcast.8), channel_id=1, source_target_pairs={{0,12},{1,13},{2,14},{3,15},{4,8},{5,9},{6,10},{7,11},{8,4},{9,5},... | collective-permute-start | bytes 147464 | tf_op jit(solution)/shard_map/ppermute | solution.py:325
  19.7 1.5 collective-permute-start.3
  21.2 0.0 collective-permute-done.5
  21.2 1.5 collective-permute-done.6
  22.7 0.0 collective-permute-done.7
  22.8 1.6 collective-permute-start.9
  24.3 0.3 shard_map.69.mine
  24.6 0.0 collective-permute-done.3.refs_0_.refs_1_.refs_3_
  24.6 0.1 collective-permute-start.8
  24.7 0.3 shard_map.70.rest
  25.0 0.9 collective-permute-done.8.refs_3_.refs_5_
  26.0 103.4 %shard_map.71 = (bf16[256,1536]{1,0:T(8,128)(2,1)S(1)}, bf16[2048,256]{1,0:T(8,128)(2,1)S(1)}, f32[1,2048]{1,0:T(1,128)S(1)}, f32[1,2048]{1,0:T(1,128)S(1)}, f32[1,2048]{1,0:T(1,128)S(1)}) custom-call(f32[1]{0:T(128)S(6)} %copy.7.inverse, f32[1,3072]{1,0:T(1,128)S(1)} %reshape.27.logws, bf16[4,64,384]{2,1,0:T(8,128)(2,1)S(1)} %pad_maximum_fusion.xs, ...), custom_call_target="tpu_custom_call" | custom-call | tf_op jit(solution)/shard_map/pallas_call | solution.py:369
  129.4 1.4 collective-permute-start.10
  130.8 0.0 collective-permute-start.11
  130.8 2.3 collective-permute-done.10.refs_1_
  133.1 0.0 collective-permute-start.12
  133.1 0.0 collective-permute-done.9.refs_0_
  133.1 0.2 shard_map.72.xaug
  133.3 0.0 collective-permute-done.11.refs_2_
  133.3 0.9 collective-permute-done.12.refs_3_
  134.3 200.2 %shard_map.73 = (f32[1,2048]{1,0:T(1,128)S(1)}, f32[1,2048]{1,0:T(1,128)S(1)}) custom-call(f32[1,3072]{1,0:T(1,128)S(1)} %reshape.27.logws, bf16[256,3072]{1,0:T(8,128)(2,1)S(1)} %shard_map.72.xaug, bf16[2048,256]{1,0:T(8,128)(2,1)S(1)} %get-tuple-element.16.old, f32[1,2048]{1,0:T(1,128)S(1)} %get-tuple-element.17.g.logw, ...), custom_call_target="tpu_custom_call" | custom-call | tf_op jit(solution)/shard_map/pallas_call | solution.py:369
  334.5 0.2 collective-permute-start.13
  334.7 1.0 collective-permute-done.13.refs_1_
  335.7 4.3 %shard_map.74 = (f32[64,384]{1,0:T(8,128)}, f32[1,128]{1,0:T(1,128)}) custom-call(bf16[256,1536]{1,0:T(8,128)(2,1)S(1)} %get-tuple-element.15.near_xaug.xaug, bf16[2048,256]{1,0:T(8,128)(2,1)S(1)} %get-tuple-element.16.old, f32[1,2048]{1,0:T(1,128)S(1)} %get-tuple-element.20.g, f32[1,2048]{1,0:T(1,128)S(1)} %get-tuple-element.18.q, ...), custom_call_target="tpu_custom_call" | custom-call | tf_op jit(solution)/shard_map/pallas_call | solution.py:369
  (7 shorter events, 0.1 us)
Async XLA Ops:
  1.5 5.7 %collective-permute-start = (bf16[1,80,128]{2,1,0:T(8,128)(2,1)S(1)}, bf16[1,80,128]{2,1,0:T(8,128)(2,1)S(1)}, u32[]{:S(2)}, u32[]{:S(2)}) collective-permute-start(bf16[1,80,128]{2,1,0:T(8,128)(2,1)S(1)} %maximum_bitcast_fusion), channel_id=1, source_target_pairs={{0,4},{1,5},{2,6},{3,7},{4,0},{5,1},{6,2},{7,3},{8,12},{9,13},{10,... | collective-permute-start | bytes 61448 | tf_op jit(solution)/shard_map/ppermute | solution.py:325
  4.6 4.9 %collective-permute-start.1 = (bf16[1,80,128]{2,1,0:T(8,128)(2,1)S(1)}, bf16[1,80,128]{2,1,0:T(8,128)(2,1)S(1)}, u32[]{:S(2)}, u32[]{:S(2)}) collective-permute-start(bf16[1,80,128]{2,1,0:T(8,128)(2,1)S(1)} %maximum_bitcast_fusion), channel_id=1, source_target_pairs={{0,8},{1,9},{2,10},{3,11},{4,12},{5,13},{6,14},{7,15},{8,0},{9,1},... | collective-permute-start | bytes 61448 | tf_op jit(solution)/shard_map/ppermute | solution.py:325
  7.2 5.6 %collective-permute-start.2 = (bf16[1,80,128]{2,1,0:T(8,128)(2,1)S(1)}, bf16[1,80,128]{2,1,0:T(8,128)(2,1)S(1)}, u32[]{:S(2)}, u32[]{:S(2)}) collective-permute-start(bf16[1,80,128]{2,1,0:T(8,128)(2,1)S(1)} %maximum_bitcast_fusion), channel_id=1, source_target_pairs={{0,12},{1,13},{2,14},{3,15},{4,8},{5,9},{6,10},{7,11},{8,4},{9,5},... | collective-permute-start | bytes 61448 | tf_op jit(solution)/shard_map/ppermute | solution.py:325
  12.8 1.3 collective-permute-start.4
  14.2 0.8 copy-start
  15.2 5.9 %collective-permute-start.5 = (bf16[1,64,384]{2,1,0:T(8,128)(2,1)S(1)}, bf16[1,64,384]{2,1,0:T(8,128)(2,1)S(1)}, u32[]{:S(2)}, u32[]{:S(2)}) collective-permute-start(bf16[1,64,384]{2,1,0:T(8,128)(2,1)S(1)} %bitcast.6), channel_id=1, source_target_pairs={{0,4},{1,5},{2,6},{3,7},{4,0},{5,1},{6,2},{7,3},{8,12},{9,13},{10,... | collective-permute-start | bytes 147464 | tf_op jit(solution)/shard_map/ppermute | solution.py:325
  15.3 7.4 %collective-permute-start.6 = (bf16[1,64,384]{2,1,0:T(8,128)(2,1)S(1)}, bf16[1,64,384]{2,1,0:T(8,128)(2,1)S(1)}, u32[]{:S(2)}, u32[]{:S(2)}) collective-permute-start(bf16[1,64,384]{2,1,0:T(8,128)(2,1)S(1)} %bitcast.7), channel_id=1, source_target_pairs={{0,8},{1,9},{2,10},{3,11},{4,12},{5,13},{6,14},{7,15},{8,0},{9,1},... | collective-permute-start | bytes 147464 | tf_op jit(solution)/shard_map/ppermute | solution.py:325
  16.1 6.6 %collective-permute-start.7 = (bf16[1,64,384]{2,1,0:T(8,128)(2,1)S(1)}, bf16[1,64,384]{2,1,0:T(8,128)(2,1)S(1)}, u32[]{:S(2)}, u32[]{:S(2)}) collective-permute-start(bf16[1,64,384]{2,1,0:T(8,128)(2,1)S(1)} %bitcast.8), channel_id=1, source_target_pairs={{0,12},{1,13},{2,14},{3,15},{4,8},{5,9},{6,10},{7,11},{8,4},{9,5},... | collective-permute-start | bytes 147464 | tf_op jit(solution)/shard_map/ppermute | solution.py:325
  19.7 4.9 %collective-permute-start.3 = (bf16[4,80,128]{2,1,0:T(8,128)(2,1)S(1)}, bf16[4,80,128]{2,1,0:T(8,128)(2,1)S(1)}, u32[]{:S(2)}, u32[]{:S(2)}) collective-permute-start(bf16[4,80,128]{2,1,0:T(8,128)(2,1)S(1)} %pad_maximum_fusion.1.refs_0_.refs_2_), channel_id=1, source_target_pairs={{0,2},{1,3},{2,0},{3,1},{4,6},{5,7},{6,4},{7,5},{8,10},{9,11},{10,... | collective-permute-start | bytes 245768 | tf_op jit(solution)/shard_map/ppermute | solution.py:325
  22.8 110.4 %collective-permute-start.9 = (bf16[4,64,384]{2,1,0:T(8,128)(2,1)S(1)}, bf16[4,64,384]{2,1,0:T(8,128)(2,1)S(1)}, u32[]{:S(2)}, u32[]{:S(2)}) collective-permute-start(bf16[4,64,384]{2,1,0:T(8,128)(2,1)S(1)} %pad_maximum_fusion.xs), channel_id=1, source_target_pairs={{0,2},{1,3},{2,0},{3,1},{4,6},{5,7},{6,4},{7,5},{8,10},{9,11},{10,... | collective-permute-start | bytes 589832 | tf_op jit(solution)/shard_map/ppermute | solution.py:325
  24.6 1.3 collective-permute-start.8
  129.4 3.7 %collective-permute-start.10 = (f32[1,2048]{1,0:T(1,128)S(1)}, f32[1,2048]{1,0:T(1,128)S(1)}, u32[]{:S(2)}, u32[]{:S(2)}) collective-permute-start(f32[1,2048]{1,0:T(1,128)S(1)} %get-tuple-element.19.refs_0_), channel_id=1, source_target_pairs={{0,2},{1,3},{2,0},{3,1},{4,6},{5,7},{6,4},{7,5},{8,10},{9,11},{10,... | collective-permute-start | bytes 24584 | tf_op jit(solution)/shard_map/ppermute | solution.py:325
  130.8 2.6 collective-permute-start.11
  133.1 1.2 collective-permute-start.12
  334.5 1.2 collective-permute-start.13

commit v8 on v7

--- a/solution.py
+++ b/solution.py
@@ -264,13 +264,6 @@
     finish_sums(xaug, logws, taug, least, p0, col_ref, out_ref)
 
 
-def far_kernel(inverse, near_xaug, *refs):
-    xs, xaug = refs[:-1], refs[-1]
-    begin = near_xaug.shape[1]
-    xaug[:, 0:begin] = near_xaug[...]
-    stage_sources(xs, inverse[0] * LOG2E, xaug, begin)
-
-
 def next_kernel(flips, parts, logws, xaug, old, g, q, logw, *refs):
     lines, refs = refs[: len(flips)], refs[len(flips) :]
     out_ref, g_ref, taug, p0, p1, col_ref = refs
@@ -334,12 +327,23 @@
     return stages
 
 
+def gather_stage(parts, count, low, width):
+    held = parts[0] if len(parts) == 1 else jnp.concatenate(parts, axis=0)
+    return [held] + [swap(held, count, digit << low) for digit in range(1, 1 << width)]
+
+
 def gather_chips(block, count):
     parts = [block[None]]
     for low, width in chip_stages(count):
-        held = parts[0] if len(parts) == 1 else jnp.concatenate(parts, axis=0)
-        parts = [held] + [swap(held, count, digit << low) for digit in range(1, 1 << width)]
+        parts = gather_stage(parts, count, low, width)
     return parts
+
+
+def gather_line(block, count):
+    parts = [block[None]]
+    for low, width in chip_stages(count)[:-1]:
+        parts = gather_stage(parts, count, low, width)
+    return jnp.concatenate(parts, axis=0)
 
 
 def on_device(source_points, target_points, source_logw, target_logw, inverse_eps, count):
@@ -357,7 +361,7 @@
         axis=0,
     )
     f32, bf16 = jnp.float32, jnp.bfloat16
-    total, chips = count * own_targets, count // 2
+    total = count * own_targets
     small = total <= 4096
     width = 2 * LANES if small else LANES
     vmem = pl.BlockSpec(memory_space=pltpu.VMEM)
@@ -402,9 +406,9 @@
         [inverse_eps] + mine[1:],
         [staged_shape(mine[1:])],
     )
-    xs = gather_chips(points, count)
-    logws = logw_line(mine)
-    near_rows, rows = xs[0].shape[0] * own_sources, chips * own_sources
+    xs = gather_line(points, count)
+    logws = logw_line(mine[:1])
+    rows = logws.shape[1]
 
     p_scratch = pltpu.VMEM((total, width), f32)
     scratch = [
@@ -412,11 +416,11 @@
         p_scratch if small else pltpu.VMEM((8, LANES), f32),
         pltpu.VMEM((total, LANES), f32),
     ]
-    near_xaug, taug, sums, logw, q = call(
+    xaug, taug, sums, logw, q = call(
         functools.partial(near_kernel, parts, feat),
-        [inverse_eps, logws, xs[0], taug_mine, taug_rest, taug_theirs] + ts,
+        [inverse_eps, logws, xs, taug_mine, taug_rest, taug_theirs] + ts,
         [
-            jax.ShapeDtypeStruct((DEPTH, near_rows), bf16),
+            jax.ShapeDtypeStruct((DEPTH, rows), bf16),
             jax.ShapeDtypeStruct((total, DEPTH), bf16),
             line,
             line,
@@ -424,27 +428,24 @@
         ],
         scratch,
     )
-    (xaug,) = call(
-        far_kernel,
-        [inverse_eps, near_xaug] + xs[1:],
-        [jax.ShapeDtypeStruct((DEPTH, rows), bf16)],
-    )
-    lines = [sums] + [swap(sums, count, digit << low) for digit in range(1, parts)]
-    lines = lines + [swap(line_, count, 1) for line_ in lines]
     flips = [(core, digit) for core in range(2) for digit in range(parts)]
+
+    def exchange(own):
+        held = [own] + [swap(own, count, digit << low) for digit in range(1, parts)]
+        return held + [swap(value, count, 1) for value in held]
+
     g = logw
     for _ in range(ITERS - 1):
         sums, g = call(
             functools.partial(next_kernel, flips, parts),
-            [logws, xaug, taug, g, q, logw] + lines,
+            [logws, xaug, taug, g, q, logw] + exchange(sums),
             [line, line],
             [pltpu.VMEM((total, DEPTH), bf16)] + scratch,
             scalars=0,
         )
-        lines, flips = [sums, swap(sums, count, 1)], [(0, 0), (1, 0)]
     mapped, potential = call(
         functools.partial(map_kernel, flips, parts, len(ts), feat),
-        [near_xaug, taug, g, q, logw] + lines + ts,
+        [xaug if small else xaug[:, :own_sources], taug, g, q, logw] + exchange(sums) + ts,
         [
             jax.ShapeDtypeStruct((feat, own_sources), f32),
             jax.ShapeDtypeStruct((1, own_targets), f32),

time: 340 us -> 240 us (0.71)
  Pallas kernels: 309 us -> 209 us
    pallas_call x7 -> x6, Pallas kernels: 309 us -> 209 us  [call(): pl.pallas_call(kernel, out_shape=outs, in_specs=[smem] * scalars + [vmem]...]
    ppermute x14 -> x15, waiting for transfers between devices: 12.9 us -> 15.3 us  [swap(): lax.ppermute(value, AXIS, [(source, source ^ step) for source in range(co...]
    ppermute x14 -> x15, starting transfers between devices: 14.9 us -> 13.1 us  [swap(): lax.ppermute(value, AXIS, [(source, source ^ step) for source in range(co...]
  transfers between devices with their start and end apart: 14 -> 15, of which waited for: 8 -> 8; matrix products, arithmetic and copies ran while one was open for 0% -> 0% of each run, Pallas kernels for 31% -> 0%
where the time goes in v8:
time: 240 us
  Pallas kernels  209 us (87%)
  waiting for transfers between devices  15.3 us (6%)
  starting transfers between devices  13.1 us (5%)
    pallas_call x6, Pallas kernels, call(): pl.pallas_call(kernel, out_shape=outs, in_specs=[smem] * scalars + [vmem]...  209 us
    ppermute x15, waiting for transfers between devices, swap(): lax.ppermute(value, AXIS, [(source, source ^ step) for source in range(co...  15.3 us
    ppermute x15, starting transfers between devices, swap(): lax.ppermute(value, AXIS, [(source, source ^ step) for source in range(co...  13.1 us
  transfers between devices with their start and end apart: 15, of which 8 were waited for; matrix products, arithmetic and copies ran while one was open for 0% of the time, Pallas kernels for 0%

profile of v8, /device:TPU:0, one launch (start us, length us, event | category | flops | bytes accessed | tf_op | source)
XLA Modules:
  0.0 240.1 jit_solution(4497597801386850455)
XLA Ops:
  0.6 0.1 pad.11.clone
  0.7 0.0 copy-start.1
  0.7 0.0 copy-start.2
  0.7 0.7 copy-done.1
  1.4 0.0 copy-done.2
  1.4 0.8 maximum_bitcast_fusion
  2.2 0.0 copy-start
  2.2 5.1 %collective-permute-start.2 = (bf16[1,80,128]{2,1,0:T(8,128)(2,1)S(1)}, bf16[1,80,128]{2,1,0:T(8,128)(2,1)S(1)}, u32[]{:S(2)}, u32[]{:S(2)}) collective-permute-start(bf16[1,80,128]{2,1,0:T(8,128)(2,1)S(1)} %maximum_bitcast_fusion), channel_id=1, source_target_pairs={{0,12},{1,13},{2,14},{3,15},{4,8},{5,9},{6,10},{7,11},{8,4},{9,5},... | collective-permute-start | bytes 61448 | tf_op jit(solution)/shard_map/ppermute | solution.py:318
  7.3 0.0 collective-permute-start.1
  7.3 0.6 collective-permute-start
  8.0 1.1 collective-permute-done.2
  9.1 2.9 %collective-permute-done.1 = bf16[1,80,128]{2,1,0:T(8,128)(2,1)S(1)} collective-permute-done((bf16[1,80,128]{2,1,0:T(8,128)(2,1)S(1)}, bf16[1,80,128]{2,1,0:T(8,128)(2,1)S(1)}, u32[]{:S(2)}, u32[]{:S(2)}) %collective-permute-start.1) | collective-permute-done | bytes 20512 | tf_op jit(solution)/shard_map/ppermute | solution.py:318
  12.0 0.0 collective-permute-done
  12.0 0.1 collective-permute-start.3
  12.7 1.6 collective-permute-start.7
  14.3 0.0 collective-permute-done.3.refs_0_.refs_2_.refs_6_
  14.3 0.0 copy-done
  14.3 0.3 shard_map.68
  14.6 1.5 collective-permute-start.6
  16.1 0.6 collective-permute-start.5
  16.7 2.3 collective-permute-start.4
  19.0 0.3 shard_map.69.mine
  19.3 0.0 collective-permute-done.7.refs_0_.refs_1_.refs_5_
  19.3 0.1 collective-permute-start.8
  19.4 0.3 shard_map.70.rest
  19.7 1.3 collective-permute-done.6
  21.0 1.5 collective-permute-done.5
  22.4 0.0 collective-permute-done.4
  22.5 0.0 collective-permute-done.8.refs_3_.refs_7_
  22.5 101.8 %shard_map.71 = (bf16[256,1536]{1,0:T(8,128)(2,1)S(1)}, bf16[2048,256]{1,0:T(8,128)(2,1)S(1)}, f32[1,2048]{1,0:T(1,128)S(1)}, f32[1,2048]{1,0:T(1,128)S(1)}, f32[1,2048]{1,0:T(1,128)S(1)}) custom-call(f32[1]{0:T(128)S(6)} %copy.7.inverse, f32[1,1536]{1,0:T(1,128)S(1)} %reshape.27.logws, bf16[4,64,384]{2,1,0:T(8,128)(2,1)S(1)} %pad_maximum_fusion.xs, ...), custom_call_target="tpu_custom_call" | custom-call | tf_op jit(solution)/shard_map/pallas_call | solution.py:373
  124.3 0.6 collective-permute-start.9
  124.9 0.0 collective-permute-start.10
  124.9 3.1 %collective-permute-done.9.refs_1_ = f32[1,2048]{1,0:T(1,128)S(1)} collective-permute-done((f32[1,2048]{1,0:T(1,128)S(1)}, f32[1,2048]{1,0:T(1,128)S(1)}, u32[]{:S(2)}, u32[]{:S(2)}) %collective-permute-start.9) | collective-permute-done | bytes 8224 | tf_op jit(solution)/shard_map/ppermute | solution.py:318
  128.0 0.0 collective-permute-start.11
  128.0 0.0 collective-permute-done.10.refs_2_
  128.0 1.2 collective-permute-done.11.refs_3_
  129.2 101.7 %shard_map.72 = (f32[1,2048]{1,0:T(1,128)S(1)}, f32[1,2048]{1,0:T(1,128)S(1)}) custom-call(f32[1,1536]{1,0:T(1,128)S(1)} %reshape.27.logws, bf16[256,1536]{1,0:T(8,128)(2,1)S(1)} %get-tuple-element.15.xaug, bf16[2048,256]{1,0:T(8,128)(2,1)S(1)} %get-tuple-element.16.old, f32[1,2048]{1,0:T(1,128)S(1)} %get-tuple-element.17.g.logw, ...), custom_call_target="tpu_custom_call" | custom-call | tf_op jit(solution)/shard_map/pallas_call | solution.py:373
  230.9 0.6 collective-permute-start.12
  231.5 0.0 collective-permute-start.13
  231.5 3.1 %collective-permute-done.12.refs_1_ = f32[1,2048]{1,0:T(1,128)S(1)} collective-permute-done((f32[1,2048]{1,0:T(1,128)S(1)}, f32[1,2048]{1,0:T(1,128)S(1)}, u32[]{:S(2)}, u32[]{:S(2)}) %collective-permute-start.12) | collective-permute-done | bytes 8224 | tf_op jit(solution)/shard_map/ppermute | solution.py:318
  234.6 0.0 collective-permute-start.14
  234.6 0.0 collective-permute-done.13.refs_2_
  234.7 1.2 collective-permute-done.14.refs_3_
  235.8 4.3 %shard_map.73 = (f32[64,384]{1,0:T(8,128)}, f32[1,128]{1,0:T(1,128)}) custom-call(bf16[256,1536]{1,0:T(8,128)(2,1)S(1)} %get-tuple-element.15.xaug, bf16[2048,256]{1,0:T(8,128)(2,1)S(1)} %get-tuple-element.16.old, f32[1,2048]{1,0:T(1,128)S(1)} %get-tuple-element.20.g, f32[1,2048]{1,0:T(1,128)S(1)} %get-tuple-element.18.q, ...), custom_call_target="tpu_custom_call" | custom-call | tf_op jit(solution)/shard_map/pallas_call | solution.py:373
  (5 shorter events, 0.1 us)
Async XLA Ops:
  0.7 0.7 copy-start.1
  0.7 0.7 copy-start.2
  2.2 12.1 %copy-start = (bf16[64,384]{1,0:T(8,128)(2,1)S(1)}, bf16[64,384]{1,0:T(8,128)(2,1)}, u32[]{:S(2)}) copy-start(bf16[64,384]{1,0:T(8,128)(2,1)} %points.1) | copy-start | bytes 147460
  2.2 6.9 %collective-permute-start.2 = (bf16[1,80,128]{2,1,0:T(8,128)(2,1)S(1)}, bf16[1,80,128]{2,1,0:T(8,128)(2,1)S(1)}, u32[]{:S(2)}, u32[]{:S(2)}) collective-permute-start(bf16[1,80,128]{2,1,0:T(8,128)(2,1)S(1)} %maximum_bitcast_fusion), channel_id=1, source_target_pairs={{0,12},{1,13},{2,14},{3,15},{4,8},{5,9},{6,10},{7,11},{8,4},{9,5},... | collective-permute-start | bytes 61448 | tf_op jit(solution)/shard_map/ppermute | solution.py:318
  7.3 4.7 %collective-permute-start.1 = (bf16[1,80,128]{2,1,0:T(8,128)(2,1)S(1)}, bf16[1,80,128]{2,1,0:T(8,128)(2,1)S(1)}, u32[]{:S(2)}, u32[]{:S(2)}) collective-permute-start(bf16[1,80,128]{2,1,0:T(8,128)(2,1)S(1)} %maximum_bitcast_fusion), channel_id=1, source_target_pairs={{0,8},{1,9},{2,10},{3,11},{4,12},{5,13},{6,14},{7,15},{8,0},{9,1},... | collective-permute-start | bytes 61448 | tf_op jit(solution)/shard_map/ppermute | solution.py:318
  7.3 4.7 %collective-permute-start = (bf16[1,80,128]{2,1,0:T(8,128)(2,1)S(1)}, bf16[1,80,128]{2,1,0:T(8,128)(2,1)S(1)}, u32[]{:S(2)}, u32[]{:S(2)}) collective-permute-start(bf16[1,80,128]{2,1,0:T(8,128)(2,1)S(1)} %maximum_bitcast_fusion), channel_id=1, source_target_pairs={{0,4},{1,5},{2,6},{3,7},{4,0},{5,1},{6,2},{7,3},{8,12},{9,13},{10,... | collective-permute-start | bytes 61448 | tf_op jit(solution)/shard_map/ppermute | solution.py:318
  12.0 2.3 collective-permute-start.3
  12.7 6.6 %collective-permute-start.7 = (bf16[4,80,128]{2,1,0:T(8,128)(2,1)S(1)}, bf16[4,80,128]{2,1,0:T(8,128)(2,1)S(1)}, u32[]{:S(2)}, u32[]{:S(2)}) collective-permute-start(bf16[4,80,128]{2,1,0:T(8,128)(2,1)S(1)} %pad_maximum_fusion.1.refs_0_.refs_4_), channel_id=1, source_target_pairs={{0,2},{1,3},{2,0},{3,1},{4,6},{5,7},{6,4},{7,5},{8,10},{9,11},{10,... | collective-permute-start | bytes 245768 | tf_op jit(solution)/shard_map/ppermute | solution.py:318
  14.6 6.4 %collective-permute-start.6 = (bf16[1,64,384]{2,1,0:T(8,128)(2,1)S(1)}, bf16[1,64,384]{2,1,0:T(8,128)(2,1)S(1)}, u32[]{:S(2)}, u32[]{:S(2)}) collective-permute-start(bf16[1,64,384]{2,1,0:T(8,128)(2,1)S(1)} %bitcast.6), channel_id=1, source_target_pairs={{0,12},{1,13},{2,14},{3,15},{4,8},{5,9},{6,10},{7,11},{8,4},{9,5},... | collective-permute-start | bytes 147464 | tf_op jit(solution)/shard_map/ppermute | solution.py:318
  16.1 6.3 %collective-permute-start.5 = (bf16[1,64,384]{2,1,0:T(8,128)(2,1)S(1)}, bf16[1,64,384]{2,1,0:T(8,128)(2,1)S(1)}, u32[]{:S(2)}, u32[]{:S(2)}) collective-permute-start(bf16[1,64,384]{2,1,0:T(8,128)(2,1)S(1)} %bitcast.7), channel_id=1, source_target_pairs={{0,8},{1,9},{2,10},{3,11},{4,12},{5,13},{6,14},{7,15},{8,0},{9,1},... | collective-permute-start | bytes 147464 | tf_op jit(solution)/shard_map/ppermute | solution.py:318
  16.7 5.7 %collective-permute-start.4 = (bf16[1,64,384]{2,1,0:T(8,128)(2,1)S(1)}, bf16[1,64,384]{2,1,0:T(8,128)(2,1)S(1)}, u32[]{:S(2)}, u32[]{:S(2)}) collective-permute-start(bf16[1,64,384]{2,1,0:T(8,128)(2,1)S(1)} %bitcast.8), channel_id=1, source_target_pairs={{0,4},{1,5},{2,6},{3,7},{4,0},{5,1},{6,2},{7,3},{8,12},{9,13},{10,... | collective-permute-start | bytes 147464 | tf_op jit(solution)/shard_map/ppermute | solution.py:318
  19.3 3.1 %collective-permute-start.8 = (bf16[4,80,128]{2,1,0:T(8,128)(2,1)S(1)}, bf16[4,80,128]{2,1,0:T(8,128)(2,1)S(1)}, u32[]{:S(2)}, u32[]{:S(2)}) collective-permute-start(bf16[4,80,128]{2,1,0:T(8,128)(2,1)S(1)} %collective-permute-done.7.refs_0_.refs_1_.refs_5_), channel_id=1, source_target_pairs={{0,1},{1,0},{2,3},{3,2},{4,5},{5,4},{6,7},{7,6},{8,9},{9,8},{10,11... | collective-permute-start | bytes 245768 | tf_op jit(solution)/shard_map/ppermute | solution.py:318
  124.3 3.7 %collective-permute-start.9 = (f32[1,2048]{1,0:T(1,128)S(1)}, f32[1,2048]{1,0:T(1,128)S(1)}, u32[]{:S(2)}, u32[]{:S(2)}) collective-permute-start(f32[1,2048]{1,0:T(1,128)S(1)} %get-tuple-element.19.refs_0_), channel_id=1, source_target_pairs={{0,2},{1,3},{2,0},{3,1},{4,6},{5,7},{6,4},{7,5},{8,10},{9,11},{10,... | collective-permute-start | bytes 24584 | tf_op jit(solution)/shard_map/ppermute | solution.py:318
  124.9 3.1 %collective-permute-start.10 = (f32[1,2048]{1,0:T(1,128)S(1)}, f32[1,2048]{1,0:T(1,128)S(1)}, u32[]{:S(2)}, u32[]{:S(2)}) collective-permute-start(f32[1,2048]{1,0:T(1,128)S(1)} %get-tuple-element.19.refs_0_), channel_id=1, source_target_pairs={{0,1},{1,0},{2,3},{3,2},{4,5},{5,4},{6,7},{7,6},{8,9},{9,8},{10,11... | collective-permute-start | bytes 24584 | tf_op jit(solution)/shard_map/ppermute | solution.py:318
  128.0 1.2 collective-permute-start.11
  230.9 3.7 %collective-permute-start.12 = (f32[1,2048]{1,0:T(1,128)S(1)}, f32[1,2048]{1,0:T(1,128)S(1)}, u32[]{:S(2)}, u32[]{:S(2)}) collective-permute-start(f32[1,2048]{1,0:T(1,128)S(1)} %get-tuple-element.21.refs_0_), channel_id=1, source_target_pairs={{0,2},{1,3},{2,0},{3,1},{4,6},{5,7},{6,4},{7,5},{8,10},{9,11},{10,... | collective-permute-start | bytes 24584 | tf_op jit(solution)/shard_map/ppermute | solution.py:318
  231.5 3.1 %collective-permute-start.13 = (f32[1,2048]{1,0:T(1,128)S(1)}, f32[1,2048]{1,0:T(1,128)S(1)}, u32[]{:S(2)}, u32[]{:S(2)}) collective-permute-start(f32[1,2048]{1,0:T(1,128)S(1)} %get-tuple-element.21.refs_0_), channel_id=1, source_target_pairs={{0,1},{1,0},{2,3},{3,2},{4,5},{5,4},{6,7},{7,6},{8,9},{9,8},{10,11... | collective-permute-start | bytes 24584 | tf_op jit(solution)/shard_map/ppermute | solution.py:318
  234.6 1.2 collective-permute-start.14

commit v9 on v8

--- a/solution.py
+++ b/solution.py
@@ -237,12 +237,6 @@
     stage_targets(refs[:-1], inverse[0] * LOG2E, refs[-1], 0, feat)
 
 
-def part_copy_kernel(feat, inverse, points, *refs):
-    ts, (taug, copy_ref) = refs[:-2], refs[-2:]
-    copy_ref[...] = points[...]
-    stage_targets(ts, inverse[0] * LOG2E, taug, 0, feat)
-
-
 def near_kernel(parts, feat, inverse, logws, xs, mine, rest, theirs, *refs):
     ts, refs = refs[: 2 * parts], refs[2 * parts :]
     xaug, taug, out_ref, g_ref, q_ref, p0, p1, col_ref = refs
@@ -387,6 +381,7 @@
         rows = [part[:, feat + 1 : feat + 1 + extra_rows] for part in parts]
         return jnp.concatenate(rows, axis=0).reshape(1, -1).astype(f32)
 
+    packed, points = lax.optimization_barrier((packed, source_points))
     mine = gather_chips(packed, count)
     theirs = [swap(part, count, 1) for part in mine]
     parts, low = len(mine), chip_stages(count)[-1][0]
@@ -396,10 +391,10 @@
         [inverse_eps, mine[0]],
         [staged_shape(mine[:1])],
     )
-    taug_theirs, points = call(
-        functools.partial(part_copy_kernel, feat),
-        [inverse_eps, source_points, theirs[0]],
-        [staged_shape(theirs[:1]), jax.ShapeDtypeStruct((feat, own_sources), bf16)],
+    (taug_theirs,) = call(
+        functools.partial(part_kernel, feat),
+        [inverse_eps, theirs[0]],
+        [staged_shape(theirs[:1])],
     )
     (taug_rest,) = call(
         functools.partial(part_kernel, feat),

time: 240 us -> 236 us (0.983)
  waiting for transfers between devices: 15.3 us -> 9.54 us
    ppermute x15, waiting for transfers between devices: 15.3 us -> 9.54 us  [swap(): lax.ppermute(value, AXIS, [(source, source ^ step) for source in range(co...]
  transfers between devices with their start and end apart: 15 -> 15, of which waited for: 8 -> 6; matrix products, arithmetic and copies ran while one was open for 0% -> 0% of each run, Pallas kernels for 0% -> 0%
where the time goes in v9:
time: 236 us
  Pallas kernels  209 us (89%)
  starting transfers between devices  15.3 us (6%)
  waiting for transfers between devices  9.54 us (4%)
    pallas_call x6, Pallas kernels, call(): pl.pallas_call(kernel, out_shape=outs, in_specs=[smem] * scalars + [vmem]...  209 us
    ppermute x15, starting transfers between devices, swap(): lax.ppermute(value, AXIS, [(source, source ^ step) for source in range(co...  15.3 us
    ppermute x15, waiting for transfers between devices, swap(): lax.ppermute(value, AXIS, [(source, source ^ step) for source in range(co...  9.54 us
  transfers between devices with their start and end apart: 15, of which 6 were waited for; matrix products, arithmetic and copies ran while one was open for 0% of the time, Pallas kernels for 0%

profile of v9, /device:TPU:0, one launch (start us, length us, event | category | flops | bytes accessed | tf_op | source)
XLA Modules:
  0.0 235.9 jit_solution(7029030044398329513)
XLA Ops:
  0.6 0.0 copy-start
  0.6 0.1 pad.11.clone
  0.7 0.8 maximum_maximum_fusion
  1.6 5.1 %collective-permute-start.2 = (bf16[1,80,128]{2,1,0:T(8,128)(2,1)S(1)}, bf16[1,80,128]{2,1,0:T(8,128)(2,1)S(1)}, u32[]{:S(2)}, u32[]{:S(2)}) collective-permute-start(bf16[1,80,128]{2,1,0:T(8,128)(2,1)S(1)} %bitcast.5), channel_id=1, source_target_pairs={{0,12},{1,13},{2,14},{3,15},{4,8},{5,9},{6,10},{7,11},{8,4},{9,5},... | collective-permute-start | bytes 61448 | tf_op jit(solution)/shard_map/ppermute | solution.py:312
  6.7 0.0 collective-permute-start.1
  6.7 0.6 collective-permute-start
  7.3 0.0 copy-done
  7.3 3.7 %collective-permute-start.5 = (bf16[1,64,384]{2,1,0:T(8,128)(2,1)S(1)}, bf16[1,64,384]{2,1,0:T(8,128)(2,1)S(1)}, u32[]{:S(2)}, u32[]{:S(2)}) collective-permute-start(bf16[1,64,384]{2,1,0:T(8,128)(2,1)S(1)} %bitcast.9), channel_id=1, source_target_pairs={{0,12},{1,13},{2,14},{3,15},{4,8},{5,9},{6,10},{7,11},{8,4},{9,5},... | collective-permute-start | bytes 147464 | tf_op jit(solution)/shard_map/ppermute | solution.py:312
  11.1 0.0 collective-permute-start.4
  11.7 0.0 collective-permute-done.2
  11.7 0.7 collective-permute-start.3
  12.4 0.0 collective-permute-done.1
  12.4 0.0 collective-permute-done
  12.4 1.7 collective-permute-start.6
  14.2 0.0 collective-permute-start.7
  14.2 0.3 shard_map.68.mine
  14.5 2.5 %collective-permute-done.6.refs_0_.refs_1_.refs_5_ = bf16[4,80,128]{2,1,0:T(8,128)(2,1)S(1)} collective-permute-done((bf16[4,80,128]{2,1,0:T(8,128)(2,1)S(1)}, bf16[4,80,128]{2,1,0:T(8,128)(2,1)S(1)}, u32[]{:S(2)}, u32[]{:S(2)}) %collective-permute-start.6) | collective-permute-done | bytes 81952 | tf_op jit(solution)/shard_map/ppermute | solution.py:312
  17.0 0.0 collective-permute-start.8
  17.0 0.0 collective-permute-done.5
  17.0 0.0 collective-permute-done.4
  17.0 0.0 collective-permute-done.3
  17.0 0.3 shard_map.69.rest
  17.3 0.0 collective-permute-done.7.refs_0_.refs_2_.refs_6_
  17.3 0.3 shard_map.70.theirs
  17.6 0.6 collective-permute-done.8.refs_3_.refs_7_
  18.2 101.8 %shard_map.71 = (bf16[256,1536]{1,0:T(8,128)(2,1)S(1)}, bf16[2048,256]{1,0:T(8,128)(2,1)S(1)}, f32[1,2048]{1,0:T(1,128)S(1)}, f32[1,2048]{1,0:T(1,128)S(1)}, f32[1,2048]{1,0:T(1,128)S(1)}) custom-call(f32[1]{0:T(128)S(6)} %copy.7.inverse, f32[1,1536]{1,0:T(1,128)S(1)} %reshape.27.logws, bf16[4,64,384]{2,1,0:T(8,128)(2,1)S(1)} %pad_maximum_fusion.xs, ...), custom_call_target="tpu_custom_call" | custom-call | tf_op jit(solution)/shard_map/pallas_call | solution.py:367
  120.1 1.7 collective-permute-start.9
  121.8 0.0 collective-permute-start.10
  121.8 2.0 collective-permute-done.9.refs_1_
  123.8 0.0 collective-permute-start.11
  123.8 0.0 collective-permute-done.10.refs_2_
  123.8 1.2 collective-permute-done.11.refs_3_
  125.0 101.7 %shard_map.72 = (f32[1,2048]{1,0:T(1,128)S(1)}, f32[1,2048]{1,0:T(1,128)S(1)}) custom-call(f32[1,1536]{1,0:T(1,128)S(1)} %reshape.27.logws, bf16[256,1536]{1,0:T(8,128)(2,1)S(1)} %get-tuple-element.15.xaug, bf16[2048,256]{1,0:T(8,128)(2,1)S(1)} %get-tuple-element.16.old, f32[1,2048]{1,0:T(1,128)S(1)} %get-tuple-element.17.g.logw, ...), custom_call_target="tpu_custom_call" | custom-call | tf_op jit(solution)/shard_map/pallas_call | solution.py:367
  226.7 1.7 collective-permute-start.12
  228.4 0.0 collective-permute-start.13
  228.4 2.0 collective-permute-done.12.refs_1_
  230.4 0.0 collective-permute-start.14
  230.4 0.0 collective-permute-done.13.refs_2_
  230.4 1.2 collective-permute-done.14.refs_3_
  231.6 4.3 %shard_map.73 = (f32[64,384]{1,0:T(8,128)}, f32[1,128]{1,0:T(1,128)}) custom-call(bf16[256,1536]{1,0:T(8,128)(2,1)S(1)} %get-tuple-element.15.xaug, bf16[2048,256]{1,0:T(8,128)(2,1)S(1)} %get-tuple-element.16.old, f32[1,2048]{1,0:T(1,128)S(1)} %get-tuple-element.20.g, f32[1,2048]{1,0:T(1,128)S(1)} %get-tuple-element.18.q, ...), custom_call_target="tpu_custom_call" | custom-call | tf_op jit(solution)/shard_map/pallas_call | solution.py:367
  (5 shorter events, 0.1 us)
Async XLA Ops:
  0.6 6.7 %copy-start = (bf16[64,384]{1,0:T(8,128)(2,1)S(1)}, bf16[64,384]{1,0:T(8,128)(2,1)}, u32[]{:S(2)}) copy-start(bf16[64,384]{1,0:T(8,128)(2,1)} %param.5) | copy-start | bytes 147460
  1.6 10.2 %collective-permute-start.2 = (bf16[1,80,128]{2,1,0:T(8,128)(2,1)S(1)}, bf16[1,80,128]{2,1,0:T(8,128)(2,1)S(1)}, u32[]{:S(2)}, u32[]{:S(2)}) collective-permute-start(bf16[1,80,128]{2,1,0:T(8,128)(2,1)S(1)} %bitcast.5), channel_id=1, source_target_pairs={{0,12},{1,13},{2,14},{3,15},{4,8},{5,9},{6,10},{7,11},{8,4},{9,5},... | collective-permute-start | bytes 61448 | tf_op jit(solution)/shard_map/ppermute | solution.py:312
  6.7 5.8 %collective-permute-start.1 = (bf16[1,80,128]{2,1,0:T(8,128)(2,1)S(1)}, bf16[1,80,128]{2,1,0:T(8,128)(2,1)S(1)}, u32[]{:S(2)}, u32[]{:S(2)}) collective-permute-start(bf16[1,80,128]{2,1,0:T(8,128)(2,1)S(1)} %bitcast.6), channel_id=1, source_target_pairs={{0,8},{1,9},{2,10},{3,11},{4,12},{5,13},{6,14},{7,15},{8,0},{9,1},... | collective-permute-start | bytes 61448 | tf_op jit(solution)/shard_map/ppermute | solution.py:312
  6.7 5.8 %collective-permute-start = (bf16[1,80,128]{2,1,0:T(8,128)(2,1)S(1)}, bf16[1,80,128]{2,1,0:T(8,128)(2,1)S(1)}, u32[]{:S(2)}, u32[]{:S(2)}) collective-permute-start(bf16[1,80,128]{2,1,0:T(8,128)(2,1)S(1)} %bitcast.7), channel_id=1, source_target_pairs={{0,4},{1,5},{2,6},{3,7},{4,0},{5,1},{6,2},{7,3},{8,12},{9,13},{10,... | collective-permute-start | bytes 61448 | tf_op jit(solution)/shard_map/ppermute | solution.py:312
  7.3 9.7 %collective-permute-start.5 = (bf16[1,64,384]{2,1,0:T(8,128)(2,1)S(1)}, bf16[1,64,384]{2,1,0:T(8,128)(2,1)S(1)}, u32[]{:S(2)}, u32[]{:S(2)}) collective-permute-start(bf16[1,64,384]{2,1,0:T(8,128)(2,1)S(1)} %bitcast.9), channel_id=1, source_target_pairs={{0,12},{1,13},{2,14},{3,15},{4,8},{5,9},{6,10},{7,11},{8,4},{9,5},... | collective-permute-start | bytes 147464 | tf_op jit(solution)/shard_map/ppermute | solution.py:312
  11.1 5.9 %collective-permute-start.4 = (bf16[1,64,384]{2,1,0:T(8,128)(2,1)S(1)}, bf16[1,64,384]{2,1,0:T(8,128)(2,1)S(1)}, u32[]{:S(2)}, u32[]{:S(2)}) collective-permute-start(bf16[1,64,384]{2,1,0:T(8,128)(2,1)S(1)} %bitcast.10), channel_id=1, source_target_pairs={{0,8},{1,9},{2,10},{3,11},{4,12},{5,13},{6,14},{7,15},{8,0},{9,1},... | collective-permute-start | bytes 147464 | tf_op jit(solution)/shard_map/ppermute | solution.py:312
  11.7 5.3 %collective-permute-start.3 = (bf16[1,64,384]{2,1,0:T(8,128)(2,1)S(1)}, bf16[1,64,384]{2,1,0:T(8,128)(2,1)S(1)}, u32[]{:S(2)}, u32[]{:S(2)}) collective-permute-start(bf16[1,64,384]{2,1,0:T(8,128)(2,1)S(1)} %bitcast.11), channel_id=1, source_target_pairs={{0,4},{1,5},{2,6},{3,7},{4,0},{5,1},{6,2},{7,3},{8,12},{9,13},{10,... | collective-permute-start | bytes 147464 | tf_op jit(solution)/shard_map/ppermute | solution.py:312
  12.4 4.5 %collective-permute-start.6 = (bf16[4,80,128]{2,1,0:T(8,128)(2,1)S(1)}, bf16[4,80,128]{2,1,0:T(8,128)(2,1)S(1)}, u32[]{:S(2)}, u32[]{:S(2)}) collective-permute-start(bf16[4,80,128]{2,1,0:T(8,128)(2,1)S(1)} %pad_maximum_fusion.1.refs_0_.refs_4_), channel_id=1, source_target_pairs={{0,2},{1,3},{2,0},{3,1},{4,6},{5,7},{6,4},{7,5},{8,10},{9,11},{10,... | collective-permute-start | bytes 245768 | tf_op jit(solution)/shard_map/ppermute | solution.py:312
  14.2 3.1 %collective-permute-start.7 = (bf16[4,80,128]{2,1,0:T(8,128)(2,1)S(1)}, bf16[4,80,128]{2,1,0:T(8,128)(2,1)S(1)}, u32[]{:S(2)}, u32[]{:S(2)}) collective-permute-start(bf16[4,80,128]{2,1,0:T(8,128)(2,1)S(1)} %pad_maximum_fusion.1.refs_0_.refs_4_), channel_id=1, source_target_pairs={{0,1},{1,0},{2,3},{3,2},{4,5},{5,4},{6,7},{7,6},{8,9},{9,8},{10,11... | collective-permute-start | bytes 245768 | tf_op jit(solution)/shard_map/ppermute | solution.py:312
  17.0 1.3 collective-permute-start.8
  120.1 3.7 %collective-permute-start.9 = (f32[1,2048]{1,0:T(1,128)S(1)}, f32[1,2048]{1,0:T(1,128)S(1)}, u32[]{:S(2)}, u32[]{:S(2)}) collective-permute-start(f32[1,2048]{1,0:T(1,128)S(1)} %get-tuple-element.19.refs_0_), channel_id=1, source_target_pairs={{0,2},{1,3},{2,0},{3,1},{4,6},{5,7},{6,4},{7,5},{8,10},{9,11},{10,... | collective-permute-start | bytes 24584 | tf_op jit(solution)/shard_map/ppermute | solution.py:312
  121.8 2.0 collective-permute-start.10
  123.8 1.2 collective-permute-start.11
  226.7 3.7 %collective-permute-start.12 = (f32[1,2048]{1,0:T(1,128)S(1)}, f32[1,2048]{1,0:T(1,128)S(1)}, u32[]{:S(2)}, u32[]{:S(2)}) collective-permute-start(f32[1,2048]{1,0:T(1,128)S(1)} %get-tuple-element.21.refs_0_), channel_id=1, source_target_pairs={{0,2},{1,3},{2,0},{3,1},{4,6},{5,7},{6,4},{7,5},{8,10},{9,11},{10,... | collective-permute-start | bytes 24584 | tf_op jit(solution)/shard_map/ppermute | solution.py:312
  228.4 2.0 collective-permute-start.13
  230.4 1.2 collective-permute-start.14

commit v10 on v9

--- a/solution.py
+++ b/solution.py
@@ -53,19 +53,16 @@
             begin += count
 
 
-def target_lines(part, block, scale, feat):
-    wide = part[block, :feat, :].astype(jnp.float32)
-    logw = part[block, feat : feat + 16, :].astype(jnp.float32)[0:1]
-    return scale * jnp.sum(wide * wide, axis=0, keepdims=True), logw * LOG2E
-
-
-def stage_targets(parts, scale, taug, begin, feat):
+def stage_targets(parts, scale, taug, q_ref, logw_ref, begin, feat):
     for part in parts:
         for block in range(part.shape[0]):
-            q, logw = target_lines(part, block, scale, feat)
+            wide = part[block, :feat, :].astype(jnp.float32)
+            q = scale * jnp.sum(wide * wide, axis=0, keepdims=True)
+            logw = part[block, feat : feat + 16, :].astype(jnp.float32)[0:1] * LOG2E
+            q_ref[:, begin : begin + LANES] = q
+            logw_ref[:, begin : begin + LANES] = logw
             terms = [term.astype(jnp.float32) for term in three_terms(logw - q)]
             extras = pick_rows((feat, LANES), terms + [1.0])
-            wide = part[block, :feat, :].astype(jnp.float32)
             turned = jnp.concatenate([extras, wide], axis=0).T
             lane = lax.broadcasted_iota(jnp.int32, turned.shape, 1)
             twice = jnp.where(lane < feat, pltpu.roll(turned, feat, 1), turned)
@@ -233,26 +230,27 @@
         lax.fori_loop(0, blocks, turned, 0)
 
 
-def part_kernel(feat, inverse, *refs):
-    stage_targets(refs[:-1], inverse[0] * LOG2E, refs[-1], 0, feat)
-
-
-def near_kernel(parts, feat, inverse, logws, xs, mine, rest, theirs, *refs):
-    ts, refs = refs[: 2 * parts], refs[2 * parts :]
-    xaug, taug, out_ref, g_ref, q_ref, p0, p1, col_ref = refs
-    scale = inverse[0] * LOG2E
-    stage_sources([xs], scale, xaug)
-    place = 0
-    for part in ts:
-        for block in range(part.shape[0]):
-            at = slice(place * LANES, (place + 1) * LANES)
-            q_ref[:, at], g_ref[:, at] = target_lines(part, block, scale, feat)
-            place += 1
+def targets_kernel(feat, inverse, *refs):
+    taug, q_ref, logw_ref = refs[-3:]
+    stage_targets(refs[:-3], inverse[0] * LOG2E, taug, q_ref, logw_ref, 0, feat)
+
+
+def sources_kernel(inverse, *refs):
+    stage_sources(refs[:-1], inverse[0] * LOG2E, refs[-1])
+
+
+def near_kernel(late, feat, inverse, logws, xaug, *refs):
+    staged, refs = refs[:9], refs[9:]
+    ts, refs = refs[:late], refs[late:]
+    taug, out_ref, q_ref, logw_ref, p0, p1, col_ref = refs
     begin = 0
-    for part in (mine, rest, theirs):
-        taug[begin : begin + part.shape[0], :] = part[...]
-        begin += part.shape[0]
-    stage_targets(ts[parts + 1 :], scale, taug, begin, feat)
+    for part, q, logw in zip(staged[0::3], staged[1::3], staged[2::3]):
+        end = begin + part.shape[0]
+        taug[begin:end, :] = part[...]
+        q_ref[:, begin:end] = q[...]
+        logw_ref[:, begin:end] = logw[...]
+        begin = end
+    stage_targets(ts, inverse[0] * LOG2E, taug, q_ref, logw_ref, begin, feat)
     col_ref[...] = jnp.zeros_like(col_ref)
     least = add_sources(xaug, logws, taug, (p0, p1), col_ref)
     finish_sums(xaug, logws, taug, least, p0, col_ref, out_ref)
@@ -268,20 +266,25 @@
     finish_sums(xaug, logws, taug, least, p0, col_ref, out_ref)
 
 
-def map_kernel(flips, parts, n_t, feat, xaug, old, g, q, logw, *refs):
+def map_kernel(flips, parts, n_t, feat, place, xaug, old, g, q, logw, *refs):
     lines, refs = refs[: len(flips)], refs[len(flips) :]
     ts = refs[:n_t]
-    mapped_ref, pot_ref, taug, p_ref, plan_ref, coords = refs[n_t:]
+    mapped_ref, pot_ref, g_ref, taug, p_ref, plan_ref, coords = refs[n_t:]
     taug[...] = old[...]
     potential = renew_targets(lines, flips, parts, g[...], q[...], logw[...], taug)[0]
-    pot_ref[...] = potential[:, :LANES] * (1.0 / LOG2E)
-    place = 0
+    g_ref[...] = potential
+    at = pl.ds(pl.multiple_of(place[0] * LANES, LANES), LANES)
+    pot_ref[...] = g_ref[:, at] * (1.0 / LOG2E)
+    begin = 0
     for part in ts:
         for block in range(part.shape[0]):
-            coords[:, place * LANES : (place + 1) * LANES] = part[block, :feat, :]
-            place += 1
-    total = taug.shape[0]
-    right = xaug[:, : p_ref.shape[1]]
+            coords[:, begin : begin + LANES] = part[block, :feat, :]
+            begin += LANES
+    total, width = p_ref.shape
+    if xaug.shape[1] == width:
+        right = xaug[...]
+    else:
+        right = xaug[:, pl.ds(pl.multiple_of(place[0] * width, LANES), width)]
     s = spread_rows(taug, right, p_ref, lambda rows: None)
     weight = 1.0 / s
     for begin in range(0, total, LANES):
@@ -326,18 +329,36 @@
     return [held] + [swap(held, count, digit << low) for digit in range(1, 1 << width)]
 
 
+def line_blocks(block, count, low, width):
+    span = 1 << width
+    mask = (span - 1) << low
+    groups = [
+        [base | (digit << low) for digit in range(span)]
+        for base in range(count)
+        if base & mask == 0
+    ]
+    spread = jnp.broadcast_to(block[None], (span,) + block.shape)
+    return lax.all_to_all(spread, AXIS, 0, 0, axis_index_groups=groups, tiled=True)
+
+
 def gather_chips(block, count):
     parts = [block[None]]
-    for low, width in chip_stages(count):
-        parts = gather_stage(parts, count, low, width)
+    for place, (low, width) in enumerate(chip_stages(count)):
+        if place == 0:
+            parts = [line_blocks(block, count, low, width)]
+        else:
+            parts = gather_stage(parts, count, low, width)
     return parts
 
 
 def gather_line(block, count):
     parts = [block[None]]
-    for low, width in chip_stages(count)[:-1]:
-        parts = gather_stage(parts, count, low, width)
-    return jnp.concatenate(parts, axis=0)
+    for place, (low, width) in enumerate(chip_stages(count)[:-1]):
+        if place == 0:
+            parts = [line_blocks(block, count, low, width)]
+        else:
+            parts = gather_stage(parts, count, low, width)
+    return parts
 
 
 def on_device(source_points, target_points, source_logw, target_logw, inverse_eps, count):
@@ -373,9 +394,15 @@
             compiler_params=params,
         )(*operands)
 
-    def staged_shape(parts):
+    def stage(parts):
         rows = sum(part.shape[0] for part in parts) * own_targets
-        return jax.ShapeDtypeStruct((rows, DEPTH), bf16)
+        lines = [jax.ShapeDtypeStruct((1, rows), f32)] * 2
+        staged = call(
+            functools.partial(targets_kernel, feat),
+            [inverse_eps] + parts,
+            [jax.ShapeDtypeStruct((rows, DEPTH), bf16)] + lines,
+        )
+        return list(staged)
 
     def logw_line(parts):
         rows = [part[:, feat + 1 : feat + 1 + extra_rows] for part in parts]
@@ -385,25 +412,19 @@
     mine = gather_chips(packed, count)
     theirs = [swap(part, count, 1) for part in mine]
     parts, low = len(mine), chip_stages(count)[-1][0]
+    first_low, first_width = chip_stages(count)[0]
+    place = (lax.axis_index(AXIS) >> first_low) & ((1 << first_width) - 1)
+    place = place.astype(jnp.int32).reshape(1)
     ts = mine + theirs
-    (taug_mine,) = call(
-        functools.partial(part_kernel, feat),
-        [inverse_eps, mine[0]],
-        [staged_shape(mine[:1])],
-    )
-    (taug_theirs,) = call(
-        functools.partial(part_kernel, feat),
-        [inverse_eps, theirs[0]],
-        [staged_shape(theirs[:1])],
-    )
-    (taug_rest,) = call(
-        functools.partial(part_kernel, feat),
-        [inverse_eps] + mine[1:],
-        [staged_shape(mine[1:])],
-    )
+    staged = stage(mine[:1]) + stage(mine[1:]) + stage(theirs[:1])
     xs = gather_line(points, count)
     logws = logw_line(mine[:1])
     rows = logws.shape[1]
+    (xaug,) = call(
+        sources_kernel,
+        [inverse_eps] + xs,
+        [jax.ShapeDtypeStruct((DEPTH, rows), bf16)],
+    )
 
     p_scratch = pltpu.VMEM((total, width), f32)
     scratch = [
@@ -411,16 +432,10 @@
         p_scratch if small else pltpu.VMEM((8, LANES), f32),
         pltpu.VMEM((total, LANES), f32),
     ]
-    xaug, taug, sums, logw, q = call(
-        functools.partial(near_kernel, parts, feat),
-        [inverse_eps, logws, xs, taug_mine, taug_rest, taug_theirs] + ts,
-        [
-            jax.ShapeDtypeStruct((DEPTH, rows), bf16),
-            jax.ShapeDtypeStruct((total, DEPTH), bf16),
-            line,
-            line,
-            line,
-        ],
+    taug, sums, q, logw = call(
+        functools.partial(near_kernel, parts - 1, feat),
+        [inverse_eps, logws, xaug] + staged + theirs[1:],
+        [jax.ShapeDtypeStruct((total, DEPTH), bf16), line, line, line],
         scratch,
     )
     flips = [(core, digit) for core in range(2) for digit in range(parts)]
@@ -438,20 +453,22 @@
             [pltpu.VMEM((total, DEPTH), bf16)] + scratch,
             scalars=0,
         )
+    if not small:
+        xaug = lax.dynamic_slice_in_dim(xaug, place[0] * own_sources, own_sources, 1)
     mapped, potential = call(
         functools.partial(map_kernel, flips, parts, len(ts), feat),
-        [xaug if small else xaug[:, :own_sources], taug, g, q, logw] + exchange(sums) + ts,
+        [place, xaug, taug, g, q, logw] + exchange(sums) + ts,
         [
             jax.ShapeDtypeStruct((feat, own_sources), f32),
             jax.ShapeDtypeStruct((1, own_targets), f32),
         ],
         [
+            pltpu.VMEM((1, total), f32),
             pltpu.VMEM((total, DEPTH), bf16),
             pltpu.VMEM((total, own_sources), f32),
             pltpu.VMEM((total, own_sources), bf16),
             pltpu.VMEM((feat, total), bf16),
         ],
-        scalars=0,
     )
     return (mapped, potential.reshape(own_targets))
 

time: 236 us -> 246 us (1.042)
  blocking collectives: 0 us -> 12 us
  starting transfers between devices: 15.3 us -> 6.65 us
  waiting for transfers between devices: 9.54 us -> 12.7 us
    all_to_all x0 -> x1, blocking collectives: none -> 12 us  [line_blocks(): lax.all_to_all(spread, AXIS, 0, 0, axis_index_groups=groups, tiled=True)]
    ppermute x15 -> x9, starting transfers between devices: 15.3 us -> 3.28 us  [swap(): lax.ppermute(value, AXIS, [(source, source ^ step) for source in range(co...]
    all_to_all x0 -> x1, waiting for transfers between devices: none -> 3.95 us  [line_blocks(): lax.all_to_all(spread, AXIS, 0, 0, axis_index_groups=groups, tiled=True)]
    all_to_all x0 -> x1, starting transfers between devices: none -> 3.36 us  [line_blocks(): lax.all_to_all(spread, AXIS, 0, 0, axis_index_groups=groups, tiled=True)]
    pallas_call x6 -> x7, Pallas kernels: 209 us -> 210 us  [call(): pl.pallas_call(kernel, out_shape=outs, in_specs=[smem] * scalars + [vmem]...]
    ppermute x15 -> x9, waiting for transfers between devices: 9.54 us -> 8.73 us  [swap(): lax.ppermute(value, AXIS, [(source, source ^ step) for source in range(co...]
  transfers between devices with their start and end apart: 15 -> 10, of which waited for: 6 -> 6; matrix products, arithmetic and copies ran while one was open for 0% -> 0% of each run, Pallas kernels for 0% -> 0%
where the time goes in v10:
time: 246 us; the launch traced here: 245 us
  Pallas kernels  210 us (85%)
  waiting for transfers between devices  12.7 us (5%)
  blocking collectives  12 us (5%)
  starting transfers between devices  6.65 us (3%)
    pallas_call x7, Pallas kernels, call(): pl.pallas_call(kernel, out_shape=outs, in_specs=[smem] * scalars + [vmem]...  210 us
    all_to_all x1, blocking collectives, line_blocks(): lax.all_to_all(spread, AXIS, 0, 0, axis_index_groups=groups, tiled=True)  12 us
    ppermute x9, waiting for transfers between devices, swap(): lax.ppermute(value, AXIS, [(source, source ^ step) for source in range(co...  8.73 us
  transfers between devices with their start and end apart: 10, of which 6 were waited for; matrix products, arithmetic and copies ran while one was open for 0% of the time, Pallas kernels for 0%

profile of v10, /device:TPU:0, one launch (start us, length us, event | category | flops | bytes accessed | tf_op | source)
XLA Modules:
  0.0 245.3 jit_solution(11844779082535979619)
XLA Ops:
  0.6 0.1 pad.3.clone
  0.7 0.0 copy-start.1
  0.7 0.0 copy-start.2
  0.7 0.7 copy-done.1
  1.4 0.0 copy-done.2
  1.4 0.8 maximum_maximum_fusion
  2.2 0.0 copy-start
  2.2 12.0 %all_to_all.10.refs_0_.refs_4_ = bf16[4,80,128]{2,1,0:T(8,128)(2,1)S(1)} all-to-all(bf16[4,80,128]{2,1,0:T(8,128)(2,1)S(1)} %broadcast_in_dim.21), channel_id=1, replica_groups={{0,4,8,12},{1,5,9,13},{2,6,10,14},{3,7,11,15},{16,20,24,28},{17,21,25,2..., dimensions={0} | all-to-all | bytes 163840 | tf_op jit(solution)/shard_map/all_to_all | solution.py:341
  14.3 1.5 collective-permute-start
  15.8 0.0 copy-done
  15.8 0.7 broadcast_in_dim.20
  16.4 3.4 %all-to-all-start = ((bf16[4,64,384]{2,1,0:T(8,128)(2,1)}), bf16[4,64,384]{2,1,0:T(8,128)(2,1)S(1)}, u32[]{:S(2)}, u32[]{:S(2)}) async-start(bf16[4,64,384]{2,1,0:T(8,128)(2,1)} %broadcast_in_dim.20), calls=%async_computation | async-start | bytes 393216 | tf_op jit(solution)/shard_map/all_to_all | solution.py:341
  20.5 0.1 collective-permute-start.1
  20.5 0.0 collective-permute-done.refs_0_.refs_5_
  20.6 0.5 collective-permute-start.2
  21.1 0.3 shard_map.69
  21.3 0.3 shard_map.70
  21.6 0.2 collective-permute-done.1.refs_0_.refs_6_
  21.8 0.3 shard_map.71
  22.1 3.9 %all-to-all-done.refs_0_ = bf16[4,64,384]{2,1,0:T(8,128)(2,1)S(1)} async-done(((bf16[4,64,384]{2,1,0:T(8,128)(2,1)}), bf16[4,64,384]{2,1,0:T(8,128)(2,1)S(1)}, u32[]{:S(2)}, u32[]{:S(2)}) %all-to-all-start) | async-done | bytes 196640 | tf_op jit(solution)/shard_map/all_to_all | solution.py:341
  26.0 0.2 shard_map.68.xaug
  26.2 0.0 collective-permute-done.2.refs_9_.refs_7_
  26.2 103.3 %shard_map.72 = (bf16[2048,256]{1,0:T(8,128)(2,1)S(1)}, f32[1,2048]{1,0:T(1,128)S(1)}, f32[1,2048]{1,0:T(1,128)S(1)}, f32[1,2048]{1,0:T(1,128)S(1)}) custom-call(f32[1]{0:T(128)S(6)} %copy.7.inverse, f32[1,1536]{1,0:T(1,128)S(1)} %reshape.33.logws, bf16[256,1536]{1,0:T(8,128)(2,1)S(1)} %shard_map.68.xaug, bf16[512,256]{1,0:T(8,128)(2,1)S(1)} %get-tuple-element.23.refs_0_, ...), custom_call_target="tpu_custom_call" | custom-call | tf_op jit(solution)/shard_map/pallas_call | solution.py:388
  129.5 0.6 collective-permute-start.3
  130.1 0.0 collective-permute-start.4
  130.1 3.1 %collective-permute-done.3.refs_1_ = f32[1,2048]{1,0:T(1,128)S(1)} collective-permute-done((f32[1,2048]{1,0:T(1,128)S(1)}, f32[1,2048]{1,0:T(1,128)S(1)}, u32[]{:S(2)}, u32[]{:S(2)}) %collective-permute-start.3) | collective-permute-done | bytes 8224 | tf_op jit(solution)/shard_map/ppermute | solution.py:315
  133.2 0.0 collective-permute-start.5
  133.2 0.0 collective-permute-done.4.refs_2_
  133.2 1.2 collective-permute-done.5.refs_3_
  134.4 101.7 %shard_map.73 = (f32[1,2048]{1,0:T(1,128)S(1)}, f32[1,2048]{1,0:T(1,128)S(1)}) custom-call(f32[1,1536]{1,0:T(1,128)S(1)} %reshape.33.logws, bf16[256,1536]{1,0:T(8,128)(2,1)S(1)} %shard_map.68.xaug, bf16[2048,256]{1,0:T(8,128)(2,1)S(1)} %get-tuple-element.32.old, f32[1,2048]{1,0:T(1,128)S(1)} %get-tuple-element.33.g.logw, ...), custom_call_target="tpu_custom_call" | custom-call | tf_op jit(solution)/shard_map/pallas_call | solution.py:388
  236.1 0.6 collective-permute-start.6
  236.7 0.0 collective-permute-start.7
  236.7 3.1 %collective-permute-done.6.refs_1_ = f32[1,2048]{1,0:T(1,128)S(1)} collective-permute-done((f32[1,2048]{1,0:T(1,128)S(1)}, f32[1,2048]{1,0:T(1,128)S(1)}, u32[]{:S(2)}, u32[]{:S(2)}) %collective-permute-start.6) | collective-permute-done | bytes 8224 | tf_op jit(solution)/shard_map/ppermute | solution.py:315
  239.8 0.0 collective-permute-start.8
  239.8 0.0 collective-permute-done.7.refs_2_
  239.8 1.2 collective-permute-done.8.refs_3_
  241.0 4.3 %shard_map.74 = (f32[64,384]{1,0:T(8,128)}, f32[1,128]{1,0:T(1,128)}) custom-call(s32[1]{0:T(128)} %bitcast.place, bf16[256,1536]{1,0:T(8,128)(2,1)S(1)} %shard_map.68.xaug, bf16[2048,256]{1,0:T(8,128)(2,1)S(1)} %get-tuple-element.32.old, f32[1,2048]{1,0:T(1,128)S(1)} %get-tuple-element.36.g, f32[1,2048]{1,0:T(1,128)S(1)} %get-tuple-element.34.q, ...), custom_call_target="tpu_custom_call" | custom-call | tf_op jit(solution)/shard_map/pallas_call | solution.py:388
  (4 shorter events, 0.0 us)
Async XLA Ops:
  0.7 0.7 copy-start.1
  0.7 0.7 copy-start.2
  2.2 13.5 %copy-start = (bf16[64,384]{1,0:T(8,128)(2,1)S(1)}, bf16[64,384]{1,0:T(8,128)(2,1)}, u32[]{:S(2)}) copy-start(bf16[64,384]{1,0:T(8,128)(2,1)} %param.5) | copy-start | bytes 147460
  14.3 6.3 %collective-permute-start = (bf16[4,80,128]{2,1,0:T(8,128)(2,1)S(1)}, bf16[4,80,128]{2,1,0:T(8,128)(2,1)S(1)}, u32[]{:S(2)}, u32[]{:S(2)}) collective-permute-start(bf16[4,80,128]{2,1,0:T(8,128)(2,1)S(1)} %all_to_all.10.refs_0_.refs_4_), channel_id=1, source_target_pairs={{0,2},{1,3},{2,0},{3,1},{4,6},{5,7},{6,4},{7,5},{8,10},{9,11},{10,... | collective-permute-start | bytes 245768 | tf_op jit(solution)/shard_map/ppermute | solution.py:315
  16.4 9.6 %all-to-all-start = ((bf16[4,64,384]{2,1,0:T(8,128)(2,1)}), bf16[4,64,384]{2,1,0:T(8,128)(2,1)S(1)}, u32[]{:S(2)}, u32[]{:S(2)}) async-start(bf16[4,64,384]{2,1,0:T(8,128)(2,1)} %broadcast_in_dim.20), calls=%async_computation | async-start | bytes 393216 | tf_op jit(solution)/shard_map/all_to_all | solution.py:341
  20.5 1.3 collective-permute-start.1
  20.6 5.6 %collective-permute-start.2 = (bf16[4,80,128]{2,1,0:T(8,128)(2,1)S(1)}, bf16[4,80,128]{2,1,0:T(8,128)(2,1)S(1)}, u32[]{:S(2)}, u32[]{:S(2)}) collective-permute-start(bf16[4,80,128]{2,1,0:T(8,128)(2,1)S(1)} %collective-permute-done.refs_0_.refs_5_), channel_id=1, source_target_pairs={{0,1},{1,0},{2,3},{3,2},{4,5},{5,4},{6,7},{7,6},{8,9},{9,8},{10,11... | collective-permute-start | bytes 245768 | tf_op jit(solution)/shard_map/ppermute | solution.py:315
  129.5 3.7 %collective-permute-start.3 = (f32[1,2048]{1,0:T(1,128)S(1)}, f32[1,2048]{1,0:T(1,128)S(1)}, u32[]{:S(2)}, u32[]{:S(2)}) collective-permute-start(f32[1,2048]{1,0:T(1,128)S(1)} %get-tuple-element.35.refs_0_), channel_id=1, source_target_pairs={{0,2},{1,3},{2,0},{3,1},{4,6},{5,7},{6,4},{7,5},{8,10},{9,11},{10,... | collective-permute-start | bytes 24584 | tf_op jit(solution)/shard_map/ppermute | solution.py:315
  130.1 3.1 %collective-permute-start.4 = (f32[1,2048]{1,0:T(1,128)S(1)}, f32[1,2048]{1,0:T(1,128)S(1)}, u32[]{:S(2)}, u32[]{:S(2)}) collective-permute-start(f32[1,2048]{1,0:T(1,128)S(1)} %get-tuple-element.35.refs_0_), channel_id=1, source_target_pairs={{0,1},{1,0},{2,3},{3,2},{4,5},{5,4},{6,7},{7,6},{8,9},{9,8},{10,11... | collective-permute-start | bytes 24584 | tf_op jit(solution)/shard_map/ppermute | solution.py:315
  133.2 1.2 collective-permute-start.5
  236.1 3.7 %collective-permute-start.6 = (f32[1,2048]{1,0:T(1,128)S(1)}, f32[1,2048]{1,0:T(1,128)S(1)}, u32[]{:S(2)}, u32[]{:S(2)}) collective-permute-start(f32[1,2048]{1,0:T(1,128)S(1)} %get-tuple-element.37.refs_0_), channel_id=1, source_target_pairs={{0,2},{1,3},{2,0},{3,1},{4,6},{5,7},{6,4},{7,5},{8,10},{9,11},{10,... | collective-permute-start | bytes 24584 | tf_op jit(solution)/shard_map/ppermute | solution.py:315
  236.7 3.1 %collective-permute-start.7 = (f32[1,2048]{1,0:T(1,128)S(1)}, f32[1,2048]{1,0:T(1,128)S(1)}, u32[]{:S(2)}, u32[]{:S(2)}) collective-permute-start(f32[1,2048]{1,0:T(1,128)S(1)} %get-tuple-element.37.refs_0_), channel_id=1, source_target_pairs={{0,1},{1,0},{2,3},{3,2},{4,5},{5,4},{6,7},{7,6},{8,9},{9,8},{10,11... | collective-permute-start | bytes 24584 | tf_op jit(solution)/shard_map/ppermute | solution.py:315
  239.8 1.2 collective-permute-start.8

commit v11 on v9

--- a/solution.py
+++ b/solution.py
@@ -333,10 +333,15 @@
     return parts
 
 
-def gather_line(block, count):
+def gather_line(block, later, count):
     parts = [block[None]]
-    for low, width in chip_stages(count)[:-1]:
-        parts = gather_stage(parts, count, low, width)
+    for place, (low, width) in enumerate(chip_stages(count)[:-1]):
+        if place == 0:
+            for digit in range(1, 1 << width):
+                source = block if digit <= 2 else later
+                parts = parts + [swap(source[None], count, digit << low)]
+        else:
+            parts = gather_stage(parts, count, low, width)
     return jnp.concatenate(parts, axis=0)
 
 
@@ -384,6 +389,7 @@
     packed, points = lax.optimization_barrier((packed, source_points))
     mine = gather_chips(packed, count)
     theirs = [swap(part, count, 1) for part in mine]
+    later, _ = lax.optimization_barrier((points, mine[0]))
     parts, low = len(mine), chip_stages(count)[-1][0]
     ts = mine + theirs
     (taug_mine,) = call(
@@ -401,7 +407,7 @@
         [inverse_eps] + mine[1:],
         [staged_shape(mine[1:])],
     )
-    xs = gather_line(points, count)
+    xs = gather_line(points, later, count)
     logws = logw_line(mine[:1])
     rows = logws.shape[1]
 
@@ -426,8 +432,8 @@
     flips = [(core, digit) for core in range(2) for digit in range(parts)]
 
     def exchange(own):
-        held = [own] + [swap(own, count, digit << low) for digit in range(1, parts)]
-        return held + [swap(value, count, 1) for value in held]
+        steps = [core | (digit << low) for core, digit in flips]
+        return [own] + [swap(own, count, step) for step in steps[1:]]
 
     g = logw
     for _ in range(ITERS - 1):

time: 236 us -> 238 us (level)
  no operation moved by 1% of the time
where the time goes in v11:
time: 238 us
  Pallas kernels  209 us (88%)
  starting transfers between devices  16.7 us (7%)
  waiting for transfers between devices  10.2 us (4%)
    pallas_call x6, Pallas kernels, call(): pl.pallas_call(kernel, out_shape=outs, in_specs=[smem] * scalars + [vmem]...  209 us
    ppermute x15, starting transfers between devices, swap(): lax.ppermute(value, AXIS, [(source, source ^ step) for source in range(co...  16.7 us
    ppermute x15, waiting for transfers between devices, swap(): lax.ppermute(value, AXIS, [(source, source ^ step) for source in range(co...  10.2 us
  transfers between devices with their start and end apart: 15, of which 6 were waited for; matrix products, arithmetic and copies ran while one was open for 0% of the time, Pallas kernels for 0%

profile of v11, /device:TPU:0, one launch (start us, length us, event | category | flops | bytes accessed | tf_op | source)
XLA Modules:
  0.0 237.9 jit_solution(17466315436129308266)
XLA Ops:
  0.6 0.0 copy-start
  0.6 0.1 pad.11.clone
  0.7 0.8 maximum_maximum_fusion
  1.6 5.1 %collective-permute-start.2 = (bf16[1,80,128]{2,1,0:T(8,128)(2,1)S(1)}, bf16[1,80,128]{2,1,0:T(8,128)(2,1)S(1)}, u32[]{:S(2)}, u32[]{:S(2)}) collective-permute-start(bf16[1,80,128]{2,1,0:T(8,128)(2,1)S(1)} %bitcast.6), channel_id=1, source_target_pairs={{0,12},{1,13},{2,14},{3,15},{4,8},{5,9},{6,10},{7,11},{8,4},{9,5},... | collective-permute-start | bytes 61448 | tf_op jit(solution)/shard_map/ppermute | solution.py:312
  6.7 0.0 collective-permute-start.1
  6.7 0.6 collective-permute-start
  7.3 0.0 copy-done
  7.3 2.3 collective-permute-start.4
  9.6 2.0 collective-permute-start.3
  12.3 0.0 collective-permute-done.2
  12.3 0.0 collective-permute-done.1
  12.3 0.0 collective-permute-done
  12.3 1.6 collective-permute-start.6
  13.9 0.7 collective-permute-start.5
  14.6 0.0 collective-permute-start.7
  14.6 0.3 shard_map.68.mine
  14.8 2.0 collective-permute-done.6.refs_0_.refs_1_.refs_5_
  16.8 0.0 collective-permute-start.8
  16.8 0.0 collective-permute-done.4
  16.8 0.0 collective-permute-done.3
  16.8 2.9 %collective-permute-done.5 = bf16[1,64,384]{2,1,0:T(8,128)(2,1)S(1)} collective-permute-done((bf16[1,64,384]{2,1,0:T(8,128)(2,1)S(1)}, bf16[1,64,384]{2,1,0:T(8,128)(2,1)S(1)}, u32[]{:S(2)}, u32[]{:S(2)}) %collective-permute-start.5) | collective-permute-done | bytes 49184 | tf_op jit(solution)/shard_map/ppermute | solution.py:312
  19.8 0.3 shard_map.69.rest
  20.1 0.0 collective-permute-done.7.refs_0_.refs_2_.refs_6_
  20.1 0.3 shard_map.70.theirs
  20.4 0.0 collective-permute-done.8.refs_3_.refs_7_
  20.4 101.8 %shard_map.71 = (bf16[256,1536]{1,0:T(8,128)(2,1)S(1)}, bf16[2048,256]{1,0:T(8,128)(2,1)S(1)}, f32[1,2048]{1,0:T(1,128)S(1)}, f32[1,2048]{1,0:T(1,128)S(1)}, f32[1,2048]{1,0:T(1,128)S(1)}) custom-call(f32[1]{0:T(128)S(6)} %copy.7.inverse, f32[1,1536]{1,0:T(1,128)S(1)} %reshape.27.logws, bf16[4,64,384]{2,1,0:T(8,128)(2,1)S(1)} %pad_maximum_fusion.xs, ...), custom_call_target="tpu_custom_call" | custom-call | tf_op jit(solution)/shard_map/pallas_call | solution.py:372
  122.2 0.1 collective-permute-start.11
  122.3 0.6 collective-permute-start.10
  122.9 1.5 collective-permute-start.9
  124.4 0.9 collective-permute-done.11.refs_3_
  125.4 0.0 collective-permute-done.10.refs_2_
  125.4 1.2 collective-permute-done.9.refs_1_
  126.6 101.7 %shard_map.72 = (f32[1,2048]{1,0:T(1,128)S(1)}, f32[1,2048]{1,0:T(1,128)S(1)}) custom-call(f32[1,1536]{1,0:T(1,128)S(1)} %reshape.27.logws, bf16[256,1536]{1,0:T(8,128)(2,1)S(1)} %get-tuple-element.17.xaug, bf16[2048,256]{1,0:T(8,128)(2,1)S(1)} %get-tuple-element.18.old, f32[1,2048]{1,0:T(1,128)S(1)} %get-tuple-element.19.g.logw, ...), custom_call_target="tpu_custom_call" | custom-call | tf_op jit(solution)/shard_map/pallas_call | solution.py:372
  228.3 0.1 collective-permute-start.14
  228.4 1.6 collective-permute-start.13
  230.0 0.5 collective-permute-start.12
  230.5 1.0 collective-permute-done.14.refs_3_
  231.5 0.0 collective-permute-done.13.refs_2_
  231.5 2.1 collective-permute-done.12.refs_1_
  233.6 4.3 %shard_map.73 = (f32[64,384]{1,0:T(8,128)}, f32[1,128]{1,0:T(1,128)}) custom-call(bf16[256,1536]{1,0:T(8,128)(2,1)S(1)} %get-tuple-element.17.xaug, bf16[2048,256]{1,0:T(8,128)(2,1)S(1)} %get-tuple-element.18.old, f32[1,2048]{1,0:T(1,128)S(1)} %get-tuple-element.22.g, f32[1,2048]{1,0:T(1,128)S(1)} %get-tuple-element.20.q, ...), custom_call_target="tpu_custom_call" | custom-call | tf_op jit(solution)/shard_map/pallas_call | solution.py:372
  (5 shorter events, 0.1 us)
Async XLA Ops:
  0.6 6.7 %copy-start = (bf16[64,384]{1,0:T(8,128)(2,1)S(1)}, bf16[64,384]{1,0:T(8,128)(2,1)}, u32[]{:S(2)}) copy-start(bf16[64,384]{1,0:T(8,128)(2,1)} %param.5) | copy-start | bytes 147460
  1.6 10.7 %collective-permute-start.2 = (bf16[1,80,128]{2,1,0:T(8,128)(2,1)S(1)}, bf16[1,80,128]{2,1,0:T(8,128)(2,1)S(1)}, u32[]{:S(2)}, u32[]{:S(2)}) collective-permute-start(bf16[1,80,128]{2,1,0:T(8,128)(2,1)S(1)} %bitcast.6), channel_id=1, source_target_pairs={{0,12},{1,13},{2,14},{3,15},{4,8},{5,9},{6,10},{7,11},{8,4},{9,5},... | collective-permute-start | bytes 61448 | tf_op jit(solution)/shard_map/ppermute | solution.py:312
  6.7 5.6 %collective-permute-start.1 = (bf16[1,80,128]{2,1,0:T(8,128)(2,1)S(1)}, bf16[1,80,128]{2,1,0:T(8,128)(2,1)S(1)}, u32[]{:S(2)}, u32[]{:S(2)}) collective-permute-start(bf16[1,80,128]{2,1,0:T(8,128)(2,1)S(1)} %bitcast.7), channel_id=1, source_target_pairs={{0,8},{1,9},{2,10},{3,11},{4,12},{5,13},{6,14},{7,15},{8,0},{9,1},... | collective-permute-start | bytes 61448 | tf_op jit(solution)/shard_map/ppermute | solution.py:312
  6.7 5.6 %collective-permute-start = (bf16[1,80,128]{2,1,0:T(8,128)(2,1)S(1)}, bf16[1,80,128]{2,1,0:T(8,128)(2,1)S(1)}, u32[]{:S(2)}, u32[]{:S(2)}) collective-permute-start(bf16[1,80,128]{2,1,0:T(8,128)(2,1)S(1)} %bitcast.8), channel_id=1, source_target_pairs={{0,4},{1,5},{2,6},{3,7},{4,0},{5,1},{6,2},{7,3},{8,12},{9,13},{10,... | collective-permute-start | bytes 61448 | tf_op jit(solution)/shard_map/ppermute | solution.py:312
  7.3 9.5 %collective-permute-start.4 = (bf16[1,64,384]{2,1,0:T(8,128)(2,1)S(1)}, bf16[1,64,384]{2,1,0:T(8,128)(2,1)S(1)}, u32[]{:S(2)}, u32[]{:S(2)}) collective-permute-start(bf16[1,64,384]{2,1,0:T(8,128)(2,1)S(1)} %bitcast.10), channel_id=1, source_target_pairs={{0,8},{1,9},{2,10},{3,11},{4,12},{5,13},{6,14},{7,15},{8,0},{9,1},... | collective-permute-start | bytes 147464 | tf_op jit(solution)/shard_map/ppermute | solution.py:312
  9.6 7.2 %collective-permute-start.3 = (bf16[1,64,384]{2,1,0:T(8,128)(2,1)S(1)}, bf16[1,64,384]{2,1,0:T(8,128)(2,1)S(1)}, u32[]{:S(2)}, u32[]{:S(2)}) collective-permute-start(bf16[1,64,384]{2,1,0:T(8,128)(2,1)S(1)} %bitcast.11), channel_id=1, source_target_pairs={{0,4},{1,5},{2,6},{3,7},{4,0},{5,1},{6,2},{7,3},{8,12},{9,13},{10,... | collective-permute-start | bytes 147464 | tf_op jit(solution)/shard_map/ppermute | solution.py:312
  12.3 4.5 %collective-permute-start.6 = (bf16[4,80,128]{2,1,0:T(8,128)(2,1)S(1)}, bf16[4,80,128]{2,1,0:T(8,128)(2,1)S(1)}, u32[]{:S(2)}, u32[]{:S(2)}) collective-permute-start(bf16[4,80,128]{2,1,0:T(8,128)(2,1)S(1)} %pad_maximum_fusion.1.refs_0_.refs_4_), channel_id=1, source_target_pairs={{0,2},{1,3},{2,0},{3,1},{4,6},{5,7},{6,4},{7,5},{8,10},{9,11},{10,... | collective-permute-start | bytes 245768 | tf_op jit(solution)/shard_map/ppermute | solution.py:312
  13.9 5.9 %collective-permute-start.5 = (bf16[1,64,384]{2,1,0:T(8,128)(2,1)S(1)}, bf16[1,64,384]{2,1,0:T(8,128)(2,1)S(1)}, u32[]{:S(2)}, u32[]{:S(2)}) collective-permute-start(bf16[1,64,384]{2,1,0:T(8,128)(2,1)S(1)} %bitcast.12), channel_id=1, source_target_pairs={{0,12},{1,13},{2,14},{3,15},{4,8},{5,9},{6,10},{7,11},{8,4},{9,5},... | collective-permute-start | bytes 147464 | tf_op jit(solution)/shard_map/ppermute | solution.py:312
  14.6 5.5 %collective-permute-start.7 = (bf16[4,80,128]{2,1,0:T(8,128)(2,1)S(1)}, bf16[4,80,128]{2,1,0:T(8,128)(2,1)S(1)}, u32[]{:S(2)}, u32[]{:S(2)}) collective-permute-start(bf16[4,80,128]{2,1,0:T(8,128)(2,1)S(1)} %pad_maximum_fusion.1.refs_0_.refs_4_), channel_id=1, source_target_pairs={{0,1},{1,0},{2,3},{3,2},{4,5},{5,4},{6,7},{7,6},{8,9},{9,8},{10,11... | collective-permute-start | bytes 245768 | tf_op jit(solution)/shard_map/ppermute | solution.py:312
  16.8 3.5 %collective-permute-start.8 = (bf16[4,80,128]{2,1,0:T(8,128)(2,1)S(1)}, bf16[4,80,128]{2,1,0:T(8,128)(2,1)S(1)}, u32[]{:S(2)}, u32[]{:S(2)}) collective-permute-start(bf16[4,80,128]{2,1,0:T(8,128)(2,1)S(1)} %collective-permute-done.6.refs_0_.refs_1_.refs_5_), channel_id=1, source_target_pairs={{0,1},{1,0},{2,3},{3,2},{4,5},{5,4},{6,7},{7,6},{8,9},{9,8},{10,11... | collective-permute-start | bytes 245768 | tf_op jit(solution)/shard_map/ppermute | solution.py:312
  122.2 3.1 %collective-permute-start.11 = (f32[1,2048]{1,0:T(1,128)S(1)}, f32[1,2048]{1,0:T(1,128)S(1)}, u32[]{:S(2)}, u32[]{:S(2)}) collective-permute-start(f32[1,2048]{1,0:T(1,128)S(1)} %get-tuple-element.21.refs_0_), channel_id=1, source_target_pairs={{0,3},{1,2},{2,1},{3,0},{4,7},{5,6},{6,5},{7,4},{8,11},{9,10},{10,... | collective-permute-start | bytes 24584 | tf_op jit(solution)/shard_map/ppermute | solution.py:312
  122.3 3.1 %collective-permute-start.10 = (f32[1,2048]{1,0:T(1,128)S(1)}, f32[1,2048]{1,0:T(1,128)S(1)}, u32[]{:S(2)}, u32[]{:S(2)}) collective-permute-start(f32[1,2048]{1,0:T(1,128)S(1)} %get-tuple-element.21.refs_0_), channel_id=1, source_target_pairs={{0,1},{1,0},{2,3},{3,2},{4,5},{5,4},{6,7},{7,6},{8,9},{9,8},{10,11... | collective-permute-start | bytes 24584 | tf_op jit(solution)/shard_map/ppermute | solution.py:312
  122.9 3.7 %collective-permute-start.9 = (f32[1,2048]{1,0:T(1,128)S(1)}, f32[1,2048]{1,0:T(1,128)S(1)}, u32[]{:S(2)}, u32[]{:S(2)}) collective-permute-start(f32[1,2048]{1,0:T(1,128)S(1)} %get-tuple-element.21.refs_0_), channel_id=1, source_target_pairs={{0,2},{1,3},{2,0},{3,1},{4,6},{5,7},{6,4},{7,5},{8,10},{9,11},{10,... | collective-permute-start | bytes 24584 | tf_op jit(solution)/shard_map/ppermute | solution.py:312
  228.3 3.2 %collective-permute-start.14 = (f32[1,2048]{1,0:T(1,128)S(1)}, f32[1,2048]{1,0:T(1,128)S(1)}, u32[]{:S(2)}, u32[]{:S(2)}) collective-permute-start(f32[1,2048]{1,0:T(1,128)S(1)} %get-tuple-element.23.refs_0_), channel_id=1, source_target_pairs={{0,3},{1,2},{2,1},{3,0},{4,7},{5,6},{6,5},{7,4},{8,11},{9,10},{10,... | collective-permute-start | bytes 24584 | tf_op jit(solution)/shard_map/ppermute | solution.py:312
  228.4 3.1 %collective-permute-start.13 = (f32[1,2048]{1,0:T(1,128)S(1)}, f32[1,2048]{1,0:T(1,128)S(1)}, u32[]{:S(2)}, u32[]{:S(2)}) collective-permute-start(f32[1,2048]{1,0:T(1,128)S(1)} %get-tuple-element.23.refs_0_), channel_id=1, source_target_pairs={{0,1},{1,0},{2,3},{3,2},{4,5},{5,4},{6,7},{7,6},{8,9},{9,8},{10,11... | collective-permute-start | bytes 24584 | tf_op jit(solution)/shard_map/ppermute | solution.py:312
  230.0 3.7 %collective-permute-start.12 = (f32[1,2048]{1,0:T(1,128)S(1)}, f32[1,2048]{1,0:T(1,128)S(1)}, u32[]{:S(2)}, u32[]{:S(2)}) collective-permute-start(f32[1,2048]{1,0:T(1,128)S(1)} %get-tuple-element.23.refs_0_), channel_id=1, source_target_pairs={{0,2},{1,3},{2,0},{3,1},{4,6},{5,7},{6,4},{7,5},{8,10},{9,11},{10,... | collective-permute-start | bytes 24584 | tf_op jit(solution)/shard_map/ppermute | solution.py:312

commit v12 on v9

--- a/solution.py
+++ b/solution.py
@@ -74,7 +74,7 @@
             begin += LANES
 
 
-def renew_targets(lines, flips, parts, g, q, logw, taug):
+def join_lines(lines, flips, parts, g):
     total = lines[0].shape[1]
     size = total // (2 * parts)
     held = []
@@ -85,14 +85,15 @@
         held.append(jnp.concatenate(pieces, axis=1))
     peak = functools.reduce(jnp.maximum, held)
     added = functools.reduce(jnp.add, [jnp.exp2(value - peak) for value in held])
-    potential = g - (peak + jnp.log2(added))
-    g = potential + logw
+    return g - (peak + jnp.log2(added))
+
+
+def renew_targets(g, q, taug):
     terms = [term.astype(jnp.float32) for term in three_terms(g - jnp.max(g) - q)]
-    for begin in range(0, total, LANES):
+    for begin in range(0, g.shape[1], LANES):
         rows = slice(begin, begin + LANES)
         extras = pick_rows((8, LANES), [term[:, rows] for term in terms] + [1.0])
         taug[rows, 0:8] = extras.T.astype(jnp.bfloat16)
-    return potential, g
 
 
 def exponents(left, right):
@@ -158,6 +159,26 @@
     return jnp.minimum(least, s)
 
 
+def keep_sources(xaug, logws, taug, p_ref, col_ref):
+    total, sources = p_ref.shape
+    width = 2 * LANES
+    held, least = None, None
+    for begin in range(0, sources + width, width):
+
+        def beside(rows):
+            if held is not None:
+                add_columns(p_ref.at[:, begin - width : begin], held, col_ref, rows)
+
+        if begin == sources:
+            for first in range(0, total, LANES):
+                beside(slice(first, first + LANES))
+            return least
+        at = slice(begin, begin + width)
+        s = spread_rows(taug, xaug[:, at], p_ref.at[:, at], beside)
+        held = jnp.exp2(logws[:, at] * LOG2E) / s
+        least = s if least is None else jnp.minimum(least, s)
+
+
 def lane_totals(col_ref, out_ref):
     total = col_ref.shape[0]
     reach = min(total, 2048)
@@ -171,20 +192,20 @@
         out_ref[:, begin : begin + reach] = added[0:1]
 
 
-def finish_sums(xaug, logws, taug, least, p_ref, col_ref, out_ref):
+def finish_sums(xaug, logws, taug, renew, factor, least, top_ref, col_ref, out_ref):
     total = taug.shape[0]
     lane_totals(col_ref, out_ref)
     cols = out_ref[...]
-    out_ref[...] = jnp.log2(cols)
+    out_ref[...] = jnp.log2(cols) + factor
     fine = jnp.logical_and(
         jnp.min(least) >= SMALL_ROW,
         jnp.logical_and(jnp.min(cols) >= SMALL_COL, jnp.max(cols) <= LARGE_COL),
     )
 
-    top_ref = p_ref.at[:, 0:LANES]
 
     @pl.when(jnp.logical_not(fine))
     def _():
+        renew()
         col_ref[...] = jnp.zeros_like(col_ref)
         top_ref[...] = jnp.full_like(top_ref, FLOOR)
         blocks = total // LANES
@@ -239,7 +260,8 @@
 
 def near_kernel(parts, feat, inverse, logws, xs, mine, rest, theirs, *refs):
     ts, refs = refs[: 2 * parts], refs[2 * parts :]
-    xaug, taug, out_ref, g_ref, q_ref, p0, p1, col_ref = refs
+    xaug, taug, out_ref, g_ref, q_ref = refs[:5]
+    p_refs, (col_ref, top_ref) = refs[5:-2], refs[-2:]
     scale = inverse[0] * LOG2E
     stage_sources([xs], scale, xaug)
     place = 0
@@ -254,18 +276,112 @@
         begin += part.shape[0]
     stage_targets(ts[parts + 1 :], scale, taug, begin, feat)
     col_ref[...] = jnp.zeros_like(col_ref)
-    least = add_sources(xaug, logws, taug, (p0, p1), col_ref)
-    finish_sums(xaug, logws, taug, least, p0, col_ref, out_ref)
+    if len(p_refs) == 1:
+        least = keep_sources(xaug, logws, taug, p_refs[0], col_ref)
+    else:
+        least = add_sources(xaug, logws, taug, p_refs, col_ref)
+    finish_sums(xaug, logws, taug, lambda: None, 0.0, least, top_ref, col_ref, out_ref)
 
 
 def next_kernel(flips, parts, logws, xaug, old, g, q, logw, *refs):
     lines, refs = refs[: len(flips)], refs[len(flips) :]
-    out_ref, g_ref, taug, p0, p1, col_ref = refs
+    out_ref, g_ref, taug, p0, p1, col_ref, top_ref = refs
     taug[...] = old[...]
-    g_ref[...] = renew_targets(lines, flips, parts, g[...], q[...], logw[...], taug)[1]
+    g_ref[...] = join_lines(lines, flips, parts, g[...]) + logw[...]
+    renew_targets(g_ref[...], q[...], taug)
     col_ref[...] = jnp.zeros_like(col_ref)
     least = add_sources(xaug, logws, taug, (p0, p1), col_ref)
-    finish_sums(xaug, logws, taug, least, p0, col_ref, out_ref)
+    finish_sums(xaug, logws, taug, lambda: None, 0.0, least, top_ref, col_ref, out_ref)
+
+
+def spread_factors(exponent, factor_ref):
+    f = jnp.exp2(exponent)
+    for begin in range(0, f.shape[1], LANES):
+        rows = slice(begin, begin + LANES)
+        turned = pick_rows((8, LANES), [f[:, rows]]).T
+        factor_ref[rows, :] = jnp.broadcast_to(turned[:, 0:1], (LANES, LANES))
+
+
+def factor_sums(p, factor_ref):
+    total, width = p.shape
+    reach = 4 * LANES
+
+    def advance(step, sums):
+        for inner in range(0, reach, LANES):
+            rows = pl.ds(pl.multiple_of(step * reach + inner, LANES), LANES)
+            factor = factor_ref[rows, :]
+            sums = [
+                held
+                + jnp.sum(
+                    (p[rows, place * LANES : (place + 1) * LANES] * factor).reshape(-1, 8, LANES),
+                    axis=0,
+                )
+                for place, held in enumerate(sums)
+            ]
+        return tuple(sums)
+
+    start = (jnp.zeros((8, LANES), jnp.float32),) * (width // LANES)
+    sums = lax.fori_loop(0, total // reach, advance, start)
+    return [jnp.sum(held, axis=0, keepdims=True) for held in sums]
+
+
+def kept_kernel(flips, parts, logws, xaug, old, g, q, logw, p, *refs):
+    lines, refs = refs[: len(flips)], refs[len(flips) :]
+    out_ref, g_ref, taug, factor_ref, col_ref, top_ref = refs
+    potential = join_lines(lines, flips, parts, g[...])
+    g_ref[...] = potential + logw[...]
+    change = potential - jnp.max(potential)
+    spread_factors(change, factor_ref)
+    sums = factor_sums(p, factor_ref)
+    tiles = [slice(place * LANES, (place + 1) * LANES) for place in range(len(sums))]
+    weights = [
+        jnp.broadcast_to(jnp.exp2(logws[:, tile] * LOG2E) / s, (8, LANES))
+        for tile, s in zip(tiles, sums)
+    ]
+    reach = 4 * LANES
+
+    def collect(step, carry):
+        for inner in range(0, reach, LANES):
+            rows = pl.ds(pl.multiple_of(step * reach + inner, LANES), LANES)
+            added = [
+                p[rows, tile].reshape(-1, 8, LANES) * weight[None]
+                for tile, weight in zip(tiles, weights)
+            ]
+            col_ref[rows, :] = functools.reduce(jnp.add, added).reshape(LANES, LANES)
+        return carry
+
+    lax.fori_loop(0, p.shape[0] // reach, collect, 0)
+
+    def renew():
+        taug[...] = old[...]
+        renew_targets(g_ref[...], q[...], taug)
+
+    least = functools.reduce(jnp.minimum, sums)
+    finish_sums(xaug, logws, taug, renew, change, least, top_ref, col_ref, out_ref)
+
+
+def write_coords(ts, feat, coords):
+    begin = 0
+    for part in ts:
+        for block in range(part.shape[0]):
+            coords[:, begin : begin + LANES] = part[block, :feat, :]
+            begin += LANES
+
+
+def careful_plan(taug, right, p_ref, plan_ref):
+    total = taug.shape[0]
+    reach = min(total, 2048)
+    pieces = [slice(begin, begin + reach) for begin in range(0, total, reach)]
+    peak = jnp.full((1, p_ref.shape[1]), FLOOR, jnp.float32)
+    for rows in pieces:
+        p_ref[rows, :] = exponents(taug[rows, :], right)
+        peak = jnp.maximum(peak, jnp.max(p_ref[rows, :], axis=0, keepdims=True))
+    sums = jnp.zeros(peak.shape, jnp.float32)
+    for rows in pieces:
+        sums += jnp.sum(jnp.exp2(p_ref[rows, :] - peak), axis=0, keepdims=True)
+    shift = peak + jnp.log2(sums)
+    for rows in pieces:
+        plan_ref[rows, :] = jnp.exp2(p_ref[rows, :] - shift).astype(jnp.bfloat16)
 
 
 def map_kernel(flips, parts, n_t, feat, xaug, old, g, q, logw, *refs):
@@ -273,13 +389,10 @@
     ts = refs[:n_t]
     mapped_ref, pot_ref, taug, p_ref, plan_ref, coords = refs[n_t:]
     taug[...] = old[...]
-    potential = renew_targets(lines, flips, parts, g[...], q[...], logw[...], taug)[0]
+    potential = join_lines(lines, flips, parts, g[...])
+    renew_targets(potential + logw[...], q[...], taug)
     pot_ref[...] = potential[:, :LANES] * (1.0 / LOG2E)
-    place = 0
-    for part in ts:
-        for block in range(part.shape[0]):
-            coords[:, place * LANES : (place + 1) * LANES] = part[block, :feat, :]
-            place += 1
+    write_coords(ts, feat, coords)
     total = taug.shape[0]
     right = xaug[:, : p_ref.shape[1]]
     s = spread_rows(taug, right, p_ref, lambda rows: None)
@@ -290,20 +403,34 @@
 
     @pl.when(jnp.logical_not(jnp.min(s) >= SMALL_ROW))
     def _():
-        reach = min(total, 2048)
-        peak = jnp.full(s.shape, FLOOR, jnp.float32)
-        for begin in range(0, total, reach):
-            rows = slice(begin, begin + reach)
-            p_ref[rows, :] = exponents(taug[rows, :], right)
-            peak = jnp.maximum(peak, jnp.max(p_ref[rows, :], axis=0, keepdims=True))
-        sums = jnp.zeros(s.shape, jnp.float32)
-        for begin in range(0, total, reach):
-            rows = slice(begin, begin + reach)
-            sums += jnp.sum(jnp.exp2(p_ref[rows, :] - peak), axis=0, keepdims=True)
-        shift = peak + jnp.log2(sums)
-        for begin in range(0, total, reach):
-            rows = slice(begin, begin + reach)
-            plan_ref[rows, :] = jnp.exp2(p_ref[rows, :] - shift).astype(jnp.bfloat16)
+        careful_plan(taug, right, p_ref, plan_ref)
+
+    mapped_ref[...] = jnp.dot(coords[...], plan_ref[...], preferred_element_type=jnp.float32)
+
+
+def map_kept_kernel(flips, parts, n_t, feat, xaug, old, g, q, logw, p, *refs):
+    lines, refs = refs[: len(flips)], refs[len(flips) :]
+    ts = refs[:n_t]
+    mapped_ref, pot_ref, taug, p_ref, plan_ref, coords, factor_ref = refs[n_t:]
+    potential = join_lines(lines, flips, parts, g[...])
+    pot_ref[...] = potential[:, :LANES] * (1.0 / LOG2E)
+    write_coords(ts, feat, coords)
+    spread_factors(potential - jnp.max(potential), factor_ref)
+    total, width = p_ref.shape
+    sums = factor_sums(p.at[:, 0:width], factor_ref)
+    for place, s in enumerate(sums):
+        tile = slice(place * LANES, (place + 1) * LANES)
+        weight = 1.0 / s
+        for begin in range(0, total, LANES):
+            rows = slice(begin, begin + LANES)
+            value = p[rows, tile] * factor_ref[rows, :] * weight
+            plan_ref[rows, tile] = value.astype(jnp.bfloat16)
+
+    @pl.when(jnp.logical_not(jnp.min(functools.reduce(jnp.minimum, sums)) >= SMALL_ROW))
+    def _():
+        taug[...] = old[...]
+        renew_targets(potential + logw[...], q[...], taug)
+        careful_plan(taug, xaug[:, 0:width], p_ref, plan_ref)
 
     mapped_ref[...] = jnp.dot(coords[...], plan_ref[...], preferred_element_type=jnp.float32)
 
@@ -357,7 +484,6 @@
     f32, bf16 = jnp.float32, jnp.bfloat16
     total = count * own_targets
     small = total <= 4096
-    width = 2 * LANES if small else LANES
     vmem = pl.BlockSpec(memory_space=pltpu.VMEM)
     smem = pl.BlockSpec(memory_space=pltpu.SMEM)
     params = pltpu.CompilerParams(vmem_limit_bytes=(24 if small else 63) << 20)
@@ -405,13 +531,16 @@
     logws = logw_line(mine[:1])
     rows = logws.shape[1]
 
-    p_scratch = pltpu.VMEM((total, width), f32)
-    scratch = [
-        p_scratch,
-        p_scratch if small else pltpu.VMEM((8, LANES), f32),
-        pltpu.VMEM((total, LANES), f32),
-    ]
-    xaug, taug, sums, logw, q = call(
+    flips = [(core, digit) for digit in range(parts) for core in range(2)]
+    kept = [jax.ShapeDtypeStruct((total, rows), f32)] if small else []
+    lanes_scratch = pltpu.VMEM((total, LANES), f32)
+    taug_scratch = pltpu.VMEM((total, DEPTH), bf16)
+    p_scratch = [] if small else [pltpu.VMEM((total, LANES), f32), pltpu.VMEM((8, LANES), f32)]
+
+    def exchange(own):
+        return [own] + [swap(own, count, core | (digit << low)) for core, digit in flips[1:]]
+
+    xaug, taug, sums, logw, q, *p = call(
         functools.partial(near_kernel, parts, feat),
         [inverse_eps, logws, xs, taug_mine, taug_rest, taug_theirs] + ts,
         [
@@ -420,37 +549,35 @@
             line,
             line,
             line,
-        ],
-        scratch,
-    )
-    flips = [(core, digit) for core in range(2) for digit in range(parts)]
-
-    def exchange(own):
-        held = [own] + [swap(own, count, digit << low) for digit in range(1, parts)]
-        return held + [swap(value, count, 1) for value in held]
-
+        ]
+        + kept,
+        p_scratch + [lanes_scratch, lanes_scratch],
+    )
     g = logw
     for _ in range(ITERS - 1):
         sums, g = call(
-            functools.partial(next_kernel, flips, parts),
-            [logws, xaug, taug, g, q, logw] + exchange(sums),
+            functools.partial(kept_kernel if small else next_kernel, flips, parts),
+            [logws, xaug, taug, g, q, logw] + p + exchange(sums),
             [line, line],
-            [pltpu.VMEM((total, DEPTH), bf16)] + scratch,
+            [taug_scratch]
+            + ([lanes_scratch] if small else p_scratch)
+            + [lanes_scratch, lanes_scratch],
             scalars=0,
         )
     mapped, potential = call(
-        functools.partial(map_kernel, flips, parts, len(ts), feat),
-        [xaug if small else xaug[:, :own_sources], taug, g, q, logw] + exchange(sums) + ts,
+        functools.partial(map_kept_kernel if small else map_kernel, flips, parts, len(ts), feat),
+        [xaug if small else xaug[:, :own_sources], taug, g, q, logw] + p + exchange(sums) + ts,
         [
             jax.ShapeDtypeStruct((feat, own_sources), f32),
             jax.ShapeDtypeStruct((1, own_targets), f32),
         ],
         [
-            pltpu.VMEM((total, DEPTH), bf16),
+            taug_scratch,
             pltpu.VMEM((total, own_sources), f32),
             pltpu.VMEM((total, own_sources), bf16),
             pltpu.VMEM((feat, total), bf16),
-        ],
+        ]
+        + ([lanes_scratch] if small else []),
         scalars=0,
     )
     return (mapped, potential.reshape(own_targets))

time: 236 us -> 241 us (1.021)
  Pallas kernels: 209 us -> 214 us
    pallas_call x6, Pallas kernels: 209 us -> 214 us  [call(): pl.pallas_call(kernel, out_shape=outs, in_specs=[smem] * scalars + [vmem]...]
  transfers between devices with their start and end apart: 15 -> 15, of which waited for: 6 -> 5; matrix products, arithmetic and copies ran while one was open for 0% -> 0% of each run, Pallas kernels for 0% -> 0%
where the time goes in v12:
time: 241 us
  Pallas kernels  214 us (89%)
  starting transfers between devices  16 us (7%)
  waiting for transfers between devices  7.65 us (3%)
    pallas_call x6, Pallas kernels, call(): pl.pallas_call(kernel, out_shape=outs, in_specs=[smem] * scalars + [vmem]...  214 us
    ppermute x15, starting transfers between devices, swap(): lax.ppermute(value, AXIS, [(source, source ^ step) for source in range(co...  16 us
    ppermute x15, waiting for transfers between devices, swap(): lax.ppermute(value, AXIS, [(source, source ^ step) for source in range(co...  7.65 us
  transfers between devices with their start and end apart: 15, of which 5 were waited for; matrix products, arithmetic and copies ran while one was open for 0% of the time, Pallas kernels for 0%

profile of v12, /device:TPU:0, one launch (start us, length us, event | category | flops | bytes accessed | tf_op | source)
XLA Modules:
  0.0 240.6 jit_solution(16462688963242303927)
XLA Ops:
  0.6 0.1 pad.11.clone
  0.7 0.8 maximum_maximum_fusion
  1.5 5.1 %collective-permute-start.2 = (bf16[1,80,128]{2,1,0:T(8,128)(2,1)S(1)}, bf16[1,80,128]{2,1,0:T(8,128)(2,1)S(1)}, u32[]{:S(2)}, u32[]{:S(2)}) collective-permute-start(bf16[1,80,128]{2,1,0:T(8,128)(2,1)S(1)} %bitcast.5), channel_id=1, source_target_pairs={{0,12},{1,13},{2,14},{3,15},{4,8},{5,9},{6,10},{7,11},{8,4},{9,5},... | collective-permute-start | bytes 61448 | tf_op jit(solution)/shard_map/ppermute | solution.py:439
  6.7 0.0 collective-permute-start.1
  6.7 0.6 collective-permute-start
  7.3 3.7 %collective-permute-start.5 = (bf16[1,64,384]{2,1,0:T(8,128)(2,1)}, bf16[1,64,384]{2,1,0:T(8,128)(2,1)S(1)}, u32[]{:S(2)}, u32[]{:S(2)}) collective-permute-start(bf16[1,64,384]{2,1,0:T(8,128)(2,1)} %bitcast.9), channel_id=1, source_target_pairs={{0,12},{1,13},{2,14},{3,15},{4,8},{5,9},{6,10},{7,11},{8,4},{9,5},... | collective-permute-start | bytes 147464 | tf_op jit(solution)/shard_map/ppermute | solution.py:439
  11.0 0.0 collective-permute-start.4
  11.7 0.0 collective-permute-done.2
  11.7 0.7 collective-permute-start.3
  12.4 0.0 collective-permute-done.1
  12.4 0.0 collective-permute-done
  12.4 1.7 collective-permute-start.6
  14.1 0.0 collective-permute-start.7
  14.2 0.3 shard_map.68.mine
  14.4 2.5 %collective-permute-done.6.refs_0_.refs_1_.refs_5_ = bf16[4,80,128]{2,1,0:T(8,128)(2,1)S(1)} collective-permute-done((bf16[4,80,128]{2,1,0:T(8,128)(2,1)S(1)}, bf16[4,80,128]{2,1,0:T(8,128)(2,1)S(1)}, u32[]{:S(2)}, u32[]{:S(2)}) %collective-permute-start.6) | collective-permute-done | bytes 81952 | tf_op jit(solution)/shard_map/ppermute | solution.py:439
  16.9 0.0 collective-permute-start.8
  16.9 0.0 collective-permute-done.5
  17.0 0.0 collective-permute-done.4
  17.0 0.0 collective-permute-done.3
  17.0 0.8 pad_maximum_fusion.xs
  17.8 0.3 shard_map.69.rest
  18.1 0.0 collective-permute-done.7.refs_0_.refs_2_.refs_6_
  18.1 0.3 shard_map.70.theirs
  18.4 0.0 collective-permute-done.8.refs_3_.refs_7_
  18.4 104.9 %shard_map.71 = (bf16[256,1536]{1,0:T(8,128)(2,1)S(1)}, bf16[2048,256]{1,0:T(8,128)(2,1)S(1)}, f32[1,2048]{1,0:T(1,128)S(1)}, f32[1,2048]{1,0:T(1,128)S(1)}, f32...) custom-call(f32[1]{0:T(128)S(6)} %copy.7.inverse, f32[1,1536]{1,0:T(1,128)S(1)} %reshape.27.logws, ...), custom_call_target="tpu_custom_call" | custom-call | tf_op jit(solution)/shard_map/pallas_call | solution.py:493
  123.3 1.8 collective-permute-start.11
  125.1 0.4 collective-permute-start.10
  125.5 0.0 collective-permute-start.9
  125.5 1.0 collective-permute-done.11.refs_3_
  126.5 2.3 collective-permute-done.10.refs_2_
  128.8 0.0 collective-permute-done.9.refs_1_
  128.8 103.1 %shard_map.72 = (f32[1,2048]{1,0:T(1,128)S(1)}, f32[1,2048]{1,0:T(1,128)S(1)}) custom-call(f32[1,1536]{1,0:T(1,128)S(1)} %reshape.27.logws, bf16[256,1536]{1,0:T(8,128)(2,1)S(1)} %get-tuple-element.16.xaug, bf16[2048,256]{1,0:T(8,128)(2,1)S(1)} %get-tuple-element.17.old, f32[1,2048]{1,0:T(1,128)S(1)} %get-tuple-element.18.g.logw, ...), custom_call_target="tpu_custom_call" | custom-call | tf_op jit(solution)/shard_map/pallas_call | solution.py:493
  231.9 0.1 collective-permute-start.14
  232.0 0.5 collective-permute-start.13
  232.5 1.4 collective-permute-start.12
  233.8 1.2 collective-permute-done.14.refs_3_
  235.1 0.7 collective-permute-done.13.refs_2_
  235.7 0.0 collective-permute-done.12.refs_1_
  235.7 4.9 %shard_map.73 = (f32[64,384]{1,0:T(8,128)}, f32[1,128]{1,0:T(1,128)}) custom-call(bf16[256,1536]{1,0:T(8,128)(2,1)S(1)} %get-tuple-element.16.xaug, bf16[2048,256]{1,0:T(8,128)(2,1)S(1)} %get-tuple-element.17.old, f32[1,2048]{1,0:T(1,128)S(1)} %get-tuple-element.22.g, f32[1,2048]{1,0:T(1,128)S(1)} %get-tuple-element.19.q, ...), custom_call_target="tpu_custom_call" | custom-call | tf_op jit(solution)/shard_map/pallas_call | solution.py:493
  (4 shorter events, 0.0 us)
Async XLA Ops:
  1.5 10.2 %collective-permute-start.2 = (bf16[1,80,128]{2,1,0:T(8,128)(2,1)S(1)}, bf16[1,80,128]{2,1,0:T(8,128)(2,1)S(1)}, u32[]{:S(2)}, u32[]{:S(2)}) collective-permute-start(bf16[1,80,128]{2,1,0:T(8,128)(2,1)S(1)} %bitcast.5), channel_id=1, source_target_pairs={{0,12},{1,13},{2,14},{3,15},{4,8},{5,9},{6,10},{7,11},{8,4},{9,5},... | collective-permute-start | bytes 61448 | tf_op jit(solution)/shard_map/ppermute | solution.py:439
  6.7 5.8 %collective-permute-start.1 = (bf16[1,80,128]{2,1,0:T(8,128)(2,1)S(1)}, bf16[1,80,128]{2,1,0:T(8,128)(2,1)S(1)}, u32[]{:S(2)}, u32[]{:S(2)}) collective-permute-start(bf16[1,80,128]{2,1,0:T(8,128)(2,1)S(1)} %bitcast.6), channel_id=1, source_target_pairs={{0,8},{1,9},{2,10},{3,11},{4,12},{5,13},{6,14},{7,15},{8,0},{9,1},... | collective-permute-start | bytes 61448 | tf_op jit(solution)/shard_map/ppermute | solution.py:439
  6.7 5.8 %collective-permute-start = (bf16[1,80,128]{2,1,0:T(8,128)(2,1)S(1)}, bf16[1,80,128]{2,1,0:T(8,128)(2,1)S(1)}, u32[]{:S(2)}, u32[]{:S(2)}) collective-permute-start(bf16[1,80,128]{2,1,0:T(8,128)(2,1)S(1)} %bitcast.7), channel_id=1, source_target_pairs={{0,4},{1,5},{2,6},{3,7},{4,0},{5,1},{6,2},{7,3},{8,12},{9,13},{10,... | collective-permute-start | bytes 61448 | tf_op jit(solution)/shard_map/ppermute | solution.py:439
  7.3 9.7 %collective-permute-start.5 = (bf16[1,64,384]{2,1,0:T(8,128)(2,1)}, bf16[1,64,384]{2,1,0:T(8,128)(2,1)S(1)}, u32[]{:S(2)}, u32[]{:S(2)}) collective-permute-start(bf16[1,64,384]{2,1,0:T(8,128)(2,1)} %bitcast.9), channel_id=1, source_target_pairs={{0,12},{1,13},{2,14},{3,15},{4,8},{5,9},{6,10},{7,11},{8,4},{9,5},... | collective-permute-start | bytes 147464 | tf_op jit(solution)/shard_map/ppermute | solution.py:439
  11.0 5.9 %collective-permute-start.4 = (bf16[1,64,384]{2,1,0:T(8,128)(2,1)}, bf16[1,64,384]{2,1,0:T(8,128)(2,1)S(1)}, u32[]{:S(2)}, u32[]{:S(2)}) collective-permute-start(bf16[1,64,384]{2,1,0:T(8,128)(2,1)} %bitcast.10), channel_id=1, source_target_pairs={{0,8},{1,9},{2,10},{3,11},{4,12},{5,13},{6,14},{7,15},{8,0},{9,1},... | collective-permute-start | bytes 147464 | tf_op jit(solution)/shard_map/ppermute | solution.py:439
  11.7 5.3 %collective-permute-start.3 = (bf16[1,64,384]{2,1,0:T(8,128)(2,1)}, bf16[1,64,384]{2,1,0:T(8,128)(2,1)S(1)}, u32[]{:S(2)}, u32[]{:S(2)}) collective-permute-start(bf16[1,64,384]{2,1,0:T(8,128)(2,1)} %bitcast.11), channel_id=1, source_target_pairs={{0,4},{1,5},{2,6},{3,7},{4,0},{5,1},{6,2},{7,3},{8,12},{9,13},{10,... | collective-permute-start | bytes 147464 | tf_op jit(solution)/shard_map/ppermute | solution.py:439
  12.4 4.5 %collective-permute-start.6 = (bf16[4,80,128]{2,1,0:T(8,128)(2,1)S(1)}, bf16[4,80,128]{2,1,0:T(8,128)(2,1)S(1)}, u32[]{:S(2)}, u32[]{:S(2)}) collective-permute-start(bf16[4,80,128]{2,1,0:T(8,128)(2,1)S(1)} %pad_maximum_fusion.1.refs_0_.refs_4_), channel_id=1, source_target_pairs={{0,2},{1,3},{2,0},{3,1},{4,6},{5,7},{6,4},{7,5},{8,10},{9,11},{10,... | collective-permute-start | bytes 245768 | tf_op jit(solution)/shard_map/ppermute | solution.py:439
  14.1 3.9 %collective-permute-start.7 = (bf16[4,80,128]{2,1,0:T(8,128)(2,1)S(1)}, bf16[4,80,128]{2,1,0:T(8,128)(2,1)S(1)}, u32[]{:S(2)}, u32[]{:S(2)}) collective-permute-start(bf16[4,80,128]{2,1,0:T(8,128)(2,1)S(1)} %pad_maximum_fusion.1.refs_0_.refs_4_), channel_id=1, source_target_pairs={{0,1},{1,0},{2,3},{3,2},{4,5},{5,4},{6,7},{7,6},{8,9},{9,8},{10,11... | collective-permute-start | bytes 245768 | tf_op jit(solution)/shard_map/ppermute | solution.py:439
  16.9 1.4 collective-permute-start.8
  123.3 3.2 %collective-permute-start.11 = (f32[1,2048]{1,0:T(1,128)S(1)}, f32[1,2048]{1,0:T(1,128)S(1)}, u32[]{:S(2)}, u32[]{:S(2)}) collective-permute-start(f32[1,2048]{1,0:T(1,128)S(1)} %get-tuple-element.21.refs_0_), channel_id=1, source_target_pairs={{0,3},{1,2},{2,1},{3,0},{4,7},{5,6},{6,5},{7,4},{8,11},{9,10},{10,... | collective-permute-start | bytes 24584 | tf_op jit(solution)/shard_map/ppermute | solution.py:439
  125.1 3.7 %collective-permute-start.10 = (f32[1,2048]{1,0:T(1,128)S(1)}, f32[1,2048]{1,0:T(1,128)S(1)}, u32[]{:S(2)}, u32[]{:S(2)}) collective-permute-start(f32[1,2048]{1,0:T(1,128)S(1)} %get-tuple-element.21.refs_0_), channel_id=1, source_target_pairs={{0,2},{1,3},{2,0},{3,1},{4,6},{5,7},{6,4},{7,5},{8,10},{9,11},{10,... | collective-permute-start | bytes 24584 | tf_op jit(solution)/shard_map/ppermute | solution.py:439
  125.5 3.3 %collective-permute-start.9 = (f32[1,2048]{1,0:T(1,128)S(1)}, f32[1,2048]{1,0:T(1,128)S(1)}, u32[]{:S(2)}, u32[]{:S(2)}) collective-permute-start(f32[1,2048]{1,0:T(1,128)S(1)} %get-tuple-element.21.refs_0_), channel_id=1, source_target_pairs={{0,1},{1,0},{2,3},{3,2},{4,5},{5,4},{6,7},{7,6},{8,9},{9,8},{10,11... | collective-permute-start | bytes 24584 | tf_op jit(solution)/shard_map/ppermute | solution.py:439
  231.9 3.1 %collective-permute-start.14 = (f32[1,2048]{1,0:T(1,128)S(1)}, f32[1,2048]{1,0:T(1,128)S(1)}, u32[]{:S(2)}, u32[]{:S(2)}) collective-permute-start(f32[1,2048]{1,0:T(1,128)S(1)} %get-tuple-element.23.refs_0_), channel_id=1, source_target_pairs={{0,3},{1,2},{2,1},{3,0},{4,7},{5,6},{6,5},{7,4},{8,11},{9,10},{10,... | collective-permute-start | bytes 24584 | tf_op jit(solution)/shard_map/ppermute | solution.py:439
  232.0 3.7 %collective-permute-start.13 = (f32[1,2048]{1,0:T(1,128)S(1)}, f32[1,2048]{1,0:T(1,128)S(1)}, u32[]{:S(2)}, u32[]{:S(2)}) collective-permute-start(f32[1,2048]{1,0:T(1,128)S(1)} %get-tuple-element.23.refs_0_), channel_id=1, source_target_pairs={{0,2},{1,3},{2,0},{3,1},{4,6},{5,7},{6,4},{7,5},{8,10},{9,11},{10,... | collective-permute-start | bytes 24584 | tf_op jit(solution)/shard_map/ppermute | solution.py:439
  232.5 3.2 %collective-permute-start.12 = (f32[1,2048]{1,0:T(1,128)S(1)}, f32[1,2048]{1,0:T(1,128)S(1)}, u32[]{:S(2)}, u32[]{:S(2)}) collective-permute-start(f32[1,2048]{1,0:T(1,128)S(1)} %get-tuple-element.23.refs_0_), channel_id=1, source_target_pairs={{0,1},{1,0},{2,3},{3,2},{4,5},{5,4},{6,7},{7,6},{8,9},{9,8},{10,11... | collective-permute-start | bytes 24584 | tf_op jit(solution)/shard_map/ppermute | solution.py:439

commit v13 on v9

--- a/solution.py
+++ b/solution.py
@@ -128,34 +128,28 @@
     return pl.ds(pl.multiple_of(tile * width, width), width)
 
 
-def add_sources(xaug, logws, taug, p_refs, col_ref):
-    total = taug.shape[0]
-    width = p_refs[0].shape[1]
+def add_sources(xaug, logws, taug, p_ref, col_ref):
+    buffers, total, width = p_ref.shape
     tiles = xaug.shape[1] // width
-    if p_refs[1].shape != p_refs[0].shape:
-        p_refs = (p_refs[0], p_refs[0])
-
-    def step(tile, slot, held):
+
+    def step(tile, held):
         def beside(rows):
             if held is not None:
-                add_columns(p_refs[1 - slot], held, col_ref, rows)
+                add_columns(p_ref.at[(tile + 1) % buffers], held, col_ref, rows)
 
         at = tile_columns(tile, width)
-        s = spread_rows(taug, xaug[:, at], p_refs[slot], beside)
+        s = spread_rows(taug, xaug[:, at], p_ref.at[tile % buffers], beside)
         return s, jnp.exp2(logws[:, at] * LOG2E) / s
 
-    def two_steps(pair, carry):
-        least, weight = carry
-        s1, weight1 = step(2 * pair + 1, 1, weight)
-        s0, weight0 = step(2 * pair + 2, 0, weight1)
-        return jnp.minimum(least, jnp.minimum(s0, s1)), weight0
-
-    s, weight = step(0, 0, None)
-    least, weight = lax.fori_loop(0, tiles // 2 - 1, two_steps, (s, weight))
-    s, weight = step(tiles - 1, 1, weight)
+    def advance(tile, carry):
+        s, weight = step(tile, carry[1])
+        return jnp.minimum(carry[0], s), weight
+
+    least, weight = lax.fori_loop(1, tiles, advance, step(0, None))
     for begin in range(0, total, LANES):
-        add_columns(p_refs[1], weight, col_ref, slice(begin, begin + LANES))
-    return jnp.minimum(least, s)
+        rows = slice(begin, begin + LANES)
+        add_columns(p_ref.at[(tiles - 1) % buffers], weight, col_ref, rows)
+    return least
 
 
 def lane_totals(col_ref, out_ref):
@@ -239,7 +233,7 @@
 
 def near_kernel(parts, feat, inverse, logws, xs, mine, rest, theirs, *refs):
     ts, refs = refs[: 2 * parts], refs[2 * parts :]
-    xaug, taug, out_ref, g_ref, q_ref, p0, p1, col_ref = refs
+    xaug, taug, out_ref, g_ref, q_ref, p_ref, col_ref = refs
     scale = inverse[0] * LOG2E
     stage_sources([xs], scale, xaug)
     place = 0
@@ -254,18 +248,18 @@
         begin += part.shape[0]
     stage_targets(ts[parts + 1 :], scale, taug, begin, feat)
     col_ref[...] = jnp.zeros_like(col_ref)
-    least = add_sources(xaug, logws, taug, (p0, p1), col_ref)
-    finish_sums(xaug, logws, taug, least, p0, col_ref, out_ref)
+    least = add_sources(xaug, logws, taug, p_ref, col_ref)
+    finish_sums(xaug, logws, taug, least, p_ref.at[0], col_ref, out_ref)
 
 
 def next_kernel(flips, parts, logws, xaug, old, g, q, logw, *refs):
     lines, refs = refs[: len(flips)], refs[len(flips) :]
-    out_ref, g_ref, taug, p0, p1, col_ref = refs
+    out_ref, g_ref, taug, p_ref, col_ref = refs
     taug[...] = old[...]
     g_ref[...] = renew_targets(lines, flips, parts, g[...], q[...], logw[...], taug)[1]
     col_ref[...] = jnp.zeros_like(col_ref)
-    least = add_sources(xaug, logws, taug, (p0, p1), col_ref)
-    finish_sums(xaug, logws, taug, least, p0, col_ref, out_ref)
+    least = add_sources(xaug, logws, taug, p_ref, col_ref)
+    finish_sums(xaug, logws, taug, least, p_ref.at[0], col_ref, out_ref)
 
 
 def map_kernel(flips, parts, n_t, feat, xaug, old, g, q, logw, *refs):
@@ -405,10 +399,8 @@
     logws = logw_line(mine[:1])
     rows = logws.shape[1]
 
-    p_scratch = pltpu.VMEM((total, width), f32)
     scratch = [
-        p_scratch,
-        p_scratch if small else pltpu.VMEM((8, LANES), f32),
+        pltpu.VMEM((2 if small else 1, total, width), f32),
         pltpu.VMEM((total, LANES), f32),
     ]
     xaug, taug, sums, logw, q = call(
@@ -423,11 +415,10 @@
         ],
         scratch,
     )
-    flips = [(core, digit) for core in range(2) for digit in range(parts)]
+    flips = [(core, digit) for digit in range(parts) for core in range(2)]
 
     def exchange(own):
-        held = [own] + [swap(own, count, digit << low) for digit in range(1, parts)]
-        return held + [swap(value, count, 1) for value in held]
+        return [own] + [swap(own, count, core | (digit << low)) for core, digit in flips[1:]]
 
     g = logw
     for _ in range(ITERS - 1):

time: 236 us -> 245 us (1.038)
  Pallas kernels: 209 us -> 219 us
    pallas_call x6, Pallas kernels: 209 us -> 219 us  [call(): pl.pallas_call(kernel, out_shape=outs, in_specs=[smem] * scalars + [vmem]...]
where the time goes in v13:
time: 245 us
  Pallas kernels  219 us (89%)
  starting transfers between devices  15.8 us (6%)
  waiting for transfers between devices  8.22 us (3%)
    pallas_call x6, Pallas kernels, call(): pl.pallas_call(kernel, out_shape=outs, in_specs=[smem] * scalars + [vmem]...  219 us
    ppermute x15, starting transfers between devices, swap(): lax.ppermute(value, AXIS, [(source, source ^ step) for source in range(co...  15.8 us
    ppermute x15, waiting for transfers between devices, swap(): lax.ppermute(value, AXIS, [(source, source ^ step) for source in range(co...  8.22 us
  transfers between devices with their start and end apart: 15, of which 6 were waited for; matrix products, arithmetic and copies ran while one was open for 0% of the time, Pallas kernels for 0%

profile of v13, /device:TPU:0, one launch (start us, length us, event | category | flops | bytes accessed | tf_op | source)
XLA Modules:
  0.0 245.0 jit_solution(1144777274187522218)
XLA Ops:
  0.6 0.0 copy-start
  0.6 0.1 pad.11.clone
  0.7 0.8 maximum_maximum_fusion
  1.6 5.1 %collective-permute-start.2 = (bf16[1,80,128]{2,1,0:T(8,128)(2,1)S(1)}, bf16[1,80,128]{2,1,0:T(8,128)(2,1)S(1)}, u32[]{:S(2)}, u32[]{:S(2)}) collective-permute-start(bf16[1,80,128]{2,1,0:T(8,128)(2,1)S(1)} %bitcast.5), channel_id=1, source_target_pairs={{0,12},{1,13},{2,14},{3,15},{4,8},{5,9},{6,10},{7,11},{8,4},{9,5},... | collective-permute-start | bytes 61448 | tf_op jit(solution)/shard_map/ppermute | solution.py:306
  6.7 0.0 collective-permute-start.1
  6.7 0.6 collective-permute-start
  7.3 0.0 copy-done
  7.3 3.7 %collective-permute-start.5 = (bf16[1,64,384]{2,1,0:T(8,128)(2,1)S(1)}, bf16[1,64,384]{2,1,0:T(8,128)(2,1)S(1)}, u32[]{:S(2)}, u32[]{:S(2)}) collective-permute-start(bf16[1,64,384]{2,1,0:T(8,128)(2,1)S(1)} %bitcast.9), channel_id=1, source_target_pairs={{0,12},{1,13},{2,14},{3,15},{4,8},{5,9},{6,10},{7,11},{8,4},{9,5},... | collective-permute-start | bytes 147464 | tf_op jit(solution)/shard_map/ppermute | solution.py:306
  11.1 0.0 collective-permute-start.4
  11.7 0.0 collective-permute-done.2
  11.7 0.7 collective-permute-start.3
  12.4 0.0 collective-permute-done.1
  12.4 0.0 collective-permute-done
  12.4 1.7 collective-permute-start.6
  14.2 0.0 collective-permute-start.7
  14.2 0.3 shard_map.68.mine
  14.5 2.5 %collective-permute-done.6.refs_0_.refs_1_.refs_5_ = bf16[4,80,128]{2,1,0:T(8,128)(2,1)S(1)} collective-permute-done((bf16[4,80,128]{2,1,0:T(8,128)(2,1)S(1)}, bf16[4,80,128]{2,1,0:T(8,128)(2,1)S(1)}, u32[]{:S(2)}, u32[]{:S(2)}) %collective-permute-start.6) | collective-permute-done | bytes 81952 | tf_op jit(solution)/shard_map/ppermute | solution.py:306
  17.0 0.0 collective-permute-start.8
  17.0 0.0 collective-permute-done.5
  17.0 0.0 collective-permute-done.4
  17.0 0.0 collective-permute-done.3
  17.0 0.3 shard_map.69.rest
  17.3 0.0 collective-permute-done.7.refs_0_.refs_2_.refs_6_
  17.3 0.3 shard_map.70.theirs
  17.6 0.6 collective-permute-done.8.refs_3_.refs_7_
  18.2 106.1 %shard_map.71 = (bf16[256,1536]{1,0:T(8,128)(2,1)S(1)}, bf16[2048,256]{1,0:T(8,128)(2,1)S(1)}, f32[1,2048]{1,0:T(1,128)S(1)}, f32[1,2048]{1,0:T(1,128)S(1)}, f32[1,2048]{1,0:T(1,128)S(1)}) custom-call(f32[1]{0:T(128)S(6)} %copy.7.inverse, f32[1,1536]{1,0:T(1,128)S(1)} %reshape.27.logws, bf16[4,64,384]{2,1,0:T(8,128)(2,1)S(1)} %pad_maximum_fusion.xs, ...), custom_call_target="tpu_custom_call" | custom-call | tf_op jit(solution)/shard_map/pallas_call | solution.py:361
  124.3 1.4 collective-permute-start.11
  125.8 0.4 collective-permute-start.10
  126.2 0.1 collective-permute-start.9
  126.2 1.2 collective-permute-done.11.refs_3_
  127.5 2.0 collective-permute-done.10.refs_2_
  129.4 0.0 collective-permute-done.9.refs_1_
  129.4 107.5 %shard_map.72 = (f32[1,2048]{1,0:T(1,128)S(1)}, f32[1,2048]{1,0:T(1,128)S(1)}) custom-call(f32[1,1536]{1,0:T(1,128)S(1)} %reshape.27.logws, bf16[256,1536]{1,0:T(8,128)(2,1)S(1)} %get-tuple-element.15.xaug, bf16[2048,256]{1,0:T(8,128)(2,1)S(1)} %get-tuple-element.16.old, f32[1,2048]{1,0:T(1,128)S(1)} %get-tuple-element.17.g.logw, ...), custom_call_target="tpu_custom_call" | custom-call | tf_op jit(solution)/shard_map/pallas_call | solution.py:361
  236.9 0.1 collective-permute-start.14
  237.0 0.8 collective-permute-start.13
  237.8 1.0 collective-permute-start.12
  238.9 1.2 collective-permute-done.14.refs_3_
  240.1 0.7 collective-permute-done.13.refs_2_
  240.7 0.0 collective-permute-done.12.refs_1_
  240.7 4.3 %shard_map.73 = (f32[64,384]{1,0:T(8,128)}, f32[1,128]{1,0:T(1,128)}) custom-call(bf16[256,1536]{1,0:T(8,128)(2,1)S(1)} %get-tuple-element.15.xaug, bf16[2048,256]{1,0:T(8,128)(2,1)S(1)} %get-tuple-element.16.old, f32[1,2048]{1,0:T(1,128)S(1)} %get-tuple-element.20.g, f32[1,2048]{1,0:T(1,128)S(1)} %get-tuple-element.18.q, ...), custom_call_target="tpu_custom_call" | custom-call | tf_op jit(solution)/shard_map/pallas_call | solution.py:361
  (5 shorter events, 0.1 us)
Async XLA Ops:
  0.6 6.7 %copy-start = (bf16[64,384]{1,0:T(8,128)(2,1)S(1)}, bf16[64,384]{1,0:T(8,128)(2,1)}, u32[]{:S(2)}) copy-start(bf16[64,384]{1,0:T(8,128)(2,1)} %param.5) | copy-start | bytes 147460
  1.6 10.2 %collective-permute-start.2 = (bf16[1,80,128]{2,1,0:T(8,128)(2,1)S(1)}, bf16[1,80,128]{2,1,0:T(8,128)(2,1)S(1)}, u32[]{:S(2)}, u32[]{:S(2)}) collective-permute-start(bf16[1,80,128]{2,1,0:T(8,128)(2,1)S(1)} %bitcast.5), channel_id=1, source_target_pairs={{0,12},{1,13},{2,14},{3,15},{4,8},{5,9},{6,10},{7,11},{8,4},{9,5},... | collective-permute-start | bytes 61448 | tf_op jit(solution)/shard_map/ppermute | solution.py:306
  6.7 5.8 %collective-permute-start.1 = (bf16[1,80,128]{2,1,0:T(8,128)(2,1)S(1)}, bf16[1,80,128]{2,1,0:T(8,128)(2,1)S(1)}, u32[]{:S(2)}, u32[]{:S(2)}) collective-permute-start(bf16[1,80,128]{2,1,0:T(8,128)(2,1)S(1)} %bitcast.6), channel_id=1, source_target_pairs={{0,8},{1,9},{2,10},{3,11},{4,12},{5,13},{6,14},{7,15},{8,0},{9,1},... | collective-permute-start | bytes 61448 | tf_op jit(solution)/shard_map/ppermute | solution.py:306
  6.7 5.8 %collective-permute-start = (bf16[1,80,128]{2,1,0:T(8,128)(2,1)S(1)}, bf16[1,80,128]{2,1,0:T(8,128)(2,1)S(1)}, u32[]{:S(2)}, u32[]{:S(2)}) collective-permute-start(bf16[1,80,128]{2,1,0:T(8,128)(2,1)S(1)} %bitcast.7), channel_id=1, source_target_pairs={{0,4},{1,5},{2,6},{3,7},{4,0},{5,1},{6,2},{7,3},{8,12},{9,13},{10,... | collective-permute-start | bytes 61448 | tf_op jit(solution)/shard_map/ppermute | solution.py:306
  7.3 9.7 %collective-permute-start.5 = (bf16[1,64,384]{2,1,0:T(8,128)(2,1)S(1)}, bf16[1,64,384]{2,1,0:T(8,128)(2,1)S(1)}, u32[]{:S(2)}, u32[]{:S(2)}) collective-permute-start(bf16[1,64,384]{2,1,0:T(8,128)(2,1)S(1)} %bitcast.9), channel_id=1, source_target_pairs={{0,12},{1,13},{2,14},{3,15},{4,8},{5,9},{6,10},{7,11},{8,4},{9,5},... | collective-permute-start | bytes 147464 | tf_op jit(solution)/shard_map/ppermute | solution.py:306
  11.1 5.9 %collective-permute-start.4 = (bf16[1,64,384]{2,1,0:T(8,128)(2,1)S(1)}, bf16[1,64,384]{2,1,0:T(8,128)(2,1)S(1)}, u32[]{:S(2)}, u32[]{:S(2)}) collective-permute-start(bf16[1,64,384]{2,1,0:T(8,128)(2,1)S(1)} %bitcast.10), channel_id=1, source_target_pairs={{0,8},{1,9},{2,10},{3,11},{4,12},{5,13},{6,14},{7,15},{8,0},{9,1},... | collective-permute-start | bytes 147464 | tf_op jit(solution)/shard_map/ppermute | solution.py:306
  11.7 5.3 %collective-permute-start.3 = (bf16[1,64,384]{2,1,0:T(8,128)(2,1)S(1)}, bf16[1,64,384]{2,1,0:T(8,128)(2,1)S(1)}, u32[]{:S(2)}, u32[]{:S(2)}) collective-permute-start(bf16[1,64,384]{2,1,0:T(8,128)(2,1)S(1)} %bitcast.11), channel_id=1, source_target_pairs={{0,4},{1,5},{2,6},{3,7},{4,0},{5,1},{6,2},{7,3},{8,12},{9,13},{10,... | collective-permute-start | bytes 147464 | tf_op jit(solution)/shard_map/ppermute | solution.py:306
  12.4 4.5 %collective-permute-start.6 = (bf16[4,80,128]{2,1,0:T(8,128)(2,1)S(1)}, bf16[4,80,128]{2,1,0:T(8,128)(2,1)S(1)}, u32[]{:S(2)}, u32[]{:S(2)}) collective-permute-start(bf16[4,80,128]{2,1,0:T(8,128)(2,1)S(1)} %pad_maximum_fusion.1.refs_0_.refs_4_), channel_id=1, source_target_pairs={{0,2},{1,3},{2,0},{3,1},{4,6},{5,7},{6,4},{7,5},{8,10},{9,11},{10,... | collective-permute-start | bytes 245768 | tf_op jit(solution)/shard_map/ppermute | solution.py:306
  14.2 3.1 %collective-permute-start.7 = (bf16[4,80,128]{2,1,0:T(8,128)(2,1)S(1)}, bf16[4,80,128]{2,1,0:T(8,128)(2,1)S(1)}, u32[]{:S(2)}, u32[]{:S(2)}) collective-permute-start(bf16[4,80,128]{2,1,0:T(8,128)(2,1)S(1)} %pad_maximum_fusion.1.refs_0_.refs_4_), channel_id=1, source_target_pairs={{0,1},{1,0},{2,3},{3,2},{4,5},{5,4},{6,7},{7,6},{8,9},{9,8},{10,11... | collective-permute-start | bytes 245768 | tf_op jit(solution)/shard_map/ppermute | solution.py:306
  17.0 1.3 collective-permute-start.8
  124.3 3.1 %collective-permute-start.11 = (f32[1,2048]{1,0:T(1,128)S(1)}, f32[1,2048]{1,0:T(1,128)S(1)}, u32[]{:S(2)}, u32[]{:S(2)}) collective-permute-start(f32[1,2048]{1,0:T(1,128)S(1)} %get-tuple-element.19.refs_0_), channel_id=1, source_target_pairs={{0,3},{1,2},{2,1},{3,0},{4,7},{5,6},{6,5},{7,4},{8,11},{9,10},{10,... | collective-permute-start | bytes 24584 | tf_op jit(solution)/shard_map/ppermute | solution.py:306
  125.8 3.7 %collective-permute-start.10 = (f32[1,2048]{1,0:T(1,128)S(1)}, f32[1,2048]{1,0:T(1,128)S(1)}, u32[]{:S(2)}, u32[]{:S(2)}) collective-permute-start(f32[1,2048]{1,0:T(1,128)S(1)} %get-tuple-element.19.refs_0_), channel_id=1, source_target_pairs={{0,2},{1,3},{2,0},{3,1},{4,6},{5,7},{6,4},{7,5},{8,10},{9,11},{10,... | collective-permute-start | bytes 24584 | tf_op jit(solution)/shard_map/ppermute | solution.py:306
  126.2 3.2 %collective-permute-start.9 = (f32[1,2048]{1,0:T(1,128)S(1)}, f32[1,2048]{1,0:T(1,128)S(1)}, u32[]{:S(2)}, u32[]{:S(2)}) collective-permute-start(f32[1,2048]{1,0:T(1,128)S(1)} %get-tuple-element.19.refs_0_), channel_id=1, source_target_pairs={{0,1},{1,0},{2,3},{3,2},{4,5},{5,4},{6,7},{7,6},{8,9},{9,8},{10,11... | collective-permute-start | bytes 24584 | tf_op jit(solution)/shard_map/ppermute | solution.py:306
  236.9 3.1 %collective-permute-start.14 = (f32[1,2048]{1,0:T(1,128)S(1)}, f32[1,2048]{1,0:T(1,128)S(1)}, u32[]{:S(2)}, u32[]{:S(2)}) collective-permute-start(f32[1,2048]{1,0:T(1,128)S(1)} %get-tuple-element.21.refs_0_), channel_id=1, source_target_pairs={{0,3},{1,2},{2,1},{3,0},{4,7},{5,6},{6,5},{7,4},{8,11},{9,10},{10,... | collective-permute-start | bytes 24584 | tf_op jit(solution)/shard_map/ppermute | solution.py:306
  237.0 3.7 %collective-permute-start.13 = (f32[1,2048]{1,0:T(1,128)S(1)}, f32[1,2048]{1,0:T(1,128)S(1)}, u32[]{:S(2)}, u32[]{:S(2)}) collective-permute-start(f32[1,2048]{1,0:T(1,128)S(1)} %get-tuple-element.21.refs_0_), channel_id=1, source_target_pairs={{0,2},{1,3},{2,0},{3,1},{4,6},{5,7},{6,4},{7,5},{8,10},{9,11},{10,... | collective-permute-start | bytes 24584 | tf_op jit(solution)/shard_map/ppermute | solution.py:306
  237.8 2.9 %collective-permute-start.12 = (f32[1,2048]{1,0:T(1,128)S(1)}, f32[1,2048]{1,0:T(1,128)S(1)}, u32[]{:S(2)}, u32[]{:S(2)}) collective-permute-start(f32[1,2048]{1,0:T(1,128)S(1)} %get-tuple-element.21.refs_0_), channel_id=1, source_target_pairs={{0,1},{1,0},{2,3},{3,2},{4,5},{5,4},{6,7},{7,6},{8,9},{9,8},{10,11... | collective-permute-start | bytes 24584 | tf_op jit(solution)/shard_map/ppermute | solution.py:306

commit v14 on v9

--- a/solution.py
+++ b/solution.py
@@ -114,12 +114,19 @@
     return jnp.sum(sums, axis=0, keepdims=True)
 
 
-def add_columns(p_ref, weight, col_ref, rows):
+def add_columns(p_ref, weight, col_refs, rows):
     width = weight.shape[1]
     added = p_ref[rows, 0:LANES] * weight[:, 0:LANES]
     for lane in range(LANES, width, LANES):
         added = added + p_ref[rows, lane : lane + LANES] * weight[:, lane : lane + LANES]
-    col_ref[rows, :] += added
+    col_ref, at = column_block(col_refs, rows)
+    col_ref[at, :] += added
+
+
+def column_block(col_refs, rows):
+    size = col_refs[0].shape[0]
+    place = rows.start // size
+    return col_refs[place], slice(rows.start - place * size, rows.stop - place * size)
 
 
 def tile_columns(tile, width):
@@ -128,7 +135,7 @@
     return pl.ds(pl.multiple_of(tile * width, width), width)
 
 
-def add_sources(xaug, logws, taug, p_refs, col_ref):
+def add_sources(xaug, logws, taug, p_refs, col_refs):
     total = taug.shape[0]
     width = p_refs[0].shape[1]
     tiles = xaug.shape[1] // width
@@ -138,7 +145,7 @@
     def step(tile, slot, held):
         def beside(rows):
             if held is not None:
-                add_columns(p_refs[1 - slot], held, col_ref, rows)
+                add_columns(p_refs[1 - slot], held, col_refs, rows)
 
         at = tile_columns(tile, width)
         s = spread_rows(taug, xaug[:, at], p_refs[slot], beside)
@@ -154,16 +161,18 @@
     least, weight = lax.fori_loop(0, tiles // 2 - 1, two_steps, (s, weight))
     s, weight = step(tiles - 1, 1, weight)
     for begin in range(0, total, LANES):
-        add_columns(p_refs[1], weight, col_ref, slice(begin, begin + LANES))
+        add_columns(p_refs[1], weight, col_refs, slice(begin, begin + LANES))
     return jnp.minimum(least, s)
 
 
-def lane_totals(col_ref, out_ref):
-    total = col_ref.shape[0]
+def lane_totals(col_refs, out_ref):
+    total = sum(col_ref.shape[0] for col_ref in col_refs)
     reach = min(total, 2048)
     ones = jnp.ones((16, 2 * LANES), jnp.bfloat16)
+    sizes = col_refs[0].shape[0]
     for begin in range(0, total, reach):
-        high, middle, _ = three_terms(col_ref[begin : begin + reach, :])
+        refs = col_refs[begin // sizes : (begin + reach) // sizes]
+        high, middle, _ = three_terms(jnp.concatenate([col_ref[...] for col_ref in refs], axis=0))
         both = jnp.concatenate([high, middle], axis=1)
         added = lax.dot_general(
             ones, both, (((1,), (1,)), ((), ())), preferred_element_type=jnp.float32
@@ -171,66 +180,69 @@
         out_ref[:, begin : begin + reach] = added[0:1]
 
 
-def finish_sums(xaug, logws, taug, least, p_ref, col_ref, out_ref):
+def finish_sums(xaug, logws, taug, least, p_ref, col_refs, out_ref):
     total = taug.shape[0]
-    lane_totals(col_ref, out_ref)
+    lane_totals(col_refs, out_ref)
     cols = out_ref[...]
     out_ref[...] = jnp.log2(cols)
     fine = jnp.logical_and(
         jnp.min(least) >= SMALL_ROW,
         jnp.logical_and(jnp.min(cols) >= SMALL_COL, jnp.max(cols) <= LARGE_COL),
     )
-
     top_ref = p_ref.at[:, 0:LANES]
 
     @pl.when(jnp.logical_not(fine))
     def _():
-        col_ref[...] = jnp.zeros_like(col_ref)
+        for col_ref in col_refs:
+            col_ref[...] = jnp.zeros_like(col_ref)
         top_ref[...] = jnp.full_like(top_ref, FLOOR)
-        blocks = total // LANES
-
-        def block_rows(block):
-            return pl.ds(pl.multiple_of(block * LANES, LANES), LANES)
 
         def careful(tile, carry):
             at = tile_columns(tile, LANES)
             right = xaug[:, at]
 
+            def block_rows(block):
+                return pl.ds(pl.multiple_of(block * LANES, LANES), LANES)
+
             def highest(block, peak):
                 e = exponents(taug[block_rows(block), :], right)
                 return jnp.maximum(peak, jnp.max(e, axis=0, keepdims=True))
 
-            peak = lax.fori_loop(0, blocks, highest, jnp.full((1, LANES), FLOOR, jnp.float32))
+            peak = jnp.full((1, LANES), FLOOR, jnp.float32)
+            peak = lax.fori_loop(0, total // LANES, highest, peak)
 
             def summed(block, s):
                 e = exponents(taug[block_rows(block), :], right)
                 return s + jnp.sum(jnp.exp2(e - peak), axis=0, keepdims=True)
 
-            s = lax.fori_loop(0, blocks, summed, jnp.zeros((1, LANES), jnp.float32))
+            s = lax.fori_loop(0, total // LANES, summed, jnp.zeros((1, LANES), jnp.float32))
             shift = logws[:, at] * LOG2E - peak - jnp.log2(s)
 
-            def collected(block, carry):
-                rows = block_rows(block)
-                term = exponents(taug[rows, :], right) + shift
-                old = top_ref[rows, :]
-                top = jnp.maximum(old, term)
-                col_ref[rows, :] = col_ref[rows, :] * jnp.exp2(old - top) + jnp.exp2(term - top)
-                top_ref[rows, :] = top
-                return carry
-
-            return lax.fori_loop(0, blocks, collected, carry)
+            size = col_refs[0].shape[0]
+            for place, col_ref in enumerate(col_refs):
+
+                def collected(block, carry, place=place, col_ref=col_ref):
+                    rows = block_rows(place * (size // LANES) + block)
+                    term = exponents(taug[rows, :], right) + shift
+                    old = top_ref[rows, :]
+                    top = jnp.maximum(old, term)
+                    here = block_rows(block)
+                    col = col_ref[here, :] * jnp.exp2(old - top) + jnp.exp2(term - top)
+                    col_ref[here, :] = col
+                    top_ref[rows, :] = top
+                    return carry
+
+                lax.fori_loop(0, size // LANES, collected, 0)
+            return carry
 
         lax.fori_loop(0, xaug.shape[1] // LANES, careful, 0)
-
-        def turned(block, carry):
-            rows = block_rows(block)
+        for begin in range(0, total, LANES):
+            rows = slice(begin, begin + LANES)
+            col_ref, at = column_block(col_refs, rows)
             tops = top_ref[rows, :].T
             top = jnp.max(tops, axis=0, keepdims=True)
-            added = jnp.sum(col_ref[rows, :].T * jnp.exp2(tops - top), axis=0, keepdims=True)
+            added = jnp.sum(col_ref[at, :].T * jnp.exp2(tops - top), axis=0, keepdims=True)
             out_ref[:, rows] = top + jnp.log2(added)
-            return carry
-
-        lax.fori_loop(0, blocks, turned, 0)
 
 
 def part_kernel(feat, inverse, *refs):
@@ -239,7 +251,7 @@
 
 def near_kernel(parts, feat, inverse, logws, xs, mine, rest, theirs, *refs):
     ts, refs = refs[: 2 * parts], refs[2 * parts :]
-    xaug, taug, out_ref, g_ref, q_ref, p0, p1, col_ref = refs
+    xaug, taug, out_ref, g_ref, q_ref, p0, p1, *col_refs = refs
     scale = inverse[0] * LOG2E
     stage_sources([xs], scale, xaug)
     place = 0
@@ -253,19 +265,21 @@
         taug[begin : begin + part.shape[0], :] = part[...]
         begin += part.shape[0]
     stage_targets(ts[parts + 1 :], scale, taug, begin, feat)
-    col_ref[...] = jnp.zeros_like(col_ref)
-    least = add_sources(xaug, logws, taug, (p0, p1), col_ref)
-    finish_sums(xaug, logws, taug, least, p0, col_ref, out_ref)
+    for col_ref in col_refs:
+        col_ref[...] = jnp.zeros_like(col_ref)
+    least = add_sources(xaug, logws, taug, (p0, p1), col_refs)
+    finish_sums(xaug, logws, taug, least, p0, col_refs, out_ref)
 
 
 def next_kernel(flips, parts, logws, xaug, old, g, q, logw, *refs):
     lines, refs = refs[: len(flips)], refs[len(flips) :]
-    out_ref, g_ref, taug, p0, p1, col_ref = refs
+    out_ref, g_ref, taug, p0, p1, *col_refs = refs
     taug[...] = old[...]
     g_ref[...] = renew_targets(lines, flips, parts, g[...], q[...], logw[...], taug)[1]
-    col_ref[...] = jnp.zeros_like(col_ref)
-    least = add_sources(xaug, logws, taug, (p0, p1), col_ref)
-    finish_sums(xaug, logws, taug, least, p0, col_ref, out_ref)
+    for col_ref in col_refs:
+        col_ref[...] = jnp.zeros_like(col_ref)
+    least = add_sources(xaug, logws, taug, (p0, p1), col_refs)
+    finish_sums(xaug, logws, taug, least, p0, col_refs, out_ref)
 
 
 def map_kernel(flips, parts, n_t, feat, xaug, old, g, q, logw, *refs):
@@ -409,8 +423,7 @@
     scratch = [
         p_scratch,
         p_scratch if small else pltpu.VMEM((8, LANES), f32),
-        pltpu.VMEM((total, LANES), f32),
-    ]
+    ] + [pltpu.VMEM((total // 16, LANES), f32)] * 16
     xaug, taug, sums, logw, q = call(
         functools.partial(near_kernel, parts, feat),
         [inverse_eps, logws, xs, taug_mine, taug_rest, taug_theirs] + ts,
@@ -423,11 +436,10 @@
         ],
         scratch,
     )
-    flips = [(core, digit) for core in range(2) for digit in range(parts)]
+    flips = [(core, digit) for digit in range(parts) for core in range(2)]
 
     def exchange(own):
-        held = [own] + [swap(own, count, digit << low) for digit in range(1, parts)]
-        return held + [swap(value, count, 1) for value in held]
+        return [own] + [swap(own, count, core | (digit << low)) for core, digit in flips[1:]]
 
     g = logw
     for _ in range(ITERS - 1):

time: 236 us -> 181 us (0.77)
  Pallas kernels: 209 us -> 154 us
    pallas_call x6, Pallas kernels: 209 us -> 154 us  [call(): pl.pallas_call(kernel, out_shape=outs, in_specs=[smem] * scalars + [vmem]...]
where the time goes in v14:
time: 181 us
  Pallas kernels  154 us (85%)
  starting transfers between devices  15.8 us (9%)
  waiting for transfers between devices  8.23 us (5%)
    pallas_call x6, Pallas kernels, call(): pl.pallas_call(kernel, out_shape=outs, in_specs=[smem] * scalars + [vmem]...  154 us
    ppermute x15, starting transfers between devices, swap(): lax.ppermute(value, AXIS, [(source, source ^ step) for source in range(co...  15.8 us
    ppermute x15, waiting for transfers between devices, swap(): lax.ppermute(value, AXIS, [(source, source ^ step) for source in range(co...  8.23 us
  transfers between devices with their start and end apart: 15, of which 6 were waited for; matrix products, arithmetic and copies ran while one was open for 0% of the time, Pallas kernels for 0%

profile of v14, /device:TPU:0, one launch (start us, length us, event | category | flops | bytes accessed | tf_op | source)
XLA Modules:
  0.0 180.8 jit_solution(14448069380618543366)
XLA Ops:
  0.6 0.0 copy-start
  0.6 0.1 pad.11.clone
  0.7 0.8 maximum_maximum_fusion
  1.6 5.1 %collective-permute-start.2 = (bf16[1,80,128]{2,1,0:T(8,128)(2,1)S(1)}, bf16[1,80,128]{2,1,0:T(8,128)(2,1)S(1)}, u32[]{:S(2)}, u32[]{:S(2)}) collective-permute-start(bf16[1,80,128]{2,1,0:T(8,128)(2,1)S(1)} %bitcast.5), channel_id=1, source_target_pairs={{0,12},{1,13},{2,14},{3,15},{4,8},{5,9},{6,10},{7,11},{8,4},{9,5},... | collective-permute-start | bytes 61448 | tf_op jit(solution)/shard_map/ppermute | solution.py:326
  6.7 0.0 collective-permute-start.1
  6.7 0.6 collective-permute-start
  7.3 0.0 copy-done
  7.3 3.7 %collective-permute-start.5 = (bf16[1,64,384]{2,1,0:T(8,128)(2,1)S(1)}, bf16[1,64,384]{2,1,0:T(8,128)(2,1)S(1)}, u32[]{:S(2)}, u32[]{:S(2)}) collective-permute-start(bf16[1,64,384]{2,1,0:T(8,128)(2,1)S(1)} %bitcast.9), channel_id=1, source_target_pairs={{0,12},{1,13},{2,14},{3,15},{4,8},{5,9},{6,10},{7,11},{8,4},{9,5},... | collective-permute-start | bytes 147464 | tf_op jit(solution)/shard_map/ppermute | solution.py:326
  11.1 0.0 collective-permute-start.4
  11.7 0.0 collective-permute-done.2
  11.7 0.7 collective-permute-start.3
  12.4 0.0 collective-permute-done.1
  12.4 0.0 collective-permute-done
  12.4 1.7 collective-permute-start.6
  14.2 0.0 collective-permute-start.7
  14.2 0.3 shard_map.68.mine
  14.5 2.5 %collective-permute-done.6.refs_0_.refs_1_.refs_5_ = bf16[4,80,128]{2,1,0:T(8,128)(2,1)S(1)} collective-permute-done((bf16[4,80,128]{2,1,0:T(8,128)(2,1)S(1)}, bf16[4,80,128]{2,1,0:T(8,128)(2,1)S(1)}, u32[]{:S(2)}, u32[]{:S(2)}) %collective-permute-start.6) | collective-permute-done | bytes 81952 | tf_op jit(solution)/shard_map/ppermute | solution.py:326
  17.0 0.0 collective-permute-start.8
  17.0 0.0 collective-permute-done.5
  17.0 0.0 collective-permute-done.4
  17.0 0.0 collective-permute-done.3
  17.0 0.3 shard_map.69.rest
  17.3 0.0 collective-permute-done.7.refs_0_.refs_2_.refs_6_
  17.3 0.3 shard_map.70.theirs
  17.6 0.6 collective-permute-done.8.refs_3_.refs_7_
  18.2 74.7 %shard_map.71 = (bf16[256,1536]{1,0:T(8,128)(2,1)S(1)}, bf16[2048,256]{1,0:T(8,128)(2,1)S(1)}, f32[1,2048]{1,0:T(1,128)S(1)}, f32[1,2048]{1,0:T(1,128)S(1)}, f32[1,2048]{1,0:T(1,128)S(1)}) custom-call(f32[1]{0:T(128)S(6)} %copy.7.inverse, f32[1,1536]{1,0:T(1,128)S(1)} %reshape.27.logws, bf16[4,64,384]{2,1,0:T(8,128)(2,1)S(1)} %pad_maximum_fusion.xs, ...), custom_call_target="tpu_custom_call" | custom-call | tf_op jit(solution)/shard_map/pallas_call | solution.py:381
  93.0 1.5 collective-permute-start.11
  94.4 0.4 collective-permute-start.10
  94.8 0.1 collective-permute-start.9
  94.9 1.2 collective-permute-done.11.refs_3_
  96.1 2.0 %collective-permute-done.10.refs_2_ = f32[1,2048]{1,0:T(1,128)S(1)} collective-permute-done((f32[1,2048]{1,0:T(1,128)S(1)}, f32[1,2048]{1,0:T(1,128)S(1)}, u32[]{:S(2)}, u32[]{:S(2)}) %collective-permute-start.10) | collective-permute-done | bytes 8224 | tf_op jit(solution)/shard_map/ppermute | solution.py:326
  98.1 0.0 collective-permute-done.9.refs_1_
  98.1 74.6 %shard_map.72 = (f32[1,2048]{1,0:T(1,128)S(1)}, f32[1,2048]{1,0:T(1,128)S(1)}) custom-call(f32[1,1536]{1,0:T(1,128)S(1)} %reshape.27.logws, bf16[256,1536]{1,0:T(8,128)(2,1)S(1)} %get-tuple-element.15.xaug, bf16[2048,256]{1,0:T(8,128)(2,1)S(1)} %get-tuple-element.16.old, f32[1,2048]{1,0:T(1,128)S(1)} %get-tuple-element.17.g.logw, ...), custom_call_target="tpu_custom_call" | custom-call | tf_op jit(solution)/shard_map/pallas_call | solution.py:381
  172.7 0.1 collective-permute-start.14
  172.8 0.8 collective-permute-start.13
  173.6 1.0 collective-permute-start.12
  174.6 1.2 collective-permute-done.14.refs_3_
  175.8 0.7 collective-permute-done.13.refs_2_
  176.5 0.0 collective-permute-done.12.refs_1_
  176.5 4.3 %shard_map.73 = (f32[64,384]{1,0:T(8,128)}, f32[1,128]{1,0:T(1,128)}) custom-call(bf16[256,1536]{1,0:T(8,128)(2,1)S(1)} %get-tuple-element.15.xaug, bf16[2048,256]{1,0:T(8,128)(2,1)S(1)} %get-tuple-element.16.old, f32[1,2048]{1,0:T(1,128)S(1)} %get-tuple-element.20.g, f32[1,2048]{1,0:T(1,128)S(1)} %get-tuple-element.18.q, ...), custom_call_target="tpu_custom_call" | custom-call | tf_op jit(solution)/shard_map/pallas_call | solution.py:381
  (5 shorter events, 0.1 us)
Async XLA Ops:
  0.6 6.7 %copy-start = (bf16[64,384]{1,0:T(8,128)(2,1)S(1)}, bf16[64,384]{1,0:T(8,128)(2,1)}, u32[]{:S(2)}) copy-start(bf16[64,384]{1,0:T(8,128)(2,1)} %param.5) | copy-start | bytes 147460
  1.6 10.2 %collective-permute-start.2 = (bf16[1,80,128]{2,1,0:T(8,128)(2,1)S(1)}, bf16[1,80,128]{2,1,0:T(8,128)(2,1)S(1)}, u32[]{:S(2)}, u32[]{:S(2)}) collective-permute-start(bf16[1,80,128]{2,1,0:T(8,128)(2,1)S(1)} %bitcast.5), channel_id=1, source_target_pairs={{0,12},{1,13},{2,14},{3,15},{4,8},{5,9},{6,10},{7,11},{8,4},{9,5},... | collective-permute-start | bytes 61448 | tf_op jit(solution)/shard_map/ppermute | solution.py:326
  6.7 5.8 %collective-permute-start.1 = (bf16[1,80,128]{2,1,0:T(8,128)(2,1)S(1)}, bf16[1,80,128]{2,1,0:T(8,128)(2,1)S(1)}, u32[]{:S(2)}, u32[]{:S(2)}) collective-permute-start(bf16[1,80,128]{2,1,0:T(8,128)(2,1)S(1)} %bitcast.6), channel_id=1, source_target_pairs={{0,8},{1,9},{2,10},{3,11},{4,12},{5,13},{6,14},{7,15},{8,0},{9,1},... | collective-permute-start | bytes 61448 | tf_op jit(solution)/shard_map/ppermute | solution.py:326
  6.7 5.8 %collective-permute-start = (bf16[1,80,128]{2,1,0:T(8,128)(2,1)S(1)}, bf16[1,80,128]{2,1,0:T(8,128)(2,1)S(1)}, u32[]{:S(2)}, u32[]{:S(2)}) collective-permute-start(bf16[1,80,128]{2,1,0:T(8,128)(2,1)S(1)} %bitcast.7), channel_id=1, source_target_pairs={{0,4},{1,5},{2,6},{3,7},{4,0},{5,1},{6,2},{7,3},{8,12},{9,13},{10,... | collective-permute-start | bytes 61448 | tf_op jit(solution)/shard_map/ppermute | solution.py:326
  7.3 9.7 %collective-permute-start.5 = (bf16[1,64,384]{2,1,0:T(8,128)(2,1)S(1)}, bf16[1,64,384]{2,1,0:T(8,128)(2,1)S(1)}, u32[]{:S(2)}, u32[]{:S(2)}) collective-permute-start(bf16[1,64,384]{2,1,0:T(8,128)(2,1)S(1)} %bitcast.9), channel_id=1, source_target_pairs={{0,12},{1,13},{2,14},{3,15},{4,8},{5,9},{6,10},{7,11},{8,4},{9,5},... | collective-permute-start | bytes 147464 | tf_op jit(solution)/shard_map/ppermute | solution.py:326
  11.1 5.9 %collective-permute-start.4 = (bf16[1,64,384]{2,1,0:T(8,128)(2,1)S(1)}, bf16[1,64,384]{2,1,0:T(8,128)(2,1)S(1)}, u32[]{:S(2)}, u32[]{:S(2)}) collective-permute-start(bf16[1,64,384]{2,1,0:T(8,128)(2,1)S(1)} %bitcast.10), channel_id=1, source_target_pairs={{0,8},{1,9},{2,10},{3,11},{4,12},{5,13},{6,14},{7,15},{8,0},{9,1},... | collective-permute-start | bytes 147464 | tf_op jit(solution)/shard_map/ppermute | solution.py:326
  11.7 5.3 %collective-permute-start.3 = (bf16[1,64,384]{2,1,0:T(8,128)(2,1)S(1)}, bf16[1,64,384]{2,1,0:T(8,128)(2,1)S(1)}, u32[]{:S(2)}, u32[]{:S(2)}) collective-permute-start(bf16[1,64,384]{2,1,0:T(8,128)(2,1)S(1)} %bitcast.11), channel_id=1, source_target_pairs={{0,4},{1,5},{2,6},{3,7},{4,0},{5,1},{6,2},{7,3},{8,12},{9,13},{10,... | collective-permute-start | bytes 147464 | tf_op jit(solution)/shard_map/ppermute | solution.py:326
  12.4 4.5 %collective-permute-start.6 = (bf16[4,80,128]{2,1,0:T(8,128)(2,1)S(1)}, bf16[4,80,128]{2,1,0:T(8,128)(2,1)S(1)}, u32[]{:S(2)}, u32[]{:S(2)}) collective-permute-start(bf16[4,80,128]{2,1,0:T(8,128)(2,1)S(1)} %pad_maximum_fusion.1.refs_0_.refs_4_), channel_id=1, source_target_pairs={{0,2},{1,3},{2,0},{3,1},{4,6},{5,7},{6,4},{7,5},{8,10},{9,11},{10,... | collective-permute-start | bytes 245768 | tf_op jit(solution)/shard_map/ppermute | solution.py:326
  14.2 3.1 %collective-permute-start.7 = (bf16[4,80,128]{2,1,0:T(8,128)(2,1)S(1)}, bf16[4,80,128]{2,1,0:T(8,128)(2,1)S(1)}, u32[]{:S(2)}, u32[]{:S(2)}) collective-permute-start(bf16[4,80,128]{2,1,0:T(8,128)(2,1)S(1)} %pad_maximum_fusion.1.refs_0_.refs_4_), channel_id=1, source_target_pairs={{0,1},{1,0},{2,3},{3,2},{4,5},{5,4},{6,7},{7,6},{8,9},{9,8},{10,11... | collective-permute-start | bytes 245768 | tf_op jit(solution)/shard_map/ppermute | solution.py:326
  17.0 1.3 collective-permute-start.8
  93.0 3.1 %collective-permute-start.11 = (f32[1,2048]{1,0:T(1,128)S(1)}, f32[1,2048]{1,0:T(1,128)S(1)}, u32[]{:S(2)}, u32[]{:S(2)}) collective-permute-start(f32[1,2048]{1,0:T(1,128)S(1)} %get-tuple-element.19.refs_0_), channel_id=1, source_target_pairs={{0,3},{1,2},{2,1},{3,0},{4,7},{5,6},{6,5},{7,4},{8,11},{9,10},{10,... | collective-permute-start | bytes 24584 | tf_op jit(solution)/shard_map/ppermute | solution.py:326
  94.4 3.7 %collective-permute-start.10 = (f32[1,2048]{1,0:T(1,128)S(1)}, f32[1,2048]{1,0:T(1,128)S(1)}, u32[]{:S(2)}, u32[]{:S(2)}) collective-permute-start(f32[1,2048]{1,0:T(1,128)S(1)} %get-tuple-element.19.refs_0_), channel_id=1, source_target_pairs={{0,2},{1,3},{2,0},{3,1},{4,6},{5,7},{6,4},{7,5},{8,10},{9,11},{10,... | collective-permute-start | bytes 24584 | tf_op jit(solution)/shard_map/ppermute | solution.py:326
  94.8 3.3 %collective-permute-start.9 = (f32[1,2048]{1,0:T(1,128)S(1)}, f32[1,2048]{1,0:T(1,128)S(1)}, u32[]{:S(2)}, u32[]{:S(2)}) collective-permute-start(f32[1,2048]{1,0:T(1,128)S(1)} %get-tuple-element.19.refs_0_), channel_id=1, source_target_pairs={{0,1},{1,0},{2,3},{3,2},{4,5},{5,4},{6,7},{7,6},{8,9},{9,8},{10,11... | collective-permute-start | bytes 24584 | tf_op jit(solution)/shard_map/ppermute | solution.py:326
  172.7 3.1 %collective-permute-start.14 = (f32[1,2048]{1,0:T(1,128)S(1)}, f32[1,2048]{1,0:T(1,128)S(1)}, u32[]{:S(2)}, u32[]{:S(2)}) collective-permute-start(f32[1,2048]{1,0:T(1,128)S(1)} %get-tuple-element.21.refs_0_), channel_id=1, source_target_pairs={{0,3},{1,2},{2,1},{3,0},{4,7},{5,6},{6,5},{7,4},{8,11},{9,10},{10,... | collective-permute-start | bytes 24584 | tf_op jit(solution)/shard_map/ppermute | solution.py:326
  172.8 3.7 %collective-permute-start.13 = (f32[1,2048]{1,0:T(1,128)S(1)}, f32[1,2048]{1,0:T(1,128)S(1)}, u32[]{:S(2)}, u32[]{:S(2)}) collective-permute-start(f32[1,2048]{1,0:T(1,128)S(1)} %get-tuple-element.21.refs_0_), channel_id=1, source_target_pairs={{0,2},{1,3},{2,0},{3,1},{4,6},{5,7},{6,4},{7,5},{8,10},{9,11},{10,... | collective-permute-start | bytes 24584 | tf_op jit(solution)/shard_map/ppermute | solution.py:326
  173.6 2.9 %collective-permute-start.12 = (f32[1,2048]{1,0:T(1,128)S(1)}, f32[1,2048]{1,0:T(1,128)S(1)}, u32[]{:S(2)}, u32[]{:S(2)}) collective-permute-start(f32[1,2048]{1,0:T(1,128)S(1)} %get-tuple-element.21.refs_0_), channel_id=1, source_target_pairs={{0,1},{1,0},{2,3},{3,2},{4,5},{5,4},{6,7},{7,6},{8,9},{9,8},{10,11... | collective-permute-start | bytes 24584 | tf_op jit(solution)/shard_map/ppermute | solution.py:326

commit v15 on v14

--- a/solution.py
+++ b/solution.py
@@ -165,6 +165,10 @@
     return jnp.minimum(least, s)
 
 
+def lane_tiles(width):
+    return [slice(begin, begin + LANES) for begin in range(0, width, LANES)]
+
+
 def lane_totals(col_refs, out_ref):
     total = sum(col_ref.shape[0] for col_ref in col_refs)
     reach = min(total, 2048)
@@ -180,22 +184,24 @@
         out_ref[:, begin : begin + reach] = added[0:1]
 
 
-def finish_sums(xaug, logws, taug, least, p_ref, col_refs, out_ref):
+def finish_sums(xaug, logws, taug, least, p0, p1, col_refs, out_ref):
     total = taug.shape[0]
     lane_totals(col_refs, out_ref)
     cols = out_ref[...]
     out_ref[...] = jnp.log2(cols)
-    fine = jnp.logical_and(
-        jnp.min(least) >= SMALL_ROW,
-        jnp.logical_and(jnp.min(cols) >= SMALL_COL, jnp.max(cols) <= LARGE_COL),
-    )
-    top_ref = p_ref.at[:, 0:LANES]
+    margins = [least[:, at] / SMALL_ROW for at in lane_tiles(least.shape[1])]
+    for at in lane_tiles(total):
+        margins += [cols[:, at] / SMALL_COL, LARGE_COL / cols[:, at]]
+    fine = jnp.min(functools.reduce(jnp.minimum, margins)) >= 1.0
+    halves = total // p0.shape[0]
+    tops_refs = [p_ref.at[:, 0:LANES] for p_ref in (p0, p1)[:halves]]
 
     @pl.when(jnp.logical_not(fine))
     def _():
         for col_ref in col_refs:
             col_ref[...] = jnp.zeros_like(col_ref)
-        top_ref[...] = jnp.full_like(top_ref, FLOOR)
+        for top_ref in tops_refs:
+            top_ref[...] = jnp.full(top_ref.shape, FLOOR, jnp.float32)
 
         def careful(tile, carry):
             at = tile_columns(tile, LANES)
@@ -220,10 +226,15 @@
 
             size = col_refs[0].shape[0]
             for place, col_ref in enumerate(col_refs):
-
-                def collected(block, carry, place=place, col_ref=col_ref):
+                top_ref = tops_refs[place * size // tops_refs[0].shape[0]]
+                skipped = place * size % tops_refs[0].shape[0] // LANES
+
+                def collected(
+                    block, carry, place=place, col_ref=col_ref, top_ref=top_ref, skipped=skipped
+                ):
                     rows = block_rows(place * (size // LANES) + block)
                     term = exponents(taug[rows, :], right) + shift
+                    rows = block_rows(skipped + block)
                     old = top_ref[rows, :]
                     top = jnp.maximum(old, term)
                     here = block_rows(block)
@@ -239,7 +250,8 @@
         for begin in range(0, total, LANES):
             rows = slice(begin, begin + LANES)
             col_ref, at = column_block(col_refs, rows)
-            tops = top_ref[rows, :].T
+            top_ref, here = column_block(tops_refs, rows)
+            tops = top_ref[here, :].T
             top = jnp.max(tops, axis=0, keepdims=True)
             added = jnp.sum(col_ref[at, :].T * jnp.exp2(tops - top), axis=0, keepdims=True)
             out_ref[:, rows] = top + jnp.log2(added)
@@ -268,7 +280,120 @@
     for col_ref in col_refs:
         col_ref[...] = jnp.zeros_like(col_ref)
     least = add_sources(xaug, logws, taug, (p0, p1), col_refs)
-    finish_sums(xaug, logws, taug, least, p0, col_refs, out_ref)
+    finish_sums(xaug, logws, taug, least, p0, p1, col_refs, out_ref)
+
+
+def head_kernel(inverse, xs, *refs):
+    ts, (xaug, p_ref, s_ref) = refs[:-3], refs[-3:]
+    stage_sources([xs], inverse[0] * LOG2E, xaug)
+    width = 2 * LANES
+    tiles = xaug.shape[1] // width
+    side = 3 if tiles % 3 == 0 else 1
+
+    def advance(step, carry):
+        for inner in range(side):
+            at = tile_columns(step * side + inner, width)
+            right, begin, s = xaug[:, at], 0, 0.0
+            for part in ts:
+                rows = pl.ds(begin, part.shape[0])
+                s = s + spread_rows(part, right, p_ref.at[rows, at], lambda rows: None)
+                begin += part.shape[0]
+            s_ref[:, at] = s
+        return carry
+
+    lax.fori_loop(0, tiles // side, advance, 0)
+
+
+def add_split_sources(xaug, logws, taug, ranges, p_head, s_head, p_refs, col_refs):
+    width = p_refs[0].shape[1]
+    tiles = xaug.shape[1] // width
+    total = taug.shape[0]
+    late = [row for begin, end in ranges for row in range(begin, end, LANES)]
+    early = [row for row in range(0, total, LANES) if row not in late]
+    share = -(-len(early) // len(late))
+
+    def collect(row, value_of, weight):
+        added = functools.reduce(
+            jnp.add, [value_of(at) * weight[:, at] for at in lane_tiles(width)]
+        )
+        col_ref, at = column_block(col_refs, slice(row, row + LANES))
+        col_ref[at, :] += added
+
+    def head_values(tile, row):
+        place = early.index(row) * LANES
+
+        def value_of(at):
+            begin = tile * width + at.start
+            if not isinstance(tile, int):
+                begin = pl.multiple_of(begin, LANES)
+            return p_head[place : place + LANES, pl.ds(begin, LANES)]
+
+        return value_of
+
+    def late_values(p_ref, row):
+        place = late.index(row) * LANES
+        return lambda at: p_ref[place : place + LANES, at]
+
+    def step(tile, slot, held):
+        at = tile_columns(tile, width)
+        right = xaug[:, at]
+        sums = jnp.zeros((8, width), jnp.float32)
+        for begin, end in ranges:
+            for first in range(begin, end, 512):
+                last = min(first + 512, end)
+                e = exponents(taug[first:last, :], right)
+                for row in range(first, last, LANES):
+                    place = late.index(row)
+                    if held is not None:
+                        for other in early[place * share : (place + 1) * share]:
+                            collect(other, head_values(tile - 1, other), held)
+                        collect(row, late_values(p_refs[1 - slot], row), held)
+                    p = jnp.exp2(e[row - first : row - first + LANES])
+                    p_refs[slot][place * LANES : (place + 1) * LANES, :] = p
+                    sums = sums + jnp.sum(p.reshape(LANES // 8, 8, width), axis=0)
+        s = s_head[:, at] + jnp.sum(sums, axis=0, keepdims=True)
+        return s, jnp.exp2(logws[:, at] * LOG2E) / s
+
+    def two_steps(pair, carry):
+        least, weight = carry
+        s1, weight1 = step(2 * pair + 1, 1, weight)
+        s0, weight0 = step(2 * pair + 2, 0, weight1)
+        return jnp.minimum(least, jnp.minimum(s0, s1)), weight0
+
+    s, weight = step(0, 0, None)
+    least, weight = lax.fori_loop(0, tiles // 2 - 1, two_steps, (s, weight))
+    s, weight = step(tiles - 1, 1, weight)
+    for row in range(0, total, LANES):
+        if row in late:
+            collect(row, late_values(p_refs[1], row), weight)
+        else:
+            collect(row, head_values(tiles - 1, row), weight)
+    return jnp.minimum(least, s)
+
+
+def tail_kernel(parts, feat, inverse, logws, xaug, p_head, s_head, mine, rest, theirs, *refs):
+    ts, refs = refs[: 2 * parts], refs[2 * parts :]
+    taug, out_ref, g_ref, q_ref, p0, p1, *col_refs = refs
+    scale = inverse[0] * LOG2E
+    place = 0
+    for part in ts:
+        for block in range(part.shape[0]):
+            at = slice(place * LANES, (place + 1) * LANES)
+            q_ref[:, at], g_ref[:, at] = target_lines(part, block, scale, feat)
+            place += 1
+    begin, ranges = 0, []
+    for part in (mine, rest, theirs):
+        end = begin + part.shape[0]
+        taug[begin:end, :] = part[...]
+        if part is rest:
+            ranges.append((begin, end))
+        begin = end
+    stage_targets(ts[parts + 1 :], scale, taug, begin, feat)
+    ranges.append((begin, taug.shape[0]))
+    for col_ref in col_refs:
+        col_ref[...] = jnp.zeros_like(col_ref)
+    least = add_split_sources(xaug, logws, taug, ranges, p_head, s_head, (p0, p1), col_refs)
+    finish_sums(xaug, logws, taug, least, p0, p1, col_refs, out_ref)
 
 
 def next_kernel(flips, parts, logws, xaug, old, g, q, logw, *refs):
@@ -279,7 +404,7 @@
     for col_ref in col_refs:
         col_ref[...] = jnp.zeros_like(col_ref)
     least = add_sources(xaug, logws, taug, (p0, p1), col_refs)
-    finish_sums(xaug, logws, taug, least, p0, col_refs, out_ref)
+    finish_sums(xaug, logws, taug, least, p0, p1, col_refs, out_ref)
 
 
 def map_kernel(flips, parts, n_t, feat, xaug, old, g, q, logw, *refs):
@@ -424,18 +549,29 @@
         p_scratch,
         p_scratch if small else pltpu.VMEM((8, LANES), f32),
     ] + [pltpu.VMEM((total // 16, LANES), f32)] * 16
-    xaug, taug, sums, logw, q = call(
-        functools.partial(near_kernel, parts, feat),
-        [inverse_eps, logws, xs, taug_mine, taug_rest, taug_theirs] + ts,
-        [
-            jax.ShapeDtypeStruct((DEPTH, rows), bf16),
-            jax.ShapeDtypeStruct((total, DEPTH), bf16),
-            line,
-            line,
-            line,
-        ],
-        scratch,
-    )
+    shape = jax.ShapeDtypeStruct
+    xaug_shape, taug_shape = shape((DEPTH, rows), bf16), shape((total, DEPTH), bf16)
+    if small:
+        head = (mine[0].shape[0] + theirs[0].shape[0]) * own_targets
+        xaug, p_head, s_head = call(
+            head_kernel,
+            [inverse_eps, xs, taug_mine, taug_theirs],
+            [xaug_shape, shape((head, rows), f32), shape((1, rows), f32)],
+        )
+        p_half = pltpu.VMEM((total - head, width), f32)
+        taug, sums, logw, q = call(
+            functools.partial(tail_kernel, parts, feat),
+            [inverse_eps, logws, xaug, p_head, s_head, taug_mine, taug_rest, taug_theirs] + ts,
+            [taug_shape, line, line, line],
+            [p_half, p_half] + scratch[2:],
+        )
+    else:
+        xaug, taug, sums, logw, q = call(
+            functools.partial(near_kernel, parts, feat),
+            [inverse_eps, logws, xs, taug_mine, taug_rest, taug_theirs] + ts,
+            [xaug_shape, taug_shape, line, line, line],
+            scratch,
+        )
     flips = [(core, digit) for digit in range(parts) for core in range(2)]
 
     def exchange(own):

time: 181 us -> 184 us (1.017)
  Pallas kernels: 154 us -> 157 us
    pallas_call x6 -> x7, Pallas kernels: 154 us -> 157 us  [call(): pl.pallas_call(kernel, out_shape=outs, in_specs=[smem] * scalars + [vmem]...]
  transfers between devices with their start and end apart: 15 -> 15, of which waited for: 6 -> 5; matrix products, arithmetic and copies ran while one was open for 0% -> 0% of each run, Pallas kernels for 0% -> 1%
where the time goes in v15:
time: 184 us
  Pallas kernels  157 us (85%)
  starting transfers between devices  16 us (9%)
  waiting for transfers between devices  7.64 us (4%)
    pallas_call x7, Pallas kernels, call(): pl.pallas_call(kernel, out_shape=outs, in_specs=[smem] * scalars + [vmem]...  157 us
    ppermute x15, starting transfers between devices, swap(): lax.ppermute(value, AXIS, [(source, source ^ step) for source in range(co...  16 us
    ppermute x15, waiting for transfers between devices, swap(): lax.ppermute(value, AXIS, [(source, source ^ step) for source in range(co...  7.64 us
  transfers between devices with their start and end apart: 15, of which 5 were waited for; matrix products, arithmetic and copies ran while one was open for 0% of the time, Pallas kernels for 1%

profile of v15, /device:TPU:0, one launch (start us, length us, event | category | flops | bytes accessed | tf_op | source)
XLA Modules:
  0.0 183.9 jit_solution(457392399161592593)
XLA Ops:
  0.6 0.1 pad.11.clone
  0.7 0.8 maximum_maximum_fusion
  1.5 5.1 %collective-permute-start.5 = (bf16[1,80,128]{2,1,0:T(8,128)(2,1)S(1)}, bf16[1,80,128]{2,1,0:T(8,128)(2,1)S(1)}, u32[]{:S(2)}, u32[]{:S(2)}) collective-permute-start(bf16[1,80,128]{2,1,0:T(8,128)(2,1)S(1)} %bitcast.5), channel_id=1, source_target_pairs={{0,12},{1,13},{2,14},{3,15},{4,8},{5,9},{6,10},{7,11},{8,4},{9,5},... | collective-permute-start | bytes 61448 | tf_op jit(solution)/shard_map/ppermute | solution.py:451
  6.7 0.0 collective-permute-start.4
  6.7 0.6 collective-permute-start.3
  7.3 3.7 %collective-permute-start.2 = (bf16[1,64,384]{2,1,0:T(8,128)(2,1)}, bf16[1,64,384]{2,1,0:T(8,128)(2,1)S(1)}, u32[]{:S(2)}, u32[]{:S(2)}) collective-permute-start(bf16[1,64,384]{2,1,0:T(8,128)(2,1)} %bitcast.9), channel_id=1, source_target_pairs={{0,12},{1,13},{2,14},{3,15},{4,8},{5,9},{6,10},{7,11},{8,4},{9,5},... | collective-permute-start | bytes 147464 | tf_op jit(solution)/shard_map/ppermute | solution.py:451
  11.0 0.0 collective-permute-start.1
  11.7 0.0 collective-permute-done.5
  11.7 0.7 collective-permute-start
  12.4 0.0 collective-permute-done.4
  12.4 0.0 collective-permute-done.3
  12.4 1.7 collective-permute-start.7
  14.1 0.0 collective-permute-start.6
  14.2 0.3 shard_map.68.refs_0_.mine
  14.4 2.5 %collective-permute-done.7.refs_0_.refs_1_.refs_5_ = bf16[4,80,128]{2,1,0:T(8,128)(2,1)S(1)} collective-permute-done((bf16[4,80,128]{2,1,0:T(8,128)(2,1)S(1)}, bf16[4,80,128]{2,1,0:T(8,128)(2,1)S(1)}, u32[]{:S(2)}, u32[]{:S(2)}) %collective-permute-start.7) | collective-permute-done | bytes 81952 | tf_op jit(solution)/shard_map/ppermute | solution.py:451
  16.9 0.0 collective-permute-start.8
  16.9 0.0 collective-permute-done.2
  17.0 0.0 collective-permute-done.1
  17.0 0.0 collective-permute-done
  17.0 0.8 pad_maximum_fusion.xs
  17.8 0.0 collective-permute-done.6.refs_0_.refs_2_.refs_6_
  17.8 0.3 shard_map.69.refs_1_.theirs
  18.1 1.4 shard_map.70
  19.5 0.3 shard_map.71.rest
  19.7 0.0 collective-permute-done.8.refs_3_.refs_7_
  19.7 75.9 %shard_map.72 = (bf16[2048,256]{1,0:T(8,128)(2,1)S(1)}, f32[1,2048]{1,0:T(1,128)S(1)}, f32[1,2048]{1,0:T(1,128)S(1)}, f32[1,2048]{1,0:T(1,128)S(1)}) custom-call(f32[1]{0:T(128)S(6)} %copy.7.inverse, f32[1,1536]{1,0:T(1,128)S(1)} %reshape.27.logws, bf16[256,1536]{1,0:T(8,128)(2,1)S(1)} %get-tuple-element.17.xaug, f32[1024,1536]{1,0:T(8,128)S(1)} %get-tuple-element.18.p_head, ...), custom_call_target="tpu_custom_call" | custom-call | tf_op jit(solution)/shard_map/pallas_call | solution.py:506
  95.7 1.8 collective-permute-start.11
  97.5 0.4 collective-permute-start.10
  97.9 0.0 collective-permute-start.9
  97.9 1.0 collective-permute-done.11.refs_3_
  98.9 2.3 %collective-permute-done.10.refs_2_ = f32[1,2048]{1,0:T(1,128)S(1)} collective-permute-done((f32[1,2048]{1,0:T(1,128)S(1)}, f32[1,2048]{1,0:T(1,128)S(1)}, u32[]{:S(2)}, u32[]{:S(2)}) %collective-permute-start.10) | collective-permute-done | bytes 8224 | tf_op jit(solution)/shard_map/ppermute | solution.py:451
  101.1 0.0 collective-permute-done.9.refs_1_
  101.1 74.6 %shard_map.73 = (f32[1,2048]{1,0:T(1,128)S(1)}, f32[1,2048]{1,0:T(1,128)S(1)}) custom-call(f32[1,1536]{1,0:T(1,128)S(1)} %reshape.27.logws, bf16[256,1536]{1,0:T(8,128)(2,1)S(1)} %get-tuple-element.17.xaug, bf16[2048,256]{1,0:T(8,128)(2,1)S(1)} %get-tuple-element.20.old, f32[1,2048]{1,0:T(1,128)S(1)} %get-tuple-element.21.g.logw, ...), custom_call_target="tpu_custom_call" | custom-call | tf_op jit(solution)/shard_map/pallas_call | solution.py:506
  175.8 0.1 collective-permute-start.14
  175.8 0.5 collective-permute-start.13
  176.3 1.4 collective-permute-start.12
  177.7 1.2 collective-permute-done.14.refs_3_
  178.9 0.7 collective-permute-done.13.refs_2_
  179.6 0.0 collective-permute-done.12.refs_1_
  179.6 4.3 %shard_map.74 = (f32[64,384]{1,0:T(8,128)}, f32[1,128]{1,0:T(1,128)}) custom-call(bf16[256,1536]{1,0:T(8,128)(2,1)S(1)} %get-tuple-element.17.xaug, bf16[2048,256]{1,0:T(8,128)(2,1)S(1)} %get-tuple-element.20.old, f32[1,2048]{1,0:T(1,128)S(1)} %get-tuple-element.24.g, f32[1,2048]{1,0:T(1,128)S(1)} %get-tuple-element.22.q, ...), custom_call_target="tpu_custom_call" | custom-call | tf_op jit(solution)/shard_map/pallas_call | solution.py:506
  (4 shorter events, 0.0 us)
Async XLA Ops:
  1.5 10.2 %collective-permute-start.5 = (bf16[1,80,128]{2,1,0:T(8,128)(2,1)S(1)}, bf16[1,80,128]{2,1,0:T(8,128)(2,1)S(1)}, u32[]{:S(2)}, u32[]{:S(2)}) collective-permute-start(bf16[1,80,128]{2,1,0:T(8,128)(2,1)S(1)} %bitcast.5), channel_id=1, source_target_pairs={{0,12},{1,13},{2,14},{3,15},{4,8},{5,9},{6,10},{7,11},{8,4},{9,5},... | collective-permute-start | bytes 61448 | tf_op jit(solution)/shard_map/ppermute | solution.py:451
  6.7 5.8 %collective-permute-start.4 = (bf16[1,80,128]{2,1,0:T(8,128)(2,1)S(1)}, bf16[1,80,128]{2,1,0:T(8,128)(2,1)S(1)}, u32[]{:S(2)}, u32[]{:S(2)}) collective-permute-start(bf16[1,80,128]{2,1,0:T(8,128)(2,1)S(1)} %bitcast.6), channel_id=1, source_target_pairs={{0,8},{1,9},{2,10},{3,11},{4,12},{5,13},{6,14},{7,15},{8,0},{9,1},... | collective-permute-start | bytes 61448 | tf_op jit(solution)/shard_map/ppermute | solution.py:451
  6.7 5.8 %collective-permute-start.3 = (bf16[1,80,128]{2,1,0:T(8,128)(2,1)S(1)}, bf16[1,80,128]{2,1,0:T(8,128)(2,1)S(1)}, u32[]{:S(2)}, u32[]{:S(2)}) collective-permute-start(bf16[1,80,128]{2,1,0:T(8,128)(2,1)S(1)} %bitcast.7), channel_id=1, source_target_pairs={{0,4},{1,5},{2,6},{3,7},{4,0},{5,1},{6,2},{7,3},{8,12},{9,13},{10,... | collective-permute-start | bytes 61448 | tf_op jit(solution)/shard_map/ppermute | solution.py:451
  7.3 9.7 %collective-permute-start.2 = (bf16[1,64,384]{2,1,0:T(8,128)(2,1)}, bf16[1,64,384]{2,1,0:T(8,128)(2,1)S(1)}, u32[]{:S(2)}, u32[]{:S(2)}) collective-permute-start(bf16[1,64,384]{2,1,0:T(8,128)(2,1)} %bitcast.9), channel_id=1, source_target_pairs={{0,12},{1,13},{2,14},{3,15},{4,8},{5,9},{6,10},{7,11},{8,4},{9,5},... | collective-permute-start | bytes 147464 | tf_op jit(solution)/shard_map/ppermute | solution.py:451
  11.0 5.9 %collective-permute-start.1 = (bf16[1,64,384]{2,1,0:T(8,128)(2,1)}, bf16[1,64,384]{2,1,0:T(8,128)(2,1)S(1)}, u32[]{:S(2)}, u32[]{:S(2)}) collective-permute-start(bf16[1,64,384]{2,1,0:T(8,128)(2,1)} %bitcast.10), channel_id=1, source_target_pairs={{0,8},{1,9},{2,10},{3,11},{4,12},{5,13},{6,14},{7,15},{8,0},{9,1},... | collective-permute-start | bytes 147464 | tf_op jit(solution)/shard_map/ppermute | solution.py:451
  11.7 5.3 %collective-permute-start = (bf16[1,64,384]{2,1,0:T(8,128)(2,1)}, bf16[1,64,384]{2,1,0:T(8,128)(2,1)S(1)}, u32[]{:S(2)}, u32[]{:S(2)}) collective-permute-start(bf16[1,64,384]{2,1,0:T(8,128)(2,1)} %bitcast.11), channel_id=1, source_target_pairs={{0,4},{1,5},{2,6},{3,7},{4,0},{5,1},{6,2},{7,3},{8,12},{9,13},{10,... | collective-permute-start | bytes 147464 | tf_op jit(solution)/shard_map/ppermute | solution.py:451
  12.4 4.5 %collective-permute-start.7 = (bf16[4,80,128]{2,1,0:T(8,128)(2,1)S(1)}, bf16[4,80,128]{2,1,0:T(8,128)(2,1)S(1)}, u32[]{:S(2)}, u32[]{:S(2)}) collective-permute-start(bf16[4,80,128]{2,1,0:T(8,128)(2,1)S(1)} %pad_maximum_fusion.1.refs_0_.refs_4_), channel_id=1, source_target_pairs={{0,2},{1,3},{2,0},{3,1},{4,6},{5,7},{6,4},{7,5},{8,10},{9,11},{10,... | collective-permute-start | bytes 245768 | tf_op jit(solution)/shard_map/ppermute | solution.py:451
  14.1 3.7 %collective-permute-start.6 = (bf16[4,80,128]{2,1,0:T(8,128)(2,1)S(1)}, bf16[4,80,128]{2,1,0:T(8,128)(2,1)S(1)}, u32[]{:S(2)}, u32[]{:S(2)}) collective-permute-start(bf16[4,80,128]{2,1,0:T(8,128)(2,1)S(1)} %pad_maximum_fusion.1.refs_0_.refs_4_), channel_id=1, source_target_pairs={{0,1},{1,0},{2,3},{3,2},{4,5},{5,4},{6,7},{7,6},{8,9},{9,8},{10,11... | collective-permute-start | bytes 245768 | tf_op jit(solution)/shard_map/ppermute | solution.py:451
  16.9 2.8 %collective-permute-start.8 = (bf16[4,80,128]{2,1,0:T(8,128)(2,1)S(1)}, bf16[4,80,128]{2,1,0:T(8,128)(2,1)S(1)}, u32[]{:S(2)}, u32[]{:S(2)}) collective-permute-start(bf16[4,80,128]{2,1,0:T(8,128)(2,1)S(1)} %collective-permute-done.7.refs_0_.refs_1_.refs_5_), channel_id=1, source_target_pairs={{0,1},{1,0},{2,3},{3,2},{4,5},{5,4},{6,7},{7,6},{8,9},{9,8},{10,11... | collective-permute-start | bytes 245768 | tf_op jit(solution)/shard_map/ppermute | solution.py:451
  95.7 3.2 %collective-permute-start.11 = (f32[1,2048]{1,0:T(1,128)S(1)}, f32[1,2048]{1,0:T(1,128)S(1)}, u32[]{:S(2)}, u32[]{:S(2)}) collective-permute-start(f32[1,2048]{1,0:T(1,128)S(1)} %get-tuple-element.23.refs_0_), channel_id=1, source_target_pairs={{0,3},{1,2},{2,1},{3,0},{4,7},{5,6},{6,5},{7,4},{8,11},{9,10},{10,... | collective-permute-start | bytes 24584 | tf_op jit(solution)/shard_map/ppermute | solution.py:451
  97.5 3.7 %collective-permute-start.10 = (f32[1,2048]{1,0:T(1,128)S(1)}, f32[1,2048]{1,0:T(1,128)S(1)}, u32[]{:S(2)}, u32[]{:S(2)}) collective-permute-start(f32[1,2048]{1,0:T(1,128)S(1)} %get-tuple-element.23.refs_0_), channel_id=1, source_target_pairs={{0,2},{1,3},{2,0},{3,1},{4,6},{5,7},{6,4},{7,5},{8,10},{9,11},{10,... | collective-permute-start | bytes 24584 | tf_op jit(solution)/shard_map/ppermute | solution.py:451
  97.9 3.3 %collective-permute-start.9 = (f32[1,2048]{1,0:T(1,128)S(1)}, f32[1,2048]{1,0:T(1,128)S(1)}, u32[]{:S(2)}, u32[]{:S(2)}) collective-permute-start(f32[1,2048]{1,0:T(1,128)S(1)} %get-tuple-element.23.refs_0_), channel_id=1, source_target_pairs={{0,1},{1,0},{2,3},{3,2},{4,5},{5,4},{6,7},{7,6},{8,9},{9,8},{10,11... | collective-permute-start | bytes 24584 | tf_op jit(solution)/shard_map/ppermute | solution.py:451
  175.8 3.1 %collective-permute-start.14 = (f32[1,2048]{1,0:T(1,128)S(1)}, f32[1,2048]{1,0:T(1,128)S(1)}, u32[]{:S(2)}, u32[]{:S(2)}) collective-permute-start(f32[1,2048]{1,0:T(1,128)S(1)} %get-tuple-element.25.refs_0_), channel_id=1, source_target_pairs={{0,3},{1,2},{2,1},{3,0},{4,7},{5,6},{6,5},{7,4},{8,11},{9,10},{10,... | collective-permute-start | bytes 24584 | tf_op jit(solution)/shard_map/ppermute | solution.py:451
  175.8 3.7 %collective-permute-start.13 = (f32[1,2048]{1,0:T(1,128)S(1)}, f32[1,2048]{1,0:T(1,128)S(1)}, u32[]{:S(2)}, u32[]{:S(2)}) collective-permute-start(f32[1,2048]{1,0:T(1,128)S(1)} %get-tuple-element.25.refs_0_), channel_id=1, source_target_pairs={{0,2},{1,3},{2,0},{3,1},{4,6},{5,7},{6,4},{7,5},{8,10},{9,11},{10,... | collective-permute-start | bytes 24584 | tf_op jit(solution)/shard_map/ppermute | solution.py:451
  176.3 3.2 %collective-permute-start.12 = (f32[1,2048]{1,0:T(1,128)S(1)}, f32[1,2048]{1,0:T(1,128)S(1)}, u32[]{:S(2)}, u32[]{:S(2)}) collective-permute-start(f32[1,2048]{1,0:T(1,128)S(1)} %get-tuple-element.25.refs_0_), channel_id=1, source_target_pairs={{0,1},{1,0},{2,3},{3,2},{4,5},{5,4},{6,7},{7,6},{8,9},{9,8},{10,11... | collective-permute-start | bytes 24584 | tf_op jit(solution)/shard_map/ppermute | solution.py:451

commit v16 on v14

--- a/solution.py
+++ b/solution.py
@@ -151,6 +151,15 @@
         s = spread_rows(taug, xaug[:, at], p_refs[slot], beside)
         return s, jnp.exp2(logws[:, at] * LOG2E) / s
 
+    if tiles == 3:
+        least, weight = step(0, 0, None)
+        for tile in range(1, tiles):
+            s, weight = step(tile, tile % 2, weight)
+            least = jnp.minimum(least, s)
+        for begin in range(0, total, LANES):
+            add_columns(p_refs[0], weight, col_refs, slice(begin, begin + LANES))
+        return least
+
     def two_steps(pair, carry):
         least, weight = carry
         s1, weight1 = step(2 * pair + 1, 1, weight)
@@ -163,6 +172,10 @@
     for begin in range(0, total, LANES):
         add_columns(p_refs[1], weight, col_refs, slice(begin, begin + LANES))
     return jnp.minimum(least, s)
+
+
+def lane_tiles(width):
+    return [slice(begin, begin + LANES) for begin in range(0, width, LANES)]
 
 
 def lane_totals(col_refs, out_ref):
@@ -282,10 +295,27 @@
     finish_sums(xaug, logws, taug, least, p0, col_refs, out_ref)
 
 
+def careful_plan(taug, right, p_ref, plan_ref):
+    total = taug.shape[0]
+    reach = min(total, 2048)
+    pieces = [slice(begin, begin + reach) for begin in range(0, total, reach)]
+    peak = jnp.full((1, p_ref.shape[1]), FLOOR, jnp.float32)
+    for rows in pieces:
+        p_ref[rows, :] = exponents(taug[rows, :], right)
+        peak = jnp.maximum(peak, jnp.max(p_ref[rows, :], axis=0, keepdims=True))
+    sums = jnp.zeros(peak.shape, jnp.float32)
+    for rows in pieces:
+        sums += jnp.sum(jnp.exp2(p_ref[rows, :] - peak), axis=0, keepdims=True)
+    shift = peak + jnp.log2(sums)
+    for rows in pieces:
+        plan_ref[rows, :] = jnp.exp2(p_ref[rows, :] - shift).astype(jnp.bfloat16)
+
+
 def map_kernel(flips, parts, n_t, feat, xaug, old, g, q, logw, *refs):
     lines, refs = refs[: len(flips)], refs[len(flips) :]
     ts = refs[:n_t]
-    mapped_ref, pot_ref, taug, p_ref, plan_ref, coords = refs[n_t:]
+    mapped_ref, pot_ref, taug, *p_refs, coords = refs[n_t:]
+    p_refs, plan_refs = p_refs[: len(p_refs) // 2], p_refs[len(p_refs) // 2 :]
     taug[...] = old[...]
     potential = renew_targets(lines, flips, parts, g[...], q[...], logw[...], taug)[0]
     pot_ref[...] = potential[:, :LANES] * (1.0 / LOG2E)
@@ -294,32 +324,28 @@
         for block in range(part.shape[0]):
             coords[:, place * LANES : (place + 1) * LANES] = part[block, :feat, :]
             place += 1
-    total = taug.shape[0]
-    right = xaug[:, : p_ref.shape[1]]
-    s = spread_rows(taug, right, p_ref, lambda rows: None)
-    weight = 1.0 / s
-    for begin in range(0, total, LANES):
-        rows = slice(begin, begin + LANES)
-        plan_ref[rows, :] = (p_ref[rows, :] * weight).astype(jnp.bfloat16)
-
-    @pl.when(jnp.logical_not(jnp.min(s) >= SMALL_ROW))
+    sides, first = [], 0
+    repeats = mapped_ref.shape[1] // p_refs[0].shape[1] if len(p_refs) == 1 else 1
+    for p_ref, plan_ref in list(zip(p_refs, plan_refs)) * repeats:
+        sides.append((slice(first, first + p_ref.shape[1]), p_ref, plan_ref))
+        first += p_ref.shape[1]
+    least = []
+    for at, p_ref, plan_ref in sides:
+        s = spread_rows(taug, xaug[:, at], p_ref, lambda rows: None)
+        least += [s[:, tile] for tile in lane_tiles(s.shape[1])]
+        weight = 1.0 / s
+        for begin in range(0, taug.shape[0], LANES):
+            rows = slice(begin, begin + LANES)
+            plan_ref[rows, :] = (p_ref[rows, :] * weight).astype(jnp.bfloat16)
+        mapped_ref[:, at] = jnp.dot(coords[...], plan_ref[...], preferred_element_type=jnp.float32)
+
+    @pl.when(jnp.logical_not(jnp.min(functools.reduce(jnp.minimum, least)) >= SMALL_ROW))
     def _():
-        reach = min(total, 2048)
-        peak = jnp.full(s.shape, FLOOR, jnp.float32)
-        for begin in range(0, total, reach):
-            rows = slice(begin, begin + reach)
-            p_ref[rows, :] = exponents(taug[rows, :], right)
-            peak = jnp.maximum(peak, jnp.max(p_ref[rows, :], axis=0, keepdims=True))
-        sums = jnp.zeros(s.shape, jnp.float32)
-        for begin in range(0, total, reach):
-            rows = slice(begin, begin + reach)
-            sums += jnp.sum(jnp.exp2(p_ref[rows, :] - peak), axis=0, keepdims=True)
-        shift = peak + jnp.log2(sums)
-        for begin in range(0, total, reach):
-            rows = slice(begin, begin + reach)
-            plan_ref[rows, :] = jnp.exp2(p_ref[rows, :] - shift).astype(jnp.bfloat16)
-
-    mapped_ref[...] = jnp.dot(coords[...], plan_ref[...], preferred_element_type=jnp.float32)
+        for at, p_ref, plan_ref in sides:
+            careful_plan(taug, xaug[:, at], p_ref, plan_ref)
+            mapped_ref[:, at] = jnp.dot(
+                coords[...], plan_ref[...], preferred_element_type=jnp.float32
+            )
 
 
 def swap(value, count, step):
@@ -424,6 +450,8 @@
         p_scratch,
         p_scratch if small else pltpu.VMEM((8, LANES), f32),
     ] + [pltpu.VMEM((total // 16, LANES), f32)] * 16
+    p_wide = pltpu.VMEM((total, 4 * LANES), f32)
+    wide_scratch = [p_wide, p_wide] + scratch[2:] if rows == 12 * LANES and small else scratch
     xaug, taug, sums, logw, q = call(
         functools.partial(near_kernel, parts, feat),
         [inverse_eps, logws, xs, taug_mine, taug_rest, taug_theirs] + ts,
@@ -447,9 +475,10 @@
             functools.partial(next_kernel, flips, parts),
             [logws, xaug, taug, g, q, logw] + exchange(sums),
             [line, line],
-            [pltpu.VMEM((total, DEPTH), bf16)] + scratch,
+            [pltpu.VMEM((total, DEPTH), bf16)] + wide_scratch,
             scalars=0,
         )
+    sides = [2 * LANES, own_sources - 2 * LANES] if small else [LANES]
     mapped, potential = call(
         functools.partial(map_kernel, flips, parts, len(ts), feat),
         [xaug if small else xaug[:, :own_sources], taug, g, q, logw] + exchange(sums) + ts,
@@ -459,10 +488,10 @@
         ],
         [
             pltpu.VMEM((total, DEPTH), bf16),
-            pltpu.VMEM((total, own_sources), f32),
-            pltpu.VMEM((total, own_sources), bf16),
-            pltpu.VMEM((feat, total), bf16),
-        ],
+        ]
+        + [pltpu.VMEM((total, side), f32) for side in sides]
+        + [pltpu.VMEM((total, side), bf16) for side in sides]
+        + [pltpu.VMEM((feat, total), bf16)],
         scalars=0,
     )
     return (mapped, potential.reshape(own_targets))

time: 181 us -> 182 us (level)
  Pallas kernels: 154 us -> 156 us
where the time goes in v16:
time: 182 us
  Pallas kernels  156 us (86%)
  starting transfers between devices  15.8 us (9%)
  waiting for transfers between devices  8.25 us (5%)
    pallas_call x6, Pallas kernels, call(): pl.pallas_call(kernel, out_shape=outs, in_specs=[smem] * scalars + [vmem]...  156 us
    ppermute x15, starting transfers between devices, swap(): lax.ppermute(value, AXIS, [(source, source ^ step) for source in range(co...  15.8 us
    ppermute x15, waiting for transfers between devices, swap(): lax.ppermute(value, AXIS, [(source, source ^ step) for source in range(co...  8.25 us
  transfers between devices with their start and end apart: 15, of which 6 were waited for; matrix products, arithmetic and copies ran while one was open for 0% of the time, Pallas kernels for 0%

profile of v16, /device:TPU:0, one launch (start us, length us, event | category | flops | bytes accessed | tf_op | source)
XLA Modules:
  0.0 182.0 jit_solution(8281042098947353729)
XLA Ops:
  0.6 0.0 copy-start
  0.6 0.1 pad.11.clone
  0.7 0.8 maximum_maximum_fusion
  1.6 5.1 %collective-permute-start.2 = (bf16[1,80,128]{2,1,0:T(8,128)(2,1)S(1)}, bf16[1,80,128]{2,1,0:T(8,128)(2,1)S(1)}, u32[]{:S(2)}, u32[]{:S(2)}) collective-permute-start(bf16[1,80,128]{2,1,0:T(8,128)(2,1)S(1)} %bitcast.5), channel_id=1, source_target_pairs={{0,12},{1,13},{2,14},{3,15},{4,8},{5,9},{6,10},{7,11},{8,4},{9,5},... | collective-permute-start | bytes 61448 | tf_op jit(solution)/shard_map/ppermute | solution.py:352
  6.7 0.0 collective-permute-start.1
  6.7 0.6 collective-permute-start
  7.3 0.0 copy-done
  7.3 3.7 %collective-permute-start.5 = (bf16[1,64,384]{2,1,0:T(8,128)(2,1)S(1)}, bf16[1,64,384]{2,1,0:T(8,128)(2,1)S(1)}, u32[]{:S(2)}, u32[]{:S(2)}) collective-permute-start(bf16[1,64,384]{2,1,0:T(8,128)(2,1)S(1)} %bitcast.9), channel_id=1, source_target_pairs={{0,12},{1,13},{2,14},{3,15},{4,8},{5,9},{6,10},{7,11},{8,4},{9,5},... | collective-permute-start | bytes 147464 | tf_op jit(solution)/shard_map/ppermute | solution.py:352
  11.1 0.0 collective-permute-start.4
  11.7 0.0 collective-permute-done.2
  11.7 0.7 collective-permute-start.3
  12.4 0.0 collective-permute-done.1
  12.4 0.0 collective-permute-done
  12.4 1.7 collective-permute-start.6
  14.2 0.0 collective-permute-start.7
  14.2 0.3 shard_map.68.mine
  14.5 2.5 %collective-permute-done.6.refs_0_.refs_1_.refs_5_ = bf16[4,80,128]{2,1,0:T(8,128)(2,1)S(1)} collective-permute-done((bf16[4,80,128]{2,1,0:T(8,128)(2,1)S(1)}, bf16[4,80,128]{2,1,0:T(8,128)(2,1)S(1)}, u32[]{:S(2)}, u32[]{:S(2)}) %collective-permute-start.6) | collective-permute-done | bytes 81952 | tf_op jit(solution)/shard_map/ppermute | solution.py:352
  17.0 0.0 collective-permute-start.8
  17.0 0.0 collective-permute-done.5
  17.0 0.0 collective-permute-done.4
  17.0 0.0 collective-permute-done.3
  17.0 0.3 shard_map.69.rest
  17.3 0.0 collective-permute-done.7.refs_0_.refs_2_.refs_6_
  17.3 0.3 shard_map.70.theirs
  17.6 0.6 collective-permute-done.8.refs_3_.refs_7_
  18.2 74.7 %shard_map.71 = (bf16[256,1536]{1,0:T(8,128)(2,1)S(1)}, bf16[2048,256]{1,0:T(8,128)(2,1)S(1)}, f32[1,2048]{1,0:T(1,128)S(1)}, f32[1,2048]{1,0:T(1,128)S(1)}, f32[1,2048]{1,0:T(1,128)S(1)}) custom-call(f32[1]{0:T(128)S(6)} %copy.7.inverse, f32[1,1536]{1,0:T(1,128)S(1)} %reshape.27.logws, bf16[4,64,384]{2,1,0:T(8,128)(2,1)S(1)} %pad_maximum_fusion.xs, ...), custom_call_target="tpu_custom_call" | custom-call | tf_op jit(solution)/shard_map/pallas_call | solution.py:407
  92.9 1.5 collective-permute-start.11
  94.4 0.4 collective-permute-start.10
  94.8 0.1 collective-permute-start.9
  94.9 1.2 collective-permute-done.11.refs_3_
  96.1 2.0 %collective-permute-done.10.refs_2_ = f32[1,2048]{1,0:T(1,128)S(1)} collective-permute-done((f32[1,2048]{1,0:T(1,128)S(1)}, f32[1,2048]{1,0:T(1,128)S(1)}, u32[]{:S(2)}, u32[]{:S(2)}) %collective-permute-start.10) | collective-permute-done | bytes 8224 | tf_op jit(solution)/shard_map/ppermute | solution.py:352
  98.1 0.0 collective-permute-done.9.refs_1_
  98.1 74.6 %shard_map.72 = (f32[1,2048]{1,0:T(1,128)S(1)}, f32[1,2048]{1,0:T(1,128)S(1)}) custom-call(f32[1,1536]{1,0:T(1,128)S(1)} %reshape.27.logws, bf16[256,1536]{1,0:T(8,128)(2,1)S(1)} %get-tuple-element.15.xaug, bf16[2048,256]{1,0:T(8,128)(2,1)S(1)} %get-tuple-element.16.old, f32[1,2048]{1,0:T(1,128)S(1)} %get-tuple-element.17.g.logw, ...), custom_call_target="tpu_custom_call" | custom-call | tf_op jit(solution)/shard_map/pallas_call | solution.py:407
  172.7 0.1 collective-permute-start.14
  172.7 0.8 collective-permute-start.13
  173.6 1.0 collective-permute-start.12
  174.6 1.2 collective-permute-done.14.refs_3_
  175.8 0.7 collective-permute-done.13.refs_2_
  176.5 0.0 collective-permute-done.12.refs_1_
  176.5 5.5 %shard_map.73 = (f32[64,384]{1,0:T(8,128)}, f32[1,128]{1,0:T(1,128)}) custom-call(bf16[256,1536]{1,0:T(8,128)(2,1)S(1)} %get-tuple-element.15.xaug, bf16[2048,256]{1,0:T(8,128)(2,1)S(1)} %get-tuple-element.16.old, f32[1,2048]{1,0:T(1,128)S(1)} %get-tuple-element.20.g, f32[1,2048]{1,0:T(1,128)S(1)} %get-tuple-element.18.q, ...), custom_call_target="tpu_custom_call" | custom-call | tf_op jit(solution)/shard_map/pallas_call | solution.py:407
  (5 shorter events, 0.1 us)
Async XLA Ops:
  0.6 6.7 %copy-start = (bf16[64,384]{1,0:T(8,128)(2,1)S(1)}, bf16[64,384]{1,0:T(8,128)(2,1)}, u32[]{:S(2)}) copy-start(bf16[64,384]{1,0:T(8,128)(2,1)} %param.5) | copy-start | bytes 147460
  1.6 10.2 %collective-permute-start.2 = (bf16[1,80,128]{2,1,0:T(8,128)(2,1)S(1)}, bf16[1,80,128]{2,1,0:T(8,128)(2,1)S(1)}, u32[]{:S(2)}, u32[]{:S(2)}) collective-permute-start(bf16[1,80,128]{2,1,0:T(8,128)(2,1)S(1)} %bitcast.5), channel_id=1, source_target_pairs={{0,12},{1,13},{2,14},{3,15},{4,8},{5,9},{6,10},{7,11},{8,4},{9,5},... | collective-permute-start | bytes 61448 | tf_op jit(solution)/shard_map/ppermute | solution.py:352
  6.7 5.8 %collective-permute-start.1 = (bf16[1,80,128]{2,1,0:T(8,128)(2,1)S(1)}, bf16[1,80,128]{2,1,0:T(8,128)(2,1)S(1)}, u32[]{:S(2)}, u32[]{:S(2)}) collective-permute-start(bf16[1,80,128]{2,1,0:T(8,128)(2,1)S(1)} %bitcast.6), channel_id=1, source_target_pairs={{0,8},{1,9},{2,10},{3,11},{4,12},{5,13},{6,14},{7,15},{8,0},{9,1},... | collective-permute-start | bytes 61448 | tf_op jit(solution)/shard_map/ppermute | solution.py:352
  6.7 5.8 %collective-permute-start = (bf16[1,80,128]{2,1,0:T(8,128)(2,1)S(1)}, bf16[1,80,128]{2,1,0:T(8,128)(2,1)S(1)}, u32[]{:S(2)}, u32[]{:S(2)}) collective-permute-start(bf16[1,80,128]{2,1,0:T(8,128)(2,1)S(1)} %bitcast.7), channel_id=1, source_target_pairs={{0,4},{1,5},{2,6},{3,7},{4,0},{5,1},{6,2},{7,3},{8,12},{9,13},{10,... | collective-permute-start | bytes 61448 | tf_op jit(solution)/shard_map/ppermute | solution.py:352
  7.3 9.7 %collective-permute-start.5 = (bf16[1,64,384]{2,1,0:T(8,128)(2,1)S(1)}, bf16[1,64,384]{2,1,0:T(8,128)(2,1)S(1)}, u32[]{:S(2)}, u32[]{:S(2)}) collective-permute-start(bf16[1,64,384]{2,1,0:T(8,128)(2,1)S(1)} %bitcast.9), channel_id=1, source_target_pairs={{0,12},{1,13},{2,14},{3,15},{4,8},{5,9},{6,10},{7,11},{8,4},{9,5},... | collective-permute-start | bytes 147464 | tf_op jit(solution)/shard_map/ppermute | solution.py:352
  11.1 5.9 %collective-permute-start.4 = (bf16[1,64,384]{2,1,0:T(8,128)(2,1)S(1)}, bf16[1,64,384]{2,1,0:T(8,128)(2,1)S(1)}, u32[]{:S(2)}, u32[]{:S(2)}) collective-permute-start(bf16[1,64,384]{2,1,0:T(8,128)(2,1)S(1)} %bitcast.10), channel_id=1, source_target_pairs={{0,8},{1,9},{2,10},{3,11},{4,12},{5,13},{6,14},{7,15},{8,0},{9,1},... | collective-permute-start | bytes 147464 | tf_op jit(solution)/shard_map/ppermute | solution.py:352
  11.7 5.3 %collective-permute-start.3 = (bf16[1,64,384]{2,1,0:T(8,128)(2,1)S(1)}, bf16[1,64,384]{2,1,0:T(8,128)(2,1)S(1)}, u32[]{:S(2)}, u32[]{:S(2)}) collective-permute-start(bf16[1,64,384]{2,1,0:T(8,128)(2,1)S(1)} %bitcast.11), channel_id=1, source_target_pairs={{0,4},{1,5},{2,6},{3,7},{4,0},{5,1},{6,2},{7,3},{8,12},{9,13},{10,... | collective-permute-start | bytes 147464 | tf_op jit(solution)/shard_map/ppermute | solution.py:352
  12.4 4.5 %collective-permute-start.6 = (bf16[4,80,128]{2,1,0:T(8,128)(2,1)S(1)}, bf16[4,80,128]{2,1,0:T(8,128)(2,1)S(1)}, u32[]{:S(2)}, u32[]{:S(2)}) collective-permute-start(bf16[4,80,128]{2,1,0:T(8,128)(2,1)S(1)} %pad_maximum_fusion.1.refs_0_.refs_4_), channel_id=1, source_target_pairs={{0,2},{1,3},{2,0},{3,1},{4,6},{5,7},{6,4},{7,5},{8,10},{9,11},{10,... | collective-permute-start | bytes 245768 | tf_op jit(solution)/shard_map/ppermute | solution.py:352
  14.2 3.1 %collective-permute-start.7 = (bf16[4,80,128]{2,1,0:T(8,128)(2,1)S(1)}, bf16[4,80,128]{2,1,0:T(8,128)(2,1)S(1)}, u32[]{:S(2)}, u32[]{:S(2)}) collective-permute-start(bf16[4,80,128]{2,1,0:T(8,128)(2,1)S(1)} %pad_maximum_fusion.1.refs_0_.refs_4_), channel_id=1, source_target_pairs={{0,1},{1,0},{2,3},{3,2},{4,5},{5,4},{6,7},{7,6},{8,9},{9,8},{10,11... | collective-permute-start | bytes 245768 | tf_op jit(solution)/shard_map/ppermute | solution.py:352
  17.0 1.3 collective-permute-start.8
  92.9 3.1 %collective-permute-start.11 = (f32[1,2048]{1,0:T(1,128)S(1)}, f32[1,2048]{1,0:T(1,128)S(1)}, u32[]{:S(2)}, u32[]{:S(2)}) collective-permute-start(f32[1,2048]{1,0:T(1,128)S(1)} %get-tuple-element.19.refs_0_), channel_id=1, source_target_pairs={{0,3},{1,2},{2,1},{3,0},{4,7},{5,6},{6,5},{7,4},{8,11},{9,10},{10,... | collective-permute-start | bytes 24584 | tf_op jit(solution)/shard_map/ppermute | solution.py:352
  94.4 3.7 %collective-permute-start.10 = (f32[1,2048]{1,0:T(1,128)S(1)}, f32[1,2048]{1,0:T(1,128)S(1)}, u32[]{:S(2)}, u32[]{:S(2)}) collective-permute-start(f32[1,2048]{1,0:T(1,128)S(1)} %get-tuple-element.19.refs_0_), channel_id=1, source_target_pairs={{0,2},{1,3},{2,0},{3,1},{4,6},{5,7},{6,4},{7,5},{8,10},{9,11},{10,... | collective-permute-start | bytes 24584 | tf_op jit(solution)/shard_map/ppermute | solution.py:352
  94.8 3.3 %collective-permute-start.9 = (f32[1,2048]{1,0:T(1,128)S(1)}, f32[1,2048]{1,0:T(1,128)S(1)}, u32[]{:S(2)}, u32[]{:S(2)}) collective-permute-start(f32[1,2048]{1,0:T(1,128)S(1)} %get-tuple-element.19.refs_0_), channel_id=1, source_target_pairs={{0,1},{1,0},{2,3},{3,2},{4,5},{5,4},{6,7},{7,6},{8,9},{9,8},{10,11... | collective-permute-start | bytes 24584 | tf_op jit(solution)/shard_map/ppermute | solution.py:352
  172.7 3.1 %collective-permute-start.14 = (f32[1,2048]{1,0:T(1,128)S(1)}, f32[1,2048]{1,0:T(1,128)S(1)}, u32[]{:S(2)}, u32[]{:S(2)}) collective-permute-start(f32[1,2048]{1,0:T(1,128)S(1)} %get-tuple-element.21.refs_0_), channel_id=1, source_target_pairs={{0,3},{1,2},{2,1},{3,0},{4,7},{5,6},{6,5},{7,4},{8,11},{9,10},{10,... | collective-permute-start | bytes 24584 | tf_op jit(solution)/shard_map/ppermute | solution.py:352
  172.7 3.7 %collective-permute-start.13 = (f32[1,2048]{1,0:T(1,128)S(1)}, f32[1,2048]{1,0:T(1,128)S(1)}, u32[]{:S(2)}, u32[]{:S(2)}) collective-permute-start(f32[1,2048]{1,0:T(1,128)S(1)} %get-tuple-element.21.refs_0_), channel_id=1, source_target_pairs={{0,2},{1,3},{2,0},{3,1},{4,6},{5,7},{6,4},{7,5},{8,10},{9,11},{10,... | collective-permute-start | bytes 24584 | tf_op jit(solution)/shard_map/ppermute | solution.py:352
  173.6 2.9 %collective-permute-start.12 = (f32[1,2048]{1,0:T(1,128)S(1)}, f32[1,2048]{1,0:T(1,128)S(1)}, u32[]{:S(2)}, u32[]{:S(2)}) collective-permute-start(f32[1,2048]{1,0:T(1,128)S(1)} %get-tuple-element.21.refs_0_), channel_id=1, source_target_pairs={{0,1},{1,0},{2,3},{3,2},{4,5},{5,4},{6,7},{7,6},{8,9},{9,8},{10,11... | collective-permute-start | bytes 24584 | tf_op jit(solution)/shard_map/ppermute | solution.py:352

commit v17 on v14

--- a/solution.py
+++ b/solution.py
@@ -150,6 +150,15 @@
         at = tile_columns(tile, width)
         s = spread_rows(taug, xaug[:, at], p_refs[slot], beside)
         return s, jnp.exp2(logws[:, at] * LOG2E) / s
+
+    if tiles == 3:
+        least, weight = step(0, 0, None)
+        for tile in range(1, tiles):
+            s, weight = step(tile, tile % 2, weight)
+            least = jnp.minimum(least, s)
+        for begin in range(0, total, LANES):
+            add_columns(p_refs[0], weight, col_refs, slice(begin, begin + LANES))
+        return least
 
     def two_steps(pair, carry):
         least, weight = carry
@@ -340,13 +349,6 @@
     return [held] + [swap(held, count, digit << low) for digit in range(1, 1 << width)]
 
 
-def gather_chips(block, count):
-    parts = [block[None]]
-    for low, width in chip_stages(count):
-        parts = gather_stage(parts, count, low, width)
-    return parts
-
-
 def gather_line(block, count):
     parts = [block[None]]
     for low, width in chip_stages(count)[:-1]:
@@ -371,7 +373,9 @@
     f32, bf16 = jnp.float32, jnp.bfloat16
     total = count * own_targets
     small = total <= 4096
-    width = 2 * LANES if small else LANES
+    width = LANES
+    if small:
+        width = 4 * LANES if source_points.shape[1] % (3 * LANES) == 0 else 2 * LANES
     vmem = pl.BlockSpec(memory_space=pltpu.VMEM)
     smem = pl.BlockSpec(memory_space=pltpu.SMEM)
     params = pltpu.CompilerParams(vmem_limit_bytes=(24 if small else 63) << 20)
@@ -396,23 +400,29 @@
         return jnp.concatenate(rows, axis=0).reshape(1, -1).astype(f32)
 
     packed, points = lax.optimization_barrier((packed, source_points))
-    mine = gather_chips(packed, count)
-    theirs = [swap(part, count, 1) for part in mine]
-    parts, low = len(mine), chip_stages(count)[-1][0]
-    ts = mine + theirs
+    low, last_width = chip_stages(count)[-1]
+    parts = 1 << last_width
+    held = gather_line(packed, count)
     (taug_mine,) = call(
         functools.partial(part_kernel, feat),
-        [inverse_eps, mine[0]],
-        [staged_shape(mine[:1])],
-    )
+        [inverse_eps, held],
+        [staged_shape([held])],
+    )
+    last, _ = lax.optimization_barrier((held, taug_mine))
+    both = [[held, swap(last, count, 1)]]
+    for digit in range(1, parts):
+        both.append([swap(held, count, core | (digit << low)) for core in range(2)])
+    mine, theirs = [pair[0] for pair in both], [pair[1] for pair in both]
+    ts = mine + theirs
     (taug_theirs,) = call(
         functools.partial(part_kernel, feat),
         [inverse_eps, theirs[0]],
         [staged_shape(theirs[:1])],
     )
+    tied = lax.optimization_barrier((*mine[1:], taug_theirs))
     (taug_rest,) = call(
         functools.partial(part_kernel, feat),
-        [inverse_eps] + mine[1:],
+        [inverse_eps] + list(tied[:-1]),
         [staged_shape(mine[1:])],
     )
     xs = gather_line(points, count)

time: 181 us -> 181 us (level)
  transfers between devices with their start and end apart: 15 -> 15, of which waited for: 6 -> 7; matrix products, arithmetic and copies ran while one was open for 0% -> 0% of each run, Pallas kernels for 0% -> 0%
where the time goes in v17:
time: 181 us
  Pallas kernels  154 us (85%)
  starting transfers between devices  16.1 us (9%)
  waiting for transfers between devices  8.16 us (5%)
    pallas_call x6, Pallas kernels, call(): pl.pallas_call(kernel, out_shape=outs, in_specs=[smem] * scalars + [vmem]...  154 us
    ppermute x15, starting transfers between devices, swap(): lax.ppermute(value, AXIS, [(source, source ^ step) for source in range(co...  16.1 us
    ppermute x15, waiting for transfers between devices, swap(): lax.ppermute(value, AXIS, [(source, source ^ step) for source in range(co...  8.16 us
  transfers between devices with their start and end apart: 15, of which 7 were waited for; matrix products, arithmetic and copies ran while one was open for 0% of the time, Pallas kernels for 0%

profile of v17, /device:TPU:0, one launch (start us, length us, event | category | flops | bytes accessed | tf_op | source)
XLA Modules:
  0.0 181.0 jit_solution(3216660559213714317)
XLA Ops:
  0.6 0.0 copy-start
  0.6 0.1 pad.11.clone
  0.7 0.8 maximum_maximum_fusion
  1.6 5.1 %collective-permute-start.2 = (bf16[1,80,128]{2,1,0:T(8,128)(2,1)S(1)}, bf16[1,80,128]{2,1,0:T(8,128)(2,1)S(1)}, u32[]{:S(2)}, u32[]{:S(2)}) collective-permute-start(bf16[1,80,128]{2,1,0:T(8,128)(2,1)S(1)} %bitcast.5), channel_id=1, source_target_pairs={{0,12},{1,13},{2,14},{3,15},{4,8},{5,9},{6,10},{7,11},{8,4},{9,5},... | collective-permute-start | bytes 61448 | tf_op jit(solution)/shard_map/ppermute | solution.py:335
  6.7 0.0 collective-permute-start.1
  6.7 0.6 collective-permute-start
  7.3 0.0 copy-done
  7.3 3.7 %collective-permute-start.5 = (bf16[1,64,384]{2,1,0:T(8,128)(2,1)S(1)}, bf16[1,64,384]{2,1,0:T(8,128)(2,1)S(1)}, u32[]{:S(2)}, u32[]{:S(2)}) collective-permute-start(bf16[1,64,384]{2,1,0:T(8,128)(2,1)S(1)} %bitcast.9), channel_id=1, source_target_pairs={{0,12},{1,13},{2,14},{3,15},{4,8},{5,9},{6,10},{7,11},{8,4},{9,5},... | collective-permute-start | bytes 147464 | tf_op jit(solution)/shard_map/ppermute | solution.py:335
  11.1 0.0 collective-permute-start.4
  11.7 0.0 collective-permute-done.2
  11.7 0.7 collective-permute-start.3
  12.4 0.0 collective-permute-done.1
  12.4 0.0 collective-permute-done
  12.5 0.1 collective-permute-start.8
  12.5 1.7 collective-permute-start.6
  14.3 0.3 shard_map.68.mine
  14.5 0.0 collective-permute-done.5
  14.5 0.2 collective-permute-start.7
  14.8 1.4 collective-permute-done.4
  16.2 0.3 collective-permute-done.3
  16.4 0.0 collective-permute-done.7.refs_0_.refs_2_.refs_6_
  16.4 0.3 shard_map.69.theirs
  16.7 2.3 %collective-permute-done.6.refs_0_.refs_1_.refs_5_ = bf16[4,80,128]{2,1,0:T(8,128)(2,1)S(1)} collective-permute-done((bf16[4,80,128]{2,1,0:T(8,128)(2,1)S(1)}, bf16[4,80,128]{2,1,0:T(8,128)(2,1)S(1)}, u32[]{:S(2)}, u32[]{:S(2)}) %collective-permute-start.6) | collective-permute-done | bytes 81952 | tf_op jit(solution)/shard_map/ppermute | solution.py:335
  19.0 0.3 shard_map.70.rest
  19.3 0.0 collective-permute-done.8.refs_3_.refs_7_
  19.3 74.6 %shard_map.71 = (bf16[256,1536]{1,0:T(8,128)(2,1)S(1)}, bf16[2048,256]{1,0:T(8,128)(2,1)S(1)}, f32[1,2048]{1,0:T(1,128)S(1)}, f32[1,2048]{1,0:T(1,128)S(1)}, f32[1,2048]{1,0:T(1,128)S(1)}) custom-call(f32[1]{0:T(128)S(6)} %copy.7.inverse, f32[1,1536]{1,0:T(1,128)S(1)} %reshape.27.logws, bf16[4,64,384]{2,1,0:T(8,128)(2,1)S(1)} %pad_maximum_fusion.xs, ...), custom_call_target="tpu_custom_call" | custom-call | tf_op jit(solution)/shard_map/pallas_call | solution.py:385
  93.9 0.3 collective-permute-start.11
  94.1 1.4 collective-permute-start.10
  95.5 0.3 collective-permute-start.9
  95.8 1.2 collective-permute-done.11.refs_3_
  97.0 0.8 collective-permute-done.10.refs_2_
  97.8 0.0 collective-permute-done.9.refs_1_
  97.8 74.7 %shard_map.72 = (f32[1,2048]{1,0:T(1,128)S(1)}, f32[1,2048]{1,0:T(1,128)S(1)}) custom-call(f32[1,1536]{1,0:T(1,128)S(1)} %reshape.27.logws, bf16[256,1536]{1,0:T(8,128)(2,1)S(1)} %get-tuple-element.19.xaug, bf16[2048,256]{1,0:T(8,128)(2,1)S(1)} %get-tuple-element.20.old, f32[1,2048]{1,0:T(1,128)S(1)} %get-tuple-element.21.g.logw, ...), custom_call_target="tpu_custom_call" | custom-call | tf_op jit(solution)/shard_map/pallas_call | solution.py:385
  172.5 0.5 collective-permute-start.14
  173.0 1.0 collective-permute-start.13
  174.1 0.4 collective-permute-start.12
  174.5 1.3 collective-permute-done.14.refs_3_
  175.7 1.0 collective-permute-done.13.refs_2_
  176.7 0.0 collective-permute-done.12.refs_1_
  176.7 4.3 %shard_map.73 = (f32[64,384]{1,0:T(8,128)}, f32[1,128]{1,0:T(1,128)}) custom-call(bf16[256,1536]{1,0:T(8,128)(2,1)S(1)} %get-tuple-element.19.xaug, bf16[2048,256]{1,0:T(8,128)(2,1)S(1)} %get-tuple-element.20.old, f32[1,2048]{1,0:T(1,128)S(1)} %get-tuple-element.24.g, f32[1,2048]{1,0:T(1,128)S(1)} %get-tuple-element.22.q, ...), custom_call_target="tpu_custom_call" | custom-call | tf_op jit(solution)/shard_map/pallas_call | solution.py:385
  (5 shorter events, 0.1 us)
Async XLA Ops:
  0.6 6.7 %copy-start = (bf16[64,384]{1,0:T(8,128)(2,1)S(1)}, bf16[64,384]{1,0:T(8,128)(2,1)}, u32[]{:S(2)}) copy-start(bf16[64,384]{1,0:T(8,128)(2,1)} %param.5) | copy-start | bytes 147460
  1.6 10.2 %collective-permute-start.2 = (bf16[1,80,128]{2,1,0:T(8,128)(2,1)S(1)}, bf16[1,80,128]{2,1,0:T(8,128)(2,1)S(1)}, u32[]{:S(2)}, u32[]{:S(2)}) collective-permute-start(bf16[1,80,128]{2,1,0:T(8,128)(2,1)S(1)} %bitcast.5), channel_id=1, source_target_pairs={{0,12},{1,13},{2,14},{3,15},{4,8},{5,9},{6,10},{7,11},{8,4},{9,5},... | collective-permute-start | bytes 61448 | tf_op jit(solution)/shard_map/ppermute | solution.py:335
  6.7 5.8 %collective-permute-start.1 = (bf16[1,80,128]{2,1,0:T(8,128)(2,1)S(1)}, bf16[1,80,128]{2,1,0:T(8,128)(2,1)S(1)}, u32[]{:S(2)}, u32[]{:S(2)}) collective-permute-start(bf16[1,80,128]{2,1,0:T(8,128)(2,1)S(1)} %bitcast.6), channel_id=1, source_target_pairs={{0,8},{1,9},{2,10},{3,11},{4,12},{5,13},{6,14},{7,15},{8,0},{9,1},... | collective-permute-start | bytes 61448 | tf_op jit(solution)/shard_map/ppermute | solution.py:335
  6.7 5.8 %collective-permute-start = (bf16[1,80,128]{2,1,0:T(8,128)(2,1)S(1)}, bf16[1,80,128]{2,1,0:T(8,128)(2,1)S(1)}, u32[]{:S(2)}, u32[]{:S(2)}) collective-permute-start(bf16[1,80,128]{2,1,0:T(8,128)(2,1)S(1)} %bitcast.7), channel_id=1, source_target_pairs={{0,4},{1,5},{2,6},{3,7},{4,0},{5,1},{6,2},{7,3},{8,12},{9,13},{10,... | collective-permute-start | bytes 61448 | tf_op jit(solution)/shard_map/ppermute | solution.py:335
  7.3 7.2 %collective-permute-start.5 = (bf16[1,64,384]{2,1,0:T(8,128)(2,1)S(1)}, bf16[1,64,384]{2,1,0:T(8,128)(2,1)S(1)}, u32[]{:S(2)}, u32[]{:S(2)}) collective-permute-start(bf16[1,64,384]{2,1,0:T(8,128)(2,1)S(1)} %bitcast.9), channel_id=1, source_target_pairs={{0,12},{1,13},{2,14},{3,15},{4,8},{5,9},{6,10},{7,11},{8,4},{9,5},... | collective-permute-start | bytes 147464 | tf_op jit(solution)/shard_map/ppermute | solution.py:335
  11.1 5.1 %collective-permute-start.4 = (bf16[1,64,384]{2,1,0:T(8,128)(2,1)S(1)}, bf16[1,64,384]{2,1,0:T(8,128)(2,1)S(1)}, u32[]{:S(2)}, u32[]{:S(2)}) collective-permute-start(bf16[1,64,384]{2,1,0:T(8,128)(2,1)S(1)} %bitcast.10), channel_id=1, source_target_pairs={{0,8},{1,9},{2,10},{3,11},{4,12},{5,13},{6,14},{7,15},{8,0},{9,1},... | collective-permute-start | bytes 147464 | tf_op jit(solution)/shard_map/ppermute | solution.py:335
  11.7 4.7 %collective-permute-start.3 = (bf16[1,64,384]{2,1,0:T(8,128)(2,1)S(1)}, bf16[1,64,384]{2,1,0:T(8,128)(2,1)S(1)}, u32[]{:S(2)}, u32[]{:S(2)}) collective-permute-start(bf16[1,64,384]{2,1,0:T(8,128)(2,1)S(1)} %bitcast.11), channel_id=1, source_target_pairs={{0,4},{1,5},{2,6},{3,7},{4,0},{5,1},{6,2},{7,3},{8,12},{9,13},{10,... | collective-permute-start | bytes 147464 | tf_op jit(solution)/shard_map/ppermute | solution.py:335
  12.5 6.8 %collective-permute-start.8 = (bf16[4,80,128]{2,1,0:T(8,128)(2,1)S(1)}, bf16[4,80,128]{2,1,0:T(8,128)(2,1)S(1)}, u32[]{:S(2)}, u32[]{:S(2)}) collective-permute-start(bf16[4,80,128]{2,1,0:T(8,128)(2,1)S(1)} %pad_maximum_fusion.1.refs_0_.refs_4_), channel_id=1, source_target_pairs={{0,3},{1,2},{2,1},{3,0},{4,7},{5,6},{6,5},{7,4},{8,11},{9,10},{10,... | collective-permute-start | bytes 245768 | tf_op jit(solution)/shard_map/ppermute | solution.py:335
  12.5 6.5 %collective-permute-start.6 = (bf16[4,80,128]{2,1,0:T(8,128)(2,1)S(1)}, bf16[4,80,128]{2,1,0:T(8,128)(2,1)S(1)}, u32[]{:S(2)}, u32[]{:S(2)}) collective-permute-start(bf16[4,80,128]{2,1,0:T(8,128)(2,1)S(1)} %pad_maximum_fusion.1.refs_0_.refs_4_), channel_id=1, source_target_pairs={{0,2},{1,3},{2,0},{3,1},{4,6},{5,7},{6,4},{7,5},{8,10},{9,11},{10,... | collective-permute-start | bytes 245768 | tf_op jit(solution)/shard_map/ppermute | solution.py:335
  14.5 1.9 %collective-permute-start.7 = (bf16[4,80,128]{2,1,0:T(8,128)(2,1)S(1)}, bf16[4,80,128]{2,1,0:T(8,128)(2,1)S(1)}, u32[]{:S(2)}, u32[]{:S(2)}) collective-permute-start(bf16[4,80,128]{2,1,0:T(8,128)(2,1)S(1)} %pad_maximum_fusion.1.refs_0_.refs_4_), channel_id=1, source_target_pairs={{0,1},{1,0},{2,3},{3,2},{4,5},{5,4},{6,7},{7,6},{8,9},{9,8},{10,11... | collective-permute-start | bytes 245768 | tf_op jit(solution)/shard_map/ppermute | solution.py:335
  93.9 3.1 %collective-permute-start.11 = (f32[1,2048]{1,0:T(1,128)S(1)}, f32[1,2048]{1,0:T(1,128)S(1)}, u32[]{:S(2)}, u32[]{:S(2)}) collective-permute-start(f32[1,2048]{1,0:T(1,128)S(1)} %get-tuple-element.23.refs_0_), channel_id=1, source_target_pairs={{0,3},{1,2},{2,1},{3,0},{4,7},{5,6},{6,5},{7,4},{8,11},{9,10},{10,... | collective-permute-start | bytes 24584 | tf_op jit(solution)/shard_map/ppermute | solution.py:335
  94.1 3.7 %collective-permute-start.10 = (f32[1,2048]{1,0:T(1,128)S(1)}, f32[1,2048]{1,0:T(1,128)S(1)}, u32[]{:S(2)}, u32[]{:S(2)}) collective-permute-start(f32[1,2048]{1,0:T(1,128)S(1)} %get-tuple-element.23.refs_0_), channel_id=1, source_target_pairs={{0,2},{1,3},{2,0},{3,1},{4,6},{5,7},{6,4},{7,5},{8,10},{9,11},{10,... | collective-permute-start | bytes 24584 | tf_op jit(solution)/shard_map/ppermute | solution.py:335
  95.5 2.3 %collective-permute-start.9 = (f32[1,2048]{1,0:T(1,128)S(1)}, f32[1,2048]{1,0:T(1,128)S(1)}, u32[]{:S(2)}, u32[]{:S(2)}) collective-permute-start(f32[1,2048]{1,0:T(1,128)S(1)} %get-tuple-element.23.refs_0_), channel_id=1, source_target_pairs={{0,1},{1,0},{2,3},{3,2},{4,5},{5,4},{6,7},{7,6},{8,9},{9,8},{10,11... | collective-permute-start | bytes 24584 | tf_op jit(solution)/shard_map/ppermute | solution.py:335
  172.5 3.2 %collective-permute-start.14 = (f32[1,2048]{1,0:T(1,128)S(1)}, f32[1,2048]{1,0:T(1,128)S(1)}, u32[]{:S(2)}, u32[]{:S(2)}) collective-permute-start(f32[1,2048]{1,0:T(1,128)S(1)} %get-tuple-element.25.refs_0_), channel_id=1, source_target_pairs={{0,3},{1,2},{2,1},{3,0},{4,7},{5,6},{6,5},{7,4},{8,11},{9,10},{10,... | collective-permute-start | bytes 24584 | tf_op jit(solution)/shard_map/ppermute | solution.py:335
  173.0 3.7 %collective-permute-start.13 = (f32[1,2048]{1,0:T(1,128)S(1)}, f32[1,2048]{1,0:T(1,128)S(1)}, u32[]{:S(2)}, u32[]{:S(2)}) collective-permute-start(f32[1,2048]{1,0:T(1,128)S(1)} %get-tuple-element.25.refs_0_), channel_id=1, source_target_pairs={{0,2},{1,3},{2,0},{3,1},{4,6},{5,7},{6,4},{7,5},{8,10},{9,11},{10,... | collective-permute-start | bytes 24584 | tf_op jit(solution)/shard_map/ppermute | solution.py:335
  174.1 2.6 %collective-permute-start.12 = (f32[1,2048]{1,0:T(1,128)S(1)}, f32[1,2048]{1,0:T(1,128)S(1)}, u32[]{:S(2)}, u32[]{:S(2)}) collective-permute-start(f32[1,2048]{1,0:T(1,128)S(1)} %get-tuple-element.25.refs_0_), channel_id=1, source_target_pairs={{0,1},{1,0},{2,3},{3,2},{4,5},{5,4},{6,7},{7,6},{8,9},{9,8},{10,11... | collective-permute-start | bytes 24584 | tf_op jit(solution)/shard_map/ppermute | solution.py:335

commit v18 on v14

--- a/solution.py
+++ b/solution.py
@@ -99,9 +99,9 @@
     return jnp.dot(left, right, preferred_element_type=jnp.float32)
 
 
-def spread_rows(taug, right, p_ref, beside):
+def spread_rows(taug, right, p_ref, beside, reach=512):
     total, width = taug.shape[0], right.shape[1]
-    reach = min(total, 512)
+    reach = min(total, reach)
     sums = jnp.zeros((8, width), jnp.float32)
     for begin in range(0, total, reach):
         e = exponents(taug[begin : begin + reach, :], right)
@@ -135,7 +135,7 @@
     return pl.ds(pl.multiple_of(tile * width, width), width)
 
 
-def add_sources(xaug, logws, taug, p_refs, col_refs):
+def add_sources(xaug, logws, taug, p_refs, col_refs, reach=512):
     total = taug.shape[0]
     width = p_refs[0].shape[1]
     tiles = xaug.shape[1] // width
@@ -148,8 +148,17 @@
                 add_columns(p_refs[1 - slot], held, col_refs, rows)
 
         at = tile_columns(tile, width)
-        s = spread_rows(taug, xaug[:, at], p_refs[slot], beside)
+        s = spread_rows(taug, xaug[:, at], p_refs[slot], beside, reach)
         return s, jnp.exp2(logws[:, at] * LOG2E) / s
+
+    if tiles == 3:
+        least, weight = step(0, 0, None)
+        for tile in range(1, tiles):
+            s, weight = step(tile, tile % 2, weight)
+            least = jnp.minimum(least, s)
+        for begin in range(0, total, LANES):
+            add_columns(p_refs[0], weight, col_refs, slice(begin, begin + LANES))
+        return least
 
     def two_steps(pair, carry):
         least, weight = carry
@@ -267,7 +276,7 @@
     stage_targets(ts[parts + 1 :], scale, taug, begin, feat)
     for col_ref in col_refs:
         col_ref[...] = jnp.zeros_like(col_ref)
-    least = add_sources(xaug, logws, taug, (p0, p1), col_refs)
+    least = add_sources(xaug, logws, taug, (p0, p1), col_refs, 256)
     finish_sums(xaug, logws, taug, least, p0, col_refs, out_ref)
 
 
@@ -371,7 +380,9 @@
     f32, bf16 = jnp.float32, jnp.bfloat16
     total = count * own_targets
     small = total <= 4096
-    width = 2 * LANES if small else LANES
+    width = LANES
+    if small:
+        width = 4 * LANES if source_points.shape[1] % (3 * LANES) == 0 else 2 * LANES
     vmem = pl.BlockSpec(memory_space=pltpu.VMEM)
     smem = pl.BlockSpec(memory_space=pltpu.SMEM)
     params = pltpu.CompilerParams(vmem_limit_bytes=(24 if small else 63) << 20)

time: 181 us -> 183 us (1.011)
  Pallas kernels: 154 us -> 156 us
where the time goes in v18:
time: 183 us; the launch traced here: 182 us
  Pallas kernels  156 us (85%)
  starting transfers between devices  15.8 us (9%)
  waiting for transfers between devices  8.24 us (5%)
    pallas_call x6, Pallas kernels, call(): pl.pallas_call(kernel, out_shape=outs, in_specs=[smem] * scalars + [vmem]...  156 us
    ppermute x15, starting transfers between devices, swap(): lax.ppermute(value, AXIS, [(source, source ^ step) for source in range(co...  15.8 us
    ppermute x15, waiting for transfers between devices, swap(): lax.ppermute(value, AXIS, [(source, source ^ step) for source in range(co...  8.24 us
  transfers between devices with their start and end apart: 15, of which 6 were waited for; matrix products, arithmetic and copies ran while one was open for 0% of the time, Pallas kernels for 0%

profile of v18, /device:TPU:0, one launch (start us, length us, event | category | flops | bytes accessed | tf_op | source)
XLA Modules:
  0.0 182.3 jit_solution(2551154437857667684)
XLA Ops:
  0.6 0.0 copy-start
  0.6 0.1 pad.11.clone
  0.7 0.8 maximum_maximum_fusion
  1.6 5.1 %collective-permute-start.2 = (bf16[1,80,128]{2,1,0:T(8,128)(2,1)S(1)}, bf16[1,80,128]{2,1,0:T(8,128)(2,1)S(1)}, u32[]{:S(2)}, u32[]{:S(2)}) collective-permute-start(bf16[1,80,128]{2,1,0:T(8,128)(2,1)S(1)} %bitcast.5), channel_id=1, source_target_pairs={{0,12},{1,13},{2,14},{3,15},{4,8},{5,9},{6,10},{7,11},{8,4},{9,5},... | collective-permute-start | bytes 61448 | tf_op jit(solution)/shard_map/ppermute | solution.py:335
  6.7 0.0 collective-permute-start.1
  6.7 0.6 collective-permute-start
  7.3 0.0 copy-done
  7.3 3.7 %collective-permute-start.5 = (bf16[1,64,384]{2,1,0:T(8,128)(2,1)S(1)}, bf16[1,64,384]{2,1,0:T(8,128)(2,1)S(1)}, u32[]{:S(2)}, u32[]{:S(2)}) collective-permute-start(bf16[1,64,384]{2,1,0:T(8,128)(2,1)S(1)} %bitcast.9), channel_id=1, source_target_pairs={{0,12},{1,13},{2,14},{3,15},{4,8},{5,9},{6,10},{7,11},{8,4},{9,5},... | collective-permute-start | bytes 147464 | tf_op jit(solution)/shard_map/ppermute | solution.py:335
  11.1 0.0 collective-permute-start.4
  11.7 0.0 collective-permute-done.2
  11.7 0.7 collective-permute-start.3
  12.4 0.0 collective-permute-done.1
  12.4 0.0 collective-permute-done
  12.4 1.7 collective-permute-start.6
  14.2 0.0 collective-permute-start.7
  14.2 0.3 shard_map.68.mine
  14.5 2.5 %collective-permute-done.6.refs_0_.refs_1_.refs_5_ = bf16[4,80,128]{2,1,0:T(8,128)(2,1)S(1)} collective-permute-done((bf16[4,80,128]{2,1,0:T(8,128)(2,1)S(1)}, bf16[4,80,128]{2,1,0:T(8,128)(2,1)S(1)}, u32[]{:S(2)}, u32[]{:S(2)}) %collective-permute-start.6) | collective-permute-done | bytes 81952 | tf_op jit(solution)/shard_map/ppermute | solution.py:335
  17.0 0.0 collective-permute-start.8
  17.0 0.0 collective-permute-done.5
  17.0 0.0 collective-permute-done.4
  17.0 0.0 collective-permute-done.3
  17.0 0.3 shard_map.69.rest
  17.3 0.0 collective-permute-done.7.refs_0_.refs_2_.refs_6_
  17.3 0.3 shard_map.70.theirs
  17.6 0.6 collective-permute-done.8.refs_3_.refs_7_
  18.2 76.1 %shard_map.71 = (bf16[256,1536]{1,0:T(8,128)(2,1)S(1)}, bf16[2048,256]{1,0:T(8,128)(2,1)S(1)}, f32[1,2048]{1,0:T(1,128)S(1)}, f32[1,2048]{1,0:T(1,128)S(1)}, f32[1,2048]{1,0:T(1,128)S(1)}) custom-call(f32[1]{0:T(128)S(6)} %copy.7.inverse, f32[1,1536]{1,0:T(1,128)S(1)} %reshape.27.logws, bf16[4,64,384]{2,1,0:T(8,128)(2,1)S(1)} %pad_maximum_fusion.xs, ...), custom_call_target="tpu_custom_call" | custom-call | tf_op jit(solution)/shard_map/pallas_call | solution.py:392
  94.3 1.5 collective-permute-start.11
  95.8 0.4 collective-permute-start.10
  96.2 0.1 collective-permute-start.9
  96.3 1.2 collective-permute-done.11.refs_3_
  97.5 2.0 %collective-permute-done.10.refs_2_ = f32[1,2048]{1,0:T(1,128)S(1)} collective-permute-done((f32[1,2048]{1,0:T(1,128)S(1)}, f32[1,2048]{1,0:T(1,128)S(1)}, u32[]{:S(2)}, u32[]{:S(2)}) %collective-permute-start.10) | collective-permute-done | bytes 8224 | tf_op jit(solution)/shard_map/ppermute | solution.py:335
  99.5 0.0 collective-permute-done.9.refs_1_
  99.5 74.7 %shard_map.72 = (f32[1,2048]{1,0:T(1,128)S(1)}, f32[1,2048]{1,0:T(1,128)S(1)}) custom-call(f32[1,1536]{1,0:T(1,128)S(1)} %reshape.27.logws, bf16[256,1536]{1,0:T(8,128)(2,1)S(1)} %get-tuple-element.15.xaug, bf16[2048,256]{1,0:T(8,128)(2,1)S(1)} %get-tuple-element.16.old, f32[1,2048]{1,0:T(1,128)S(1)} %get-tuple-element.17.g.logw, ...), custom_call_target="tpu_custom_call" | custom-call | tf_op jit(solution)/shard_map/pallas_call | solution.py:392
  174.2 0.1 collective-permute-start.14
  174.3 0.8 collective-permute-start.13
  175.1 1.0 collective-permute-start.12
  176.1 1.2 collective-permute-done.14.refs_3_
  177.3 0.7 collective-permute-done.13.refs_2_
  178.0 0.0 collective-permute-done.12.refs_1_
  178.0 4.3 %shard_map.73 = (f32[64,384]{1,0:T(8,128)}, f32[1,128]{1,0:T(1,128)}) custom-call(bf16[256,1536]{1,0:T(8,128)(2,1)S(1)} %get-tuple-element.15.xaug, bf16[2048,256]{1,0:T(8,128)(2,1)S(1)} %get-tuple-element.16.old, f32[1,2048]{1,0:T(1,128)S(1)} %get-tuple-element.20.g, f32[1,2048]{1,0:T(1,128)S(1)} %get-tuple-element.18.q, ...), custom_call_target="tpu_custom_call" | custom-call | tf_op jit(solution)/shard_map/pallas_call | solution.py:392
  (5 shorter events, 0.1 us)
Async XLA Ops:
  0.6 6.7 %copy-start = (bf16[64,384]{1,0:T(8,128)(2,1)S(1)}, bf16[64,384]{1,0:T(8,128)(2,1)}, u32[]{:S(2)}) copy-start(bf16[64,384]{1,0:T(8,128)(2,1)} %param.5) | copy-start | bytes 147460
  1.6 10.2 %collective-permute-start.2 = (bf16[1,80,128]{2,1,0:T(8,128)(2,1)S(1)}, bf16[1,80,128]{2,1,0:T(8,128)(2,1)S(1)}, u32[]{:S(2)}, u32[]{:S(2)}) collective-permute-start(bf16[1,80,128]{2,1,0:T(8,128)(2,1)S(1)} %bitcast.5), channel_id=1, source_target_pairs={{0,12},{1,13},{2,14},{3,15},{4,8},{5,9},{6,10},{7,11},{8,4},{9,5},... | collective-permute-start | bytes 61448 | tf_op jit(solution)/shard_map/ppermute | solution.py:335
  6.7 5.8 %collective-permute-start.1 = (bf16[1,80,128]{2,1,0:T(8,128)(2,1)S(1)}, bf16[1,80,128]{2,1,0:T(8,128)(2,1)S(1)}, u32[]{:S(2)}, u32[]{:S(2)}) collective-permute-start(bf16[1,80,128]{2,1,0:T(8,128)(2,1)S(1)} %bitcast.6), channel_id=1, source_target_pairs={{0,8},{1,9},{2,10},{3,11},{4,12},{5,13},{6,14},{7,15},{8,0},{9,1},... | collective-permute-start | bytes 61448 | tf_op jit(solution)/shard_map/ppermute | solution.py:335
  6.7 5.8 %collective-permute-start = (bf16[1,80,128]{2,1,0:T(8,128)(2,1)S(1)}, bf16[1,80,128]{2,1,0:T(8,128)(2,1)S(1)}, u32[]{:S(2)}, u32[]{:S(2)}) collective-permute-start(bf16[1,80,128]{2,1,0:T(8,128)(2,1)S(1)} %bitcast.7), channel_id=1, source_target_pairs={{0,4},{1,5},{2,6},{3,7},{4,0},{5,1},{6,2},{7,3},{8,12},{9,13},{10,... | collective-permute-start | bytes 61448 | tf_op jit(solution)/shard_map/ppermute | solution.py:335
  7.3 9.7 %collective-permute-start.5 = (bf16[1,64,384]{2,1,0:T(8,128)(2,1)S(1)}, bf16[1,64,384]{2,1,0:T(8,128)(2,1)S(1)}, u32[]{:S(2)}, u32[]{:S(2)}) collective-permute-start(bf16[1,64,384]{2,1,0:T(8,128)(2,1)S(1)} %bitcast.9), channel_id=1, source_target_pairs={{0,12},{1,13},{2,14},{3,15},{4,8},{5,9},{6,10},{7,11},{8,4},{9,5},... | collective-permute-start | bytes 147464 | tf_op jit(solution)/shard_map/ppermute | solution.py:335
  11.1 5.9 %collective-permute-start.4 = (bf16[1,64,384]{2,1,0:T(8,128)(2,1)S(1)}, bf16[1,64,384]{2,1,0:T(8,128)(2,1)S(1)}, u32[]{:S(2)}, u32[]{:S(2)}) collective-permute-start(bf16[1,64,384]{2,1,0:T(8,128)(2,1)S(1)} %bitcast.10), channel_id=1, source_target_pairs={{0,8},{1,9},{2,10},{3,11},{4,12},{5,13},{6,14},{7,15},{8,0},{9,1},... | collective-permute-start | bytes 147464 | tf_op jit(solution)/shard_map/ppermute | solution.py:335
  11.7 5.3 %collective-permute-start.3 = (bf16[1,64,384]{2,1,0:T(8,128)(2,1)S(1)}, bf16[1,64,384]{2,1,0:T(8,128)(2,1)S(1)}, u32[]{:S(2)}, u32[]{:S(2)}) collective-permute-start(bf16[1,64,384]{2,1,0:T(8,128)(2,1)S(1)} %bitcast.11), channel_id=1, source_target_pairs={{0,4},{1,5},{2,6},{3,7},{4,0},{5,1},{6,2},{7,3},{8,12},{9,13},{10,... | collective-permute-start | bytes 147464 | tf_op jit(solution)/shard_map/ppermute | solution.py:335
  12.4 4.5 %collective-permute-start.6 = (bf16[4,80,128]{2,1,0:T(8,128)(2,1)S(1)}, bf16[4,80,128]{2,1,0:T(8,128)(2,1)S(1)}, u32[]{:S(2)}, u32[]{:S(2)}) collective-permute-start(bf16[4,80,128]{2,1,0:T(8,128)(2,1)S(1)} %pad_maximum_fusion.1.refs_0_.refs_4_), channel_id=1, source_target_pairs={{0,2},{1,3},{2,0},{3,1},{4,6},{5,7},{6,4},{7,5},{8,10},{9,11},{10,... | collective-permute-start | bytes 245768 | tf_op jit(solution)/shard_map/ppermute | solution.py:335
  14.2 3.1 %collective-permute-start.7 = (bf16[4,80,128]{2,1,0:T(8,128)(2,1)S(1)}, bf16[4,80,128]{2,1,0:T(8,128)(2,1)S(1)}, u32[]{:S(2)}, u32[]{:S(2)}) collective-permute-start(bf16[4,80,128]{2,1,0:T(8,128)(2,1)S(1)} %pad_maximum_fusion.1.refs_0_.refs_4_), channel_id=1, source_target_pairs={{0,1},{1,0},{2,3},{3,2},{4,5},{5,4},{6,7},{7,6},{8,9},{9,8},{10,11... | collective-permute-start | bytes 245768 | tf_op jit(solution)/shard_map/ppermute | solution.py:335
  17.0 1.3 collective-permute-start.8
  94.3 3.1 %collective-permute-start.11 = (f32[1,2048]{1,0:T(1,128)S(1)}, f32[1,2048]{1,0:T(1,128)S(1)}, u32[]{:S(2)}, u32[]{:S(2)}) collective-permute-start(f32[1,2048]{1,0:T(1,128)S(1)} %get-tuple-element.19.refs_0_), channel_id=1, source_target_pairs={{0,3},{1,2},{2,1},{3,0},{4,7},{5,6},{6,5},{7,4},{8,11},{9,10},{10,... | collective-permute-start | bytes 24584 | tf_op jit(solution)/shard_map/ppermute | solution.py:335
  95.8 3.7 %collective-permute-start.10 = (f32[1,2048]{1,0:T(1,128)S(1)}, f32[1,2048]{1,0:T(1,128)S(1)}, u32[]{:S(2)}, u32[]{:S(2)}) collective-permute-start(f32[1,2048]{1,0:T(1,128)S(1)} %get-tuple-element.19.refs_0_), channel_id=1, source_target_pairs={{0,2},{1,3},{2,0},{3,1},{4,6},{5,7},{6,4},{7,5},{8,10},{9,11},{10,... | collective-permute-start | bytes 24584 | tf_op jit(solution)/shard_map/ppermute | solution.py:335
  96.2 3.3 %collective-permute-start.9 = (f32[1,2048]{1,0:T(1,128)S(1)}, f32[1,2048]{1,0:T(1,128)S(1)}, u32[]{:S(2)}, u32[]{:S(2)}) collective-permute-start(f32[1,2048]{1,0:T(1,128)S(1)} %get-tuple-element.19.refs_0_), channel_id=1, source_target_pairs={{0,1},{1,0},{2,3},{3,2},{4,5},{5,4},{6,7},{7,6},{8,9},{9,8},{10,11... | collective-permute-start | bytes 24584 | tf_op jit(solution)/shard_map/ppermute | solution.py:335
  174.2 3.1 %collective-permute-start.14 = (f32[1,2048]{1,0:T(1,128)S(1)}, f32[1,2048]{1,0:T(1,128)S(1)}, u32[]{:S(2)}, u32[]{:S(2)}) collective-permute-start(f32[1,2048]{1,0:T(1,128)S(1)} %get-tuple-element.21.refs_0_), channel_id=1, source_target_pairs={{0,3},{1,2},{2,1},{3,0},{4,7},{5,6},{6,5},{7,4},{8,11},{9,10},{10,... | collective-permute-start | bytes 24584 | tf_op jit(solution)/shard_map/ppermute | solution.py:335
  174.3 3.7 %collective-permute-start.13 = (f32[1,2048]{1,0:T(1,128)S(1)}, f32[1,2048]{1,0:T(1,128)S(1)}, u32[]{:S(2)}, u32[]{:S(2)}) collective-permute-start(f32[1,2048]{1,0:T(1,128)S(1)} %get-tuple-element.21.refs_0_), channel_id=1, source_target_pairs={{0,2},{1,3},{2,0},{3,1},{4,6},{5,7},{6,4},{7,5},{8,10},{9,11},{10,... | collective-permute-start | bytes 24584 | tf_op jit(solution)/shard_map/ppermute | solution.py:335
  175.1 2.9 %collective-permute-start.12 = (f32[1,2048]{1,0:T(1,128)S(1)}, f32[1,2048]{1,0:T(1,128)S(1)}, u32[]{:S(2)}, u32[]{:S(2)}) collective-permute-start(f32[1,2048]{1,0:T(1,128)S(1)} %get-tuple-element.21.refs_0_), channel_id=1, source_target_pairs={{0,1},{1,0},{2,3},{3,2},{4,5},{5,4},{6,7},{7,6},{8,9},{9,8},{10,11... | collective-permute-start | bytes 24584 | tf_op jit(solution)/shard_map/ppermute | solution.py:335

commit v19 on v14

--- a/solution.py
+++ b/solution.py
@@ -150,6 +150,15 @@
         at = tile_columns(tile, width)
         s = spread_rows(taug, xaug[:, at], p_refs[slot], beside)
         return s, jnp.exp2(logws[:, at] * LOG2E) / s
+
+    if tiles == 3:
+        least, weight = step(0, 0, None)
+        for tile in range(1, tiles):
+            s, weight = step(tile, tile % 2, weight)
+            least = jnp.minimum(least, s)
+        for begin in range(0, total, LANES):
+            add_columns(p_refs[0], weight, col_refs, slice(begin, begin + LANES))
+        return least
 
     def two_steps(pair, carry):
         least, weight = carry
@@ -424,6 +433,8 @@
         p_scratch,
         p_scratch if small else pltpu.VMEM((8, LANES), f32),
     ] + [pltpu.VMEM((total // 16, LANES), f32)] * 16
+    p_wide = pltpu.VMEM((total, 4 * LANES), f32)
+    near_scratch = [p_wide, p_wide] + scratch[2:] if rows == 12 * LANES and small else scratch
     xaug, taug, sums, logw, q = call(
         functools.partial(near_kernel, parts, feat),
         [inverse_eps, logws, xs, taug_mine, taug_rest, taug_theirs] + ts,
@@ -434,7 +445,7 @@
             line,
             line,
         ],
-        scratch,
+        near_scratch,
     )
     flips = [(core, digit) for digit in range(parts) for core in range(2)]
 

time: 181 us -> 181 us (level)
  no operation moved by 1% of the time
where the time goes in v19:
time: 181 us
  Pallas kernels  154 us (85%)
  starting transfers between devices  15.8 us (9%)
  waiting for transfers between devices  8.24 us (5%)
    pallas_call x6, Pallas kernels, call(): pl.pallas_call(kernel, out_shape=outs, in_specs=[smem] * scalars + [vmem]...  154 us
    ppermute x15, starting transfers between devices, swap(): lax.ppermute(value, AXIS, [(source, source ^ step) for source in range(co...  15.8 us
    ppermute x15, waiting for transfers between devices, swap(): lax.ppermute(value, AXIS, [(source, source ^ step) for source in range(co...  8.24 us
  transfers between devices with their start and end apart: 15, of which 6 were waited for; matrix products, arithmetic and copies ran while one was open for 0% of the time, Pallas kernels for 0%

profile of v19, /device:TPU:0, one launch (start us, length us, event | category | flops | bytes accessed | tf_op | source)
XLA Modules:
  0.0 180.6 jit_solution(14958947396549169207)
XLA Ops:
  0.6 0.0 copy-start
  0.6 0.1 pad.11.clone
  0.7 0.8 maximum_maximum_fusion
  1.6 5.1 %collective-permute-start.2 = (bf16[1,80,128]{2,1,0:T(8,128)(2,1)S(1)}, bf16[1,80,128]{2,1,0:T(8,128)(2,1)S(1)}, u32[]{:S(2)}, u32[]{:S(2)}) collective-permute-start(bf16[1,80,128]{2,1,0:T(8,128)(2,1)S(1)} %bitcast.5), channel_id=1, source_target_pairs={{0,12},{1,13},{2,14},{3,15},{4,8},{5,9},{6,10},{7,11},{8,4},{9,5},... | collective-permute-start | bytes 61448 | tf_op jit(solution)/shard_map/ppermute | solution.py:335
  6.7 0.0 collective-permute-start.1
  6.7 0.6 collective-permute-start
  7.3 0.0 copy-done
  7.3 3.7 %collective-permute-start.5 = (bf16[1,64,384]{2,1,0:T(8,128)(2,1)S(1)}, bf16[1,64,384]{2,1,0:T(8,128)(2,1)S(1)}, u32[]{:S(2)}, u32[]{:S(2)}) collective-permute-start(bf16[1,64,384]{2,1,0:T(8,128)(2,1)S(1)} %bitcast.9), channel_id=1, source_target_pairs={{0,12},{1,13},{2,14},{3,15},{4,8},{5,9},{6,10},{7,11},{8,4},{9,5},... | collective-permute-start | bytes 147464 | tf_op jit(solution)/shard_map/ppermute | solution.py:335
  11.1 0.0 collective-permute-start.4
  11.7 0.0 collective-permute-done.2
  11.7 0.7 collective-permute-start.3
  12.4 0.0 collective-permute-done.1
  12.4 0.0 collective-permute-done
  12.4 1.7 collective-permute-start.6
  14.2 0.0 collective-permute-start.7
  14.2 0.3 shard_map.68.mine
  14.5 2.5 %collective-permute-done.6.refs_0_.refs_1_.refs_5_ = bf16[4,80,128]{2,1,0:T(8,128)(2,1)S(1)} collective-permute-done((bf16[4,80,128]{2,1,0:T(8,128)(2,1)S(1)}, bf16[4,80,128]{2,1,0:T(8,128)(2,1)S(1)}, u32[]{:S(2)}, u32[]{:S(2)}) %collective-permute-start.6) | collective-permute-done | bytes 81952 | tf_op jit(solution)/shard_map/ppermute | solution.py:335
  17.0 0.0 collective-permute-start.8
  17.0 0.0 collective-permute-done.5
  17.0 0.0 collective-permute-done.4
  17.0 0.0 collective-permute-done.3
  17.0 0.3 shard_map.69.rest
  17.3 0.0 collective-permute-done.7.refs_0_.refs_2_.refs_6_
  17.3 0.3 shard_map.70.theirs
  17.6 0.6 collective-permute-done.8.refs_3_.refs_7_
  18.2 74.5 %shard_map.71 = (bf16[256,1536]{1,0:T(8,128)(2,1)S(1)}, bf16[2048,256]{1,0:T(8,128)(2,1)S(1)}, f32[1,2048]{1,0:T(1,128)S(1)}, f32[1,2048]{1,0:T(1,128)S(1)}, f32[1,2048]{1,0:T(1,128)S(1)}) custom-call(f32[1]{0:T(128)S(6)} %copy.7.inverse, f32[1,1536]{1,0:T(1,128)S(1)} %reshape.27.logws, bf16[4,64,384]{2,1,0:T(8,128)(2,1)S(1)} %pad_maximum_fusion.xs, ...), custom_call_target="tpu_custom_call" | custom-call | tf_op jit(solution)/shard_map/pallas_call | solution.py:390
  92.8 1.5 collective-permute-start.11
  94.2 0.4 collective-permute-start.10
  94.6 0.1 collective-permute-start.9
  94.7 1.2 collective-permute-done.11.refs_3_
  95.9 2.0 %collective-permute-done.10.refs_2_ = f32[1,2048]{1,0:T(1,128)S(1)} collective-permute-done((f32[1,2048]{1,0:T(1,128)S(1)}, f32[1,2048]{1,0:T(1,128)S(1)}, u32[]{:S(2)}, u32[]{:S(2)}) %collective-permute-start.10) | collective-permute-done | bytes 8224 | tf_op jit(solution)/shard_map/ppermute | solution.py:335
  97.9 0.0 collective-permute-done.9.refs_1_
  97.9 74.6 %shard_map.72 = (f32[1,2048]{1,0:T(1,128)S(1)}, f32[1,2048]{1,0:T(1,128)S(1)}) custom-call(f32[1,1536]{1,0:T(1,128)S(1)} %reshape.27.logws, bf16[256,1536]{1,0:T(8,128)(2,1)S(1)} %get-tuple-element.15.xaug, bf16[2048,256]{1,0:T(8,128)(2,1)S(1)} %get-tuple-element.16.old, f32[1,2048]{1,0:T(1,128)S(1)} %get-tuple-element.17.g.logw, ...), custom_call_target="tpu_custom_call" | custom-call | tf_op jit(solution)/shard_map/pallas_call | solution.py:390
  172.5 0.1 collective-permute-start.14
  172.6 0.8 collective-permute-start.13
  173.4 1.0 collective-permute-start.12
  174.5 1.2 collective-permute-done.14.refs_3_
  175.7 0.7 collective-permute-done.13.refs_2_
  176.3 0.0 collective-permute-done.12.refs_1_
  176.3 4.3 %shard_map.73 = (f32[64,384]{1,0:T(8,128)}, f32[1,128]{1,0:T(1,128)}) custom-call(bf16[256,1536]{1,0:T(8,128)(2,1)S(1)} %get-tuple-element.15.xaug, bf16[2048,256]{1,0:T(8,128)(2,1)S(1)} %get-tuple-element.16.old, f32[1,2048]{1,0:T(1,128)S(1)} %get-tuple-element.20.g, f32[1,2048]{1,0:T(1,128)S(1)} %get-tuple-element.18.q, ...), custom_call_target="tpu_custom_call" | custom-call | tf_op jit(solution)/shard_map/pallas_call | solution.py:390
  (5 shorter events, 0.1 us)
Async XLA Ops:
  0.6 6.7 %copy-start = (bf16[64,384]{1,0:T(8,128)(2,1)S(1)}, bf16[64,384]{1,0:T(8,128)(2,1)}, u32[]{:S(2)}) copy-start(bf16[64,384]{1,0:T(8,128)(2,1)} %param.5) | copy-start | bytes 147460
  1.6 10.2 %collective-permute-start.2 = (bf16[1,80,128]{2,1,0:T(8,128)(2,1)S(1)}, bf16[1,80,128]{2,1,0:T(8,128)(2,1)S(1)}, u32[]{:S(2)}, u32[]{:S(2)}) collective-permute-start(bf16[1,80,128]{2,1,0:T(8,128)(2,1)S(1)} %bitcast.5), channel_id=1, source_target_pairs={{0,12},{1,13},{2,14},{3,15},{4,8},{5,9},{6,10},{7,11},{8,4},{9,5},... | collective-permute-start | bytes 61448 | tf_op jit(solution)/shard_map/ppermute | solution.py:335
  6.7 5.8 %collective-permute-start.1 = (bf16[1,80,128]{2,1,0:T(8,128)(2,1)S(1)}, bf16[1,80,128]{2,1,0:T(8,128)(2,1)S(1)}, u32[]{:S(2)}, u32[]{:S(2)}) collective-permute-start(bf16[1,80,128]{2,1,0:T(8,128)(2,1)S(1)} %bitcast.6), channel_id=1, source_target_pairs={{0,8},{1,9},{2,10},{3,11},{4,12},{5,13},{6,14},{7,15},{8,0},{9,1},... | collective-permute-start | bytes 61448 | tf_op jit(solution)/shard_map/ppermute | solution.py:335
  6.7 5.8 %collective-permute-start = (bf16[1,80,128]{2,1,0:T(8,128)(2,1)S(1)}, bf16[1,80,128]{2,1,0:T(8,128)(2,1)S(1)}, u32[]{:S(2)}, u32[]{:S(2)}) collective-permute-start(bf16[1,80,128]{2,1,0:T(8,128)(2,1)S(1)} %bitcast.7), channel_id=1, source_target_pairs={{0,4},{1,5},{2,6},{3,7},{4,0},{5,1},{6,2},{7,3},{8,12},{9,13},{10,... | collective-permute-start | bytes 61448 | tf_op jit(solution)/shard_map/ppermute | solution.py:335
  7.3 9.7 %collective-permute-start.5 = (bf16[1,64,384]{2,1,0:T(8,128)(2,1)S(1)}, bf16[1,64,384]{2,1,0:T(8,128)(2,1)S(1)}, u32[]{:S(2)}, u32[]{:S(2)}) collective-permute-start(bf16[1,64,384]{2,1,0:T(8,128)(2,1)S(1)} %bitcast.9), channel_id=1, source_target_pairs={{0,12},{1,13},{2,14},{3,15},{4,8},{5,9},{6,10},{7,11},{8,4},{9,5},... | collective-permute-start | bytes 147464 | tf_op jit(solution)/shard_map/ppermute | solution.py:335
  11.1 5.9 %collective-permute-start.4 = (bf16[1,64,384]{2,1,0:T(8,128)(2,1)S(1)}, bf16[1,64,384]{2,1,0:T(8,128)(2,1)S(1)}, u32[]{:S(2)}, u32[]{:S(2)}) collective-permute-start(bf16[1,64,384]{2,1,0:T(8,128)(2,1)S(1)} %bitcast.10), channel_id=1, source_target_pairs={{0,8},{1,9},{2,10},{3,11},{4,12},{5,13},{6,14},{7,15},{8,0},{9,1},... | collective-permute-start | bytes 147464 | tf_op jit(solution)/shard_map/ppermute | solution.py:335
  11.7 5.3 %collective-permute-start.3 = (bf16[1,64,384]{2,1,0:T(8,128)(2,1)S(1)}, bf16[1,64,384]{2,1,0:T(8,128)(2,1)S(1)}, u32[]{:S(2)}, u32[]{:S(2)}) collective-permute-start(bf16[1,64,384]{2,1,0:T(8,128)(2,1)S(1)} %bitcast.11), channel_id=1, source_target_pairs={{0,4},{1,5},{2,6},{3,7},{4,0},{5,1},{6,2},{7,3},{8,12},{9,13},{10,... | collective-permute-start | bytes 147464 | tf_op jit(solution)/shard_map/ppermute | solution.py:335
  12.4 4.5 %collective-permute-start.6 = (bf16[4,80,128]{2,1,0:T(8,128)(2,1)S(1)}, bf16[4,80,128]{2,1,0:T(8,128)(2,1)S(1)}, u32[]{:S(2)}, u32[]{:S(2)}) collective-permute-start(bf16[4,80,128]{2,1,0:T(8,128)(2,1)S(1)} %pad_maximum_fusion.1.refs_0_.refs_4_), channel_id=1, source_target_pairs={{0,2},{1,3},{2,0},{3,1},{4,6},{5,7},{6,4},{7,5},{8,10},{9,11},{10,... | collective-permute-start | bytes 245768 | tf_op jit(solution)/shard_map/ppermute | solution.py:335
  14.2 3.1 %collective-permute-start.7 = (bf16[4,80,128]{2,1,0:T(8,128)(2,1)S(1)}, bf16[4,80,128]{2,1,0:T(8,128)(2,1)S(1)}, u32[]{:S(2)}, u32[]{:S(2)}) collective-permute-start(bf16[4,80,128]{2,1,0:T(8,128)(2,1)S(1)} %pad_maximum_fusion.1.refs_0_.refs_4_), channel_id=1, source_target_pairs={{0,1},{1,0},{2,3},{3,2},{4,5},{5,4},{6,7},{7,6},{8,9},{9,8},{10,11... | collective-permute-start | bytes 245768 | tf_op jit(solution)/shard_map/ppermute | solution.py:335
  17.0 1.3 collective-permute-start.8
  92.8 3.1 %collective-permute-start.11 = (f32[1,2048]{1,0:T(1,128)S(1)}, f32[1,2048]{1,0:T(1,128)S(1)}, u32[]{:S(2)}, u32[]{:S(2)}) collective-permute-start(f32[1,2048]{1,0:T(1,128)S(1)} %get-tuple-element.19.refs_0_), channel_id=1, source_target_pairs={{0,3},{1,2},{2,1},{3,0},{4,7},{5,6},{6,5},{7,4},{8,11},{9,10},{10,... | collective-permute-start | bytes 24584 | tf_op jit(solution)/shard_map/ppermute | solution.py:335
  94.2 3.7 %collective-permute-start.10 = (f32[1,2048]{1,0:T(1,128)S(1)}, f32[1,2048]{1,0:T(1,128)S(1)}, u32[]{:S(2)}, u32[]{:S(2)}) collective-permute-start(f32[1,2048]{1,0:T(1,128)S(1)} %get-tuple-element.19.refs_0_), channel_id=1, source_target_pairs={{0,2},{1,3},{2,0},{3,1},{4,6},{5,7},{6,4},{7,5},{8,10},{9,11},{10,... | collective-permute-start | bytes 24584 | tf_op jit(solution)/shard_map/ppermute | solution.py:335
  94.6 3.3 %collective-permute-start.9 = (f32[1,2048]{1,0:T(1,128)S(1)}, f32[1,2048]{1,0:T(1,128)S(1)}, u32[]{:S(2)}, u32[]{:S(2)}) collective-permute-start(f32[1,2048]{1,0:T(1,128)S(1)} %get-tuple-element.19.refs_0_), channel_id=1, source_target_pairs={{0,1},{1,0},{2,3},{3,2},{4,5},{5,4},{6,7},{7,6},{8,9},{9,8},{10,11... | collective-permute-start | bytes 24584 | tf_op jit(solution)/shard_map/ppermute | solution.py:335
  172.5 3.1 %collective-permute-start.14 = (f32[1,2048]{1,0:T(1,128)S(1)}, f32[1,2048]{1,0:T(1,128)S(1)}, u32[]{:S(2)}, u32[]{:S(2)}) collective-permute-start(f32[1,2048]{1,0:T(1,128)S(1)} %get-tuple-element.21.refs_0_), channel_id=1, source_target_pairs={{0,3},{1,2},{2,1},{3,0},{4,7},{5,6},{6,5},{7,4},{8,11},{9,10},{10,... | collective-permute-start | bytes 24584 | tf_op jit(solution)/shard_map/ppermute | solution.py:335
  172.6 3.7 %collective-permute-start.13 = (f32[1,2048]{1,0:T(1,128)S(1)}, f32[1,2048]{1,0:T(1,128)S(1)}, u32[]{:S(2)}, u32[]{:S(2)}) collective-permute-start(f32[1,2048]{1,0:T(1,128)S(1)} %get-tuple-element.21.refs_0_), channel_id=1, source_target_pairs={{0,2},{1,3},{2,0},{3,1},{4,6},{5,7},{6,4},{7,5},{8,10},{9,11},{10,... | collective-permute-start | bytes 24584 | tf_op jit(solution)/shard_map/ppermute | solution.py:335
  173.4 2.9 %collective-permute-start.12 = (f32[1,2048]{1,0:T(1,128)S(1)}, f32[1,2048]{1,0:T(1,128)S(1)}, u32[]{:S(2)}, u32[]{:S(2)}) collective-permute-start(f32[1,2048]{1,0:T(1,128)S(1)} %get-tuple-element.21.refs_0_), channel_id=1, source_target_pairs={{0,1},{1,0},{2,3},{3,2},{4,5},{5,4},{6,7},{7,6},{8,9},{9,8},{10,11... | collective-permute-start | bytes 24584 | tf_op jit(solution)/shard_map/ppermute | solution.py:335
